TPU v7x, 32 devices: a whole 2x2x4 slice. The times are simulated.
32 devices in a mesh: req: 4 (over x, core), exp: 8 (over z, y).
Axes of the slice: x: 2, y: 2, z: 4, core: 2. Of those that a mesh axis runs over, the one named last changes fastest.
Arguments:
- queries: bfloat16 [4096, 2048], P('req', 'exp'), may hold values from -6 to 6
- keys: bfloat16 [4096, 2048], P('req', 'exp'), may hold values from -15 to 15
- values: bfloat16 [4096, 2048], P('req', 'exp'), may hold values from -6 to 6
- prefix_keys: bfloat16 [4, 4096, 2048], P(None, 'req', 'exp'), may hold values from -15 to 15
- prefix_values: bfloat16 [4, 4096, 2048], P(None, 'req', 'exp'), may hold values from -6 to 6
- lengths: int32 [4, 8], P('req'), may hold values from 1 to 512, 1024 in all within a row
- groups: int32 [4, 8], P('req'), may hold values from 0 to 3
- residual: bfloat16 [4096, 2048], P(('req', 'exp')), may hold values from -6 to 6
- out_proj: bfloat16 [2048, 2048], P('exp'), may hold values from -0.125 to 0.125
- norm_gain: bfloat16 [2048], replicated, may hold values from 0.099609375 to 1.8984375
- expert_ids: int32 [4096, 4], P(('req', 'exp')), may hold values from 0 to 31, all different within a row; in each aligned block of 128 rows (0 to 127, 128 to 255, ...) at most 32 rows name the same one
- expert_gates: bfloat16 [4096, 4], P(('req', 'exp')), may hold values from 0.049804688 to 0.5
- w_gate: bfloat16 [32, 2048, 704], P('exp'), may hold values from -0.125 to 0.125
- w_up: bfloat16 [32, 2048, 704], P('exp'), may hold values from -0.125 to 0.125
- w_down: bfloat16 [32, 704, 2048], P('exp'), may hold values from -0.21875 to 0.21875
Outputs:
- layer_out: bfloat16 [4096, 2048], P(('req', 'exp'))
Inputs may be any that keep to these rules, and one draw needn't show every extreme that they name: The 8 lengths of a row sum to 1024; the longest request of each row has half of 1024 tokens. `expert_ids`: each row names 4 different experts. Among the 128 tokens of one device, no expert is named more than 32 times; on some device some expert is named exactly 32 times.
All inputs are finite; a program needn't handle non-finite values.
Results may differ from a plain program's by a relative error of at most 0.02.
Values may be sent and summed in bfloat16 or wider, within the bound.
No kernel may reach another device: no remote copies, remote signals or barrier semaphores. Data moves between devices by JAX's collectives and lax.ppermute only.
A program may use at most 256 MiB of HBM per device.

v0:
```python
import math

import jax
import jax.numpy as jnp
from jax import lax
from jax.sharding import PartitionSpec as P

HEAD = 128
TOPK = 4
EXPERTS = 32
G = 4
RQ = 8
ROW_TOK = 1024


NEG = -1e30


def token_layout(lengths, groups):
    req_ends = jnp.cumsum(lengths, axis=-1)
    starts = req_ends - lengths
    position = jnp.arange(ROW_TOK, dtype=jnp.int32)
    request = jnp.sum((position[None, :, None] >= req_ends[:, None, :]).astype(jnp.int32), axis=-1)
    onehot = request[:, :, None] == jnp.arange(RQ, dtype=jnp.int32)[None, None, :]
    first_tok = jnp.sum(jnp.where(onehot, starts[:, None, :], 0), axis=-1)
    tok_group = jnp.sum(jnp.where(onehot, groups[:, None, :], 0), axis=-1)
    return (request, position[None, :] - first_tok, tok_group)


def split_blocks(row_count):
    if row_count % 1024 == 0 and row_count > 1024:
        return row_count // 1024
    return 1


def pack_parts(parts):
    return jnp.concatenate([parts[0], parts[1], parts[2]], axis=1)


def unpack_parts(packed, head_count):
    columns = head_count * HEAD
    return (
        packed[:, :columns],
        packed[:, columns : columns + head_count],
        packed[:, columns + head_count :],
    )


def attend_prefix(query_rows, query_group, prefix_k, prefix_v):
    row_count, columns = query_rows.shape
    head_count = columns // HEAD
    span = prefix_k.shape[1]
    key_grid = prefix_k.reshape(G, span, head_count, HEAD)
    val_grid = prefix_v.reshape(G, span, head_count, HEAD)
    blocks = split_blocks(row_count)
    block_len = row_count // blocks
    scaling = 1.0 / math.sqrt(HEAD)

    def per_block(pieces):
        block_q, block_g = pieces
        query_grid = block_q.reshape(block_len, head_count, HEAD)
        scores = (
            jnp.einsum("qhd,gkhd->hqgk", query_grid, key_grid, preferred_element_type=jnp.float32)
            * scaling
        )
        member = block_g[:, None] == jnp.arange(G, dtype=jnp.int32)[None, :]
        scores = jnp.where(member[None, :, :, None], scores, NEG)
        maxima = jnp.max(scores, axis=(2, 3))
        exp_terms = jnp.exp(scores - maxima[:, :, None, None])
        totals = jnp.sum(exp_terms, axis=(2, 3))
        weighted = jnp.einsum(
            "hqgk,gkhd->qhd",
            exp_terms.astype(jnp.bfloat16),
            val_grid,
            preferred_element_type=jnp.float32,
        )
        return (weighted.reshape(block_len, columns), maxima.T, totals.T)

    weighted, maxima, totals = lax.map(
        per_block,
        (query_rows.reshape(blocks, block_len, columns), query_group.reshape(blocks, block_len)),
    )
    return (
        weighted.reshape(row_count, columns),
        maxima.reshape(row_count, head_count),
        totals.reshape(row_count, head_count),
    )


def attend_suffix(queries, keys, values, request, position):
    row_count, columns = queries.shape
    head_count = columns // HEAD
    blocks = split_blocks(row_count)
    block_len = row_count // blocks
    scaling = 1.0 / math.sqrt(HEAD)
    key_grid = keys.reshape(row_count, head_count, HEAD)
    val_grid = values.reshape(row_count, head_count, HEAD)

    def per_block(pieces):
        block_q, block_req, block_pos = pieces
        query_grid = block_q.reshape(block_len, head_count, HEAD)
        scores = (
            jnp.einsum("qhd,khd->hqk", query_grid, key_grid, preferred_element_type=jnp.float32)
            * scaling
        )
        allowed = (request[None, :] == block_req[:, None]) & (
            position[None, :] <= block_pos[:, None]
        )
        scores = jnp.where(allowed[None, :, :], scores, NEG)
        maxima = jnp.max(scores, axis=2)
        exp_terms = jnp.exp(scores - maxima[:, :, None])
        totals = jnp.sum(exp_terms, axis=2)
        weighted = jnp.einsum(
            "hqk,khd->qhd",
            exp_terms.astype(jnp.bfloat16),
            val_grid,
            preferred_element_type=jnp.float32,
        )
        return (weighted.reshape(block_len, columns), maxima.T, totals.T)

    weighted, maxima, totals = lax.map(
        per_block,
        (
            queries.reshape(blocks, block_len, columns),
            request.reshape(blocks, block_len),
            position.reshape(blocks, block_len),
        ),
    )
    return (
        weighted.reshape(row_count, columns),
        maxima.reshape(row_count, head_count),
        totals.reshape(row_count, head_count),
    )


def combine(former, latter):
    weighted_a, maxima_a, totals_a = former
    weighted_b, maxima_b, totals_b = latter
    row_count, head_count = maxima_a.shape
    maxima = jnp.maximum(maxima_a, maxima_b)
    factor_a = jnp.exp(maxima_a - maxima)
    factor_b = jnp.exp(maxima_b - maxima)
    weighted = (
        weighted_a.reshape(row_count, head_count, HEAD) * factor_a[:, :, None]
        + weighted_b.reshape(row_count, head_count, HEAD) * factor_b[:, :, None]
    )
    return (
        weighted.reshape(row_count, head_count * HEAD),
        maxima,
        totals_a * factor_a + totals_b * factor_b,
    )


def per_device(
    queries,
    keys,
    values,
    prefix_keys,
    prefix_values,
    lengths,
    groups,
    residual,
    out_proj,
    norm_gain,
    expert_ids,
    expert_gates,
    w_gate,
    w_up,
    w_down,
):
    row_tok, columns = queries.shape
    head_count = columns // HEAD
    tok_dev = residual.shape[0]
    request, position, tok_group = token_layout(lengths, groups)
    request, position, tok_group = (request[0], position[0], tok_group[0])
    all_groups = lax.all_gather(tok_group, "req", axis=0, tiled=True)
    partial_value = pack_parts(
        attend_prefix(
            lax.all_gather(queries, "req", axis=0, tiled=True),
            all_groups,
            prefix_keys,
            prefix_values,
        )
    )
    returned = lax.all_to_all(partial_value, "req", split_axis=0, concat_axis=0, tiled=True)
    owners = returned.shape[0] // row_tok
    back_w, back_m, back_t = unpack_parts(returned, head_count)
    all_weighted = back_w.reshape(owners, row_tok, head_count, HEAD)
    all_maxima = back_m.reshape(owners, row_tok, head_count)
    all_totals = back_t.reshape(owners, row_tok, head_count)
    maxima = jnp.max(all_maxima, axis=0)
    factor = jnp.exp(all_maxima - maxima[None])
    weighted = jnp.sum(all_weighted * factor[..., None], axis=0).reshape(row_tok, columns)
    prefix_part = (weighted, maxima, jnp.sum(all_totals * factor, axis=0))
    suffix_part = attend_suffix(queries, keys, values, request, position)
    weighted, maxima, totals = combine(prefix_part, suffix_part)
    attended = (
        (weighted.reshape(row_tok, head_count, HEAD) / totals[:, :, None])
        .reshape(row_tok, columns)
        .astype(jnp.bfloat16)
    )
    projected = lax.psum_scatter(
        jnp.dot(attended, out_proj, preferred_element_type=jnp.float32),
        "exp",
        scatter_dimension=0,
        tiled=True,
    )
    stream = residual.astype(jnp.float32) + projected
    meansq = jnp.mean(stream * stream, axis=-1, keepdims=True)
    normed = (stream * lax.rsqrt(meansq + 1e-06) * norm_gain.astype(jnp.float32)).astype(
        jnp.bfloat16
    )
    capacity = max(2, tok_dev // 4)
    flat_ids = expert_ids.reshape(-1)
    onehot = (flat_ids[:, None] == jnp.arange(EXPERTS, dtype=jnp.int32)[None, :]).astype(jnp.int32)
    slot_of = jnp.sum(onehot * (jnp.cumsum(onehot, axis=0) - 1), axis=1)
    source_rows = jnp.arange(tok_dev * TOPK, dtype=jnp.int32) // TOPK
    buffer = (
        jnp.zeros((EXPERTS, capacity, normed.shape[1]), jnp.bfloat16)
        .at[flat_ids, slot_of]
        .set(normed[source_rows])
    )
    exp_count = lax.axis_size("exp")
    exp_dev = w_gate.shape[0]
    received = lax.all_to_all(buffer, "exp", split_axis=0, concat_axis=0, tiled=True)
    slots = received.shape[1]
    grid_in = received.reshape(exp_count, exp_dev, slots, received.shape[2])
    gate_h = jnp.einsum("secd,edf->secf", grid_in, w_gate, preferred_element_type=jnp.float32)
    up_h = jnp.einsum("secd,edf->secf", grid_in, w_up, preferred_element_type=jnp.float32)
    hidden = (jax.nn.silu(gate_h) * up_h).astype(jnp.bfloat16)
    expert_out = jnp.einsum("secf,efd->secd", hidden, w_down, preferred_element_type=jnp.float32)
    returned = lax.all_to_all(
        expert_out.reshape(EXPERTS, slots, received.shape[2]),
        "exp",
        split_axis=0,
        concat_axis=0,
        tiled=True,
    )
    gathered = returned[flat_ids, slot_of] * expert_gates.reshape(-1).astype(jnp.float32)[:, None]
    mixture = jnp.sum(gathered.reshape(tok_dev, TOPK, gathered.shape[1]), axis=1)
    return (stream + mixture).astype(jnp.bfloat16)


def solution(mesh):
    in_specs = (
        P("req", "exp"),
        P("req", "exp"),
        P("req", "exp"),
        P(None, "req", "exp"),
        P(None, "req", "exp"),
        P("req", None),
        P("req", None),
        P(("req", "exp"), None),
        P("exp", None),
        P(),
        P(("req", "exp"), None),
        P(("req", "exp"), None),
        P("exp", None, None),
        P("exp", None, None),
        P("exp", None, None),
    )
    out_specs = P(("req", "exp"), None)
    return jax.shard_map(
        per_device, mesh=mesh, in_specs=in_specs, out_specs=out_specs, check_vma=False
    )
```

profile of v0, /device:TPU:0, one launch (start us, length us, event | category | flops | bytes accessed | tf_op | source)
XLA Modules:
  0.0 921.6 jit_solution(615895969516858211)
XLA Ops:
  8.9 1.3 select_reduce_fusion.1
  10.2 6.2 all_gather.6
  16.4 4.1 copy.83
  20.5 3.0 copy.86
  23.5 4.0 copy.84
  27.5 3.1 copy.87
  30.6 3.6 all-gather.2.cloned.1.call-done
  34.2 191.8 %while.2 = (s32[]{:T(128)}, f32[4,1024,256]{1,2,0:T(8,128)}, f32[4,1024,2]{1,2,0:T(2,128)S(1)}, f32[4,1024,2]{1,2,0:T(2,128)S(1)}, s32[4,1024]{1,0:T(4,128)S(1)}...) while((s32[]{:T(128)}, f32[4,1024,256]{1,2,0:T(8,128)}, ...), condition=%wide.region_6.7_spmd, body=%wide.region_3.6_spmd.sunk | while | flops 4387241984 | bytes 119108224 | solution.py:79
  34.3 1.9 constant_dynamic-slice_fusion.5
  36.1 2.1 copy.140
  38.2 14.1 %fusion.88 = (f32[2,1024]{1,0:T(2,128)S(1)}, f32[2,1024,4,1024]{1,3,2,0:T(8,128)}) fusion(pred[1024,4]{0,1:T(4,128)(4,1)S(1)} %iota_compare_fusion.6, bf16[1024,2,128,1]{0,2,3,1:T(8,128)(2,1)} %bitcast.162, bf16[4,1024,2,128]{3,1,0,2:T(8,128)(2,1)S(1)} %get-tuple-element.225), kind=kOutput, calls=%fused_computation.5.clone.1 | convolution fusion | flops 2172647424 | bytes 36188160 | tf_op jit(solution)/shard_map/while/body/eval_jaxpr/qhd,gkhd->hqgk/dot_general | solution.py:63
  52.3 14.3 %fusion.90 = f32[2,1024]{1,0:T(2,128)S(1)} fusion(f32[2,1024,4,1024]{1,3,2,0:T(8,128)} %get-tuple-element.197, f32[2,1024]{1,0:T(2,128)S(1)} %get-tuple-element.198, pred[1024,4]{0,1:T(4,128)(4,1)S(1)} %iota_compare_fusion.6), kind=kLoop, calls=%fused_computation.6.clone.1 | loop fusion | flops 33552384 | bytes 33574912 | tf_op jit(solution)/shard_map/while/body/eval_jaxpr/reduce_sum | solution.py:70
  66.7 14.5 %fusion.89 = f32[2,1024,128,1]{1,2,3,0:T(8,128)S(1)} fusion(bf16[4,1024,2,128]{1,3,0,2:T(8,128)(2,1)S(1)} %copy-done.4, f32[2,1024,4,1024]{1,3,2,0:T(8,128)} %get-tuple-element.197, f32[2,1024]{1,0:T(2,128)S(1)} %get-tuple-element.198, pred[1024,4]{0,1:T(4,128)(4,1)S(1)} %iota_compare_fusion.6), kind=kOutput, calls=%fused_computation.8.clone.1 | convolution fusion | flops 2181038080 | bytes 36712448 | tf_op jit(solution)/shard_map/while/body/eval_jaxpr/hqgk,gkhd->qhd/dot_general | solution.py:71
  81.1 1.1 constant_dynamic-update-slice_fusion.2
  82.2 1.9 constant_dynamic-slice_fusion.5
  84.1 2.1 copy.140
  86.1 14.1 %fusion.88 = (f32[2,1024]{1,0:T(2,128)S(1)}, f32[2,1024,4,1024]{1,3,2,0:T(8,128)}) fusion(pred[1024,4]{0,1:T(4,128)(4,1)S(1)} %iota_compare_fusion.6, bf16[1024,2,128,1]{0,2,3,1:T(8,128)(2,1)} %bitcast.162, bf16[4,1024,2,128]{3,1,0,2:T(8,128)(2,1)S(1)} %get-tuple-element.225), kind=kOutput, calls=%fused_computation.5.clone.1 | convolution fusion | flops 2172647424 | bytes 36188160 | tf_op jit(solution)/shard_map/while/body/eval_jaxpr/qhd,gkhd->hqgk/dot_general | solution.py:63
  100.3 14.3 %fusion.90 = f32[2,1024]{1,0:T(2,128)S(1)} fusion(f32[2,1024,4,1024]{1,3,2,0:T(8,128)} %get-tuple-element.197, f32[2,1024]{1,0:T(2,128)S(1)} %get-tuple-element.198, pred[1024,4]{0,1:T(4,128)(4,1)S(1)} %iota_compare_fusion.6), kind=kLoop, calls=%fused_computation.6.clone.1 | loop fusion | flops 33552384 | bytes 33574912 | tf_op jit(solution)/shard_map/while/body/eval_jaxpr/reduce_sum | solution.py:70
  114.6 14.5 %fusion.89 = f32[2,1024,128,1]{1,2,3,0:T(8,128)S(1)} fusion(bf16[4,1024,2,128]{1,3,0,2:T(8,128)(2,1)S(1)} %copy-done.4, f32[2,1024,4,1024]{1,3,2,0:T(8,128)} %get-tuple-element.197, f32[2,1024]{1,0:T(2,128)S(1)} %get-tuple-element.198, pred[1024,4]{0,1:T(4,128)(4,1)S(1)} %iota_compare_fusion.6), kind=kOutput, calls=%fused_computation.8.clone.1 | convolution fusion | flops 2181038080 | bytes 36712448 | tf_op jit(solution)/shard_map/while/body/eval_jaxpr/hqgk,gkhd->qhd/dot_general | solution.py:71
  129.1 1.1 constant_dynamic-update-slice_fusion.2
  130.2 1.9 constant_dynamic-slice_fusion.5
  132.0 2.1 copy.140
  134.1 14.1 %fusion.88 = (f32[2,1024]{1,0:T(2,128)S(1)}, f32[2,1024,4,1024]{1,3,2,0:T(8,128)}) fusion(pred[1024,4]{0,1:T(4,128)(4,1)S(1)} %iota_compare_fusion.6, bf16[1024,2,128,1]{0,2,3,1:T(8,128)(2,1)} %bitcast.162, bf16[4,1024,2,128]{3,1,0,2:T(8,128)(2,1)S(1)} %get-tuple-element.225), kind=kOutput, calls=%fused_computation.5.clone.1 | convolution fusion | flops 2172647424 | bytes 36188160 | tf_op jit(solution)/shard_map/while/body/eval_jaxpr/qhd,gkhd->hqgk/dot_general | solution.py:63
  148.2 14.3 %fusion.90 = f32[2,1024]{1,0:T(2,128)S(1)} fusion(f32[2,1024,4,1024]{1,3,2,0:T(8,128)} %get-tuple-element.197, f32[2,1024]{1,0:T(2,128)S(1)} %get-tuple-element.198, pred[1024,4]{0,1:T(4,128)(4,1)S(1)} %iota_compare_fusion.6), kind=kLoop, calls=%fused_computation.6.clone.1 | loop fusion | flops 33552384 | bytes 33574912 | tf_op jit(solution)/shard_map/while/body/eval_jaxpr/reduce_sum | solution.py:70
  162.6 14.5 %fusion.89 = f32[2,1024,128,1]{1,2,3,0:T(8,128)S(1)} fusion(bf16[4,1024,2,128]{1,3,0,2:T(8,128)(2,1)S(1)} %copy-done.4, f32[2,1024,4,1024]{1,3,2,0:T(8,128)} %get-tuple-element.197, f32[2,1024]{1,0:T(2,128)S(1)} %get-tuple-element.198, pred[1024,4]{0,1:T(4,128)(4,1)S(1)} %iota_compare_fusion.6), kind=kOutput, calls=%fused_computation.8.clone.1 | convolution fusion | flops 2181038080 | bytes 36712448 | tf_op jit(solution)/shard_map/while/body/eval_jaxpr/hqgk,gkhd->qhd/dot_general | solution.py:71
  177.0 1.1 constant_dynamic-update-slice_fusion.2
  178.1 1.9 constant_dynamic-slice_fusion.5
  180.0 2.1 copy.140
  182.0 14.1 %fusion.88 = (f32[2,1024]{1,0:T(2,128)S(1)}, f32[2,1024,4,1024]{1,3,2,0:T(8,128)}) fusion(pred[1024,4]{0,1:T(4,128)(4,1)S(1)} %iota_compare_fusion.6, bf16[1024,2,128,1]{0,2,3,1:T(8,128)(2,1)} %bitcast.162, bf16[4,1024,2,128]{3,1,0,2:T(8,128)(2,1)S(1)} %get-tuple-element.225), kind=kOutput, calls=%fused_computation.5.clone.1 | convolution fusion | flops 2172647424 | bytes 36188160 | tf_op jit(solution)/shard_map/while/body/eval_jaxpr/qhd,gkhd->hqgk/dot_general | solution.py:63
  196.2 14.3 %fusion.90 = f32[2,1024]{1,0:T(2,128)S(1)} fusion(f32[2,1024,4,1024]{1,3,2,0:T(8,128)} %get-tuple-element.197, f32[2,1024]{1,0:T(2,128)S(1)} %get-tuple-element.198, pred[1024,4]{0,1:T(4,128)(4,1)S(1)} %iota_compare_fusion.6), kind=kLoop, calls=%fused_computation.6.clone.1 | loop fusion | flops 33552384 | bytes 33574912 | tf_op jit(solution)/shard_map/while/body/eval_jaxpr/reduce_sum | solution.py:70
  210.5 14.5 %fusion.89 = f32[2,1024,128,1]{1,2,3,0:T(8,128)S(1)} fusion(bf16[4,1024,2,128]{1,3,0,2:T(8,128)(2,1)S(1)} %copy-done.4, f32[2,1024,4,1024]{1,3,2,0:T(8,128)} %get-tuple-element.197, f32[2,1024]{1,0:T(2,128)S(1)} %get-tuple-element.198, pred[1024,4]{0,1:T(4,128)(4,1)S(1)} %iota_compare_fusion.6), kind=kOutput, calls=%fused_computation.8.clone.1 | convolution fusion | flops 2181038080 | bytes 36712448 | tf_op jit(solution)/shard_map/while/body/eval_jaxpr/hqgk,gkhd->qhd/dot_general | solution.py:71
  225.0 1.1 constant_dynamic-update-slice_fusion.2
  226.1 4.8 pad_maximum_fusion
  230.9 5.1 all-to-all-start
  236.5 1.2 compare_and_fusion
  237.7 2.9 fusion.14
  240.6 3.2 copy-done.2
  243.8 2.0 fusion.15
  245.8 39.9 %all-to-all-done = f32[4,1024,260]{1,2,0:T(8,128)} async-done(((f32[4,1024,260]{1,2,0:T(8,128)}), f32[4,1024,260]{1,2,0:T(8,128)}, u32[]{:S(2)}, u32[]{:S(2)}) %all-to-all-start) | async-done | bytes 4259872 | tf_op jit(solution)/shard_map/all_to_all | solution.py:185
  285.6 5.0 copy.138
  290.6 1.0 pad.4
  291.7 3.9 copy.115
  295.6 2.3 slice.26
  298.0 6.2 reshape.481
  304.3 5.3 multiply_reduce_fusion.1
  309.6 6.0 divide_convert_fusion
  315.7 4.5 fusion.68
  321.3 1.2 reduce-window.6
  322.9 146.5 %reduce-scatter.2.cloned.1.call-done = f32[128,2048]{1,0:T(8,128)} async-done(((f32[1024,2048]{1,0:T(8,128)}), f32[128,2048]{1,0:T(8,128)}) %reduce-scatter.2.cloned.1.call-update) | async-done | bytes 1048592 | tf_op jit(solution)/shard_map/reduce_scatter | solution.py:202
  469.4 1.5 multiply_reduce_fusion.2
  470.9 1.4 multiply_convert_fusion
  472.3 3.3 gather_fusion
  475.6 2.4 broadcast_in_dim.117
  478.1 91.9 %scatter_fusion = bf16[32,32,2048]{2,1,0:T(8,128)(2,1)} fusion(bf16[32,32,2048]{2,1,0:T(8,128)(2,1)} %broadcast_in_dim.117, s32[512]{0:T(512)S(1)} %bitcast.164, bf16[512,2048]{1,0:T(8,128)(2,1)} %gather_fusion), kind=kCustom, calls=%fused_computation.2 | custom fusion | bytes 6295552 | tf_op jit(solution)/shard_map/scatter | solution.py:221
  570.0 98.5 %all_to_all.19 = bf16[32,32,2048]{2,1,0:T(8,128)(2,1)} all-to-all(bf16[32,32,2048]{2,1,0:T(8,128)(2,1)} %scatter_fusion), channel_id=1, replica_groups=mesh['req'=4,'exp'=8] {'exp'}, dimensions={0} | all-to-all | bytes 8388608 | tf_op jit(solution)/shard_map/all_to_all | solution.py:225
  668.5 10.7 %fusion.10 = f32[4,8,32,704]{3,2,1,0:T(8,128)} fusion(bf16[4,2048,704]{1,2,0:T(8,128)(2,1)} %param.30, bf16[8,4,32,2048]{3,2,1,0:T(8,128)(2,1)} %bitcast.173), kind=kOutput, calls=%fused_computation.20 | convolution fusion | flops 2952790016 | bytes 18612224 | tf_op jit(solution)/shard_map/secd,edf->secf/dot_general | solution.py:229
  679.1 15.2 %fusion.17 = f32[8,4,32,2048]{3,2,0,1:T(8,128)} fusion(bf16[4,704,2048]{2,1,0:T(8,128)(2,1)} %param.31, f32[4,8,32,704]{3,2,1,0:T(8,128)} %fusion.10, bf16[4,2048,704]{1,2,0:T(8,128)(2,1)} %param.29, bf16[8,4,32,2048]{3,2,1,0:T(8,128)(2,1)} %bitcast.174), kind=kOutput, calls=%fused_computation.30 | convolution fusion | flops 5909905408 | bytes 38535168 | tf_op jit(solution)/shard_map/secf,efd->secd/dot_general | solution.py:231
  694.3 7.7 copy.99
  702.0 5.3 all-to-all-start.2
  707.4 182.2 %all-to-all-done.2 = f32[32,32,2048]{2,1,0:T(8,128)} async-done(((f32[32,32,2048]{2,1,0:T(8,128)}), f32[32,32,2048]{2,1,0:T(8,128)}, u32[]{:S(2)}, u32[]{:S(2)}) %all-to-all-start.2) | async-done | bytes 8388640 | tf_op jit(solution)/shard_map/all_to_all | solution.py:232
  889.6 13.3 %gather_fusion.1 = f32[512,2048]{1,0:T(8,128)} fusion(f32[32,32,2048]{2,1,0:T(8,128)} %all-to-all-done.2, s32[512]{0:T(512)S(1)} %bitcast.163), kind=kCustom, calls=%fused_computation.1 | custom fusion | bytes 8392704 | tf_op jit(solution)/shard_map/gather | solution.py:239
  902.9 5.2 gather.10
  908.1 5.5 multiply_reduce_fusion
  913.6 1.0 add_convert_fusion
  (77 shorter events, 4.7 us)
Async XLA Ops:
  6.5 309.1 %copy-start = (bf16[256,2048]{1,0:T(8,128)(2,1)S(1)}, bf16[256,2048]{1,0:T(8,128)(2,1)}, u32[]{:S(2)}) copy-start(bf16[256,2048]{1,0:T(8,128)(2,1)} %param.25) | copy-start | bytes 3145732
  6.5 27.7 %all-gather.2.cloned.1.call-start = ((), (), s32[]{:S(2)}) async-start(), calls=%async_computation.4 | async-start | bytes 2621440 | tf_op jit(solution)/shard_map/all_gather | solution.py:179
  8.2 2.0 copy-start.7
  52.3 14.3 %copy-start.4 = (bf16[4,1024,2,128]{1,3,0,2:T(8,128)(2,1)S(1)}, bf16[4,1024,2,128]{1,3,0,2:T(8,128)(2,1)}, u32[]{:S(2)}) copy-start(bf16[4,1024,2,128]{1,3,0,2:T(8,128)(2,1)} %get-tuple-element.226) | copy-start | bytes 6291460 | tf_op jit(solution)/shard_map/while
  100.3 14.3 %copy-start.4 = (bf16[4,1024,2,128]{1,3,0,2:T(8,128)(2,1)S(1)}, bf16[4,1024,2,128]{1,3,0,2:T(8,128)(2,1)}, u32[]{:S(2)}) copy-start(bf16[4,1024,2,128]{1,3,0,2:T(8,128)(2,1)} %get-tuple-element.226) | copy-start | bytes 6291460 | tf_op jit(solution)/shard_map/while
  148.2 14.3 %copy-start.4 = (bf16[4,1024,2,128]{1,3,0,2:T(8,128)(2,1)S(1)}, bf16[4,1024,2,128]{1,3,0,2:T(8,128)(2,1)}, u32[]{:S(2)}) copy-start(bf16[4,1024,2,128]{1,3,0,2:T(8,128)(2,1)} %get-tuple-element.226) | copy-start | bytes 6291460 | tf_op jit(solution)/shard_map/while
  196.2 14.3 %copy-start.4 = (bf16[4,1024,2,128]{1,3,0,2:T(8,128)(2,1)S(1)}, bf16[4,1024,2,128]{1,3,0,2:T(8,128)(2,1)}, u32[]{:S(2)}) copy-start(bf16[4,1024,2,128]{1,3,0,2:T(8,128)(2,1)} %get-tuple-element.226) | copy-start | bytes 6291460 | tf_op jit(solution)/shard_map/while
  230.9 5.3 copy-start.5
  230.9 5.5 copy-start.9
  230.9 5.6 copy-start.8
  230.9 6.8 copy-start.6
  230.9 54.7 %all-to-all-start = ((f32[4,1024,260]{1,2,0:T(8,128)}), f32[4,1024,260]{1,2,0:T(8,128)}, u32[]{:S(2)}, u32[]{:S(2)}) async-start(f32[4,1024,260]{1,2,0:T(8,128)} %pad_maximum_fusion), calls=%async_computation | async-start | bytes 8650752 | tf_op jit(solution)/shard_map/all_to_all | solution.py:185
  236.0 233.4 %reduce-scatter.2.cloned.1.call-start = ((), (), s32[]{:S(2)}) async-start(), calls=%async_computation.5 | async-start | bytes 9437184 | tf_op jit(solution)/shard_map/reduce_scatter | solution.py:202
  240.6 3.2 copy-start.2
  320.2 0.7 copy-start.11
  320.2 1.1 copy-start.10
  320.2 149.2 %copy-start.3 = (bf16[128,2048]{1,0:T(8,128)(2,1)S(1)}, bf16[128,2048]{1,0:T(8,128)(2,1)}, u32[]{:S(2)}) copy-start(bf16[128,2048]{1,0:T(8,128)(2,1)} %param.24) | copy-start | bytes 1572868
  702.0 5.3 copy-start.12
  702.0 187.6 %all-to-all-start.2 = ((f32[32,32,2048]{2,1,0:T(8,128)}), f32[32,32,2048]{2,1,0:T(8,128)}, u32[]{:S(2)}, u32[]{:S(2)}) async-start(f32[32,32,2048]{2,1,0:T(8,128)} %bitcast.165), calls=%async_computation.3 | async-start | bytes 16777216 | tf_op jit(solution)/shard_map/all_to_all | solution.py:232
  908.1 5.5 copy-start.1
Sparse Core Ops, SparseCore 0:
  8.9 25.2 all-gather.1
  320.3 149.0 reduce-scatter.1
where the time goes:
time: 932 us; the launch traced here: 922 us
  waiting for transfers between devices  373 us (40%)
  local copies, waits for them, and re-layouts  182 us (20%)
  matrix products  154 us (17%)
  blocking collectives  105 us (11%)
  other arithmetic  84.3 us (9%)
  between operations  13.9 us (1%)
  starting transfers between devices  10.6 us (1%)
    all_to_all x1, waiting for transfers between devices, per_device(): lax.all_to_all(expert_out.reshape(EXPERTS, slots, received.shape[2]), 'ex...  182 us
    reduce_scatter x1, waiting for transfers between devices, per_device(): lax.psum_scatter(jnp.dot(attended, out_proj, preferred_element_type=jnp.f...  146 us
    all_to_all x1, blocking collectives, per_device(): lax.all_to_all(buffer, 'exp', split_axis=0, concat_axis=0, tiled=True)  98.5 us
    scatter x1, local copies, waits for them, and re-layouts, per_device(): buffer = jnp.zeros((EXPERTS, capacity, normed.shape[1]), jnp.bfloat16).at...  91.9 us
    dot_general x4, matrix products, per_block(): jnp.einsum('hqgk,gkhd->qhd', exp_terms.astype(jnp.bfloat16), val_grid, pr...  57.8 us
    reduce_sum x4, other arithmetic, per_block(): totals = jnp.sum(exp_terms, axis=(2, 3))  57.2 us
    dot_general x4, matrix products, per_block(): jnp.einsum('qhd,gkhd->hqgk', query_grid, key_grid, preferred_element_type...  56.5 us
    all_to_all x1, waiting for transfers between devices, per_device(): lax.all_to_all(partial_value, 'req', split_axis=0, concat_axis=0, tiled=T...  39.9 us
  transfers between devices with their start and end apart: 4, of which 4 were waited for; matrix products, arithmetic and copies ran while one was open for 3% of the time, Pallas kernels for 0%

commit v1 on v0

--- a/solution.py
+++ b/solution.py
@@ -3,6 +3,8 @@
 import jax
 import jax.numpy as jnp
 from jax import lax
+from jax.experimental import pallas as pl
+from jax.experimental.pallas import tpu as pltpu
 from jax.sharding import PartitionSpec as P
 
 HEAD = 128
@@ -151,7 +153,7 @@
     )
 
 
-def per_device(
+def general_device(
     queries,
     keys,
     values,
@@ -241,6 +243,574 @@
     return (stream + mixture).astype(jnp.bfloat16)
 
 
+BLK = 128
+LOG2E = 1.4426950408889634
+SCORE_SCALE = LOG2E / math.sqrt(HEAD)
+VMEM_BIG = 56 * 1024 * 1024
+
+
+def core_swap(array):
+    return lax.ppermute(array, "req", [(i, i ^ 1) for i in range(4)])
+
+
+def x_swap(array):
+    return lax.ppermute(array, "req", [(i, i ^ 2) for i in range(4)])
+
+
+def y_swap(array):
+    return lax.ppermute(array, "exp", [(i, i ^ 1) for i in range(8)])
+
+
+def z_up(array, sources=3):
+    return lax.ppermute(array, "exp", [(i, i + 2) for i in range(2 * sources)])
+
+
+def z_down(array, sources=3):
+    return lax.ppermute(array, "exp", [(i, i - 2) for i in range(8 - 2 * sources, 8)])
+
+
+def row_meta(lengths, groups):
+    ends = jnp.cumsum(lengths, axis=-1)
+    starts = ends - lengths
+    blocks = jnp.arange(ROW_TOK // BLK, dtype=jnp.int32)[None, :, None] * BLK
+    overlap = (starts[:, None, :] < blocks + BLK) & (ends[:, None, :] > blocks)
+    bits = jnp.zeros(overlap.shape[:2], jnp.int32)
+    for g in range(G):
+        present = jnp.any(overlap & (groups[:, None, :] == g), axis=-1)
+        bits = bits + (present.astype(jnp.int32) << g)
+    return jnp.concatenate([starts, groups, bits], axis=1)
+
+
+def send_halves_kernel(sc_ref, q, k, v, pk, pv, out_qkv, out_pk, out_pv):
+    out_qkv[0] = q[...]
+    out_qkv[1] = k[...]
+    out_qkv[2] = v[...]
+    out_pk[...] = pk[...]
+    out_pv[...] = pv[...]
+
+
+def send_halves(core, q, k, v, pk, pv):
+    rows, span = q.shape[0], pk.shape[1]
+    part = rows // G
+    token_in = pl.BlockSpec((part, HEAD), lambda i, s: (i, 1 - s[0]))
+    prefix_in = pl.BlockSpec((1, span, HEAD), lambda i, s: (i, 0, 1 - s[0]))
+    prefix_out = pl.BlockSpec((1, span, HEAD), lambda i, s: (i, 0, 0))
+    return pl.pallas_call(
+        send_halves_kernel,
+        grid_spec=pltpu.PrefetchScalarGridSpec(
+            num_scalar_prefetch=1,
+            grid=(G,),
+            in_specs=[token_in] * 3 + [prefix_in] * 2,
+            out_specs=[
+                pl.BlockSpec((3, part, HEAD), lambda i, s: (0, i, 0)),
+                prefix_out,
+                prefix_out,
+            ],
+        ),
+        out_shape=(
+            jax.ShapeDtypeStruct((3, rows, HEAD), q.dtype),
+            jax.ShapeDtypeStruct((G, span, HEAD), q.dtype),
+            jax.ShapeDtypeStruct((G, span, HEAD), q.dtype),
+        ),
+        name="send_halves",
+    )(core, q, k, v, pk, pv)
+
+
+def token_columns(meta_ref, row, first_token, count):
+    token = first_token + lax.broadcasted_iota(jnp.int32, (count, 1), 0)
+    group = jnp.full((count, 1), meta_ref[row, RQ], jnp.int32)
+    first = jnp.zeros((count, 1), jnp.int32)
+    for j in range(1, RQ):
+        start = meta_ref[row, j]
+        later = token >= start
+        group = jnp.where(later, meta_ref[row, RQ + j], group)
+        first = jnp.where(later, start, first)
+    return token, group, first
+
+
+def as_row(column):
+    return jnp.transpose(jnp.broadcast_to(column, (BLK, BLK)))[0:1, :]
+
+
+def prefix_kernel(meta_ref, sc_ref, q_ref, ka, kb, va, vb, o_ref, lse_ref):
+    row, block = pl.program_id(0), pl.program_id(1)
+    token, group, unused = token_columns(meta_ref, row, block * BLK, BLK)
+    bits = meta_ref[row, 2 * RQ + block]
+    contract = (((1,), (1,)), ((), ()))
+
+    def attend(g, carry):
+        @pl.when((bits >> g) & 1 == 1)
+        def held():
+            q = q_ref[0]
+            sa = lax.dot_general(q, ka[g], contract, preferred_element_type=jnp.float32)
+            sb = lax.dot_general(q, kb[g], contract, preferred_element_type=jnp.float32)
+            top = jnp.maximum(
+                jnp.max(sa, axis=1, keepdims=True), jnp.max(sb, axis=1, keepdims=True)
+            )
+            pa = jnp.exp2((sa - top) * SCORE_SCALE)
+            pb = jnp.exp2((sb - top) * SCORE_SCALE)
+            total = jnp.sum(pa, axis=1, keepdims=True) + jnp.sum(pb, axis=1, keepdims=True)
+            out = jnp.dot(
+                pa.astype(jnp.bfloat16), va[g], preferred_element_type=jnp.float32
+            ) + jnp.dot(pb.astype(jnp.bfloat16), vb[g], preferred_element_type=jnp.float32)
+            mine = group == g
+            o_ref[0] = jnp.where(mine, out / total, o_ref[0].astype(jnp.float32)).astype(o_ref.dtype)
+            lse = as_row(top * SCORE_SCALE + jnp.log2(total))
+            mine_row = as_row(mine.astype(jnp.float32)) > 0.5
+            here = pl.ds(block, 1)
+            lse_ref[0, here, :] = jnp.where(mine_row, lse, lse_ref[0, here, :])
+
+        return carry
+
+    lax.fori_loop(0, G, attend, 0)
+
+
+def prefix_attend(meta, core, q, pk, pk_other, pv, pv_other, out_dtype):
+    rows, tokens, unused = q.shape
+    span = pk.shape[1]
+    own = pl.BlockSpec((G, span, HEAD), lambda r, b, m, s: (0, 0, s[0]))
+    other = pl.BlockSpec((G, span, HEAD), lambda r, b, m, s: (0, 0, 0))
+    blocks = tokens // BLK
+    return pl.pallas_call(
+        prefix_kernel,
+        grid_spec=pltpu.PrefetchScalarGridSpec(
+            num_scalar_prefetch=2,
+            grid=(rows, blocks),
+            in_specs=[
+                pl.BlockSpec((1, BLK, HEAD), lambda r, b, m, s: (r, b, 0)),
+                own,
+                other,
+                own,
+                other,
+            ],
+            out_specs=[
+                pl.BlockSpec((1, BLK, HEAD), lambda r, b, m, s: (r, b, 0)),
+                pl.BlockSpec((1, blocks, BLK), lambda r, b, m, s: (r, 0, 0)),
+            ],
+        ),
+        out_shape=(
+            jax.ShapeDtypeStruct((rows, tokens, HEAD), out_dtype),
+            jax.ShapeDtypeStruct((rows, blocks, BLK), jnp.float32),
+        ),
+        compiler_params=pltpu.CompilerParams(vmem_limit_bytes=VMEM_BIG),
+        cost_estimate=pl.CostEstimate(
+            flops=rows * tokens * span * HEAD * 8 * 4,
+            bytes_accessed=4 * G * span * HEAD * 2,
+            transcendentals=0,
+        ),
+        name="prefix_attend",
+    )(meta, core, q, pk, pk_other, pv, pv_other)
+
+
+SUF = 256
+
+
+def suffix_kernel(meta_ref, q_ref, k_ref, v_ref, o_ref, lse_ref):
+    row, block = pl.program_id(0), pl.program_id(1)
+    for i in range(ROW_TOK // SUF):
+
+        @pl.when(block == i)
+        def held():
+            width = (i + 1) * SUF
+            token, unused, first = token_columns(meta_ref, row, i * SUF, SUF)
+            s = lax.dot_general(
+                q_ref[0],
+                k_ref[0, :width, :],
+                (((1,), (1,)), ((), ())),
+                preferred_element_type=jnp.float32,
+            )
+            other = lax.broadcasted_iota(jnp.int32, (SUF, width), 1)
+            s = jnp.where((other >= first) & (other <= token), s, NEG)
+            top = jnp.max(s, axis=1, keepdims=True)
+            p = jnp.exp2((s - top) * SCORE_SCALE)
+            total = jnp.sum(p, axis=1, keepdims=True)
+            out = jnp.dot(
+                p.astype(jnp.bfloat16), v_ref[0, :width, :], preferred_element_type=jnp.float32
+            )
+            o_ref[0] = out / total
+            lse = top * SCORE_SCALE + jnp.log2(total)
+            for part in range(SUF // BLK):
+                place = i * (SUF // BLK) + part
+                lse_ref[0, place : place + 1, :] = as_row(lse[part * BLK : (part + 1) * BLK])
+
+
+def suffix_attend(meta, q, k, v):
+    rows, tokens, unused = q.shape
+    whole = pl.BlockSpec((1, tokens, HEAD), lambda r, b, m: (r, 0, 0))
+    blocks = tokens // BLK
+    return pl.pallas_call(
+        suffix_kernel,
+        grid_spec=pltpu.PrefetchScalarGridSpec(
+            num_scalar_prefetch=1,
+            grid=(rows, tokens // SUF),
+            in_specs=[pl.BlockSpec((1, SUF, HEAD), lambda r, b, m: (r, b, 0)), whole, whole],
+            out_specs=[
+                pl.BlockSpec((1, SUF, HEAD), lambda r, b, m: (r, b, 0)),
+                pl.BlockSpec((1, blocks, BLK), lambda r, b, m: (r, 0, 0)),
+            ],
+        ),
+        out_shape=(
+            jax.ShapeDtypeStruct((rows, tokens, HEAD), jnp.float32),
+            jax.ShapeDtypeStruct((rows, blocks, BLK), jnp.float32),
+        ),
+        compiler_params=pltpu.CompilerParams(vmem_limit_bytes=VMEM_BIG),
+        cost_estimate=pl.CostEstimate(
+            flops=rows * tokens * tokens * HEAD * 4 * 4, bytes_accessed=1 << 20, transcendentals=0
+        ),
+        name="suffix_attend",
+    )(meta, q, k, v)
+
+
+def merge_kernel(*refs):
+    parts, out_ref = refs[:-1], refs[-1]
+    block = pl.program_id(0)
+    half = len(parts) // 2
+    for row in range(2):
+        sources = parts[row * half : (row + 1) * half]
+        lses = [
+            jnp.transpose(jnp.broadcast_to(lse[0, pl.ds(block, 1), :], (BLK, BLK)))
+            for lse in sources[1::2]
+        ]
+        top = lses[0]
+        for lse in lses[1:]:
+            top = jnp.maximum(top, lse)
+        weights = [jnp.exp2(lse - top) for lse in lses]
+        total = weights[0]
+        summed = weights[0] * sources[0][0].astype(jnp.float32)
+        for weight, o in zip(weights[1:], sources[2::2]):
+            total = total + weight
+            summed = summed + weight * o[0].astype(jnp.float32)
+        out_ref[0, row * BLK : (row + 1) * BLK, :] = (summed / total).astype(out_ref.dtype)
+
+
+def merge_parts(parts):
+    blocks = parts[0][0][0].shape[1] // BLK
+    specs, operands = [], []
+    for row in parts:
+        for o, lse, index in row:
+            operands += [o, lse]
+            specs += [
+                pl.BlockSpec((1, BLK, HEAD), lambda b, index=index: (index, b, 0)),
+                pl.BlockSpec((1, blocks, BLK), lambda b, index=index: (index, 0, 0)),
+            ]
+    return pl.pallas_call(
+        merge_kernel,
+        grid=(blocks,),
+        in_specs=specs,
+        out_specs=pl.BlockSpec((1, 2 * BLK, HEAD), lambda b: (b, 0, 0)),
+        out_shape=jax.ShapeDtypeStruct((blocks, 2 * BLK, HEAD), jnp.bfloat16),
+        name="merge_parts",
+    )(*operands)
+
+
+def project_kernel(a_ref, w_ref, keep_ref, send_ref, lhs):
+    @pl.when(pl.program_id(0) == 0)
+    def first():
+        for h in range(a_ref.shape[0]):
+            lhs[:, h * HEAD : (h + 1) * HEAD] = a_ref[h]
+
+    out = jnp.dot(lhs[...], w_ref[...], preferred_element_type=jnp.float32)
+    rows = keep_ref.shape[0]
+    keep_ref[...] = out[:rows]
+    send_ref[...] = out[rows:].astype(send_ref.dtype)
+
+
+def project(attended, weights):
+    heads, tokens, unused = attended.shape
+    depth, width = weights.shape
+    rows, tile = tokens // 2, 512
+    out_spec = pl.BlockSpec((rows, tile), lambda i: (0, i))
+    return pl.pallas_call(
+        project_kernel,
+        grid=(width // tile,),
+        in_specs=[
+            pl.BlockSpec((heads, tokens, HEAD), lambda i: (0, 0, 0)),
+            pl.BlockSpec((depth, tile), lambda i: (0, i)),
+        ],
+        out_specs=[out_spec, out_spec],
+        out_shape=(
+            jax.ShapeDtypeStruct((rows, width), jnp.float32),
+            jax.ShapeDtypeStruct((rows, width), jnp.bfloat16),
+        ),
+        scratch_shapes=[pltpu.VMEM((tokens, depth), jnp.bfloat16)],
+        name="project",
+    )(attended, weights)
+
+
+def norm_kernel(keep, got, residual, gain, stream_ref, normed_ref):
+    stream = residual[...].astype(jnp.float32) + (keep[...] + got[...].astype(jnp.float32))
+    meansq = jnp.mean(stream * stream, axis=-1, keepdims=True)
+    stream_ref[...] = stream
+    normed = stream * lax.rsqrt(meansq + 1e-06) * gain[...].astype(jnp.float32)
+    normed_ref[...] = normed.astype(normed_ref.dtype)
+
+
+def norm_rows(keep, got, residual, gain):
+    return pl.pallas_call(
+        norm_kernel,
+        out_shape=(
+            jax.ShapeDtypeStruct(keep.shape, jnp.float32),
+            jax.ShapeDtypeStruct(keep.shape, jnp.bfloat16),
+        ),
+        name="norm_rows",
+    )(keep, got, residual, gain.reshape(1, -1))
+
+
+EXP_DEV = 4
+CAP_ROWS = 256
+
+
+def route_kernel(sc_ref, tab_ref, row_ref, col_ref, scr):
+    for slot in range(8):
+        tab = tab_ref[sc_ref[slot]].astype(jnp.float32)
+        ids, gates = tab[:TOPK], tab[TOPK:]
+        here = slice(slot * BLK, (slot + 1) * BLK)
+        for j in range(EXP_DEV):
+            chosen = ids == (sc_ref[8] + j).astype(jnp.float32)
+            scr[j : j + 1, here] = jnp.sum(chosen.astype(jnp.float32), axis=0, keepdims=True)
+            scr[EXP_DEV + j : EXP_DEV + j + 1, here] = jnp.sum(
+                jnp.where(chosen, gates, 0.0), axis=0, keepdims=True
+            )
+    held = scr[...]
+    count = held.shape[1]
+    before = (
+        lax.broadcasted_iota(jnp.int32, (count, count), 0)
+        < lax.broadcasted_iota(jnp.int32, (count, count), 1)
+    ).astype(jnp.bfloat16)
+    places = jnp.dot(held.astype(jnp.bfloat16), before, preferred_element_type=jnp.float32)
+    place_row = lax.broadcasted_iota(jnp.int32, held.shape, 0) < EXP_DEV
+    chosen = jnp.concatenate([held[:EXP_DEV], held[:EXP_DEV]], axis=0) > 0.5
+    table = jnp.where(place_row, jnp.where(chosen, places, -1.0), held)
+    row_ref[...] = table
+    for slot in range(8):
+        here = slice(slot * BLK, (slot + 1) * BLK)
+        tall = jnp.concatenate([table[:, here], jnp.zeros((BLK - 8, BLK), jnp.float32)], axis=0)
+        col_ref[here, :] = jnp.transpose(tall)
+
+
+def route(scalars, tab):
+    tokens = tab.shape[0] * BLK
+    return pl.pallas_call(
+        route_kernel,
+        in_specs=[
+            pl.BlockSpec(memory_space=pltpu.SMEM),
+            pl.BlockSpec(memory_space=pltpu.VMEM),
+        ],
+        out_shape=(
+            jax.ShapeDtypeStruct((8, tokens), jnp.float32),
+            jax.ShapeDtypeStruct((tokens, BLK), jnp.float32),
+        ),
+        scratch_shapes=[pltpu.VMEM((8, tokens), jnp.float32)],
+        name="route",
+    )(scalars, tab)
+
+
+def experts_kernel(*refs):
+    chunks = refs[:8]
+    row_ref, col_ref, wg, wu, wd, out_ref, rows_in, rows_out, sems = refs[8:]
+    expert = pl.program_id(0)
+    tokens = rows_in.shape[0]
+
+    @pl.when(expert == 0)
+    def first():
+        copies = [
+            pltpu.make_async_copy(
+                chunk, rows_in.at[i * BLK : (i + 1) * BLK, :], sems.at[i]
+            )
+            for i, chunk in enumerate(chunks)
+        ]
+        for copy in copies:
+            copy.start()
+        for copy in copies:
+            copy.wait()
+
+    places = row_ref[pl.ds(expert, 1), :]
+    slots = lax.broadcasted_iota(jnp.int32, (CAP_ROWS, tokens), 0).astype(jnp.float32)
+    pick = (slots == places).astype(jnp.bfloat16)
+    picked = jnp.dot(pick, rows_in[...], preferred_element_type=jnp.float32).astype(jnp.bfloat16)
+    contract = (((1,), (1,)), ((), ()))
+    gate_h = lax.dot_general(picked, wg[0], contract, preferred_element_type=jnp.float32)
+    up_h = lax.dot_general(picked, wu[0], contract, preferred_element_type=jnp.float32)
+    hidden = (gate_h / (1.0 + jnp.exp(-gate_h)) * up_h).astype(jnp.bfloat16)
+    out = jnp.dot(hidden, wd[0], preferred_element_type=jnp.float32)
+    rows_out[pl.ds(pl.multiple_of(expert * CAP_ROWS, CAP_ROWS), CAP_ROWS), :] = out.astype(
+        jnp.bfloat16
+    )
+
+    @pl.when(expert == EXP_DEV - 1)
+    def last():
+        def give(i, carry):
+            here = pl.ds(pl.multiple_of(i * BLK, BLK), BLK)
+            cols = col_ref[here, :]
+            slot = lax.broadcasted_iota(jnp.int32, (BLK, CAP_ROWS), 1).astype(jnp.float32)
+            weights = jnp.concatenate(
+                [
+                    jnp.where(
+                        slot == cols[:, j : j + 1], cols[:, EXP_DEV + j : EXP_DEV + j + 1], 0.0
+                    ).astype(jnp.bfloat16)
+                    for j in range(EXP_DEV)
+                ],
+                axis=1,
+            )
+            out_ref[i] = jnp.dot(
+                weights, rows_out[...], preferred_element_type=jnp.float32
+            ).astype(out_ref.dtype)
+            return carry
+
+        lax.fori_loop(0, tokens // BLK, give, 0)
+
+
+def run_experts(chunks, row_tab, col_tab, w_gate, w_up, w_down):
+    width = chunks[0].shape[1]
+    hidden = w_down.shape[1]
+    tokens = len(chunks) * BLK
+    once = pl.Buffered(1)
+    return pl.pallas_call(
+        experts_kernel,
+        grid=(EXP_DEV,),
+        in_specs=[pl.BlockSpec(memory_space=pl.ANY)] * 8
+        + [
+            pl.BlockSpec((8, tokens), lambda j: (0, 0)),
+            pl.BlockSpec((tokens, BLK), lambda j: (0, 0)),
+            pl.BlockSpec((1, hidden, width), lambda j: (j, 0, 0)),
+            pl.BlockSpec((1, hidden, width), lambda j: (j, 0, 0)),
+            pl.BlockSpec((1, hidden, width), lambda j: (j, 0, 0)),
+        ],
+        out_specs=pl.BlockSpec((8, BLK, width), lambda j: (0, 0, 0), pipeline_mode=once),
+        out_shape=jax.ShapeDtypeStruct((8, BLK, width), jnp.bfloat16),
+        scratch_shapes=[
+            pltpu.VMEM((tokens, width), jnp.bfloat16),
+            pltpu.VMEM((EXP_DEV * CAP_ROWS, width), jnp.bfloat16),
+            pltpu.SemaphoreType.DMA((8,)),
+        ],
+        compiler_params=pltpu.CompilerParams(vmem_limit_bytes=VMEM_BIG),
+        name="experts",
+    )(*chunks, row_tab, col_tab, w_gate.transpose(0, 2, 1), w_up.transpose(0, 2, 1), w_down)
+
+
+def pick_by_z(z, *choices):
+    picked = choices[-1]
+    for i in range(len(choices) - 2, -1, -1):
+        if choices[i] is not picked:
+            picked = jnp.where(z == i, choices[i], picked)
+    return picked
+
+
+SLOT_Z = ((0, 1, 2, 3), (1, 0, 2, 3), (2, 1, 3, 0), (3, 2, 1, 0))
+
+
+def gather_rows(z, own):
+    up, down = z_up(own), z_down(own)
+    there = [y_swap(own)]
+    first = pick_by_z(z, down, up, up, up)
+    up2, down2 = z_up(up), z_down(down)
+    there.append(y_swap(first))
+    second = pick_by_z(z, down2, down, down, up2)
+    up3, down3 = z_up(up2), z_down(down2)
+    there.append(y_swap(second))
+    third = pick_by_z(z, down3, down2, up2, up3)
+    there.append(y_swap(third))
+    return [own, first, second, third] + there
+
+
+def scatter_sums(z, sums):
+    def plus(a, b):
+        return (a.astype(jnp.float32) + b.astype(jnp.float32)).astype(jnp.bfloat16)
+
+    s3 = plus(sums[3], y_swap(sums[7]))
+    up, down = z_up(s3, 1), z_down(s3, 1)
+    s2 = plus(sums[2], y_swap(sums[6]))
+    up = z_up(pick_by_z(z, s2, plus(s3, up), s2, s2), 2)
+    down = z_down(pick_by_z(z, s2, s2, plus(s3, down), s2), 2)
+    s1 = plus(sums[1], y_swap(sums[5]))
+    up = z_up(pick_by_z(z, s1, plus(s2, up), plus(s2, up), s1), 3)
+    down = z_down(pick_by_z(z, s1, plus(s1, down), plus(s1, down), s1), 3)
+    s0 = (sums[0], y_swap(sums[4]))
+    return [part.astype(jnp.float32) for part in (*s0, up, down)]
+
+
+def tabled(values, index):
+    return jnp.asarray(values, jnp.int32)[index]
+
+
+def block_device(
+    queries,
+    keys,
+    values,
+    prefix_keys,
+    prefix_values,
+    lengths,
+    groups,
+    residual,
+    out_proj,
+    norm_gain,
+    expert_ids,
+    expert_gates,
+    w_gate,
+    w_up,
+    w_down,
+):
+    row_tok = queries.shape[0]
+    core = lax.rem(lax.axis_index("req"), 2)
+    place = lax.axis_index("exp")
+    z = place // 2
+    core_arg = core.astype(jnp.int32).reshape(1)
+
+    proj_rows = lax.dynamic_slice_in_dim(out_proj, core * HEAD, HEAD, 0)
+    proj_rows = lax.all_gather(proj_rows, "exp", axis=0, tiled=True)
+
+    shape = jnp.concatenate([lengths, groups], axis=1)
+    shapes = jnp.concatenate([shape, core_swap(shape)], axis=0)
+    shapes = jnp.concatenate([shapes, x_swap(shapes)], axis=0)
+    meta = row_meta(shapes[:, :RQ], shapes[:, RQ:])
+
+    qkv_theirs, pk_theirs, pv_theirs = send_halves(
+        core_arg, queries, keys, values, prefix_keys, prefix_values
+    )
+    qkv_other = core_swap(qkv_theirs)
+    pk_other, pv_other = core_swap(pk_theirs), core_swap(pv_theirs)
+
+    def mine(array):
+        return jnp.where(core == 0, array[:, :HEAD], array[:, HEAD:])
+
+    q_two = jnp.stack([mine(queries), qkv_other[0]])
+    k_two = jnp.stack([mine(keys), qkv_other[1]])
+    v_two = jnp.stack([mine(values), qkv_other[2]])
+    q_far = x_swap(q_two)
+
+    tab = jnp.concatenate([expert_ids.T.astype(jnp.bfloat16), expert_gates.T], axis=0)[None]
+    for step in (1, 2, 4):
+        tab = jnp.concatenate(
+            [tab, lax.ppermute(tab, "exp", [(i, i ^ step) for i in range(8)])], axis=0
+        )
+    slot_z = tabled(SLOT_Z, z)
+    slot_place = jnp.concatenate(
+        [slot_z * 2 + lax.rem(place, 2), slot_z * 2 + 1 - lax.rem(place, 2)]
+    )
+    scalars = jnp.concatenate([slot_place ^ place, (place * EXP_DEV).reshape(1)])
+    row_tab, col_tab = route(scalars.astype(jnp.int32), tab)
+
+    def prefix(q, rows, dtype):
+        return prefix_attend(
+            meta[rows], core_arg, q, prefix_keys, pk_other, prefix_values, pv_other, dtype
+        )
+
+    suffix = suffix_attend(meta[:2], q_two, k_two, v_two)
+    near = prefix(q_two, slice(0, 2), jnp.float32)
+    far = prefix(q_far, slice(2, 4), jnp.bfloat16)
+    back = (x_swap(far[0]), x_swap(far[1]))
+    attended = merge_parts(
+        [[(*part, row) for part in (suffix, near, back)] for row in range(2)]
+    )
+    heads = lax.all_to_all(attended, "exp", split_axis=0, concat_axis=0, tiled=True)
+    keep, send = project(heads, proj_rows)
+    stream, normed = norm_rows(keep, core_swap(send), residual, norm_gain)
+    rows = gather_rows(z, normed)
+    sums = run_experts(rows, row_tab, col_tab, w_gate, w_up, w_down)
+    parts = scatter_sums(z, sums)
+    return (stream + sum(parts[1:], parts[0])).astype(jnp.bfloat16)
+
+
 def solution(mesh):
     in_specs = (
         P("req", "exp"),
@@ -260,6 +830,8 @@
         P("exp", None, None),
     )
     out_specs = P(("req", "exp"), None)
+    blocked = mesh.shape["req"] == 4 and mesh.shape["exp"] == 8
     return jax.shard_map(
-        per_device, mesh=mesh, in_specs=in_specs, out_specs=out_specs, check_vma=False
-    )
+        block_device if blocked else general_device,
+        mesh=mesh, in_specs=in_specs, out_specs=out_specs, check_vma=False
+    )

time: 932 us -> 306 us (0.33)
  waiting for transfers between devices: 373 us -> 87.8 us
  local copies, waits for them, and re-layouts: 182 us -> 8.36 us
  matrix products: 154 us -> 0 us
  Pallas kernels: 0 us -> 105 us
  blocking collectives: 105 us -> 18.6 us
  other arithmetic: 84.3 us -> 9.19 us
  starting transfers between devices: 10.6 us -> 62.2 us
    all_to_all x2 -> x0, waiting for transfers between devices: 222 us -> none  [the longest x1 182 us: per_device(): lax.all_to_all(expert_out.reshape(EXPERTS, slots, received.shape[2]), 'ex...]
    dot_general x13 -> x0, matrix products: 154 us -> none  [the longest x4 57.8 us: per_block(): jnp.einsum('hqgk,gkhd->qhd', exp_terms.astype(jnp.bfloat16), val_grid, pr...]
    reduce_scatter x1 -> x0, waiting for transfers between devices: 146 us -> none  [per_device(): lax.psum_scatter(jnp.dot(attended, out_proj, preferred_element_type=jnp.f...]
    pallas_call x0 -> x9, Pallas kernels: none -> 105 us  [the longest x2 45.9 us: prefix_attend(): pl.pallas_call(prefix_kernel, grid_spec=pltpu.PrefetchScalarGridSpec(num_...]
    scatter x1 -> x0, local copies, waits for them, and re-layouts: 91.9 us -> none  [per_device(): buffer = jnp.zeros((EXPERTS, capacity, normed.shape[1]), jnp.bfloat16).at...]
    ppermute x0 -> x32, waiting for transfers between devices: none -> 87.7 us  [the longest x8 46.5 us: y_swap(): return lax.ppermute(array, 'exp', [(i, i ^ 1) for i in range(8)])]
    all_to_all x1, blocking collectives: 98.5 us -> 18.6 us  [block_device(): lax.all_to_all(attended, 'exp', split_axis=0, concat_axis=0, tiled=True)]
    reduce_sum x12 -> x0, other arithmetic: 73 us -> none  [the longest x4 57.2 us: per_block(): totals = jnp.sum(exp_terms, axis=(2, 3))]
  transfers between devices with their start and end apart: 4 -> 33, of which waited for: 4 -> 18; matrix products, arithmetic and copies ran while one was open for 3% -> 3% of each run, Pallas kernels for 0% -> 22%
where the time goes in v1:
time: 306 us; the launch traced here: 305 us
  Pallas kernels  105 us (34%)
  waiting for transfers between devices  87.8 us (29%)
  starting transfers between devices  62.2 us (20%)
  blocking collectives  18.6 us (6%)
  between operations  13.8 us (5%)
  other arithmetic  9.19 us (3%)
  local copies, waits for them, and re-layouts  8.36 us (3%)
    ppermute x8, waiting for transfers between devices, y_swap(): return lax.ppermute(array, 'exp', [(i, i ^ 1) for i in range(8)])  46.5 us
    pallas_call x2, Pallas kernels, prefix_attend(): pl.pallas_call(prefix_kernel, grid_spec=pltpu.PrefetchScalarGridSpec(num_...  45.9 us
    ppermute x6, starting transfers between devices, z_up(): return lax.ppermute(array, 'exp', [(i, i + 2) for i in range(2 * sources)])  31.6 us
    pallas_call x1, Pallas kernels, run_experts(): pl.pallas_call(experts_kernel, grid=(EXP_DEV,), in_specs=[pl.BlockSpec(me...  30.6 us
    ppermute x6, waiting for transfers between devices, z_down(): lax.ppermute(array, 'exp', [(i, i - 2) for i in range(8 - 2 * sources, 8)])  29.1 us
    all_to_all x1, blocking collectives, block_device(): lax.all_to_all(attended, 'exp', split_axis=0, concat_axis=0, tiled=True)  18.6 us
    ppermute x8, starting transfers between devices, y_swap(): return lax.ppermute(array, 'exp', [(i, i ^ 1) for i in range(8)])  9.2 us
    pallas_call x1, Pallas kernels, suffix_attend(): pl.pallas_call(suffix_kernel, grid_spec=pltpu.PrefetchScalarGridSpec(num_...  8.28 us
  transfers between devices with their start and end apart: 33, of which 18 were waited for; matrix products, arithmetic and copies ran while one was open for 3% of the time, Pallas kernels for 22%

profile of v1, /device:TPU:0, one launch (start us, length us, event | category | flops | bytes accessed | tf_op | source)
XLA Modules:
  0.0 304.8 jit_solution(16960800013017684365)
XLA Ops:
  6.6 1.2 copy-done
  7.8 0.9 constant_dynamic-slice_fusion
  8.7 0.8 pad_add_fusion.3
  9.9 4.1 %send_halves.1 = (bf16[3,1024,128]{2,1,0:T(8,128)(2,1)}, bf16[4,1024,128]{2,1,0:T(8,128)(2,1)}, bf16[4,1024,128]{2,1,0:T(8,128)(2,1)}) custom-call(s32[1]{0:T(128)} %bitcast.1.sc_ref, bf16[1024,256]{1,0:T(8,128)(2,1)} %q.1, bf16[1024,256]{1,0:T(8,128)(2,1)} %k.1, bf16[1024,256]{1,0:T(8,128)(2,1)} %v.1, bf16[4,1024,256]{2,1,0:T(8,128)(2,1)} %ka.3, ...), custom_call_target="tpu_custom_call" | custom-call | tf_op jit(solution)/shard_map/send_halves/pallas_call | solution.py:298
  14.9 2.9 collective-permute-start.1
  17.8 1.5 collective-permute-done.1
  21.0 2.1 collective-permute-start.5
  23.1 1.1 pad_maximum_fusion.1
  24.2 8.3 %suffix_attend.1 = (f32[2,1024,128]{2,1,0:T(8,128)}, f32[2,8,128]{2,1,0:T(8,128)}) custom-call(s32[2,24]{1,0:T(2,128)} %get-tuple-element.56.meta_ref, bf16[2,1024,128]{2,1,0:T(8,128)(2,1)} %copy-done.14, bf16[2,1024,128]{2,1,0:T(8,128)(2,1)} %get-tuple-element.65.k_ref, bf16[2,1024,128]{2,1,0:T(8,128)(2,1)} %get-tuple-element.66.v_ref), custom_call_target="tpu_custom_call" | custom-call | flops 4294967296 | bytes 1048576 | tf_op jit(solution)/shard_map/suffix_attend/pallas_call | solution.py:441
  32.5 1.6 collective-permute-done.5.q_ref
  34.1 0.8 copy-done.25
  34.9 22.2 %prefix_attend.3 = (bf16[2,1024,128]{2,1,0:T(8,128)(2,1)}, f32[2,8,128]{2,1,0:T(8,128)}) custom-call(s32[2,24]{1,0:T(2,128)} %get-tuple-element.55.meta_ref, s32[1]{0:T(128)} %bitcast.1.sc_ref, bf16[2,1024,128]{2,1,0:T(8,128)(2,1)} %copy-done.25, bf16[4,1024,256]{2,1,0:T(8,128)(2,1)} %ka.3, bf16[4,1024,128]{2,1,0:T(8,128)(2,1)} %collective-permute-done.3.kb, ...), custom_call_target="tpu_custom_call" | custom-call | flops 8589934592 | bytes 4194304 | tf_op jit(solution)/shard_map/prefix_attend/pallas_call | solution.py:374
  57.1 3.2 %collective-permute-start.6 = (bf16[2,1024,128]{2,1,0:T(8,128)(2,1)}, bf16[2,1024,128]{2,1,0:T(8,128)(2,1)S(1)}, u32[]{:S(2)}, u32[]{:S(2)}) collective-permute-start(bf16[2,1024,128]{2,1,0:T(8,128)(2,1)} %get-tuple-element.27), channel_id=1, source_target_pairs={{0,16},{8,24},{16,0},{24,8},{1,17},{9,25},{17,1},{25,9},{2,18},{10... | collective-permute-start | bytes 1572872 | tf_op jit(solution)/shard_map/ppermute | solution.py:257
  60.3 23.6 %prefix_attend.2 = (f32[2,1024,128]{2,1,0:T(8,128)}, f32[2,8,128]{2,1,0:T(8,128)}) custom-call(s32[2,24]{1,0:T(2,128)} %get-tuple-element.56.meta_ref, s32[1]{0:T(128)} %bitcast.1.sc_ref, bf16[2,1024,128]{2,1,0:T(8,128)(2,1)} %copy-done.14, bf16[4,1024,256]{2,1,0:T(8,128)(2,1)} %ka.3, bf16[4,1024,128]{2,1,0:T(8,128)(2,1)} %collective-permute-done.3.kb, ...), custom_call_target="tpu_custom_call" | custom-call | flops 8589934592 | bytes 4194304 | tf_op jit(solution)/shard_map/prefix_attend/pallas_call | solution.py:374
  84.8 6.0 %merge_parts.1 = bf16[8,256,128]{2,1,0:T(8,128)(2,1)} custom-call(f32[2,1024,128]{2,1,0:T(8,128)} %get-tuple-element.21.refs_0_.refs_6_, f32[2,8,128]{2,1,0:T(8,128)} %get-tuple-element.22.refs_1_.refs_7_, f32[2,1024,128]{2,1,0:T(8,128)} %get-tuple-element.25.refs_2_.refs_8_, f32[2,8,128]{2,1,0:T(8,128)} %get-tuple-element.26.refs_3_.refs_9_, ...), custom_call_target="tpu_custom_call" | custom-call | tf_op jit(solution)/shard_map/merge_parts/pallas_call | solution.py:496
  90.8 18.6 %all_to_all.5.a_ref = bf16[8,256,128]{2,1,0:T(8,128)(2,1)} all-to-all(bf16[8,256,128]{2,1,0:T(8,128)(2,1)} %merge_parts.1), channel_id=1, replica_groups=mesh['req'=4,'exp'=8] {'exp'}, dimensions={0} | all-to-all | bytes 1048576 | tf_op jit(solution)/shard_map/all_to_all | solution.py:805
  109.4 5.1 %project.1 = (f32[128,2048]{1,0:T(8,128)}, bf16[128,2048]{1,0:T(8,128)(2,1)}) custom-call(bf16[8,256,128]{2,1,0:T(8,128)(2,1)} %all_to_all.5.a_ref, bf16[1024,2048]{1,0:T(8,128)(2,1)} %all-gather.2.cloned.1.call-done.w_ref), custom_call_target="tpu_custom_call" | custom-call | tf_op jit(solution)/shard_map/project/pallas_call | solution.py:523
  115.1 1.5 collective-permute-done.8.got
  116.6 0.8 copy-done.15
  117.4 2.9 norm_rows.1
  120.3 1.3 collective-permute-start.9
  121.6 4.6 %collective-permute-start.10 = (bf16[128,2048]{1,0:T(8,128)(2,1)}, bf16[128,2048]{1,0:T(8,128)(2,1)S(1)}, u32[]{:S(2)}, u32[]{:S(2)}) collective-permute-start(bf16[128,2048]{1,0:T(8,128)(2,1)} %get-tuple-element.32.refs_0_), channel_id=1, source_target_pairs={{0,2},{1,3},{2,4},{3,5},{4,6},{5,7},{8,10},{9,11},{10,12},{11,13},... | collective-permute-start | bytes 1572872 | tf_op jit(solution)/shard_map/ppermute | solution.py:265
  126.2 10.2 %collective-permute-done.9 = bf16[128,2048]{1,0:T(8,128)(2,1)S(1)} collective-permute-done((bf16[128,2048]{1,0:T(8,128)(2,1)}, bf16[128,2048]{1,0:T(8,128)(2,1)S(1)}, u32[]{:S(2)}, u32[]{:S(2)}) %collective-permute-start.9) | collective-permute-done | bytes 524320 | tf_op jit(solution)/shard_map/ppermute | solution.py:269
  136.3 1.3 collective-permute-start.11
  137.6 4.6 %collective-permute-start.12 = (bf16[128,2048]{1,0:T(8,128)(2,1)S(1)}, bf16[128,2048]{1,0:T(8,128)(2,1)S(1)}, u32[]{:S(2)}, u32[]{:S(2)}) collective-permute-start(bf16[128,2048]{1,0:T(8,128)(2,1)S(1)} %collective-permute-done.10), channel_id=1, source_target_pairs={{0,2},{1,3},{2,4},{3,5},{4,6},{5,7},{8,10},{9,11},{10,12},{11,13},... | collective-permute-start | bytes 1572872 | tf_op jit(solution)/shard_map/ppermute | solution.py:265
  142.2 9.1 %collective-permute-done.11 = bf16[128,2048]{1,0:T(8,128)(2,1)S(1)} collective-permute-done((bf16[128,2048]{1,0:T(8,128)(2,1)S(1)}, bf16[128,2048]{1,0:T(8,128)(2,1)S(1)}, u32[]{:S(2)}, u32[]{:S(2)}) %collective-permute-start.11) | collective-permute-done | bytes 524320 | tf_op jit(solution)/shard_map/ppermute | solution.py:269
  151.4 1.3 collective-permute-start.13
  152.7 5.4 %collective-permute-start.14 = (bf16[128,2048]{1,0:T(8,128)(2,1)S(1)}, bf16[128,2048]{1,0:T(8,128)(2,1)}, u32[]{:S(2)}, u32[]{:S(2)}) collective-permute-start(bf16[128,2048]{1,0:T(8,128)(2,1)S(1)} %collective-permute-done.12), channel_id=1, source_target_pairs={{0,2},{1,3},{2,4},{3,5},{4,6},{5,7},{8,10},{9,11},{10,12},{11,13},... | collective-permute-start | bytes 1572872 | tf_op jit(solution)/shard_map/ppermute | solution.py:265
  158.1 1.5 collective-permute-start.19
  159.6 0.7 add_bitcast_fusion
  160.8 4.6 %collective-permute-done.13 = bf16[128,2048]{1,0:T(8,128)(2,1)S(1)} collective-permute-done((bf16[128,2048]{1,0:T(8,128)(2,1)S(1)}, bf16[128,2048]{1,0:T(8,128)(2,1)S(1)}, u32[]{:S(2)}, u32[]{:S(2)}) %collective-permute-start.13) | collective-permute-done | bytes 524320 | tf_op jit(solution)/shard_map/ppermute | solution.py:269
  165.5 0.8 copy-done.18
  166.7 1.7 select_select_fusion.5
  168.4 1.5 collective-permute-start.16
  170.5 1.5 collective-permute-start.18
  171.9 2.5 collective-permute-start.20
  174.5 1.5 collective-permute-done.20
  176.0 1.6 collective-permute-start.21
  177.6 0.6 pad_add_fusion.4.sc_ref
  178.2 2.3 collective-permute-done.21
  181.2 2.1 route.1
  183.3 3.3 %collective-permute-done.16.refs_5_ = bf16[128,2048]{1,0:T(8,128)(2,1)S(1)} collective-permute-done((bf16[128,2048]{1,0:T(8,128)(2,1)S(1)}, bf16[128,2048]{1,0:T(8,128)(2,1)S(1)}, u32[]{:S(2)}, u32[]{:S(2)}) %collective-permute-start.16) | collective-permute-done | bytes 524320 | tf_op jit(solution)/shard_map/ppermute | solution.py:261
  186.6 11.2 %collective-permute-done.17.refs_6_ = bf16[128,2048]{1,0:T(8,128)(2,1)S(1)} collective-permute-done((bf16[128,2048]{1,0:T(8,128)(2,1)S(1)}, bf16[128,2048]{1,0:T(8,128)(2,1)S(1)}, u32[]{:S(2)}, u32[]{:S(2)}) %collective-permute-start.17) | collective-permute-done | bytes 524320 | tf_op jit(solution)/shard_map/ppermute | solution.py:261
  197.8 7.9 %collective-permute-done.18.refs_7_ = bf16[128,2048]{1,0:T(8,128)(2,1)} collective-permute-done((bf16[128,2048]{1,0:T(8,128)(2,1)S(1)}, bf16[128,2048]{1,0:T(8,128)(2,1)}, u32[]{:S(2)}, u32[]{:S(2)}) %collective-permute-start.18) | collective-permute-done | bytes 524320 | tf_op jit(solution)/shard_map/ppermute | solution.py:261
  205.7 30.6 %experts.1 = bf16[8,128,2048]{2,1,0:T(8,128)(2,1)} custom-call(bf16[128,2048]{1,0:T(8,128)(2,1)} %get-tuple-element.32.refs_0_, bf16[128,2048]{1,0:T(8,128)(2,1)} %copy-done.5, bf16[128,2048]{1,0:T(8,128)(2,1)} %copy-done.4, bf16[128,2048]{1,0:T(8,128)(2,1)} %copy-done.3, bf16[128,2048]{1,0:T(8,128)(2,1)} %copy-done.11, bf16[128,2048]{1,0:T(8,128)(2,1)} %copy-done.12, ...), custom_call_target="tpu_custom_call" | custom-call | tf_op jit(solution)/shard_map/experts/pallas_call | solution.py:668
  236.3 1.8 slice_bitcast_fusion.6
  238.1 0.6 collective-permute-start.25
  238.8 1.5 collective-permute-start.24
  240.2 12.8 %collective-permute-done.25 = bf16[128,2048]{1,0:T(8,128)(2,1)S(1)} collective-permute-done((bf16[128,2048]{1,0:T(8,128)(2,1)S(1)}, bf16[128,2048]{1,0:T(8,128)(2,1)S(1)}, u32[]{:S(2)}, u32[]{:S(2)}) %collective-permute-start.25) | collective-permute-done | bytes 524320 | tf_op jit(solution)/shard_map/ppermute | solution.py:261
  253.2 1.8 collective-permute-start.26
  255.0 0.7 collective-permute-start.29
  255.7 1.4 collective-permute-start.23
  257.1 7.2 %collective-permute-done.24 = bf16[128,2048]{1,0:T(8,128)(2,1)S(1)} collective-permute-done((bf16[128,2048]{1,0:T(8,128)(2,1)S(1)}, bf16[128,2048]{1,0:T(8,128)(2,1)S(1)}, u32[]{:S(2)}, u32[]{:S(2)}) %collective-permute-start.24) | collective-permute-done | bytes 524320 | tf_op jit(solution)/shard_map/ppermute | solution.py:261
  264.8 4.4 %collective-permute-start.27 = (bf16[128,2048]{1,0:T(8,128)(2,1)S(1)}, bf16[128,2048]{1,0:T(8,128)(2,1)S(1)}, u32[]{:S(2)}, u32[]{:S(2)}) collective-permute-start(bf16[128,2048]{1,0:T(8,128)(2,1)S(1)} %get-tuple-element.39), channel_id=1, source_target_pairs={{0,2},{1,3},{2,4},{3,5},{8,10},{9,11},{10,12},{11,13},{16,18},{17,... | collective-permute-start | bytes 1572872 | tf_op jit(solution)/shard_map/ppermute | solution.py:265
  269.2 0.7 collective-permute-start.30
  269.9 1.6 collective-permute-start.22
  271.5 4.0 %collective-permute-done.23 = bf16[128,2048]{1,0:T(8,128)(2,1)S(1)} collective-permute-done((bf16[128,2048]{1,0:T(8,128)(2,1)S(1)}, bf16[128,2048]{1,0:T(8,128)(2,1)S(1)}, u32[]{:S(2)}, u32[]{:S(2)}) %collective-permute-start.23) | collective-permute-done | bytes 524320 | tf_op jit(solution)/shard_map/ppermute | solution.py:261
  275.5 1.7 collective-permute-done.27
  277.3 0.6 fusion.10
  277.9 1.3 collective-permute-start.31
  279.2 10.9 %collective-permute-start.28 = (bf16[128,2048]{1,0:T(8,128)(2,1)S(1)}, bf16[128,2048]{1,0:T(8,128)(2,1)S(1)}, u32[]{:S(2)}, u32[]{:S(2)}) collective-permute-start(bf16[128,2048]{1,0:T(8,128)(2,1)S(1)} %get-tuple-element.41), channel_id=1, source_target_pairs={{0,2},{1,3},{2,4},{3,5},{4,6},{5,7},{8,10},{9,11},{10,12},{11,13},... | collective-permute-start | bytes 1572872 | tf_op jit(solution)/shard_map/ppermute | solution.py:265
  290.1 5.2 %collective-permute-done.31 = bf16[128,2048]{1,0:T(8,128)(2,1)S(1)} collective-permute-done((bf16[128,2048]{1,0:T(8,128)(2,1)S(1)}, bf16[128,2048]{1,0:T(8,128)(2,1)S(1)}, u32[]{:S(2)}, u32[]{:S(2)}) %collective-permute-start.31) | collective-permute-done | bytes 524320 | tf_op jit(solution)/shard_map/ppermute | solution.py:269
  295.3 1.5 collective-permute-done.28
  296.8 1.2 fusion.8
  (98 shorter events, 7.3 us)
Async XLA Ops:
  6.5 1.2 copy-start
  6.5 8.1 %copy-start.6 = (bf16[1024,256]{1,0:T(8,128)(2,1)S(1)}, bf16[1024,256]{1,0:T(8,128)(2,1)}, u32[]{:S(2)}) copy-start(bf16[1024,256]{1,0:T(8,128)(2,1)} %q.1) | copy-start | bytes 1572868
  6.5 8.1 %copy-start.7 = (bf16[1024,256]{1,0:T(8,128)(2,1)S(1)}, bf16[1024,256]{1,0:T(8,128)(2,1)}, u32[]{:S(2)}) copy-start(bf16[1024,256]{1,0:T(8,128)(2,1)} %k.1) | copy-start | bytes 1572868
  6.5 102.8 %all-gather.2.cloned.1.call-start = ((), (), s32[]{:S(2)}) async-start(), calls=%async_computation.1 | async-start | bytes 4718592 | tf_op jit(solution)/shard_map/all_gather | solution.py:760
  8.6 6.1 %copy-start.8 = (bf16[1024,256]{1,0:T(8,128)(2,1)S(1)}, bf16[1024,256]{1,0:T(8,128)(2,1)}, u32[]{:S(2)}) copy-start(bf16[1024,256]{1,0:T(8,128)(2,1)} %v.1) | copy-start | bytes 1572868
  8.7 6.1 %copy-start.21 = (s32[1,8]{1,0:T(1,128)S(1)}, s32[1,8]{1,0:T(1,128)}, u32[]{:S(2)}) copy-start(s32[1,8]{1,0:T(1,128)} %param.22) | copy-start | bytes 100
  8.7 6.1 %copy-start.22 = (s32[1,8]{1,0:T(1,128)S(1)}, s32[1,8]{1,0:T(1,128)}, u32[]{:S(2)}) copy-start(s32[1,8]{1,0:T(1,128)} %param.21) | copy-start | bytes 100
  9.5 5.3 %collective-permute-start = (s32[1,16]{1,0:T(1,128)S(1)}, s32[1,16]{1,0:T(1,128)S(1)}, u32[]{:S(2)}, u32[]{:S(2)}) collective-permute-start(s32[1,16]{1,0:T(1,128)S(1)} %pad_add_fusion.3), channel_id=1, source_target_pairs={{0,8},{8,0},{16,24},{24,16},{1,9},{9,1},{17,25},{25,17},{2,10},{10... | collective-permute-start | bytes 200 | tf_op jit(solution)/shard_map/ppermute | solution.py:253
  14.0 6.8 %collective-permute-start.2 = (bf16[3,1024,128]{2,1,0:T(8,128)(2,1)}, bf16[3,1024,128]{2,1,0:T(8,128)(2,1)S(1)}, u32[]{:S(2)}, u32[]{:S(2)}) collective-permute-start(bf16[3,1024,128]{2,1,0:T(8,128)(2,1)} %get-tuple-element.20), channel_id=1, source_target_pairs={{0,8},{8,0},{16,24},{24,16},{1,9},{9,1},{17,25},{25,17},{2,10},{10... | collective-permute-start | bytes 2359304 | tf_op jit(solution)/shard_map/ppermute | solution.py:253
  14.1 18.4 %collective-permute-start.3 = (bf16[4,1024,128]{2,1,0:T(8,128)(2,1)}, bf16[4,1024,128]{2,1,0:T(8,128)(2,1)}, u32[]{:S(2)}, u32[]{:S(2)}) collective-permute-start(bf16[4,1024,128]{2,1,0:T(8,128)(2,1)} %get-tuple-element.23), channel_id=1, source_target_pairs={{0,8},{8,0},{16,24},{24,16},{1,9},{9,1},{17,25},{25,17},{2,10},{10... | collective-permute-start | bytes 3145736 | tf_op jit(solution)/shard_map/ppermute | solution.py:253
  14.6 17.9 %collective-permute-start.4 = (bf16[4,1024,128]{2,1,0:T(8,128)(2,1)}, bf16[4,1024,128]{2,1,0:T(8,128)(2,1)}, u32[]{:S(2)}, u32[]{:S(2)}) collective-permute-start(bf16[4,1024,128]{2,1,0:T(8,128)(2,1)} %get-tuple-element.24), channel_id=1, source_target_pairs={{0,8},{8,0},{16,24},{24,16},{1,9},{9,1},{17,25},{25,17},{2,10},{10... | collective-permute-start | bytes 3145736 | tf_op jit(solution)/shard_map/ppermute | solution.py:253
  14.9 4.5 %collective-permute-start.1 = (s32[2,16]{1,0:T(2,128)S(1)}, s32[2,16]{1,0:T(2,128)S(1)}, u32[]{:S(2)}, u32[]{:S(2)}) collective-permute-start(s32[2,16]{1,0:T(2,128)S(1)} %pad_add_fusion.2), channel_id=1, source_target_pairs={{0,16},{8,24},{16,0},{24,8},{1,17},{9,25},{17,1},{25,9},{2,18},{10... | collective-permute-start | bytes 392 | tf_op jit(solution)/shard_map/ppermute | solution.py:257
  21.0 3.2 %copy-start.14 = (bf16[2,1024,128]{2,1,0:T(8,128)(2,1)}, bf16[2,1024,128]{2,1,0:T(8,128)(2,1)S(1)}, u32[]{:S(2)}) copy-start(bf16[2,1024,128]{2,1,0:T(8,128)(2,1)S(1)} %pad_maximum_fusion.q_ref) | copy-start | bytes 1572868
  21.0 13.1 %collective-permute-start.5 = (bf16[2,1024,128]{2,1,0:T(8,128)(2,1)S(1)}, bf16[2,1024,128]{2,1,0:T(8,128)(2,1)S(1)}, u32[]{:S(2)}, u32[]{:S(2)}) collective-permute-start(bf16[2,1024,128]{2,1,0:T(8,128)(2,1)S(1)} %pad_maximum_fusion.q_ref), channel_id=1, source_target_pairs={{0,16},{8,24},{16,0},{24,8},{1,17},{9,25},{17,1},{25,9},{2,18},{10... | collective-permute-start | bytes 1572872 | tf_op jit(solution)/shard_map/ppermute | solution.py:257
  34.1 0.8 copy-start.25
  57.1 26.9 %collective-permute-start.6 = (bf16[2,1024,128]{2,1,0:T(8,128)(2,1)}, bf16[2,1024,128]{2,1,0:T(8,128)(2,1)S(1)}, u32[]{:S(2)}, u32[]{:S(2)}) collective-permute-start(bf16[2,1024,128]{2,1,0:T(8,128)(2,1)} %get-tuple-element.27), channel_id=1, source_target_pairs={{0,16},{8,24},{16,0},{24,8},{1,17},{9,25},{17,1},{25,9},{2,18},{10... | collective-permute-start | bytes 1572872 | tf_op jit(solution)/shard_map/ppermute | solution.py:257
  60.3 23.7 %collective-permute-start.7 = (f32[2,8,128]{2,1,0:T(8,128)}, f32[2,8,128]{2,1,0:T(8,128)S(1)}, u32[]{:S(2)}, u32[]{:S(2)}) collective-permute-start(f32[2,8,128]{2,1,0:T(8,128)} %get-tuple-element.28), channel_id=1, source_target_pairs={{0,16},{8,24},{16,0},{24,8},{1,17},{9,25},{17,1},{25,9},{2,18},{10... | collective-permute-start | bytes 24584 | tf_op jit(solution)/shard_map/ppermute | solution.py:257
  84.0 0.6 copy-start.19
  84.0 0.8 copy-start.9
  90.8 23.7 %copy-start.20 = (bf16[2048]{0:T(1024)(128)(2,1)S(1)}, bf16[2048]{0:T(1024)(128)(2,1)}, u32[]{:S(2)}) copy-start(bf16[2048]{0:T(1024)(128)(2,1)} %param.25) | copy-start | bytes 12292
  90.8 67.3 %copy-start.23 = (s32[128,4]{0,1:T(4,128)S(1)}, s32[128,4]{0,1:T(4,128)}, u32[]{:S(2)}) copy-start(s32[128,4]{0,1:T(4,128)} %param.26) | copy-start | bytes 6148
  90.8 67.3 %copy-start.24 = (bf16[128,4]{0,1:T(4,128)(2,1)S(1)}, bf16[128,4]{0,1:T(4,128)(2,1)}, u32[]{:S(2)}) copy-start(bf16[128,4]{0,1:T(4,128)(2,1)} %param.27) | copy-start | bytes 3076
  114.5 2.1 collective-permute-start.8
  116.6 0.8 copy-start.15
  120.3 16.1 %collective-permute-start.9 = (bf16[128,2048]{1,0:T(8,128)(2,1)}, bf16[128,2048]{1,0:T(8,128)(2,1)S(1)}, u32[]{:S(2)}, u32[]{:S(2)}) collective-permute-start(bf16[128,2048]{1,0:T(8,128)(2,1)} %get-tuple-element.32.refs_0_), channel_id=1, source_target_pairs={{2,0},{3,1},{4,2},{5,3},{6,4},{7,5},{10,8},{11,9},{12,10},{13,11},... | collective-permute-start | bytes 1572872 | tf_op jit(solution)/shard_map/ppermute | solution.py:269
  121.6 16.1 %collective-permute-start.10 = (bf16[128,2048]{1,0:T(8,128)(2,1)}, bf16[128,2048]{1,0:T(8,128)(2,1)S(1)}, u32[]{:S(2)}, u32[]{:S(2)}) collective-permute-start(bf16[128,2048]{1,0:T(8,128)(2,1)} %get-tuple-element.32.refs_0_), channel_id=1, source_target_pairs={{0,2},{1,3},{2,4},{3,5},{4,6},{5,7},{8,10},{9,11},{10,12},{11,13},... | collective-permute-start | bytes 1572872 | tf_op jit(solution)/shard_map/ppermute | solution.py:265
  136.3 15.0 %collective-permute-start.11 = (bf16[128,2048]{1,0:T(8,128)(2,1)S(1)}, bf16[128,2048]{1,0:T(8,128)(2,1)S(1)}, u32[]{:S(2)}, u32[]{:S(2)}) collective-permute-start(bf16[128,2048]{1,0:T(8,128)(2,1)S(1)} %collective-permute-done.9), channel_id=1, source_target_pairs={{2,0},{3,1},{4,2},{5,3},{6,4},{7,5},{10,8},{11,9},{12,10},{13,11},... | collective-permute-start | bytes 1572872 | tf_op jit(solution)/shard_map/ppermute | solution.py:269
  137.6 15.0 %collective-permute-start.12 = (bf16[128,2048]{1,0:T(8,128)(2,1)S(1)}, bf16[128,2048]{1,0:T(8,128)(2,1)S(1)}, u32[]{:S(2)}, u32[]{:S(2)}) collective-permute-start(bf16[128,2048]{1,0:T(8,128)(2,1)S(1)} %collective-permute-done.10), channel_id=1, source_target_pairs={{0,2},{1,3},{2,4},{3,5},{4,6},{5,7},{8,10},{9,11},{10,12},{11,13},... | collective-permute-start | bytes 1572872 | tf_op jit(solution)/shard_map/ppermute | solution.py:265
  151.4 14.1 %copy-start.16 = (bf16[128,2048]{1,0:T(8,128)(2,1)}, bf16[128,2048]{1,0:T(8,128)(2,1)S(1)}, u32[]{:S(2)}) copy-start(bf16[128,2048]{1,0:T(8,128)(2,1)S(1)} %collective-permute-done.11) | copy-start | bytes 1572868
  151.4 14.1 %collective-permute-start.13 = (bf16[128,2048]{1,0:T(8,128)(2,1)S(1)}, bf16[128,2048]{1,0:T(8,128)(2,1)S(1)}, u32[]{:S(2)}, u32[]{:S(2)}) collective-permute-start(bf16[128,2048]{1,0:T(8,128)(2,1)S(1)} %collective-permute-done.11), channel_id=1, source_target_pairs={{2,0},{3,1},{4,2},{5,3},{6,4},{7,5},{10,8},{11,9},{12,10},{13,11},... | collective-permute-start | bytes 1572872 | tf_op jit(solution)/shard_map/ppermute | solution.py:269
  152.7 12.8 %copy-start.17 = (bf16[128,2048]{1,0:T(8,128)(2,1)}, bf16[128,2048]{1,0:T(8,128)(2,1)S(1)}, u32[]{:S(2)}) copy-start(bf16[128,2048]{1,0:T(8,128)(2,1)S(1)} %collective-permute-done.12) | copy-start | bytes 1572868
  152.7 14.0 %collective-permute-start.14 = (bf16[128,2048]{1,0:T(8,128)(2,1)S(1)}, bf16[128,2048]{1,0:T(8,128)(2,1)}, u32[]{:S(2)}, u32[]{:S(2)}) collective-permute-start(bf16[128,2048]{1,0:T(8,128)(2,1)S(1)} %collective-permute-done.12), channel_id=1, source_target_pairs={{0,2},{1,3},{2,4},{3,5},{4,6},{5,7},{8,10},{9,11},{10,12},{11,13},... | collective-permute-start | bytes 1572872 | tf_op jit(solution)/shard_map/ppermute | solution.py:265
  158.1 13.9 %collective-permute-start.19 = (bf16[1,8,128]{2,1,0:T(8,128)(2,1)S(1)}, bf16[1,8,128]{2,1,0:T(8,128)(2,1)S(1)}, u32[]{:S(2)}, u32[]{:S(2)}) collective-permute-start(bf16[1,8,128]{2,1,0:T(8,128)(2,1)S(1)} %maximum_bitcast_fusion), channel_id=1, source_target_pairs={{0,1},{1,0},{2,3},{3,2},{4,5},{5,4},{6,7},{7,6},{8,9},{9,8},{10,11... | collective-permute-start | bytes 6152 | tf_op jit(solution)/shard_map/ppermute | solution.py:784
  160.3 23.0 %collective-permute-start.15 = (bf16[128,2048]{1,0:T(8,128)(2,1)}, bf16[128,2048]{1,0:T(8,128)(2,1)S(1)}, u32[]{:S(2)}, u32[]{:S(2)}) collective-permute-start(bf16[128,2048]{1,0:T(8,128)(2,1)} %get-tuple-element.32.refs_0_), channel_id=1, source_target_pairs={{0,1},{1,0},{2,3},{3,2},{4,5},{5,4},{6,7},{7,6},{8,9},{9,8},{10,11... | collective-permute-start | bytes 1572872 | tf_op jit(solution)/shard_map/ppermute | solution.py:261
  165.5 0.8 copy-start.18
  168.3 37.4 %copy-start.3 = (bf16[128,2048]{1,0:T(8,128)(2,1)}, bf16[128,2048]{1,0:T(8,128)(2,1)S(1)}, u32[]{:S(2)}) copy-start(bf16[128,2048]{1,0:T(8,128)(2,1)S(1)} %get-tuple-element.47.refs_3_) | copy-start | bytes 1572868
  168.3 37.4 %copy-start.4 = (bf16[128,2048]{1,0:T(8,128)(2,1)}, bf16[128,2048]{1,0:T(8,128)(2,1)S(1)}, u32[]{:S(2)}) copy-start(bf16[128,2048]{1,0:T(8,128)(2,1)S(1)} %get-tuple-element.48.refs_2_) | copy-start | bytes 1572868
  168.4 37.3 %copy-start.5 = (bf16[128,2048]{1,0:T(8,128)(2,1)}, bf16[128,2048]{1,0:T(8,128)(2,1)S(1)}, u32[]{:S(2)}) copy-start(bf16[128,2048]{1,0:T(8,128)(2,1)S(1)} %get-tuple-element.52.refs_1_) | copy-start | bytes 1572868
  168.4 18.2 %collective-permute-start.16 = (bf16[128,2048]{1,0:T(8,128)(2,1)S(1)}, bf16[128,2048]{1,0:T(8,128)(2,1)S(1)}, u32[]{:S(2)}, u32[]{:S(2)}) collective-permute-start(bf16[128,2048]{1,0:T(8,128)(2,1)S(1)} %get-tuple-element.52.refs_1_), channel_id=1, source_target_pairs={{0,1},{1,0},{2,3},{3,2},{4,5},{5,4},{6,7},{7,6},{8,9},{9,8},{10,11... | collective-permute-start | bytes 1572872 | tf_op jit(solution)/shard_map/ppermute | solution.py:261
  169.9 27.9 %collective-permute-start.17 = (bf16[128,2048]{1,0:T(8,128)(2,1)S(1)}, bf16[128,2048]{1,0:T(8,128)(2,1)S(1)}, u32[]{:S(2)}, u32[]{:S(2)}) collective-permute-start(bf16[128,2048]{1,0:T(8,128)(2,1)S(1)} %get-tuple-element.48.refs_2_), channel_id=1, source_target_pairs={{0,1},{1,0},{2,3},{3,2},{4,5},{5,4},{6,7},{7,6},{8,9},{9,8},{10,11... | collective-permute-start | bytes 1572872 | tf_op jit(solution)/shard_map/ppermute | solution.py:261
  170.5 35.2 %collective-permute-start.18 = (bf16[128,2048]{1,0:T(8,128)(2,1)S(1)}, bf16[128,2048]{1,0:T(8,128)(2,1)}, u32[]{:S(2)}, u32[]{:S(2)}) collective-permute-start(bf16[128,2048]{1,0:T(8,128)(2,1)S(1)} %get-tuple-element.47.refs_3_), channel_id=1, source_target_pairs={{0,1},{1,0},{2,3},{3,2},{4,5},{5,4},{6,7},{7,6},{8,9},{9,8},{10,11... | collective-permute-start | bytes 1572872 | tf_op jit(solution)/shard_map/ppermute | solution.py:261
  171.9 4.1 %collective-permute-start.20 = (bf16[2,8,128]{2,1,0:T(8,128)(2,1)S(1)}, bf16[2,8,128]{2,1,0:T(8,128)(2,1)S(1)}, u32[]{:S(2)}, u32[]{:S(2)}) collective-permute-start(bf16[2,8,128]{2,1,0:T(8,128)(2,1)S(1)} %pad_maximum_fusion.5), channel_id=1, source_target_pairs={{0,2},{1,3},{2,0},{3,1},{4,6},{5,7},{6,4},{7,5},{8,10},{9,11},{10,... | collective-permute-start | bytes 12296 | tf_op jit(solution)/shard_map/ppermute | solution.py:784
  176.0 4.5 %collective-permute-start.21 = (bf16[4,8,128]{2,1,0:T(8,128)(2,1)S(1)}, bf16[4,8,128]{2,1,0:T(8,128)(2,1)S(1)}, u32[]{:S(2)}, u32[]{:S(2)}) collective-permute-start(bf16[4,8,128]{2,1,0:T(8,128)(2,1)S(1)} %pad_maximum_fusion.4), channel_id=1, source_target_pairs={{0,4},{1,5},{2,6},{3,7},{4,0},{5,1},{6,2},{7,3},{8,12},{9,13},{10,... | collective-permute-start | bytes 24584 | tf_op jit(solution)/shard_map/ppermute | solution.py:784
  183.3 22.4 %copy-start.11 = (bf16[128,2048]{1,0:T(8,128)(2,1)}, bf16[128,2048]{1,0:T(8,128)(2,1)S(1)}, u32[]{:S(2)}) copy-start(bf16[128,2048]{1,0:T(8,128)(2,1)S(1)} %collective-permute-done.15.refs_4_) | copy-start | bytes 1572868
  186.6 19.1 %copy-start.12 = (bf16[128,2048]{1,0:T(8,128)(2,1)}, bf16[128,2048]{1,0:T(8,128)(2,1)S(1)}, u32[]{:S(2)}) copy-start(bf16[128,2048]{1,0:T(8,128)(2,1)S(1)} %collective-permute-done.16.refs_5_) | copy-start | bytes 1572868
  197.8 7.9 %copy-start.13 = (bf16[128,2048]{1,0:T(8,128)(2,1)}, bf16[128,2048]{1,0:T(8,128)(2,1)S(1)}, u32[]{:S(2)}) copy-start(bf16[128,2048]{1,0:T(8,128)(2,1)S(1)} %collective-permute-done.17.refs_6_) | copy-start | bytes 1572868
  236.3 16.7 %copy-start.2 = (bf16[8,128,2048]{2,1,0:T(8,128)(2,1)S(1)}, bf16[8,128,2048]{2,1,0:T(8,128)(2,1)}, u32[]{:S(2)}) copy-start(bf16[8,128,2048]{2,1,0:T(8,128)(2,1)} %experts.1) | copy-start | bytes 12582916
  238.1 14.9 %collective-permute-start.25 = (bf16[128,2048]{1,0:T(8,128)(2,1)S(1)}, bf16[128,2048]{1,0:T(8,128)(2,1)S(1)}, u32[]{:S(2)}, u32[]{:S(2)}) collective-permute-start(bf16[128,2048]{1,0:T(8,128)(2,1)S(1)} %get-tuple-element.44), channel_id=1, source_target_pairs={{0,1},{1,0},{2,3},{3,2},{4,5},{5,4},{6,7},{7,6},{8,9},{9,8},{10,11... | collective-permute-start | bytes 1572872 | tf_op jit(solution)/shard_map/ppermute | solution.py:261
  238.8 25.5 %collective-permute-start.24 = (bf16[128,2048]{1,0:T(8,128)(2,1)S(1)}, bf16[128,2048]{1,0:T(8,128)(2,1)S(1)}, u32[]{:S(2)}, u32[]{:S(2)}) collective-permute-start(bf16[128,2048]{1,0:T(8,128)(2,1)S(1)} %get-tuple-element.45), channel_id=1, source_target_pairs={{0,1},{1,0},{2,3},{3,2},{4,5},{5,4},{6,7},{7,6},{8,9},{9,8},{10,11... | collective-permute-start | bytes 1572872 | tf_op jit(solution)/shard_map/ppermute | solution.py:261
  253.2 43.6 %copy-start.10 = (f32[128,2048]{1,0:T(8,128)S(1)}, f32[128,2048]{1,0:T(8,128)}, u32[]{:S(2)}) copy-start(f32[128,2048]{1,0:T(8,128)} %get-tuple-element.31) | copy-start | bytes 3145732
  253.2 11.1 %collective-permute-start.26 = (bf16[128,2048]{1,0:T(8,128)(2,1)S(1)}, bf16[128,2048]{1,0:T(8,128)(2,1)S(1)}, u32[]{:S(2)}, u32[]{:S(2)}) collective-permute-start(bf16[128,2048]{1,0:T(8,128)(2,1)S(1)} %fusion.2), channel_id=1, source_target_pairs={{0,2},{1,3},{8,10},{9,11},{16,18},{17,19},{24,26},{25,27}} | collective-permute-start | bytes 1572872 | tf_op jit(solution)/shard_map/ppermute | solution.py:265
  255.0 9.3 %collective-permute-start.29 = (bf16[128,2048]{1,0:T(8,128)(2,1)S(1)}, bf16[128,2048]{1,0:T(8,128)(2,1)S(1)}, u32[]{:S(2)}, u32[]{:S(2)}) collective-permute-start(bf16[128,2048]{1,0:T(8,128)(2,1)S(1)} %fusion.2), channel_id=1, source_target_pairs={{6,4},{7,5},{14,12},{15,13},{22,20},{23,21},{30,28},{31,29}} | collective-permute-start | bytes 1572872 | tf_op jit(solution)/shard_map/ppermute | solution.py:269
  255.7 19.8 %collective-permute-start.23 = (bf16[128,2048]{1,0:T(8,128)(2,1)S(1)}, bf16[128,2048]{1,0:T(8,128)(2,1)S(1)}, u32[]{:S(2)}, u32[]{:S(2)}) collective-permute-start(bf16[128,2048]{1,0:T(8,128)(2,1)S(1)} %get-tuple-element.46), channel_id=1, source_target_pairs={{0,1},{1,0},{2,3},{3,2},{4,5},{5,4},{6,7},{7,6},{8,9},{9,8},{10,11... | collective-permute-start | bytes 1572872 | tf_op jit(solution)/shard_map/ppermute | solution.py:261
  264.3 33.6 %copy-start.1 = (bf16[256,2048]{1,0:T(8,128)(2,1)S(1)}, bf16[256,2048]{1,0:T(8,128)(2,1)}, u32[]{:S(2)}) copy-start(bf16[256,2048]{1,0:T(8,128)(2,1)} %param.24) | copy-start | bytes 3145732
  264.8 12.4 %collective-permute-start.27 = (bf16[128,2048]{1,0:T(8,128)(2,1)S(1)}, bf16[128,2048]{1,0:T(8,128)(2,1)S(1)}, u32[]{:S(2)}, u32[]{:S(2)}) collective-permute-start(bf16[128,2048]{1,0:T(8,128)(2,1)S(1)} %get-tuple-element.39), channel_id=1, source_target_pairs={{0,2},{1,3},{2,4},{3,5},{8,10},{9,11},{10,12},{11,13},{16,18},{17,... | collective-permute-start | bytes 1572872 | tf_op jit(solution)/shard_map/ppermute | solution.py:265
  269.2 8.0 %collective-permute-start.30 = (bf16[128,2048]{1,0:T(8,128)(2,1)S(1)}, bf16[128,2048]{1,0:T(8,128)(2,1)S(1)}, u32[]{:S(2)}, u32[]{:S(2)}) collective-permute-start(bf16[128,2048]{1,0:T(8,128)(2,1)S(1)} %get-tuple-element.40), channel_id=1, source_target_pairs={{4,2},{5,3},{6,4},{7,5},{12,10},{13,11},{14,12},{15,13},{20,18},{2... | collective-permute-start | bytes 1572872 | tf_op jit(solution)/shard_map/ppermute | solution.py:269
  269.9 20.2 %collective-permute-start.22 = (bf16[128,2048]{1,0:T(8,128)(2,1)S(1)}, bf16[128,2048]{1,0:T(8,128)(2,1)S(1)}, u32[]{:S(2)}, u32[]{:S(2)}) collective-permute-start(bf16[128,2048]{1,0:T(8,128)(2,1)S(1)} %get-tuple-element.43), channel_id=1, source_target_pairs={{0,1},{1,0},{2,3},{3,2},{4,5},{5,4},{6,7},{7,6},{8,9},{9,8},{10,11... | collective-permute-start | bytes 1572872 | tf_op jit(solution)/shard_map/ppermute | solution.py:261
  277.9 17.4 %collective-permute-start.31 = (bf16[128,2048]{1,0:T(8,128)(2,1)S(1)}, bf16[128,2048]{1,0:T(8,128)(2,1)S(1)}, u32[]{:S(2)}, u32[]{:S(2)}) collective-permute-start(bf16[128,2048]{1,0:T(8,128)(2,1)S(1)} %get-tuple-element.42), channel_id=1, source_target_pairs={{2,0},{3,1},{4,2},{5,3},{6,4},{7,5},{10,8},{11,9},{12,10},{13,11},... | collective-permute-start | bytes 1572872 | tf_op jit(solution)/shard_map/ppermute | solution.py:269
  279.2 17.6 %collective-permute-start.28 = (bf16[128,2048]{1,0:T(8,128)(2,1)S(1)}, bf16[128,2048]{1,0:T(8,128)(2,1)S(1)}, u32[]{:S(2)}, u32[]{:S(2)}) collective-permute-start(bf16[128,2048]{1,0:T(8,128)(2,1)S(1)} %get-tuple-element.41), channel_id=1, source_target_pairs={{0,2},{1,3},{2,4},{3,5},{4,6},{5,7},{8,10},{9,11},{10,12},{11,13},... | collective-permute-start | bytes 1572872 | tf_op jit(solution)/shard_map/ppermute | solution.py:265
Sparse Core Ops, SparseCore 0:
  9.5 76.1 all-gather.1

commit v2 on v1

--- a/solution.py
+++ b/solution.py
@@ -269,18 +269,6 @@
     return lax.ppermute(array, "exp", [(i, i - 2) for i in range(8 - 2 * sources, 8)])
 
 
-def row_meta(lengths, groups):
-    ends = jnp.cumsum(lengths, axis=-1)
-    starts = ends - lengths
-    blocks = jnp.arange(ROW_TOK // BLK, dtype=jnp.int32)[None, :, None] * BLK
-    overlap = (starts[:, None, :] < blocks + BLK) & (ends[:, None, :] > blocks)
-    bits = jnp.zeros(overlap.shape[:2], jnp.int32)
-    for g in range(G):
-        present = jnp.any(overlap & (groups[:, None, :] == g), axis=-1)
-        bits = bits + (present.astype(jnp.int32) << g)
-    return jnp.concatenate([starts, groups, bits], axis=1)
-
-
 def send_halves_kernel(sc_ref, q, k, v, pk, pv, out_qkv, out_pk, out_pv):
     out_qkv[0] = q[...]
     out_qkv[1] = k[...]
@@ -316,138 +304,234 @@
     )(core, q, k, v, pk, pv)
 
 
-def token_columns(meta_ref, row, first_token, count):
-    token = first_token + lax.broadcasted_iota(jnp.int32, (count, 1), 0)
-    group = jnp.full((count, 1), meta_ref[row, RQ], jnp.int32)
-    first = jnp.zeros((count, 1), jnp.int32)
+def as_row(column):
+    return jnp.transpose(jnp.broadcast_to(column, (BLK, BLK)))[0:1, :]
+
+
+SUF = 256
+SUB = 32
+PER_ITEM = 8
+ITEMS = 16
+
+
+def prefix_work(lengths, groups):
+    rows = lengths.shape[0]
+    ends = jnp.cumsum(lengths, axis=-1)
+    starts = ends - lengths
+    blocks = rows * ROW_TOK // SUB
+    at = (jnp.arange(ROW_TOK // SUB, dtype=jnp.int32) * SUB)[None, :, None]
+    overlap = (starts[:, None, :] < at + SUB) & (ends[:, None, :] > at)
+    of_group = groups[None, :, None, :] == jnp.arange(G, dtype=jnp.int32)[:, None, None, None]
+    present = jnp.any(overlap[None] & of_group, axis=-1).reshape(G, blocks).astype(jnp.int32)
+    items = (jnp.sum(present, axis=1) + PER_ITEM - 1) // PER_ITEM
+    base = (jnp.cumsum(items) - items) * PER_ITEM
+    slot = jnp.where(present > 0, base[:, None] + jnp.cumsum(present, axis=1) - 1, -1)
+    value = jnp.arange(G * blocks, dtype=jnp.int32) + 1
+    hit = slot.reshape(1, -1) == jnp.arange(ITEMS * PER_ITEM, dtype=jnp.int32)[:, None]
+    held = jnp.sum(jnp.where(hit, value[None, :], 0), axis=1).reshape(ITEMS, PER_ITEM)
+    held = jnp.where(held > 0, held, held[:, :1])
+    held = (jnp.where(held > 0, held, held[:1, :1]) - 1).reshape(-1)
+    return jnp.concatenate(
+        [starts.reshape(-1), groups.reshape(-1), jnp.sum(items).reshape(1), held // blocks, held % blocks]
+    )
+
+
+def prefix_kernel(work_ref, q_ref, ka, kb, va, vb, o_ref, lse_ref, grp, lse, sa, sb, ta, tb):
+    tokens = q_ref.shape[0]
+    rows = tokens // ROW_TOK
+    span = va.shape[1]
+    head = 2 * rows * RQ
+    for r in range(rows):
+        token = lax.broadcasted_iota(jnp.int32, (ROW_TOK, HEAD), 0)
+        group = jnp.full((ROW_TOK, HEAD), work_ref[(rows + r) * RQ], jnp.int32)
+        for j in range(1, RQ):
+            group = jnp.where(
+                token >= work_ref[r * RQ + j], work_ref[(rows + r) * RQ + j], group
+            )
+        grp[r * ROW_TOK : (r + 1) * ROW_TOK, :] = group
+    step = 512
+
+    def places(item):
+        at = head + 1 + ITEMS * PER_ITEM + item * PER_ITEM
+        return [
+            pl.ds(pl.multiple_of(work_ref[at + i] * SUB, SUB), SUB) for i in range(PER_ITEM)
+        ]
+
+    def group_of(item):
+        return work_ref[head + 1 + item * PER_ITEM]
+
+    def lanes(x, op):
+        parts = [x[:, c : c + HEAD] for c in range(0, x.shape[1], HEAD)]
+        while len(parts) > 1:
+            parts = [op(a, b) for a, b in zip(parts[::2], parts[1::2])]
+        return parts[0]
+
+    def score(item, s, tops):
+        g = group_of(item)
+        q = jnp.concatenate([q_ref[place, :] for place in places(item)], axis=0)
+        for half, k in enumerate((ka, kb)):
+            for c in range(0, span, step):
+                x = lax.dot_general(
+                    q,
+                    k[g, c : c + step, :],
+                    (((1,), (1,)), ((), ())),
+                    preferred_element_type=jnp.float32,
+                )
+                s[:, half * span + c : half * span + c + step] = x
+                top = lanes(x, jnp.maximum)
+                tops[...] = top if half == 0 and c == 0 else jnp.maximum(tops[...], top)
+
+    def weigh(item, s, tops):
+        g = group_of(item)
+        where = places(item)
+        for part in range(2):
+            here = slice(part * BLK, (part + 1) * BLK)
+            top = jnp.max(tops[here, :], axis=1, keepdims=True)
+            out = jnp.zeros((BLK, HEAD), jnp.float32)
+            total = jnp.zeros((BLK, HEAD), jnp.float32)
+            for half, v in enumerate((va, vb)):
+                for c in range(0, span, step):
+                    x = s[here, half * span + c : half * span + c + step]
+                    p = jnp.exp2((x - top) * SCORE_SCALE)
+                    total = total + lanes(p, jnp.add)
+                    out = out + jnp.dot(
+                        p.astype(jnp.bfloat16),
+                        v[g, c : c + step, :],
+                        preferred_element_type=jnp.float32,
+                    )
+            total = jnp.sum(total, axis=1, keepdims=True)
+            out = out * (1.0 / total)
+            here_lse = jnp.broadcast_to(top * SCORE_SCALE + jnp.log2(total), (BLK, HEAD))
+            for i in range(BLK // SUB):
+                place = where[part * (BLK // SUB) + i]
+                sub = slice(i * SUB, (i + 1) * SUB)
+                mine = grp[place, :] == g
+                o_ref[place, :] = jnp.where(
+                    mine, out[sub], o_ref[place, :].astype(jnp.float32)
+                ).astype(o_ref.dtype)
+                lse[place, :] = jnp.where(mine, here_lse[sub], lse[place, :])
+
+    count = work_ref[head]
+    score(0, sa, ta)
+
+    def pair(i, carry):
+        second = jnp.minimum(2 * i + 1, ITEMS - 1)
+        third = jnp.minimum(2 * i + 2, ITEMS - 1)
+        score(second, sb, tb)
+        weigh(2 * i, sa, ta)
+        score(third, sa, ta)
+        weigh(second, sb, tb)
+        return carry
+
+    lax.fori_loop(0, (count + 1) // 2, pair, 0)
+    for b in range(tokens // BLK):
+        lse_ref[b : b + 1, :] = jnp.transpose(lse[b * BLK : (b + 1) * BLK, :])[0:1, :]
+
+
+def prefix_attend(work, core, q, pk, pk_other, pv, pv_other, out_dtype):
+    tokens, unused = q.shape
+    span = pv.shape[1]
+    own = pl.BlockSpec((G, span, HEAD), lambda i, s: (0, 0, s[0]))
+    whole = pl.BlockSpec((G, span, HEAD), lambda i, s: (0, 0, 0))
+    blocks = tokens // BLK
+
+    def body(core_ref, *refs):
+        prefix_kernel(*refs)
+
+    return pl.pallas_call(
+        body,
+        grid_spec=pltpu.PrefetchScalarGridSpec(
+            num_scalar_prefetch=1,
+            grid=(1,),
+            in_specs=[
+                pl.BlockSpec(memory_space=pltpu.SMEM),
+                pl.BlockSpec((tokens, HEAD), lambda i, s: (0, 0)),
+                own,
+                whole,
+                own,
+                whole,
+            ],
+            out_specs=[
+                pl.BlockSpec((tokens, HEAD), lambda i, s: (0, 0)),
+                pl.BlockSpec((blocks, BLK), lambda i, s: (0, 0)),
+            ],
+            scratch_shapes=[
+                pltpu.VMEM((tokens, HEAD), jnp.int32),
+                pltpu.VMEM((tokens, HEAD), jnp.float32),
+                pltpu.VMEM((PER_ITEM * SUB, 2 * span), jnp.float32),
+                pltpu.VMEM((PER_ITEM * SUB, 2 * span), jnp.float32),
+                pltpu.VMEM((PER_ITEM * SUB, HEAD), jnp.float32),
+                pltpu.VMEM((PER_ITEM * SUB, HEAD), jnp.float32),
+            ],
+        ),
+        out_shape=(
+            jax.ShapeDtypeStruct((tokens, HEAD), out_dtype),
+            jax.ShapeDtypeStruct((blocks, BLK), jnp.float32),
+        ),
+        compiler_params=pltpu.CompilerParams(vmem_limit_bytes=VMEM_BIG),
+        cost_estimate=pl.CostEstimate(
+            flops=tokens * span * HEAD * 8 * 4,
+            bytes_accessed=4 * G * span * HEAD * 2,
+            transcendentals=0,
+        ),
+        name="prefix_attend",
+    )(core, work, q, pk, pk_other, pv, pv_other)
+
+
+def suffix_kernel(meta_ref, q_ref, k_ref, v_ref, o_ref, lse_ref):
+    row = pl.program_id(0)
+    token = lax.broadcasted_iota(jnp.int32, (ROW_TOK, 1), 0)
+    first = jnp.zeros((ROW_TOK, 1), jnp.int32)
     for j in range(1, RQ):
         start = meta_ref[row, j]
-        later = token >= start
-        group = jnp.where(later, meta_ref[row, RQ + j], group)
-        first = jnp.where(later, start, first)
-    return token, group, first
-
-
-def as_row(column):
-    return jnp.transpose(jnp.broadcast_to(column, (BLK, BLK)))[0:1, :]
-
-
-def prefix_kernel(meta_ref, sc_ref, q_ref, ka, kb, va, vb, o_ref, lse_ref):
-    row, block = pl.program_id(0), pl.program_id(1)
-    token, group, unused = token_columns(meta_ref, row, block * BLK, BLK)
-    bits = meta_ref[row, 2 * RQ + block]
-    contract = (((1,), (1,)), ((), ()))
-
-    def attend(g, carry):
-        @pl.when((bits >> g) & 1 == 1)
-        def held():
-            q = q_ref[0]
-            sa = lax.dot_general(q, ka[g], contract, preferred_element_type=jnp.float32)
-            sb = lax.dot_general(q, kb[g], contract, preferred_element_type=jnp.float32)
-            top = jnp.maximum(
-                jnp.max(sa, axis=1, keepdims=True), jnp.max(sb, axis=1, keepdims=True)
-            )
-            pa = jnp.exp2((sa - top) * SCORE_SCALE)
-            pb = jnp.exp2((sb - top) * SCORE_SCALE)
-            total = jnp.sum(pa, axis=1, keepdims=True) + jnp.sum(pb, axis=1, keepdims=True)
-            out = jnp.dot(
-                pa.astype(jnp.bfloat16), va[g], preferred_element_type=jnp.float32
-            ) + jnp.dot(pb.astype(jnp.bfloat16), vb[g], preferred_element_type=jnp.float32)
-            mine = group == g
-            o_ref[0] = jnp.where(mine, out / total, o_ref[0].astype(jnp.float32)).astype(o_ref.dtype)
-            lse = as_row(top * SCORE_SCALE + jnp.log2(total))
-            mine_row = as_row(mine.astype(jnp.float32)) > 0.5
-            here = pl.ds(block, 1)
-            lse_ref[0, here, :] = jnp.where(mine_row, lse, lse_ref[0, here, :])
-
-        return carry
-
-    lax.fori_loop(0, G, attend, 0)
-
-
-def prefix_attend(meta, core, q, pk, pk_other, pv, pv_other, out_dtype):
+        first = jnp.where(token >= start, start, first)
+
+    def score(i):
+        low = max(0, i * SUF - ROW_TOK // 2)
+        here, seen = slice(i * SUF, (i + 1) * SUF), slice(low, (i + 1) * SUF)
+        s = lax.dot_general(
+            q_ref[0, here, :],
+            k_ref[0, seen, :],
+            (((1,), (1,)), ((), ())),
+            preferred_element_type=jnp.float32,
+        )
+        other = low + lax.broadcasted_iota(jnp.int32, s.shape, 1)
+        return jnp.where((other >= first[here]) & (other <= token[here]), s, NEG)
+
+    def weigh(i, s):
+        low = max(0, i * SUF - ROW_TOK // 2)
+        here, seen = slice(i * SUF, (i + 1) * SUF), slice(low, (i + 1) * SUF)
+        top = jnp.max(s, axis=1, keepdims=True)
+        p = jnp.exp2((s - top) * SCORE_SCALE)
+        total = jnp.sum(p, axis=1, keepdims=True)
+        out = jnp.dot(
+            p.astype(jnp.bfloat16), v_ref[0, seen, :], preferred_element_type=jnp.float32
+        )
+        o_ref[0, here, :] = out * (1.0 / total)
+        lse = top * SCORE_SCALE + jnp.log2(total)
+        for part in range(SUF // BLK):
+            at = i * (SUF // BLK) + part
+            lse_ref[0, at : at + 1, :] = as_row(lse[part * BLK : (part + 1) * BLK])
+
+    count = ROW_TOK // SUF
+    held = score(0)
+    for i in range(count):
+        later = score(i + 1) if i + 1 < count else None
+        weigh(i, held)
+        held = later
+
+
+def suffix_attend(starts, q, k, v):
     rows, tokens, unused = q.shape
-    span = pk.shape[1]
-    own = pl.BlockSpec((G, span, HEAD), lambda r, b, m, s: (0, 0, s[0]))
-    other = pl.BlockSpec((G, span, HEAD), lambda r, b, m, s: (0, 0, 0))
-    blocks = tokens // BLK
-    return pl.pallas_call(
-        prefix_kernel,
-        grid_spec=pltpu.PrefetchScalarGridSpec(
-            num_scalar_prefetch=2,
-            grid=(rows, blocks),
-            in_specs=[
-                pl.BlockSpec((1, BLK, HEAD), lambda r, b, m, s: (r, b, 0)),
-                own,
-                other,
-                own,
-                other,
-            ],
-            out_specs=[
-                pl.BlockSpec((1, BLK, HEAD), lambda r, b, m, s: (r, b, 0)),
-                pl.BlockSpec((1, blocks, BLK), lambda r, b, m, s: (r, 0, 0)),
-            ],
-        ),
-        out_shape=(
-            jax.ShapeDtypeStruct((rows, tokens, HEAD), out_dtype),
-            jax.ShapeDtypeStruct((rows, blocks, BLK), jnp.float32),
-        ),
-        compiler_params=pltpu.CompilerParams(vmem_limit_bytes=VMEM_BIG),
-        cost_estimate=pl.CostEstimate(
-            flops=rows * tokens * span * HEAD * 8 * 4,
-            bytes_accessed=4 * G * span * HEAD * 2,
-            transcendentals=0,
-        ),
-        name="prefix_attend",
-    )(meta, core, q, pk, pk_other, pv, pv_other)
-
-
-SUF = 256
-
-
-def suffix_kernel(meta_ref, q_ref, k_ref, v_ref, o_ref, lse_ref):
-    row, block = pl.program_id(0), pl.program_id(1)
-    for i in range(ROW_TOK // SUF):
-
-        @pl.when(block == i)
-        def held():
-            width = (i + 1) * SUF
-            token, unused, first = token_columns(meta_ref, row, i * SUF, SUF)
-            s = lax.dot_general(
-                q_ref[0],
-                k_ref[0, :width, :],
-                (((1,), (1,)), ((), ())),
-                preferred_element_type=jnp.float32,
-            )
-            other = lax.broadcasted_iota(jnp.int32, (SUF, width), 1)
-            s = jnp.where((other >= first) & (other <= token), s, NEG)
-            top = jnp.max(s, axis=1, keepdims=True)
-            p = jnp.exp2((s - top) * SCORE_SCALE)
-            total = jnp.sum(p, axis=1, keepdims=True)
-            out = jnp.dot(
-                p.astype(jnp.bfloat16), v_ref[0, :width, :], preferred_element_type=jnp.float32
-            )
-            o_ref[0] = out / total
-            lse = top * SCORE_SCALE + jnp.log2(total)
-            for part in range(SUF // BLK):
-                place = i * (SUF // BLK) + part
-                lse_ref[0, place : place + 1, :] = as_row(lse[part * BLK : (part + 1) * BLK])
-
-
-def suffix_attend(meta, q, k, v):
-    rows, tokens, unused = q.shape
-    whole = pl.BlockSpec((1, tokens, HEAD), lambda r, b, m: (r, 0, 0))
+    whole = pl.BlockSpec((1, tokens, HEAD), lambda r, b: (r, 0, 0))
     blocks = tokens // BLK
     return pl.pallas_call(
         suffix_kernel,
         grid_spec=pltpu.PrefetchScalarGridSpec(
             num_scalar_prefetch=1,
-            grid=(rows, tokens // SUF),
-            in_specs=[pl.BlockSpec((1, SUF, HEAD), lambda r, b, m: (r, b, 0)), whole, whole],
-            out_specs=[
-                pl.BlockSpec((1, SUF, HEAD), lambda r, b, m: (r, b, 0)),
-                pl.BlockSpec((1, blocks, BLK), lambda r, b, m: (r, 0, 0)),
-            ],
+            grid=(rows,),
+            in_specs=[whole] * 3,
+            out_specs=[whole, pl.BlockSpec((1, blocks, BLK), lambda r, b: (r, 0, 0))],
         ),
         out_shape=(
             jax.ShapeDtypeStruct((rows, tokens, HEAD), jnp.float32),
@@ -458,29 +542,33 @@
             flops=rows * tokens * tokens * HEAD * 4 * 4, bytes_accessed=1 << 20, transcendentals=0
         ),
         name="suffix_attend",
-    )(meta, q, k, v)
+    )(starts, q, k, v)
+
+
+MERGE_BLOCKS = 4
 
 
 def merge_kernel(*refs):
     parts, out_ref = refs[:-1], refs[-1]
-    block = pl.program_id(0)
+    step = pl.program_id(0)
     half = len(parts) // 2
     for row in range(2):
         sources = parts[row * half : (row + 1) * half]
-        lses = [
-            jnp.transpose(jnp.broadcast_to(lse[0, pl.ds(block, 1), :], (BLK, BLK)))
-            for lse in sources[1::2]
-        ]
-        top = lses[0]
-        for lse in lses[1:]:
-            top = jnp.maximum(top, lse)
-        weights = [jnp.exp2(lse - top) for lse in lses]
-        total = weights[0]
-        summed = weights[0] * sources[0][0].astype(jnp.float32)
-        for weight, o in zip(weights[1:], sources[2::2]):
-            total = total + weight
-            summed = summed + weight * o[0].astype(jnp.float32)
-        out_ref[0, row * BLK : (row + 1) * BLK, :] = (summed / total).astype(out_ref.dtype)
+        for block in range(MERGE_BLOCKS):
+            here = slice(block * BLK, (block + 1) * BLK)
+            at = pl.ds(step * MERGE_BLOCKS + block, 1)
+            lses = [
+                jnp.transpose(jnp.broadcast_to(lse[0, at, :], (BLK, BLK))) for lse in sources[1::2]
+            ]
+            top = lses[0]
+            for lse in lses[1:]:
+                top = jnp.maximum(top, lse)
+            total, summed = 0.0, 0.0
+            for lse, o in zip(lses, sources[0::2]):
+                weight = jnp.exp2(lse - top)
+                total = total + weight
+                summed = summed + weight * o[0, here, :].astype(jnp.float32)
+            out_ref[block, row * BLK : (row + 1) * BLK, :] = (summed / total).astype(out_ref.dtype)
 
 
 def merge_parts(parts):
@@ -490,14 +578,14 @@
         for o, lse, index in row:
             operands += [o, lse]
             specs += [
-                pl.BlockSpec((1, BLK, HEAD), lambda b, index=index: (index, b, 0)),
+                pl.BlockSpec((1, MERGE_BLOCKS * BLK, HEAD), lambda b, index=index: (index, b, 0)),
                 pl.BlockSpec((1, blocks, BLK), lambda b, index=index: (index, 0, 0)),
             ]
     return pl.pallas_call(
         merge_kernel,
-        grid=(blocks,),
+        grid=(blocks // MERGE_BLOCKS,),
         in_specs=specs,
-        out_specs=pl.BlockSpec((1, 2 * BLK, HEAD), lambda b: (b, 0, 0)),
+        out_specs=pl.BlockSpec((MERGE_BLOCKS, 2 * BLK, HEAD), lambda b: (b, 0, 0)),
         out_shape=jax.ShapeDtypeStruct((blocks, 2 * BLK, HEAD), jnp.bfloat16),
         name="merge_parts",
     )(*operands)
@@ -557,135 +645,87 @@
 
 
 EXP_DEV = 4
-CAP_ROWS = 256
-
-
-def route_kernel(sc_ref, tab_ref, row_ref, col_ref, scr):
+SLOTS = 32
+
+
+def route_kernel(sc_ref, tab_ref, pick_ref, give_ref):
+    before = (
+        lax.broadcasted_iota(jnp.int32, (BLK, BLK), 0)
+        < lax.broadcasted_iota(jnp.int32, (BLK, BLK), 1)
+    ).astype(jnp.bfloat16)
+    place = lax.broadcasted_iota(jnp.int32, (SLOTS, BLK), 0).astype(jnp.float32)
     for slot in range(8):
         tab = tab_ref[sc_ref[slot]].astype(jnp.float32)
         ids, gates = tab[:TOPK], tab[TOPK:]
-        here = slice(slot * BLK, (slot + 1) * BLK)
+        chosen, weights = [], []
         for j in range(EXP_DEV):
-            chosen = ids == (sc_ref[8] + j).astype(jnp.float32)
-            scr[j : j + 1, here] = jnp.sum(chosen.astype(jnp.float32), axis=0, keepdims=True)
-            scr[EXP_DEV + j : EXP_DEV + j + 1, here] = jnp.sum(
-                jnp.where(chosen, gates, 0.0), axis=0, keepdims=True
-            )
-    held = scr[...]
-    count = held.shape[1]
-    before = (
-        lax.broadcasted_iota(jnp.int32, (count, count), 0)
-        < lax.broadcasted_iota(jnp.int32, (count, count), 1)
-    ).astype(jnp.bfloat16)
-    places = jnp.dot(held.astype(jnp.bfloat16), before, preferred_element_type=jnp.float32)
-    place_row = lax.broadcasted_iota(jnp.int32, held.shape, 0) < EXP_DEV
-    chosen = jnp.concatenate([held[:EXP_DEV], held[:EXP_DEV]], axis=0) > 0.5
-    table = jnp.where(place_row, jnp.where(chosen, places, -1.0), held)
-    row_ref[...] = table
-    for slot in range(8):
-        here = slice(slot * BLK, (slot + 1) * BLK)
-        tall = jnp.concatenate([table[:, here], jnp.zeros((BLK - 8, BLK), jnp.float32)], axis=0)
-        col_ref[here, :] = jnp.transpose(tall)
+            match = ids == (sc_ref[8] + j).astype(jnp.float32)
+            chosen.append(jnp.sum(match.astype(jnp.float32), axis=0, keepdims=True))
+            weights.append(jnp.sum(jnp.where(match, gates, 0.0), axis=0, keepdims=True))
+        held = jnp.concatenate(chosen + chosen, axis=0)
+        places = jnp.dot(held.astype(jnp.bfloat16), before, preferred_element_type=jnp.float32)
+        places = jnp.where(held > 0.5, places, -1.0)
+        hits = [place == places[j : j + 1] for j in range(EXP_DEV)]
+        pick_ref[slot] = jnp.concatenate(
+            [hit.astype(jnp.float32) for hit in hits], axis=0
+        ).astype(jnp.bfloat16)
+        spread = jnp.concatenate(
+            [jnp.where(hit, weight, 0.0) for hit, weight in zip(hits, weights)], axis=0
+        )
+        give_ref[slot] = jnp.transpose(spread).astype(jnp.bfloat16)
 
 
 def route(scalars, tab):
-    tokens = tab.shape[0] * BLK
+    shape = jax.ShapeDtypeStruct((8, BLK, EXP_DEV * SLOTS), jnp.bfloat16)
     return pl.pallas_call(
         route_kernel,
         in_specs=[
             pl.BlockSpec(memory_space=pltpu.SMEM),
             pl.BlockSpec(memory_space=pltpu.VMEM),
         ],
-        out_shape=(
-            jax.ShapeDtypeStruct((8, tokens), jnp.float32),
-            jax.ShapeDtypeStruct((tokens, BLK), jnp.float32),
-        ),
-        scratch_shapes=[pltpu.VMEM((8, tokens), jnp.float32)],
+        out_shape=(shape, shape),
         name="route",
     )(scalars, tab)
 
 
 def experts_kernel(*refs):
-    chunks = refs[:8]
-    row_ref, col_ref, wg, wu, wd, out_ref, rows_in, rows_out, sems = refs[8:]
+    picked = refs[:8]
+    give_ref, wg, wu, wd, out_ref, rows_out = refs[8:]
     expert = pl.program_id(0)
-    tokens = rows_in.shape[0]
-
-    @pl.when(expert == 0)
-    def first():
-        copies = [
-            pltpu.make_async_copy(
-                chunk, rows_in.at[i * BLK : (i + 1) * BLK, :], sems.at[i]
-            )
-            for i, chunk in enumerate(chunks)
-        ]
-        for copy in copies:
-            copy.start()
-        for copy in copies:
-            copy.wait()
-
-    places = row_ref[pl.ds(expert, 1), :]
-    slots = lax.broadcasted_iota(jnp.int32, (CAP_ROWS, tokens), 0).astype(jnp.float32)
-    pick = (slots == places).astype(jnp.bfloat16)
-    picked = jnp.dot(pick, rows_in[...], preferred_element_type=jnp.float32).astype(jnp.bfloat16)
+    rows = jnp.concatenate([part[...] for part in picked], axis=0)
     contract = (((1,), (1,)), ((), ()))
-    gate_h = lax.dot_general(picked, wg[0], contract, preferred_element_type=jnp.float32)
-    up_h = lax.dot_general(picked, wu[0], contract, preferred_element_type=jnp.float32)
+    gate_h = lax.dot_general(rows, wg[0], contract, preferred_element_type=jnp.float32)
+    up_h = lax.dot_general(rows, wu[0], contract, preferred_element_type=jnp.float32)
     hidden = (gate_h / (1.0 + jnp.exp(-gate_h)) * up_h).astype(jnp.bfloat16)
-    out = jnp.dot(hidden, wd[0], preferred_element_type=jnp.float32)
-    rows_out[pl.ds(pl.multiple_of(expert * CAP_ROWS, CAP_ROWS), CAP_ROWS), :] = out.astype(
-        jnp.bfloat16
-    )
+    out = jnp.dot(hidden, wd[0], preferred_element_type=jnp.float32).astype(jnp.bfloat16)
+    here = pl.ds(pl.multiple_of(expert * SLOTS, SLOTS), SLOTS)
+    for slot in range(8):
+        rows_out[slot, here, :] = out[slot * SLOTS : (slot + 1) * SLOTS]
 
     @pl.when(expert == EXP_DEV - 1)
     def last():
-        def give(i, carry):
-            here = pl.ds(pl.multiple_of(i * BLK, BLK), BLK)
-            cols = col_ref[here, :]
-            slot = lax.broadcasted_iota(jnp.int32, (BLK, CAP_ROWS), 1).astype(jnp.float32)
-            weights = jnp.concatenate(
-                [
-                    jnp.where(
-                        slot == cols[:, j : j + 1], cols[:, EXP_DEV + j : EXP_DEV + j + 1], 0.0
-                    ).astype(jnp.bfloat16)
-                    for j in range(EXP_DEV)
-                ],
-                axis=1,
-            )
-            out_ref[i] = jnp.dot(
-                weights, rows_out[...], preferred_element_type=jnp.float32
+        for slot in range(8):
+            out_ref[slot] = jnp.dot(
+                give_ref[slot], rows_out[slot], preferred_element_type=jnp.float32
             ).astype(out_ref.dtype)
-            return carry
-
-        lax.fori_loop(0, tokens // BLK, give, 0)
-
-
-def run_experts(chunks, row_tab, col_tab, w_gate, w_up, w_down):
-    width = chunks[0].shape[1]
+
+
+def run_experts(picked, give, w_gate, w_up, w_down):
+    width = picked[0].shape[1]
     hidden = w_down.shape[1]
-    tokens = len(chunks) * BLK
     once = pl.Buffered(1)
     return pl.pallas_call(
         experts_kernel,
         grid=(EXP_DEV,),
-        in_specs=[pl.BlockSpec(memory_space=pl.ANY)] * 8
-        + [
-            pl.BlockSpec((8, tokens), lambda j: (0, 0)),
-            pl.BlockSpec((tokens, BLK), lambda j: (0, 0)),
-            pl.BlockSpec((1, hidden, width), lambda j: (j, 0, 0)),
-            pl.BlockSpec((1, hidden, width), lambda j: (j, 0, 0)),
-            pl.BlockSpec((1, hidden, width), lambda j: (j, 0, 0)),
-        ],
+        in_specs=[pl.BlockSpec((SLOTS, width), lambda j: (j, 0))] * 8
+        + [pl.BlockSpec((8, BLK, BLK), lambda j: (0, 0, 0))]
+        + [pl.BlockSpec((1, hidden, width), lambda j: (j, 0, 0))] * 3,
         out_specs=pl.BlockSpec((8, BLK, width), lambda j: (0, 0, 0), pipeline_mode=once),
         out_shape=jax.ShapeDtypeStruct((8, BLK, width), jnp.bfloat16),
-        scratch_shapes=[
-            pltpu.VMEM((tokens, width), jnp.bfloat16),
-            pltpu.VMEM((EXP_DEV * CAP_ROWS, width), jnp.bfloat16),
-            pltpu.SemaphoreType.DMA((8,)),
-        ],
+        scratch_shapes=[pltpu.VMEM((8, EXP_DEV * SLOTS, width), jnp.bfloat16)],
         compiler_params=pltpu.CompilerParams(vmem_limit_bytes=VMEM_BIG),
         name="experts",
-    )(*chunks, row_tab, col_tab, w_gate.transpose(0, 2, 1), w_up.transpose(0, 2, 1), w_down)
+    )(*picked, give, w_gate.transpose(0, 2, 1), w_up.transpose(0, 2, 1), w_down)
 
 
 def pick_by_z(z, *choices):
@@ -699,18 +739,18 @@
 SLOT_Z = ((0, 1, 2, 3), (1, 0, 2, 3), (2, 1, 3, 0), (3, 2, 1, 0))
 
 
+def together(*arrays):
+    return lax.optimization_barrier(arrays)
+
+
 def gather_rows(z, own):
-    up, down = z_up(own), z_down(own)
-    there = [y_swap(own)]
+    up, down, there0 = together(z_up(own), z_down(own), y_swap(own))
     first = pick_by_z(z, down, up, up, up)
-    up2, down2 = z_up(up), z_down(down)
-    there.append(y_swap(first))
+    up2, down2, there1 = together(z_up(up), z_down(down), y_swap(first))
     second = pick_by_z(z, down2, down, down, up2)
-    up3, down3 = z_up(up2), z_down(down2)
-    there.append(y_swap(second))
+    up3, down3, there2 = together(z_up(up2), z_down(down2), y_swap(second))
     third = pick_by_z(z, down3, down2, up2, up3)
-    there.append(y_swap(third))
-    return [own, first, second, third] + there
+    return [own, first, second, third, there0, there1, there2, y_swap(third)]
 
 
 def scatter_sums(z, sums):
@@ -762,7 +802,6 @@
     shape = jnp.concatenate([lengths, groups], axis=1)
     shapes = jnp.concatenate([shape, core_swap(shape)], axis=0)
     shapes = jnp.concatenate([shapes, x_swap(shapes)], axis=0)
-    meta = row_meta(shapes[:, :RQ], shapes[:, RQ:])
 
     qkv_theirs, pk_theirs, pv_theirs = send_halves(
         core_arg, queries, keys, values, prefix_keys, prefix_values
@@ -788,17 +827,28 @@
         [slot_z * 2 + lax.rem(place, 2), slot_z * 2 + 1 - lax.rem(place, 2)]
     )
     scalars = jnp.concatenate([slot_place ^ place, (place * EXP_DEV).reshape(1)])
-    row_tab, col_tab = route(scalars.astype(jnp.int32), tab)
+    pick, give = route(scalars.astype(jnp.int32), tab)
 
     def prefix(q, rows, dtype):
-        return prefix_attend(
-            meta[rows], core_arg, q, prefix_keys, pk_other, prefix_values, pv_other, dtype
-        )
-
-    suffix = suffix_attend(meta[:2], q_two, k_two, v_two)
-    near = prefix(q_two, slice(0, 2), jnp.float32)
+        count = q.shape[0]
+        work = prefix_work(shapes[rows, :RQ], shapes[rows, RQ:])
+        o, lse = prefix_attend(
+            work,
+            core_arg,
+            q.reshape(count * row_tok, HEAD),
+            prefix_keys,
+            pk_other,
+            prefix_values,
+            pv_other,
+            dtype,
+        )
+        return o.reshape(q.shape), lse.reshape(count, row_tok // BLK, BLK)
+
+    near_lengths = shapes[:2, :RQ]
+    suffix = suffix_attend(jnp.cumsum(near_lengths, axis=1) - near_lengths, q_two, k_two, v_two)
     far = prefix(q_far, slice(2, 4), jnp.bfloat16)
     back = (x_swap(far[0]), x_swap(far[1]))
+    near = prefix(q_two, slice(0, 2), jnp.float32)
     attended = merge_parts(
         [[(*part, row) for part in (suffix, near, back)] for row in range(2)]
     )
@@ -806,7 +856,11 @@
     keep, send = project(heads, proj_rows)
     stream, normed = norm_rows(keep, core_swap(send), residual, norm_gain)
     rows = gather_rows(z, normed)
-    sums = run_experts(rows, row_tab, col_tab, w_gate, w_up, w_down)
+    picked = [
+        jnp.dot(pick[i], part, preferred_element_type=jnp.float32).astype(jnp.bfloat16)
+        for i, part in enumerate(rows)
+    ]
+    sums = run_experts(picked, give, w_gate, w_up, w_down)
     parts = scatter_sums(z, sums)
     return (stream + sum(parts[1:], parts[0])).astype(jnp.bfloat16)
 
@@ -833,5 +887,8 @@
     blocked = mesh.shape["req"] == 4 and mesh.shape["exp"] == 8
     return jax.shard_map(
         block_device if blocked else general_device,
-        mesh=mesh, in_specs=in_specs, out_specs=out_specs, check_vma=False
-    )
+        mesh=mesh,
+        in_specs=in_specs,
+        out_specs=out_specs,
+        check_vma=False,
+    )

time: 306 us -> 273 us (0.89)
  Pallas kernels: 105 us -> 73.4 us
  waiting for transfers between devices: 87.8 us -> 73.7 us
  matrix products: 0 us -> 11.8 us
  starting transfers between devices: 62.2 us -> 53.3 us
    pallas_call x4, Pallas kernels: 82.4 us -> 53.8 us  [the longest x2 30.4 us: prefix_attend(): pl.pallas_call(body, grid_spec=pltpu.PrefetchScalarGridSpec(num_scalar_pr...]
    ppermute x8, waiting for transfers between devices: 46.5 us -> 22.7 us  [y_swap(): return lax.ppermute(array, 'exp', [(i, i ^ 1) for i in range(8)])]
    ppermute x6, waiting for transfers between devices: 29.1 us -> 9.33 us  [z_down(): lax.ppermute(array, 'exp', [(i, i - 2) for i in range(8 - 2 * sources, 8)])]
    ppermute x3, waiting for transfers between devices: 3.86 us -> 19.3 us  [block_device(): lax.ppermute(tab, 'exp', [(i, i ^ step) for i in range(8)])]
    dot_general x0 -> x8, matrix products: none -> 11.8 us  [block_device(): jnp.dot(pick[i], part, preferred_element_type=jnp.float32)]
    ppermute x6, waiting for transfers between devices: 3.59 us -> 15 us  [z_up(): return lax.ppermute(array, 'exp', [(i, i + 2) for i in range(2 * sources)])]
    ppermute x6, starting transfers between devices: 31.6 us -> 20.8 us  [z_up(): return lax.ppermute(array, 'exp', [(i, i + 2) for i in range(2 * sources)])]
  transfers between devices with their start and end apart: 33 -> 33, of which waited for: 18 -> 16; matrix products, arithmetic and copies ran while one was open for 3% -> 10% of each run, Pallas kernels for 22% -> 17%
where the time goes in v2:
time: 273 us; the launch traced here: 271 us
  waiting for transfers between devices  73.7 us (27%)
  Pallas kernels  73.4 us (27%)
  starting transfers between devices  53.3 us (20%)
  blocking collectives  20.6 us (8%)
  between operations  16.4 us (6%)
  matrix products  11.8 us (4%)
  local copies, waits for them, and re-layouts  11 us (4%)
  other arithmetic  10.7 us (4%)
    pallas_call x2, Pallas kernels, prefix_attend(): pl.pallas_call(body, grid_spec=pltpu.PrefetchScalarGridSpec(num_scalar_pr...  30.4 us
    ppermute x8, waiting for transfers between devices, y_swap(): return lax.ppermute(array, 'exp', [(i, i ^ 1) for i in range(8)])  22.7 us
    ppermute x6, starting transfers between devices, z_up(): return lax.ppermute(array, 'exp', [(i, i + 2) for i in range(2 * sources)])  20.8 us
    all_to_all x1, blocking collectives, block_device(): lax.all_to_all(attended, 'exp', split_axis=0, concat_axis=0, tiled=True)  20.6 us
    pallas_call x1, Pallas kernels, run_experts(): pl.pallas_call(experts_kernel, grid=(EXP_DEV,), in_specs=[pl.BlockSpec((S...  20.3 us
    ppermute x3, waiting for transfers between devices, block_device(): lax.ppermute(tab, 'exp', [(i, i ^ step) for i in range(8)])  19.3 us
    ppermute x6, waiting for transfers between devices, z_up(): return lax.ppermute(array, 'exp', [(i, i + 2) for i in range(2 * sources)])  15 us
    dot_general x8, matrix products, block_device(): jnp.dot(pick[i], part, preferred_element_type=jnp.float32)  11.8 us
  transfers between devices with their start and end apart: 33, of which 16 were waited for; matrix products, arithmetic and copies ran while one was open for 10% of the time, Pallas kernels for 17%

profile of v2, /device:TPU:0, one launch (start us, length us, event | category | flops | bytes accessed | tf_op | source)
XLA Modules:
  0.0 270.9 jit_solution(10844118476888352670)
XLA Ops:
  6.5 0.9 pad_add_fusion.1
  7.9 4.2 %send_halves.1 = (bf16[3,1024,128]{2,1,0:T(8,128)(2,1)}, bf16[4,1024,128]{2,1,0:T(8,128)(2,1)}, bf16[4,1024,128]{2,1,0:T(8,128)(2,1)}) custom-call(s32[1]{0:T(128)} %bitcast.1.sc_ref.core_ref, bf16[1024,256]{1,0:T(8,128)(2,1)} %q.1, bf16[1024,256]{1,0:T(8,128)(2,1)} %k.1, bf16[1024,256]{1,0:T(8,128)(2,1)} %v.1, bf16[4,1024,256]{2,1,0:T(8,128)(2,1)} %refs_2_.3, ...), custom_call_target="tpu_custom_call" | custom-call | tf_op jit(solution)/shard_map/send_halves/pallas_call | solution.py:286
  12.7 0.8 constant_dynamic-slice_fusion
  14.2 2.9 %collective-permute-start.4 = (s32[2,16]{1,0:T(2,128)S(1)}, s32[2,16]{1,0:T(2,128)S(1)}, u32[]{:S(2)}, u32[]{:S(2)}) collective-permute-start(s32[2,16]{1,0:T(2,128)S(1)} %pad_add_fusion), channel_id=1, source_target_pairs={{0,16},{8,24},{16,0},{24,8},{1,17},{9,25},{17,1},{25,9},{2,18},{10... | collective-permute-start | bytes 392 | tf_op jit(solution)/shard_map/ppermute | solution.py:257
  17.2 1.5 collective-permute-done.4
  27.2 1.3 concatenate.34.refs_0_
  28.4 1.2 concatenate.35.refs_0_
  29.8 2.1 collective-permute-start.5
  31.9 1.1 pad_maximum_fusion.1
  33.0 5.6 %suffix_attend.1 = (f32[2,1024,128]{2,1,0:T(8,128)}, f32[2,8,128]{2,1,0:T(8,128)}) custom-call(s32[2,8]{1,0:T(2,128)} %copy-done.13, bf16[2,1024,128]{2,1,0:T(8,128)(2,1)} %copy-done.8, bf16[2,1024,128]{2,1,0:T(8,128)(2,1)} %get-tuple-element.88.k_ref, bf16[2,1024,128]{2,1,0:T(8,128)(2,1)} %get-tuple-element.89.v_ref), custom_call_target="tpu_custom_call" | custom-call | flops 4294967296 | bytes 1048576 | tf_op jit(solution)/shard_map/suffix_attend/pallas_call | solution.py:528
  38.6 4.3 %collective-permute-done.5 = bf16[2,1024,128]{2,1,0:T(8,128)(2,1)S(1)} collective-permute-done((bf16[2,1024,128]{2,1,0:T(8,128)(2,1)S(1)}, bf16[2,1024,128]{2,1,0:T(8,128)(2,1)S(1)}, u32[]{:S(2)}, u32[]{:S(2)}) %collective-permute-start.5) | collective-permute-done | bytes 524320 | tf_op jit(solution)/shard_map/ppermute | solution.py:257
  42.9 0.9 copy-done.18
  43.8 15.2 %prefix_attend.3 = (bf16[2048,128]{1,0:T(8,128)(2,1)}, f32[16,128]{1,0:T(8,128)}) custom-call(s32[1]{0:T(128)} %bitcast.1.sc_ref.core_ref, s32[289]{0:T(512)} %concatenate.35.refs_0_, bf16[2048,128]{1,0:T(8,128)(2,1)} %bitcast.142, bf16[4,1024,256]{2,1,0:T(8,128)(2,1)} %refs_2_.3, bf16[4,1024,128]{2,1,0:T(8,128)(2,1)} %collective-permute-done.2.refs_3_, ...), custom_call_target="tpu_custom_call" | custom-call | flops 8589934592 | bytes 4194304 | tf_op jit(solution)/shard_map/prefix_attend/pallas_call | solution.py:441
  58.9 1.7 collective-permute-start.6
  61.0 15.2 %prefix_attend.2 = (f32[2048,128]{1,0:T(8,128)}, f32[16,128]{1,0:T(8,128)}) custom-call(s32[1]{0:T(128)} %bitcast.1.sc_ref.core_ref, s32[289]{0:T(512)} %concatenate.34.refs_0_, bf16[2048,128]{1,0:T(8,128)(2,1)} %bitcast.134, bf16[4,1024,256]{2,1,0:T(8,128)(2,1)} %refs_2_.3, bf16[4,1024,128]{2,1,0:T(8,128)(2,1)} %collective-permute-done.2.refs_3_, ...), custom_call_target="tpu_custom_call" | custom-call | flops 8589934592 | bytes 4194304 | tf_op jit(solution)/shard_map/prefix_attend/pallas_call | solution.py:441
  77.0 3.1 %merge_parts.1 = bf16[8,256,128]{2,1,0:T(8,128)(2,1)} custom-call(f32[2,1024,128]{2,1,0:T(8,128)} %get-tuple-element.30.refs_0_.refs_6_, f32[2,8,128]{2,1,0:T(8,128)} %get-tuple-element.31.refs_1_.refs_7_, f32[2,1024,128]{2,1,0:T(8,128)} %bitcast.132, f32[2,8,128]{2,1,0:T(8,128)} %bitcast.135, bf16[2,1024,128]{2,1,0:T(8,128)(2,1)} %copy-done.6, ...), custom_call_target="tpu_custom_call" | custom-call | tf_op jit(solution)/shard_map/merge_parts/pallas_call | solution.py:584
  80.2 20.6 %all_to_all.5.a_ref = bf16[8,256,128]{2,1,0:T(8,128)(2,1)} all-to-all(bf16[8,256,128]{2,1,0:T(8,128)(2,1)} %merge_parts.1), channel_id=1, replica_groups=mesh['req'=4,'exp'=8] {'exp'}, dimensions={0} | all-to-all | bytes 1048576 | tf_op jit(solution)/shard_map/all_to_all | solution.py:855
  100.7 5.1 %project.1 = (f32[128,2048]{1,0:T(8,128)}, bf16[128,2048]{1,0:T(8,128)(2,1)}) custom-call(bf16[8,256,128]{2,1,0:T(8,128)(2,1)} %all_to_all.5.a_ref, bf16[1024,2048]{1,0:T(8,128)(2,1)} %all-gather.2.cloned.1.call-done.w_ref), custom_call_target="tpu_custom_call" | custom-call | tf_op jit(solution)/shard_map/project/pallas_call | solution.py:611
  106.5 1.5 collective-permute-done.8.got
  108.0 0.8 copy-done.9
  108.8 2.9 %norm_rows.1 = (f32[128,2048]{1,0:T(8,128)}, bf16[128,2048]{1,0:T(8,128)(2,1)}) custom-call(f32[128,2048]{1,0:T(8,128)} %get-tuple-element.38.keep, bf16[128,2048]{1,0:T(8,128)(2,1)} %copy-done.9, bf16[128,2048]{1,0:T(8,128)(2,1)} %residual.1, bf16[1,2048]{1,0:T(2,128)(2,1)} %reshape.336.gain), custom_call_target="tpu_custom_call" | custom-call | tf_op jit(solution)/shard_map/norm_rows/pallas_call | solution.py:637
  111.6 2.1 collective-permute-start.12
  113.8 1.3 collective-permute-start.13
  115.1 0.8 collective-permute-start.14
  115.9 1.3 collective-permute-start.9
  118.0 11.1 %collective-permute-done.9 = bf16[1,8,128]{2,1,0:T(8,128)(2,1)S(1)} collective-permute-done((bf16[1,8,128]{2,1,0:T(8,128)(2,1)S(1)}, bf16[1,8,128]{2,1,0:T(8,128)(2,1)S(1)}, u32[]{:S(2)}, u32[]{:S(2)}) %collective-permute-start.9) | collective-permute-done | bytes 2080 | tf_op jit(solution)/shard_map/ppermute | solution.py:823
  129.1 2.4 collective-permute-start.10
  131.5 2.0 collective-permute-start.15
  133.4 1.3 collective-permute-start.16
  134.8 0.8 collective-permute-start.17
  135.6 4.8 %collective-permute-start.11 = (bf16[4,8,128]{2,1,0:T(8,128)(2,1)S(1)}, bf16[4,8,128]{2,1,0:T(8,128)(2,1)S(1)}, u32[]{:S(2)}, u32[]{:S(2)}) collective-permute-start(bf16[4,8,128]{2,1,0:T(8,128)(2,1)S(1)} %pad_maximum_fusion.4), channel_id=1, source_target_pairs={{0,4},{1,5},{2,6},{3,7},{4,0},{5,1},{6,2},{7,3},{8,12},{9,13},{10,... | collective-permute-start | bytes 24584 | tf_op jit(solution)/shard_map/ppermute | solution.py:823
  141.0 8.3 %collective-permute-done.11 = bf16[4,8,128]{2,1,0:T(8,128)(2,1)S(1)} collective-permute-done((bf16[4,8,128]{2,1,0:T(8,128)(2,1)S(1)}, bf16[4,8,128]{2,1,0:T(8,128)(2,1)S(1)}, u32[]{:S(2)}, u32[]{:S(2)}) %collective-permute-start.11) | collective-permute-done | bytes 8224 | tf_op jit(solution)/shard_map/ppermute | solution.py:823
  149.9 1.8 route.1
  151.7 2.2 convolution_convert_fusion.7.refs_0_
  153.9 2.3 collective-permute-start.18
  156.2 1.3 collective-permute-start.19
  157.7 1.3 collective-permute-start.20
  158.9 1.9 convolution_convert_fusion.6.refs_1_
  160.8 1.1 convolution_convert_fusion.3.refs_4_
  161.9 1.1 convolution_convert_fusion.5.refs_2_
  163.0 1.5 collective-permute-done.18
  164.5 4.1 %collective-permute-done.19 = bf16[128,2048]{1,0:T(8,128)(2,1)S(1)} collective-permute-done((bf16[128,2048]{1,0:T(8,128)(2,1)S(1)}, bf16[128,2048]{1,0:T(8,128)(2,1)S(1)}, u32[]{:S(2)}, u32[]{:S(2)}) %collective-permute-start.19) | collective-permute-done | bytes 524320 | tf_op jit(solution)/shard_map/ppermute | solution.py:269
  169.3 1.3 collective-permute-start.21
  170.6 2.1 convolution_convert_fusion.2.refs_5_
  172.8 1.1 convolution_convert_fusion.4.refs_3_
  173.9 1.1 convolution_convert_fusion.1.refs_6_
  175.0 4.5 %collective-permute-done.21 = bf16[128,2048]{1,0:T(8,128)(2,1)S(1)} collective-permute-done((bf16[128,2048]{1,0:T(8,128)(2,1)S(1)}, bf16[128,2048]{1,0:T(8,128)(2,1)S(1)}, u32[]{:S(2)}, u32[]{:S(2)}) %collective-permute-start.21) | collective-permute-done | bytes 524320 | tf_op jit(solution)/shard_map/ppermute | solution.py:261
  179.5 1.2 convolution_convert_fusion.refs_7_
  180.6 20.3 %experts.1 = bf16[8,128,2048]{2,1,0:T(8,128)(2,1)} custom-call(bf16[128,2048]{1,0:T(8,128)(2,1)} %convolution_convert_fusion.7.refs_0_, bf16[128,2048]{1,0:T(8,128)(2,1)} %convolution_convert_fusion.6.refs_1_, bf16[128,2048]{1,0:T(8,128)(2,1)} %convolution_convert_fusion.5.refs_2_, bf16[128,2048]{1,0:T(8,128)(2,1)} %convolution_convert_fusion.4.refs_3_, ...), custom_call_target="tpu_custom_call" | custom-call | tf_op jit(solution)/shard_map/experts/pallas_call | solution.py:717
  201.0 1.9 slice_bitcast_fusion.6
  202.8 1.4 collective-permute-start.25
  204.9 12.8 %collective-permute-done.25 = bf16[128,2048]{1,0:T(8,128)(2,1)S(1)} collective-permute-done((bf16[128,2048]{1,0:T(8,128)(2,1)S(1)}, bf16[128,2048]{1,0:T(8,128)(2,1)S(1)}, u32[]{:S(2)}, u32[]{:S(2)}) %collective-permute-start.25) | collective-permute-done | bytes 524320 | tf_op jit(solution)/shard_map/ppermute | solution.py:261
  217.9 4.4 %collective-permute-start.26 = (bf16[128,2048]{1,0:T(8,128)(2,1)S(1)}, bf16[128,2048]{1,0:T(8,128)(2,1)S(1)}, u32[]{:S(2)}, u32[]{:S(2)}) collective-permute-start(bf16[128,2048]{1,0:T(8,128)(2,1)S(1)} %fusion.2), channel_id=1, source_target_pairs={{0,2},{1,3},{8,10},{9,11},{16,18},{17,19},{24,26},{25,27}} | collective-permute-start | bytes 1572872 | tf_op jit(solution)/shard_map/ppermute | solution.py:265
  223.0 1.4 collective-permute-start.23
  224.4 4.5 %collective-permute-done.24 = bf16[128,2048]{1,0:T(8,128)(2,1)S(1)} collective-permute-done((bf16[128,2048]{1,0:T(8,128)(2,1)S(1)}, bf16[128,2048]{1,0:T(8,128)(2,1)S(1)}, u32[]{:S(2)}, u32[]{:S(2)}) %collective-permute-start.24) | collective-permute-done | bytes 524320 | tf_op jit(solution)/shard_map/ppermute | solution.py:261
  229.0 3.5 %collective-permute-done.26 = bf16[128,2048]{1,0:T(8,128)(2,1)S(1)} collective-permute-done((bf16[128,2048]{1,0:T(8,128)(2,1)S(1)}, bf16[128,2048]{1,0:T(8,128)(2,1)S(1)}, u32[]{:S(2)}, u32[]{:S(2)}) %collective-permute-start.26) | collective-permute-done | bytes 524320 | tf_op jit(solution)/shard_map/ppermute | solution.py:265
  233.0 4.4 %collective-permute-start.27 = (bf16[128,2048]{1,0:T(8,128)(2,1)S(1)}, bf16[128,2048]{1,0:T(8,128)(2,1)S(1)}, u32[]{:S(2)}, u32[]{:S(2)}) collective-permute-start(bf16[128,2048]{1,0:T(8,128)(2,1)S(1)} %get-tuple-element.63), channel_id=1, source_target_pairs={{0,2},{1,3},{2,4},{3,5},{8,10},{9,11},{10,12},{11,13},{16,18},{17,... | collective-permute-start | bytes 1572872 | tf_op jit(solution)/shard_map/ppermute | solution.py:265
  238.1 1.7 collective-permute-start.22
  240.1 8.6 %collective-permute-done.27 = bf16[128,2048]{1,0:T(8,128)(2,1)S(1)} collective-permute-done((bf16[128,2048]{1,0:T(8,128)(2,1)S(1)}, bf16[128,2048]{1,0:T(8,128)(2,1)S(1)}, u32[]{:S(2)}, u32[]{:S(2)}) %collective-permute-start.27) | collective-permute-done | bytes 524320 | tf_op jit(solution)/shard_map/ppermute | solution.py:265
  249.3 1.3 collective-permute-start.31
  250.6 5.5 %collective-permute-start.28 = (bf16[128,2048]{1,0:T(8,128)(2,1)S(1)}, bf16[128,2048]{1,0:T(8,128)(2,1)S(1)}, u32[]{:S(2)}, u32[]{:S(2)}) collective-permute-start(bf16[128,2048]{1,0:T(8,128)(2,1)S(1)} %get-tuple-element.65), channel_id=1, source_target_pairs={{0,2},{1,3},{2,4},{3,5},{4,6},{5,7},{8,10},{9,11},{10,12},{11,13},... | collective-permute-start | bytes 1572872 | tf_op jit(solution)/shard_map/ppermute | solution.py:265
  256.2 5.2 %collective-permute-done.31 = bf16[128,2048]{1,0:T(8,128)(2,1)S(1)} collective-permute-done((bf16[128,2048]{1,0:T(8,128)(2,1)S(1)}, bf16[128,2048]{1,0:T(8,128)(2,1)S(1)}, u32[]{:S(2)}, u32[]{:S(2)}) %collective-permute-start.31) | collective-permute-done | bytes 524320 | tf_op jit(solution)/shard_map/ppermute | solution.py:269
  261.4 1.5 collective-permute-done.28
  262.8 1.2 fusion.8
  (141 shorter events, 16.0 us)
Async XLA Ops:
  6.5 6.1 %copy-start = (bf16[256,2048]{1,0:T(8,128)(2,1)S(1)}, bf16[256,2048]{1,0:T(8,128)(2,1)}, u32[]{:S(2)}) copy-start(bf16[256,2048]{1,0:T(8,128)(2,1)} %param.24) | copy-start | bytes 3145732
  6.5 7.0 %copy-start.3 = (bf16[1024,256]{1,0:T(8,128)(2,1)S(1)}, bf16[1024,256]{1,0:T(8,128)(2,1)}, u32[]{:S(2)}) copy-start(bf16[1024,256]{1,0:T(8,128)(2,1)} %q.1) | copy-start | bytes 1572868
  6.5 7.1 %copy-start.4 = (bf16[1024,256]{1,0:T(8,128)(2,1)S(1)}, bf16[1024,256]{1,0:T(8,128)(2,1)}, u32[]{:S(2)}) copy-start(bf16[1024,256]{1,0:T(8,128)(2,1)} %k.1) | copy-start | bytes 1572868
  6.5 94.2 %all-gather.2.cloned.1.call-start = ((), (), s32[]{:S(2)}) async-start(), calls=%async_computation.1 | async-start | bytes 4718592 | tf_op jit(solution)/shard_map/all_gather | solution.py:800
  7.4 6.3 %collective-permute-start = (s32[1,16]{1,0:T(1,128)S(1)}, s32[1,16]{1,0:T(1,128)S(1)}, u32[]{:S(2)}, u32[]{:S(2)}) collective-permute-start(s32[1,16]{1,0:T(1,128)S(1)} %pad_add_fusion.1), channel_id=1, source_target_pairs={{0,8},{8,0},{16,24},{24,16},{1,9},{9,1},{17,25},{25,17},{2,10},{10... | collective-permute-start | bytes 200 | tf_op jit(solution)/shard_map/ppermute | solution.py:253
  7.9 5.8 %copy-start.5 = (bf16[1024,256]{1,0:T(8,128)(2,1)S(1)}, bf16[1024,256]{1,0:T(8,128)(2,1)}, u32[]{:S(2)}) copy-start(bf16[1024,256]{1,0:T(8,128)(2,1)} %v.1) | copy-start | bytes 1572868
  7.9 5.9 %copy-start.16 = (s32[1,8]{1,0:T(1,128)S(1)}, s32[1,8]{1,0:T(1,128)}, u32[]{:S(2)}) copy-start(s32[1,8]{1,0:T(1,128)} %param.22) | copy-start | bytes 100
  7.9 5.9 %copy-start.17 = (s32[1,8]{1,0:T(1,128)S(1)}, s32[1,8]{1,0:T(1,128)}, u32[]{:S(2)}) copy-start(s32[1,8]{1,0:T(1,128)} %param.21) | copy-start | bytes 100
  12.1 17.6 %collective-permute-start.1 = (bf16[3,1024,128]{2,1,0:T(8,128)(2,1)}, bf16[3,1024,128]{2,1,0:T(8,128)(2,1)S(1)}, u32[]{:S(2)}, u32[]{:S(2)}) collective-permute-start(bf16[3,1024,128]{2,1,0:T(8,128)(2,1)} %get-tuple-element.29), channel_id=1, source_target_pairs={{0,8},{8,0},{16,24},{24,16},{1,9},{9,1},{17,25},{25,17},{2,10},{10... | collective-permute-start | bytes 2359304 | tf_op jit(solution)/shard_map/ppermute | solution.py:253
  12.2 26.4 %collective-permute-start.2 = (bf16[4,1024,128]{2,1,0:T(8,128)(2,1)}, bf16[4,1024,128]{2,1,0:T(8,128)(2,1)}, u32[]{:S(2)}, u32[]{:S(2)}) collective-permute-start(bf16[4,1024,128]{2,1,0:T(8,128)(2,1)} %get-tuple-element.32), channel_id=1, source_target_pairs={{0,8},{8,0},{16,24},{24,16},{1,9},{9,1},{17,25},{25,17},{2,10},{10... | collective-permute-start | bytes 3145736 | tf_op jit(solution)/shard_map/ppermute | solution.py:253
  12.6 26.0 %collective-permute-start.3 = (bf16[4,1024,128]{2,1,0:T(8,128)(2,1)}, bf16[4,1024,128]{2,1,0:T(8,128)(2,1)}, u32[]{:S(2)}, u32[]{:S(2)}) collective-permute-start(bf16[4,1024,128]{2,1,0:T(8,128)(2,1)} %get-tuple-element.33), channel_id=1, source_target_pairs={{0,8},{8,0},{16,24},{24,16},{1,9},{9,1},{17,25},{25,17},{2,10},{10... | collective-permute-start | bytes 3145736 | tf_op jit(solution)/shard_map/ppermute | solution.py:253
  14.1 18.9 %copy-start.13 = (s32[2,8]{1,0:T(2,128)}, s32[2,8]{1,0:T(2,128)S(1)}, u32[]{:S(2)}) copy-start(s32[2,8]{1,0:T(2,128)S(1)} %get-tuple-element.85.meta_ref) | copy-start | bytes 196
  14.2 4.5 %collective-permute-start.4 = (s32[2,16]{1,0:T(2,128)S(1)}, s32[2,16]{1,0:T(2,128)S(1)}, u32[]{:S(2)}, u32[]{:S(2)}) collective-permute-start(s32[2,16]{1,0:T(2,128)S(1)} %pad_add_fusion), channel_id=1, source_target_pairs={{0,16},{8,24},{16,0},{24,8},{1,17},{9,25},{17,1},{25,9},{2,18},{10... | collective-permute-start | bytes 392 | tf_op jit(solution)/shard_map/ppermute | solution.py:257
  29.8 3.2 %copy-start.8 = (bf16[2,1024,128]{2,1,0:T(8,128)(2,1)}, bf16[2,1024,128]{2,1,0:T(8,128)(2,1)S(1)}, u32[]{:S(2)}) copy-start(bf16[2,1024,128]{2,1,0:T(8,128)(2,1)S(1)} %pad_maximum_fusion.q_ref) | copy-start | bytes 1572868
  29.8 13.1 %collective-permute-start.5 = (bf16[2,1024,128]{2,1,0:T(8,128)(2,1)S(1)}, bf16[2,1024,128]{2,1,0:T(8,128)(2,1)S(1)}, u32[]{:S(2)}, u32[]{:S(2)}) collective-permute-start(bf16[2,1024,128]{2,1,0:T(8,128)(2,1)S(1)} %pad_maximum_fusion.q_ref), channel_id=1, source_target_pairs={{0,16},{8,24},{16,0},{24,8},{1,17},{9,25},{17,1},{25,9},{2,18},{10... | collective-permute-start | bytes 1572872 | tf_op jit(solution)/shard_map/ppermute | solution.py:257
  42.9 0.9 copy-start.18
  58.9 17.3 %collective-permute-start.6 = (bf16[2,1024,128]{2,1,0:T(8,128)(2,1)}, bf16[2,1024,128]{2,1,0:T(8,128)(2,1)S(1)}, u32[]{:S(2)}, u32[]{:S(2)}) collective-permute-start(bf16[2,1024,128]{2,1,0:T(8,128)(2,1)} %bitcast.143), channel_id=1, source_target_pairs={{0,16},{8,24},{16,0},{24,8},{1,17},{9,25},{17,1},{25,9},{2,18},{10... | collective-permute-start | bytes 1572872 | tf_op jit(solution)/shard_map/ppermute | solution.py:257
  60.7 15.5 %collective-permute-start.7 = (f32[2,8,128]{2,1,0:T(8,128)}, f32[2,8,128]{2,1,0:T(8,128)S(1)}, u32[]{:S(2)}, u32[]{:S(2)}) collective-permute-start(f32[2,8,128]{2,1,0:T(8,128)} %bitcast.144), channel_id=1, source_target_pairs={{0,16},{8,24},{16,0},{24,8},{1,17},{9,25},{17,1},{25,9},{2,18},{10... | collective-permute-start | bytes 24584 | tf_op jit(solution)/shard_map/ppermute | solution.py:257
  76.2 0.6 copy-start.11
  76.2 0.8 copy-start.6
  80.1 25.7 %copy-start.12 = (bf16[2048]{0:T(1024)(128)(2,1)S(1)}, bf16[2048]{0:T(1024)(128)(2,1)}, u32[]{:S(2)}) copy-start(bf16[2048]{0:T(1024)(128)(2,1)} %param.25) | copy-start | bytes 12292
  80.1 35.8 %copy-start.14 = (s32[128,4]{0,1:T(4,128)S(1)}, s32[128,4]{0,1:T(4,128)}, u32[]{:S(2)}) copy-start(s32[128,4]{0,1:T(4,128)} %param.26) | copy-start | bytes 6148
  80.1 35.8 %copy-start.15 = (bf16[128,4]{0,1:T(4,128)(2,1)S(1)}, bf16[128,4]{0,1:T(4,128)(2,1)}, u32[]{:S(2)}) copy-start(bf16[128,4]{0,1:T(4,128)(2,1)} %param.27) | copy-start | bytes 3076
  105.9 2.1 collective-permute-start.8
  108.0 0.8 copy-start.9
  111.6 19.8 %collective-permute-start.12 = (bf16[128,2048]{1,0:T(8,128)(2,1)}, bf16[128,2048]{1,0:T(8,128)(2,1)S(1)}, u32[]{:S(2)}, u32[]{:S(2)}) collective-permute-start(bf16[128,2048]{1,0:T(8,128)(2,1)} %get-tuple-element.42), channel_id=1, source_target_pairs={{0,2},{1,3},{2,4},{3,5},{4,6},{5,7},{8,10},{9,11},{10,12},{11,13},... | collective-permute-start | bytes 1572872 | tf_op jit(solution)/shard_map/ppermute | solution.py:265
  113.8 17.7 %collective-permute-start.13 = (bf16[128,2048]{1,0:T(8,128)(2,1)}, bf16[128,2048]{1,0:T(8,128)(2,1)S(1)}, u32[]{:S(2)}, u32[]{:S(2)}) collective-permute-start(bf16[128,2048]{1,0:T(8,128)(2,1)} %get-tuple-element.42), channel_id=1, source_target_pairs={{2,0},{3,1},{4,2},{5,3},{6,4},{7,5},{10,8},{11,9},{12,10},{13,11},... | collective-permute-start | bytes 1572872 | tf_op jit(solution)/shard_map/ppermute | solution.py:269
  115.1 16.4 %collective-permute-start.14 = (bf16[128,2048]{1,0:T(8,128)(2,1)}, bf16[128,2048]{1,0:T(8,128)(2,1)S(1)}, u32[]{:S(2)}, u32[]{:S(2)}) collective-permute-start(bf16[128,2048]{1,0:T(8,128)(2,1)} %get-tuple-element.42), channel_id=1, source_target_pairs={{0,1},{1,0},{2,3},{3,2},{4,5},{5,4},{6,7},{7,6},{8,9},{9,8},{10,11... | collective-permute-start | bytes 1572872 | tf_op jit(solution)/shard_map/ppermute | solution.py:261
  115.9 13.1 %collective-permute-start.9 = (bf16[1,8,128]{2,1,0:T(8,128)(2,1)S(1)}, bf16[1,8,128]{2,1,0:T(8,128)(2,1)S(1)}, u32[]{:S(2)}, u32[]{:S(2)}) collective-permute-start(bf16[1,8,128]{2,1,0:T(8,128)(2,1)S(1)} %maximum_bitcast_fusion), channel_id=1, source_target_pairs={{0,1},{1,0},{2,3},{3,2},{4,5},{5,4},{6,7},{7,6},{8,9},{9,8},{10,11... | collective-permute-start | bytes 6152 | tf_op jit(solution)/shard_map/ppermute | solution.py:823
  129.1 6.5 %collective-permute-start.10 = (bf16[2,8,128]{2,1,0:T(8,128)(2,1)S(1)}, bf16[2,8,128]{2,1,0:T(8,128)(2,1)S(1)}, u32[]{:S(2)}, u32[]{:S(2)}) collective-permute-start(bf16[2,8,128]{2,1,0:T(8,128)(2,1)S(1)} %pad_maximum_fusion.5), channel_id=1, source_target_pairs={{0,2},{1,3},{2,0},{3,1},{4,6},{5,7},{6,4},{7,5},{8,10},{9,11},{10,... | collective-permute-start | bytes 12296 | tf_op jit(solution)/shard_map/ppermute | solution.py:823
  131.5 22.4 %collective-permute-start.15 = (bf16[128,2048]{1,0:T(8,128)(2,1)S(1)}, bf16[128,2048]{1,0:T(8,128)(2,1)S(1)}, u32[]{:S(2)}, u32[]{:S(2)}) collective-permute-start(bf16[128,2048]{1,0:T(8,128)(2,1)S(1)} %collective-permute-done.12), channel_id=1, source_target_pairs={{0,2},{1,3},{2,4},{3,5},{4,6},{5,7},{8,10},{9,11},{10,12},{11,13},... | collective-permute-start | bytes 1572872 | tf_op jit(solution)/shard_map/ppermute | solution.py:265
  133.4 20.4 %collective-permute-start.16 = (bf16[128,2048]{1,0:T(8,128)(2,1)S(1)}, bf16[128,2048]{1,0:T(8,128)(2,1)S(1)}, u32[]{:S(2)}, u32[]{:S(2)}) collective-permute-start(bf16[128,2048]{1,0:T(8,128)(2,1)S(1)} %collective-permute-done.13), channel_id=1, source_target_pairs={{2,0},{3,1},{4,2},{5,3},{6,4},{7,5},{10,8},{11,9},{12,10},{13,11},... | collective-permute-start | bytes 1572872 | tf_op jit(solution)/shard_map/ppermute | solution.py:269
  134.8 19.1 %collective-permute-start.17 = (bf16[128,2048]{1,0:T(8,128)(2,1)S(1)}, bf16[128,2048]{1,0:T(8,128)(2,1)}, u32[]{:S(2)}, u32[]{:S(2)}) collective-permute-start(bf16[128,2048]{1,0:T(8,128)(2,1)S(1)} %broadcast_select_fusion), channel_id=1, source_target_pairs={{0,1},{1,0},{2,3},{3,2},{4,5},{5,4},{6,7},{7,6},{8,9},{9,8},{10,11... | collective-permute-start | bytes 1572872 | tf_op jit(solution)/shard_map/ppermute | solution.py:261
  135.6 13.7 %collective-permute-start.11 = (bf16[4,8,128]{2,1,0:T(8,128)(2,1)S(1)}, bf16[4,8,128]{2,1,0:T(8,128)(2,1)S(1)}, u32[]{:S(2)}, u32[]{:S(2)}) collective-permute-start(bf16[4,8,128]{2,1,0:T(8,128)(2,1)S(1)} %pad_maximum_fusion.4), channel_id=1, source_target_pairs={{0,4},{1,5},{2,6},{3,7},{4,0},{5,1},{6,2},{7,3},{8,12},{9,13},{10,... | collective-permute-start | bytes 24584 | tf_op jit(solution)/shard_map/ppermute | solution.py:823
  151.7 9.1 %copy-start.10 = (bf16[8,128,128]{2,1,0:T(8,128)(2,1)S(1)}, bf16[8,128,128]{2,1,0:T(8,128)(2,1)}, u32[]{:S(2)}) copy-start(bf16[8,128,128]{2,1,0:T(8,128)(2,1)} %get-tuple-element.41) | copy-start | bytes 786436
  153.9 10.6 %collective-permute-start.18 = (bf16[128,2048]{1,0:T(8,128)(2,1)S(1)}, bf16[128,2048]{1,0:T(8,128)(2,1)S(1)}, u32[]{:S(2)}, u32[]{:S(2)}) collective-permute-start(bf16[128,2048]{1,0:T(8,128)(2,1)S(1)} %collective-permute-done.15), channel_id=1, source_target_pairs={{0,2},{1,3},{2,4},{3,5},{4,6},{5,7},{8,10},{9,11},{10,12},{11,13},... | collective-permute-start | bytes 1572872 | tf_op jit(solution)/shard_map/ppermute | solution.py:265
  156.2 12.4 %collective-permute-start.19 = (bf16[128,2048]{1,0:T(8,128)(2,1)S(1)}, bf16[128,2048]{1,0:T(8,128)(2,1)S(1)}, u32[]{:S(2)}, u32[]{:S(2)}) collective-permute-start(bf16[128,2048]{1,0:T(8,128)(2,1)S(1)} %collective-permute-done.16), channel_id=1, source_target_pairs={{2,0},{3,1},{4,2},{5,3},{6,4},{7,5},{10,8},{11,9},{12,10},{13,11},... | collective-permute-start | bytes 1572872 | tf_op jit(solution)/shard_map/ppermute | solution.py:269
  157.7 11.5 %collective-permute-start.20 = (bf16[128,2048]{1,0:T(8,128)(2,1)S(1)}, bf16[128,2048]{1,0:T(8,128)(2,1)S(1)}, u32[]{:S(2)}, u32[]{:S(2)}) collective-permute-start(bf16[128,2048]{1,0:T(8,128)(2,1)S(1)} %fusion.11), channel_id=1, source_target_pairs={{0,1},{1,0},{2,3},{3,2},{4,5},{5,4},{6,7},{7,6},{8,9},{9,8},{10,11... | collective-permute-start | bytes 1572872 | tf_op jit(solution)/shard_map/ppermute | solution.py:261
  169.3 10.1 %collective-permute-start.21 = (bf16[128,2048]{1,0:T(8,128)(2,1)S(1)}, bf16[128,2048]{1,0:T(8,128)(2,1)S(1)}, u32[]{:S(2)}, u32[]{:S(2)}) collective-permute-start(bf16[128,2048]{1,0:T(8,128)(2,1)S(1)} %select_select_fusion.5), channel_id=1, source_target_pairs={{0,1},{1,0},{2,3},{3,2},{4,5},{5,4},{6,7},{7,6},{8,9},{9,8},{10,11... | collective-permute-start | bytes 1572872 | tf_op jit(solution)/shard_map/ppermute | solution.py:261
  200.9 16.8 %copy-start.2 = (bf16[8,128,2048]{2,1,0:T(8,128)(2,1)S(1)}, bf16[8,128,2048]{2,1,0:T(8,128)(2,1)}, u32[]{:S(2)}) copy-start(bf16[8,128,2048]{2,1,0:T(8,128)(2,1)} %experts.1) | copy-start | bytes 12582916
  202.8 14.9 %collective-permute-start.25 = (bf16[128,2048]{1,0:T(8,128)(2,1)S(1)}, bf16[128,2048]{1,0:T(8,128)(2,1)S(1)}, u32[]{:S(2)}, u32[]{:S(2)}) collective-permute-start(bf16[128,2048]{1,0:T(8,128)(2,1)S(1)} %get-tuple-element.68), channel_id=1, source_target_pairs={{0,1},{1,0},{2,3},{3,2},{4,5},{5,4},{6,7},{7,6},{8,9},{9,8},{10,11... | collective-permute-start | bytes 1572872 | tf_op jit(solution)/shard_map/ppermute | solution.py:261
  204.2 24.7 %collective-permute-start.24 = (bf16[128,2048]{1,0:T(8,128)(2,1)S(1)}, bf16[128,2048]{1,0:T(8,128)(2,1)S(1)}, u32[]{:S(2)}, u32[]{:S(2)}) collective-permute-start(bf16[128,2048]{1,0:T(8,128)(2,1)S(1)} %get-tuple-element.69), channel_id=1, source_target_pairs={{0,1},{1,0},{2,3},{3,2},{4,5},{5,4},{6,7},{7,6},{8,9},{9,8},{10,11... | collective-permute-start | bytes 1572872 | tf_op jit(solution)/shard_map/ppermute | solution.py:261
  217.9 44.9 %copy-start.7 = (f32[128,2048]{1,0:T(8,128)S(1)}, f32[128,2048]{1,0:T(8,128)}, u32[]{:S(2)}) copy-start(f32[128,2048]{1,0:T(8,128)} %get-tuple-element.40) | copy-start | bytes 3145732
  217.9 14.6 %collective-permute-start.26 = (bf16[128,2048]{1,0:T(8,128)(2,1)S(1)}, bf16[128,2048]{1,0:T(8,128)(2,1)S(1)}, u32[]{:S(2)}, u32[]{:S(2)}) collective-permute-start(bf16[128,2048]{1,0:T(8,128)(2,1)S(1)} %fusion.2), channel_id=1, source_target_pairs={{0,2},{1,3},{8,10},{9,11},{16,18},{17,19},{24,26},{25,27}} | collective-permute-start | bytes 1572872 | tf_op jit(solution)/shard_map/ppermute | solution.py:265
  222.3 10.1 %collective-permute-start.29 = (bf16[128,2048]{1,0:T(8,128)(2,1)S(1)}, bf16[128,2048]{1,0:T(8,128)(2,1)S(1)}, u32[]{:S(2)}, u32[]{:S(2)}) collective-permute-start(bf16[128,2048]{1,0:T(8,128)(2,1)S(1)} %fusion.2), channel_id=1, source_target_pairs={{6,4},{7,5},{14,12},{15,13},{22,20},{23,21},{30,28},{31,29}} | collective-permute-start | bytes 1572872 | tf_op jit(solution)/shard_map/ppermute | solution.py:269
  223.0 17.1 %collective-permute-start.23 = (bf16[128,2048]{1,0:T(8,128)(2,1)S(1)}, bf16[128,2048]{1,0:T(8,128)(2,1)S(1)}, u32[]{:S(2)}, u32[]{:S(2)}) collective-permute-start(bf16[128,2048]{1,0:T(8,128)(2,1)S(1)} %get-tuple-element.70), channel_id=1, source_target_pairs={{0,1},{1,0},{2,3},{3,2},{4,5},{5,4},{6,7},{7,6},{8,9},{9,8},{10,11... | collective-permute-start | bytes 1572872 | tf_op jit(solution)/shard_map/ppermute | solution.py:261
  232.5 31.5 %copy-start.1 = (bf16[256,2048]{1,0:T(8,128)(2,1)S(1)}, bf16[256,2048]{1,0:T(8,128)(2,1)}, u32[]{:S(2)}) copy-start(bf16[256,2048]{1,0:T(8,128)(2,1)} %param.24) | copy-start | bytes 3145732
  233.0 15.7 %collective-permute-start.27 = (bf16[128,2048]{1,0:T(8,128)(2,1)S(1)}, bf16[128,2048]{1,0:T(8,128)(2,1)S(1)}, u32[]{:S(2)}, u32[]{:S(2)}) collective-permute-start(bf16[128,2048]{1,0:T(8,128)(2,1)S(1)} %get-tuple-element.63), channel_id=1, source_target_pairs={{0,2},{1,3},{2,4},{3,5},{8,10},{9,11},{10,12},{11,13},{16,18},{17,... | collective-permute-start | bytes 1572872 | tf_op jit(solution)/shard_map/ppermute | solution.py:265
  237.4 11.3 %collective-permute-start.30 = (bf16[128,2048]{1,0:T(8,128)(2,1)S(1)}, bf16[128,2048]{1,0:T(8,128)(2,1)S(1)}, u32[]{:S(2)}, u32[]{:S(2)}) collective-permute-start(bf16[128,2048]{1,0:T(8,128)(2,1)S(1)} %get-tuple-element.64), channel_id=1, source_target_pairs={{4,2},{5,3},{6,4},{7,5},{12,10},{13,11},{14,12},{15,13},{20,18},{2... | collective-permute-start | bytes 1572872 | tf_op jit(solution)/shard_map/ppermute | solution.py:269
  238.1 18.0 %collective-permute-start.22 = (bf16[128,2048]{1,0:T(8,128)(2,1)S(1)}, bf16[128,2048]{1,0:T(8,128)(2,1)S(1)}, u32[]{:S(2)}, u32[]{:S(2)}) collective-permute-start(bf16[128,2048]{1,0:T(8,128)(2,1)S(1)} %get-tuple-element.67), channel_id=1, source_target_pairs={{0,1},{1,0},{2,3},{3,2},{4,5},{5,4},{6,7},{7,6},{8,9},{9,8},{10,11... | collective-permute-start | bytes 1572872 | tf_op jit(solution)/shard_map/ppermute | solution.py:261
  249.3 12.0 %collective-permute-start.31 = (bf16[128,2048]{1,0:T(8,128)(2,1)S(1)}, bf16[128,2048]{1,0:T(8,128)(2,1)S(1)}, u32[]{:S(2)}, u32[]{:S(2)}) collective-permute-start(bf16[128,2048]{1,0:T(8,128)(2,1)S(1)} %get-tuple-element.66), channel_id=1, source_target_pairs={{2,0},{3,1},{4,2},{5,3},{6,4},{7,5},{10,8},{11,9},{12,10},{13,11},... | collective-permute-start | bytes 1572872 | tf_op jit(solution)/shard_map/ppermute | solution.py:269
  250.6 12.2 %collective-permute-start.28 = (bf16[128,2048]{1,0:T(8,128)(2,1)S(1)}, bf16[128,2048]{1,0:T(8,128)(2,1)S(1)}, u32[]{:S(2)}, u32[]{:S(2)}) collective-permute-start(bf16[128,2048]{1,0:T(8,128)(2,1)S(1)} %get-tuple-element.65), channel_id=1, source_target_pairs={{0,2},{1,3},{2,4},{3,5},{4,6},{5,7},{8,10},{9,11},{10,12},{11,13},... | collective-permute-start | bytes 1572872 | tf_op jit(solution)/shard_map/ppermute | solution.py:265
Sparse Core Ops, SparseCore 0:
  13.7 77.3 all-gather.1

commit v3 on v2

--- a/solution.py
+++ b/solution.py
@@ -261,47 +261,58 @@
     return lax.ppermute(array, "exp", [(i, i ^ 1) for i in range(8)])
 
 
-def z_up(array, sources=3):
-    return lax.ppermute(array, "exp", [(i, i + 2) for i in range(2 * sources)])
-
-
-def z_down(array, sources=3):
-    return lax.ppermute(array, "exp", [(i, i - 2) for i in range(8 - 2 * sources, 8)])
-
-
-def send_halves_kernel(sc_ref, q, k, v, pk, pv, out_qkv, out_pk, out_pv):
-    out_qkv[0] = q[...]
-    out_qkv[1] = k[...]
-    out_qkv[2] = v[...]
+def z_up(array, first=0, last=2):
+    return lax.ppermute(array, "exp", [(i, i + 2) for i in range(2 * first, 2 * last + 2)])
+
+
+def z_down(array, first=3, last=1):
+    return lax.ppermute(array, "exp", [(i, i - 2) for i in range(2 * last, 2 * first + 2)])
+
+
+def split_tokens_kernel(sc_ref, *refs):
+    for i in range(3):
+        refs[6][i] = refs[i][...]
+        refs[7][i] = refs[3 + i][...]
+
+
+def split_tokens(core, q, k, v):
+    rows = q.shape[0]
+    part = rows // 2
+    mine = pl.BlockSpec((part, HEAD), lambda i, s: (i, s[0]))
+    theirs = pl.BlockSpec((part, HEAD), lambda i, s: (i, 1 - s[0]))
+    out = pl.BlockSpec((3, part, HEAD), lambda i, s: (0, i, 0))
+    shape = jax.ShapeDtypeStruct((3, rows, HEAD), q.dtype)
+    return pl.pallas_call(
+        split_tokens_kernel,
+        grid_spec=pltpu.PrefetchScalarGridSpec(
+            num_scalar_prefetch=1,
+            grid=(2,),
+            in_specs=[mine] * 3 + [theirs] * 3,
+            out_specs=[out, out],
+        ),
+        out_shape=(shape, shape),
+        name="split_tokens",
+    )(core, q, k, v, q, k, v)
+
+
+def split_prefix_kernel(sc_ref, pk, pv, out_pk, out_pv):
     out_pk[...] = pk[...]
     out_pv[...] = pv[...]
 
 
-def send_halves(core, q, k, v, pk, pv):
-    rows, span = q.shape[0], pk.shape[1]
-    part = rows // G
-    token_in = pl.BlockSpec((part, HEAD), lambda i, s: (i, 1 - s[0]))
-    prefix_in = pl.BlockSpec((1, span, HEAD), lambda i, s: (i, 0, 1 - s[0]))
-    prefix_out = pl.BlockSpec((1, span, HEAD), lambda i, s: (i, 0, 0))
+def split_prefix(core, pk, pv):
+    span = pk.shape[1]
+    theirs = pl.BlockSpec((1, span, HEAD), lambda i, s: (i, 0, 1 - s[0]))
+    out = pl.BlockSpec((1, span, HEAD), lambda i, s: (i, 0, 0))
+    shape = jax.ShapeDtypeStruct((G, span, HEAD), pk.dtype)
     return pl.pallas_call(
-        send_halves_kernel,
+        split_prefix_kernel,
         grid_spec=pltpu.PrefetchScalarGridSpec(
-            num_scalar_prefetch=1,
-            grid=(G,),
-            in_specs=[token_in] * 3 + [prefix_in] * 2,
-            out_specs=[
-                pl.BlockSpec((3, part, HEAD), lambda i, s: (0, i, 0)),
-                prefix_out,
-                prefix_out,
-            ],
+            num_scalar_prefetch=1, grid=(G,), in_specs=[theirs] * 2, out_specs=[out] * 2
         ),
-        out_shape=(
-            jax.ShapeDtypeStruct((3, rows, HEAD), q.dtype),
-            jax.ShapeDtypeStruct((G, span, HEAD), q.dtype),
-            jax.ShapeDtypeStruct((G, span, HEAD), q.dtype),
-        ),
-        name="send_halves",
-    )(core, q, k, v, pk, pv)
+        out_shape=(shape, shape),
+        name="split_prefix",
+    )(core, pk, pv)
 
 
 def as_row(column):
@@ -314,51 +325,90 @@
 ITEMS = 16
 
 
-def prefix_work(lengths, groups):
-    rows = lengths.shape[0]
-    ends = jnp.cumsum(lengths, axis=-1)
-    starts = ends - lengths
-    blocks = rows * ROW_TOK // SUB
-    at = (jnp.arange(ROW_TOK // SUB, dtype=jnp.int32) * SUB)[None, :, None]
-    overlap = (starts[:, None, :] < at + SUB) & (ends[:, None, :] > at)
-    of_group = groups[None, :, None, :] == jnp.arange(G, dtype=jnp.int32)[:, None, None, None]
-    present = jnp.any(overlap[None] & of_group, axis=-1).reshape(G, blocks).astype(jnp.int32)
-    items = (jnp.sum(present, axis=1) + PER_ITEM - 1) // PER_ITEM
-    base = (jnp.cumsum(items) - items) * PER_ITEM
-    slot = jnp.where(present > 0, base[:, None] + jnp.cumsum(present, axis=1) - 1, -1)
-    value = jnp.arange(G * blocks, dtype=jnp.int32) + 1
-    hit = slot.reshape(1, -1) == jnp.arange(ITEMS * PER_ITEM, dtype=jnp.int32)[:, None]
-    held = jnp.sum(jnp.where(hit, value[None, :], 0), axis=1).reshape(ITEMS, PER_ITEM)
-    held = jnp.where(held > 0, held, held[:, :1])
-    held = (jnp.where(held > 0, held, held[:1, :1]) - 1).reshape(-1)
-    return jnp.concatenate(
-        [starts.reshape(-1), groups.reshape(-1), jnp.sum(items).reshape(1), held // blocks, held % blocks]
-    )
-
-
-def prefix_kernel(work_ref, q_ref, ka, kb, va, vb, o_ref, lse_ref, grp, lse, sa, sb, ta, tb):
+def build_work(shape_ref, rows, item_group, item_block):
+    per_row = ROW_TOK // SUB
+    spans = []
+    for r in range(rows):
+        start = 0
+        for j in range(RQ):
+            end = start + shape_ref[r, j]
+            first, last = r * per_row + start // SUB, r * per_row + (end - 1) // SUB
+            spans.append((first, last, shape_ref[r, RQ + j]))
+            start = end
+
+    def of_group(g, begin):
+        at, done = begin, jnp.int32(-1)
+        for first, last, group in spans:
+            first = jnp.maximum(first, done + 1)
+            match = group == g
+            count = jnp.where(match, last - first + 1, 0)
+
+            def put(i, carry, at=at, first=first):
+                item_block[at + i] = first + i
+                return carry
+
+            lax.fori_loop(0, count, put, 0)
+            at = at + count
+            done = jnp.where(match, last, done)
+        stop = (at + PER_ITEM - 1) // PER_ITEM * PER_ITEM
+
+        def fill(i, carry):
+            item_block[i] = item_block[begin]
+            return carry
+
+        def name(i, carry):
+            item_group[i] = g
+            return carry
+
+        lax.fori_loop(at, stop, fill, 0)
+        lax.fori_loop(begin // PER_ITEM, stop // PER_ITEM, name, 0)
+        return stop
+
+    return lax.fori_loop(0, G, of_group, jnp.int32(0)) // PER_ITEM
+
+
+def prefix_kernel(
+    core_ref, shape_ref, q0, q1, pk, pk_other, pv, pv_other, o_ref, lse_ref,
+    q_ref, ka, kb, va, vb, grp, lse, sa, sb, ta, tb, item_group, item_block, sems,
+):
     tokens = q_ref.shape[0]
     rows = tokens // ROW_TOK
-    span = va.shape[1]
-    head = 2 * rows * RQ
+    span = ka.shape[1]
+    mine_cols = pl.ds(pl.multiple_of(core_ref[0] * HEAD, HEAD), HEAD)
+    copies = [
+        pltpu.make_async_copy(q0, q_ref.at[:ROW_TOK, :], sems.at[0]),
+        pltpu.make_async_copy(q1, q_ref.at[ROW_TOK:, :], sems.at[1]),
+        pltpu.make_async_copy(pk.at[:, :, mine_cols], ka, sems.at[2]),
+        pltpu.make_async_copy(pk_other, kb, sems.at[3]),
+        pltpu.make_async_copy(pv.at[:, :, mine_cols], va, sems.at[4]),
+        pltpu.make_async_copy(pv_other, vb, sems.at[5]),
+    ]
+    for copy in copies:
+        copy.start()
     for r in range(rows):
         token = lax.broadcasted_iota(jnp.int32, (ROW_TOK, HEAD), 0)
-        group = jnp.full((ROW_TOK, HEAD), work_ref[(rows + r) * RQ], jnp.int32)
+        group = jnp.full((ROW_TOK, HEAD), shape_ref[r, RQ], jnp.int32)
+        start = 0
         for j in range(1, RQ):
-            group = jnp.where(
-                token >= work_ref[r * RQ + j], work_ref[(rows + r) * RQ + j], group
-            )
+            start = start + shape_ref[r, j - 1]
+            group = jnp.where(token >= start, shape_ref[r, RQ + j], group)
         grp[r * ROW_TOK : (r + 1) * ROW_TOK, :] = group
+    count = build_work(shape_ref, rows, item_group, item_block)
+    for copy in copies:
+        copy.wait()
     step = 512
 
+    def held(item):
+        return jnp.where(item < count, item, 0)
+
     def places(item):
-        at = head + 1 + ITEMS * PER_ITEM + item * PER_ITEM
+        at = held(item) * PER_ITEM
         return [
-            pl.ds(pl.multiple_of(work_ref[at + i] * SUB, SUB), SUB) for i in range(PER_ITEM)
+            pl.ds(pl.multiple_of(item_block[at + i] * SUB, SUB), SUB) for i in range(PER_ITEM)
         ]
 
     def group_of(item):
-        return work_ref[head + 1 + item * PER_ITEM]
+        return item_group[held(item)]
 
     def lanes(x, op):
         parts = [x[:, c : c + HEAD] for c in range(0, x.shape[1], HEAD)]
@@ -411,63 +461,58 @@
                 ).astype(o_ref.dtype)
                 lse[place, :] = jnp.where(mine, here_lse[sub], lse[place, :])
 
-    count = work_ref[head]
     score(0, sa, ta)
 
     def pair(i, carry):
-        second = jnp.minimum(2 * i + 1, ITEMS - 1)
-        third = jnp.minimum(2 * i + 2, ITEMS - 1)
-        score(second, sb, tb)
+        score(2 * i + 1, sb, tb)
         weigh(2 * i, sa, ta)
-        score(third, sa, ta)
-        weigh(second, sb, tb)
+        score(2 * i + 2, sa, ta)
+        weigh(2 * i + 1, sb, tb)
         return carry
 
     lax.fori_loop(0, (count + 1) // 2, pair, 0)
     for b in range(tokens // BLK):
-        lse_ref[b : b + 1, :] = jnp.transpose(lse[b * BLK : (b + 1) * BLK, :])[0:1, :]
-
-
-def prefix_attend(work, core, q, pk, pk_other, pv, pv_other, out_dtype):
-    tokens, unused = q.shape
-    span = pv.shape[1]
-    own = pl.BlockSpec((G, span, HEAD), lambda i, s: (0, 0, s[0]))
-    whole = pl.BlockSpec((G, span, HEAD), lambda i, s: (0, 0, 0))
-    blocks = tokens // BLK
-
-    def body(core_ref, *refs):
-        prefix_kernel(*refs)
-
+        lse_ref[b // 8, b % 8 : b % 8 + 1, :] = jnp.transpose(lse[b * BLK : (b + 1) * BLK, :])[
+            0:1, :
+        ]
+
+
+def prefix_attend(core, shape, q0, q1, pk, pk_other, pv, pv_other, out_dtype):
+    rows = shape.shape[0]
+    tokens = rows * ROW_TOK
+    span = pk.shape[1]
+    blocks = ROW_TOK // BLK
+    smem = pl.BlockSpec(memory_space=pltpu.SMEM)
+    vmem = pl.BlockSpec(memory_space=pltpu.VMEM)
+    anywhere = pl.BlockSpec(memory_space=pl.ANY)
+    prefix_buffer = pltpu.VMEM((G, span, HEAD), pk.dtype)
+    per_token = pltpu.VMEM((tokens, HEAD), jnp.float32)
+    scores = pltpu.VMEM((PER_ITEM * SUB, 2 * span), jnp.float32)
+    tops = pltpu.VMEM((PER_ITEM * SUB, HEAD), jnp.float32)
     return pl.pallas_call(
-        body,
-        grid_spec=pltpu.PrefetchScalarGridSpec(
-            num_scalar_prefetch=1,
-            grid=(1,),
-            in_specs=[
-                pl.BlockSpec(memory_space=pltpu.SMEM),
-                pl.BlockSpec((tokens, HEAD), lambda i, s: (0, 0)),
-                own,
-                whole,
-                own,
-                whole,
-            ],
-            out_specs=[
-                pl.BlockSpec((tokens, HEAD), lambda i, s: (0, 0)),
-                pl.BlockSpec((blocks, BLK), lambda i, s: (0, 0)),
-            ],
-            scratch_shapes=[
-                pltpu.VMEM((tokens, HEAD), jnp.int32),
-                pltpu.VMEM((tokens, HEAD), jnp.float32),
-                pltpu.VMEM((PER_ITEM * SUB, 2 * span), jnp.float32),
-                pltpu.VMEM((PER_ITEM * SUB, 2 * span), jnp.float32),
-                pltpu.VMEM((PER_ITEM * SUB, HEAD), jnp.float32),
-                pltpu.VMEM((PER_ITEM * SUB, HEAD), jnp.float32),
-            ],
-        ),
+        prefix_kernel,
+        in_specs=[smem, smem] + [anywhere] * 6,
+        out_specs=(vmem, vmem),
         out_shape=(
             jax.ShapeDtypeStruct((tokens, HEAD), out_dtype),
-            jax.ShapeDtypeStruct((blocks, BLK), jnp.float32),
+            jax.ShapeDtypeStruct((rows, blocks, BLK), jnp.float32),
         ),
+        scratch_shapes=[
+            pltpu.VMEM((tokens, HEAD), q0.dtype),
+            prefix_buffer,
+            prefix_buffer,
+            prefix_buffer,
+            prefix_buffer,
+            pltpu.VMEM((tokens, HEAD), jnp.int32),
+            per_token,
+            scores,
+            scores,
+            tops,
+            tops,
+            pltpu.SMEM((ITEMS,), jnp.int32),
+            pltpu.SMEM((ITEMS * PER_ITEM,), jnp.int32),
+            pltpu.SemaphoreType.DMA((6,)),
+        ],
         compiler_params=pltpu.CompilerParams(vmem_limit_bytes=VMEM_BIG),
         cost_estimate=pl.CostEstimate(
             flops=tokens * span * HEAD * 8 * 4,
@@ -475,74 +520,73 @@
             transcendentals=0,
         ),
         name="prefix_attend",
-    )(core, work, q, pk, pk_other, pv, pv_other)
-
-
-def suffix_kernel(meta_ref, q_ref, k_ref, v_ref, o_ref, lse_ref):
-    row = pl.program_id(0)
-    token = lax.broadcasted_iota(jnp.int32, (ROW_TOK, 1), 0)
-    first = jnp.zeros((ROW_TOK, 1), jnp.int32)
-    for j in range(1, RQ):
-        start = meta_ref[row, j]
-        first = jnp.where(token >= start, start, first)
-
-    def score(i):
-        low = max(0, i * SUF - ROW_TOK // 2)
-        here, seen = slice(i * SUF, (i + 1) * SUF), slice(low, (i + 1) * SUF)
-        s = lax.dot_general(
-            q_ref[0, here, :],
-            k_ref[0, seen, :],
-            (((1,), (1,)), ((), ())),
-            preferred_element_type=jnp.float32,
-        )
-        other = low + lax.broadcasted_iota(jnp.int32, s.shape, 1)
-        return jnp.where((other >= first[here]) & (other <= token[here]), s, NEG)
-
-    def weigh(i, s):
-        low = max(0, i * SUF - ROW_TOK // 2)
-        here, seen = slice(i * SUF, (i + 1) * SUF), slice(low, (i + 1) * SUF)
-        top = jnp.max(s, axis=1, keepdims=True)
-        p = jnp.exp2((s - top) * SCORE_SCALE)
-        total = jnp.sum(p, axis=1, keepdims=True)
-        out = jnp.dot(
-            p.astype(jnp.bfloat16), v_ref[0, seen, :], preferred_element_type=jnp.float32
-        )
-        o_ref[0, here, :] = out * (1.0 / total)
-        lse = top * SCORE_SCALE + jnp.log2(total)
-        for part in range(SUF // BLK):
-            at = i * (SUF // BLK) + part
-            lse_ref[0, at : at + 1, :] = as_row(lse[part * BLK : (part + 1) * BLK])
-
+    )(core, shape, q0, q1, pk, pk_other, pv, pv_other)
+
+
+def suffix_kernel(shape_ref, row0, row1, o_ref, lse_ref):
     count = ROW_TOK // SUF
-    held = score(0)
-    for i in range(count):
-        later = score(i + 1) if i + 1 < count else None
-        weigh(i, held)
-        held = later
-
-
-def suffix_attend(starts, q, k, v):
-    rows, tokens, unused = q.shape
-    whole = pl.BlockSpec((1, tokens, HEAD), lambda r, b: (r, 0, 0))
-    blocks = tokens // BLK
+    for row, qkv in enumerate((row0, row1)):
+        token = lax.broadcasted_iota(jnp.int32, (ROW_TOK, 1), 0)
+        first = jnp.zeros((ROW_TOK, 1), jnp.int32)
+        start = 0
+        for j in range(1, RQ):
+            start = start + shape_ref[row, j - 1]
+            first = jnp.where(token >= start, start, first)
+
+        def bounds(i):
+            low = max(0, i * SUF - ROW_TOK // 2)
+            return low, slice(i * SUF, (i + 1) * SUF), slice(low, (i + 1) * SUF)
+
+        def score(i, qkv=qkv, first=first, token=token):
+            low, here, seen = bounds(i)
+            s = lax.dot_general(
+                qkv[0, here, :],
+                qkv[1, seen, :],
+                (((1,), (1,)), ((), ())),
+                preferred_element_type=jnp.float32,
+            )
+            other = low + lax.broadcasted_iota(jnp.int32, s.shape, 1)
+            return jnp.where((other >= first[here]) & (other <= token[here]), s, NEG)
+
+        def weigh(i, s, row=row, qkv=qkv):
+            unused, here, seen = bounds(i)
+            top = jnp.max(s, axis=1, keepdims=True)
+            p = jnp.exp2((s - top) * SCORE_SCALE)
+            total = jnp.sum(p, axis=1, keepdims=True)
+            out = jnp.dot(
+                p.astype(jnp.bfloat16), qkv[2, seen, :], preferred_element_type=jnp.float32
+            )
+            o_ref[row * ROW_TOK + i * SUF : row * ROW_TOK + (i + 1) * SUF, :] = out * (1.0 / total)
+            lse = top * SCORE_SCALE + jnp.log2(total)
+            for part in range(SUF // BLK):
+                at = i * (SUF // BLK) + part
+                lse_ref[row, at : at + 1, :] = as_row(lse[part * BLK : (part + 1) * BLK])
+
+        held = score(0)
+        for i in range(count):
+            later = score(i + 1) if i + 1 < count else None
+            weigh(i, held)
+            held = later
+
+
+def suffix_attend(shape, row0, row1):
+    rows, tokens = shape.shape[0], row0.shape[1]
+    smem = pl.BlockSpec(memory_space=pltpu.SMEM)
+    vmem = pl.BlockSpec(memory_space=pltpu.VMEM)
     return pl.pallas_call(
         suffix_kernel,
-        grid_spec=pltpu.PrefetchScalarGridSpec(
-            num_scalar_prefetch=1,
-            grid=(rows,),
-            in_specs=[whole] * 3,
-            out_specs=[whole, pl.BlockSpec((1, blocks, BLK), lambda r, b: (r, 0, 0))],
-        ),
+        in_specs=[smem, vmem, vmem],
+        out_specs=(vmem, vmem),
         out_shape=(
-            jax.ShapeDtypeStruct((rows, tokens, HEAD), jnp.float32),
-            jax.ShapeDtypeStruct((rows, blocks, BLK), jnp.float32),
+            jax.ShapeDtypeStruct((rows * tokens, HEAD), jnp.float32),
+            jax.ShapeDtypeStruct((rows, tokens // BLK, BLK), jnp.float32),
         ),
         compiler_params=pltpu.CompilerParams(vmem_limit_bytes=VMEM_BIG),
         cost_estimate=pl.CostEstimate(
             flops=rows * tokens * tokens * HEAD * 4 * 4, bytes_accessed=1 << 20, transcendentals=0
         ),
         name="suffix_attend",
-    )(starts, q, k, v)
+    )(shape, row0, row1)
 
 
 MERGE_BLOCKS = 4
@@ -567,23 +611,24 @@
             for lse, o in zip(lses, sources[0::2]):
                 weight = jnp.exp2(lse - top)
                 total = total + weight
-                summed = summed + weight * o[0, here, :].astype(jnp.float32)
+                summed = summed + weight * o[here, :].astype(jnp.float32)
             out_ref[block, row * BLK : (row + 1) * BLK, :] = (summed / total).astype(out_ref.dtype)
 
 
 def merge_parts(parts):
-    blocks = parts[0][0][0].shape[1] // BLK
+    blocks = ROW_TOK // BLK
+    steps = blocks // MERGE_BLOCKS
     specs, operands = [], []
-    for row in parts:
-        for o, lse, index in row:
+    for row in range(2):
+        for o, lse in parts:
             operands += [o, lse]
             specs += [
-                pl.BlockSpec((1, MERGE_BLOCKS * BLK, HEAD), lambda b, index=index: (index, b, 0)),
-                pl.BlockSpec((1, blocks, BLK), lambda b, index=index: (index, 0, 0)),
+                pl.BlockSpec((MERGE_BLOCKS * BLK, HEAD), lambda b, row=row: (row * steps + b, 0)),
+                pl.BlockSpec((1, blocks, BLK), lambda b, row=row: (row, 0, 0)),
             ]
     return pl.pallas_call(
         merge_kernel,
-        grid=(blocks // MERGE_BLOCKS,),
+        grid=(steps,),
         in_specs=specs,
         out_specs=pl.BlockSpec((MERGE_BLOCKS, 2 * BLK, HEAD), lambda b: (b, 0, 0)),
         out_shape=jax.ShapeDtypeStruct((blocks, 2 * BLK, HEAD), jnp.bfloat16),
@@ -606,7 +651,7 @@
 def project(attended, weights):
     heads, tokens, unused = attended.shape
     depth, width = weights.shape
-    rows, tile = tokens // 2, 512
+    rows, tile = tokens // 2, 1024
     out_spec = pl.BlockSpec((rows, tile), lambda i: (0, i))
     return pl.pallas_call(
         project_kernel,
@@ -621,6 +666,7 @@
             jax.ShapeDtypeStruct((rows, width), jnp.bfloat16),
         ),
         scratch_shapes=[pltpu.VMEM((tokens, depth), jnp.bfloat16)],
+        compiler_params=pltpu.CompilerParams(vmem_limit_bytes=VMEM_BIG),
         name="project",
     )(attended, weights)
 
@@ -641,7 +687,7 @@
             jax.ShapeDtypeStruct(keep.shape, jnp.bfloat16),
         ),
         name="norm_rows",
-    )(keep, got, residual, gain.reshape(1, -1))
+    )(keep, got, residual, gain)
 
 
 EXP_DEV = 4
@@ -690,7 +736,8 @@
 
 def experts_kernel(*refs):
     picked = refs[:8]
-    give_ref, wg, wu, wd, out_ref, rows_out = refs[8:]
+    give_ref, wg, wu, wd = refs[8:12]
+    outs, rows_out = refs[12:21], refs[21]
     expert = pl.program_id(0)
     rows = jnp.concatenate([part[...] for part in picked], axis=0)
     contract = (((1,), (1,)), ((), ()))
@@ -705,23 +752,28 @@
     @pl.when(expert == EXP_DEV - 1)
     def last():
         for slot in range(8):
-            out_ref[slot] = jnp.dot(
-                give_ref[slot], rows_out[slot], preferred_element_type=jnp.float32
-            ).astype(out_ref.dtype)
+            out = jnp.dot(give_ref[slot], rows_out[slot], preferred_element_type=jnp.float32)
+            out = out.astype(jnp.bfloat16)
+            if slot < 7:
+                outs[slot][...] = out
+            else:
+                outs[7][...] = out[: BLK // 2]
+                outs[8][...] = out[BLK // 2 :]
 
 
 def run_experts(picked, give, w_gate, w_up, w_down):
     width = picked[0].shape[1]
     hidden = w_down.shape[1]
     once = pl.Buffered(1)
+    heights = [BLK] * 7 + [BLK // 2] * 2
     return pl.pallas_call(
         experts_kernel,
         grid=(EXP_DEV,),
         in_specs=[pl.BlockSpec((SLOTS, width), lambda j: (j, 0))] * 8
         + [pl.BlockSpec((8, BLK, BLK), lambda j: (0, 0, 0))]
         + [pl.BlockSpec((1, hidden, width), lambda j: (j, 0, 0))] * 3,
-        out_specs=pl.BlockSpec((8, BLK, width), lambda j: (0, 0, 0), pipeline_mode=once),
-        out_shape=jax.ShapeDtypeStruct((8, BLK, width), jnp.bfloat16),
+        out_specs=[pl.BlockSpec((n, width), lambda j: (0, 0), pipeline_mode=once) for n in heights],
+        out_shape=[jax.ShapeDtypeStruct((n, width), jnp.bfloat16) for n in heights],
         scratch_shapes=[pltpu.VMEM((8, EXP_DEV * SLOTS, width), jnp.bfloat16)],
         compiler_params=pltpu.CompilerParams(vmem_limit_bytes=VMEM_BIG),
         name="experts",
@@ -736,7 +788,7 @@
     return picked
 
 
-SLOT_Z = ((0, 1, 2, 3), (1, 0, 2, 3), (2, 1, 3, 0), (3, 2, 1, 0))
+SLOT_Z = ((0, 1, 2, 3), (1, 0, 3, 2), (2, 3, 0, 1), (3, 2, 1, 0))
 
 
 def together(*arrays):
@@ -744,29 +796,52 @@
 
 
 def gather_rows(z, own):
+    half = own.shape[0] // 2
     up, down, there0 = together(z_up(own), z_down(own), y_swap(own))
-    first = pick_by_z(z, down, up, up, up)
+    first = pick_by_z(z, down, up, down, up)
     up2, down2, there1 = together(z_up(up), z_down(down), y_swap(first))
-    second = pick_by_z(z, down2, down, down, up2)
+    second = pick_by_z(z, down2, down2, up2, up2)
     up3, down3, there2 = together(z_up(up2), z_down(down2), y_swap(second))
-    third = pick_by_z(z, down3, down2, up2, up3)
-    return [own, first, second, third, there0, there1, there2, y_swap(third)]
+    third = pick_by_z(z, down3, down, up, up3)
+    late_up = z_up(pick_by_z(z, there0, there0, there2, there2)[half:], 1, 2)
+    late_down = z_down(pick_by_z(z, there2, there2, there0, there0)[half:], 2, 1)
+    late, late_up, late_down = together(y_swap(third[:half]), late_up, late_down)
+    there3 = jnp.concatenate([late, pick_by_z(z, late_down, late_down, late_up, late_up)], axis=0)
+    return [own, first, second, third, there0, there1, there2, there3]
+
+
+def plus(*parts):
+    return sum([part.astype(jnp.float32) for part in parts[1:]], parts[0].astype(jnp.float32))
+
+
+def plus16(*parts):
+    return plus(*parts).astype(jnp.bfloat16)
 
 
 def scatter_sums(z, sums):
-    def plus(a, b):
-        return (a.astype(jnp.float32) + b.astype(jnp.float32)).astype(jnp.bfloat16)
-
-    s3 = plus(sums[3], y_swap(sums[7]))
-    up, down = z_up(s3, 1), z_down(s3, 1)
-    s2 = plus(sums[2], y_swap(sums[6]))
-    up = z_up(pick_by_z(z, s2, plus(s3, up), s2, s2), 2)
-    down = z_down(pick_by_z(z, s2, s2, plus(s3, down), s2), 2)
-    s1 = plus(sums[1], y_swap(sums[5]))
-    up = z_up(pick_by_z(z, s1, plus(s2, up), plus(s2, up), s1), 3)
-    down = z_down(pick_by_z(z, s1, plus(s1, down), plus(s1, down), s1), 3)
-    s0 = (sums[0], y_swap(sums[4]))
-    return [part.astype(jnp.float32) for part in (*s0, up, down)]
+    half = sums[7].shape[0]
+    got, late_up, late_down = together(
+        y_swap(sums[7]), z_up(sums[8], 0, 1), z_down(sums[8], 3, 2)
+    )
+    s3 = jnp.concatenate([plus16(sums[3][:half], got), sums[3][half:]], axis=0)
+    fourth = plus16(sums[4][half:], pick_by_z(z, late_down, late_down, late_up, late_up))
+    sixth = plus16(sums[6][half:], pick_by_z(z, late_up, late_up, late_down, late_down))
+    fourth = jnp.concatenate([sums[4][:half], fourth], axis=0)
+    sixth = jnp.concatenate([sums[6][:half], sixth], axis=0)
+    got, up, down = together(y_swap(sixth), z_up(s3, 0, 0), z_down(s3, 3, 3))
+    s2 = plus16(sums[2], got)
+    got, up, down = together(
+        y_swap(sums[5]),
+        z_up(pick_by_z(z, s2, plus16(s2, up), s2, s2), 0, 1),
+        z_down(pick_by_z(z, s2, s2, plus16(s2, down), s2), 3, 2),
+    )
+    s1 = plus16(sums[1], got)
+    got, up, down = together(
+        y_swap(fourth),
+        z_up(pick_by_z(z, s1, plus16(s3, up), plus16(s1, up), s1)),
+        z_down(pick_by_z(z, s1, plus16(s1, down), plus16(s3, down), s1)),
+    )
+    return plus(sums[0], got, up, down)
 
 
 def tabled(values, index):
@@ -796,26 +871,20 @@
     z = place // 2
     core_arg = core.astype(jnp.int32).reshape(1)
 
+    mine, theirs = split_tokens(core_arg, queries, keys, values)
+    q_far0 = x_swap(mine[0])
+    other = core_swap(theirs)
+
+    shape = jnp.concatenate([lengths, groups], axis=1)
+    near_shape = jnp.concatenate([shape, core_swap(shape)], axis=0)
+    far_shape = x_swap(near_shape)
+
+    pk_theirs, pv_theirs = split_prefix(core_arg, prefix_keys, prefix_values)
+    pk_other, pv_other = core_swap(pk_theirs), core_swap(pv_theirs)
+    q_far1 = x_swap(other[0])
+
     proj_rows = lax.dynamic_slice_in_dim(out_proj, core * HEAD, HEAD, 0)
     proj_rows = lax.all_gather(proj_rows, "exp", axis=0, tiled=True)
-
-    shape = jnp.concatenate([lengths, groups], axis=1)
-    shapes = jnp.concatenate([shape, core_swap(shape)], axis=0)
-    shapes = jnp.concatenate([shapes, x_swap(shapes)], axis=0)
-
-    qkv_theirs, pk_theirs, pv_theirs = send_halves(
-        core_arg, queries, keys, values, prefix_keys, prefix_values
-    )
-    qkv_other = core_swap(qkv_theirs)
-    pk_other, pv_other = core_swap(pk_theirs), core_swap(pv_theirs)
-
-    def mine(array):
-        return jnp.where(core == 0, array[:, :HEAD], array[:, HEAD:])
-
-    q_two = jnp.stack([mine(queries), qkv_other[0]])
-    k_two = jnp.stack([mine(keys), qkv_other[1]])
-    v_two = jnp.stack([mine(values), qkv_other[2]])
-    q_far = x_swap(q_two)
 
     tab = jnp.concatenate([expert_ids.T.astype(jnp.bfloat16), expert_gates.T], axis=0)[None]
     for step in (1, 2, 4):
@@ -829,40 +898,27 @@
     scalars = jnp.concatenate([slot_place ^ place, (place * EXP_DEV).reshape(1)])
     pick, give = route(scalars.astype(jnp.int32), tab)
 
-    def prefix(q, rows, dtype):
-        count = q.shape[0]
-        work = prefix_work(shapes[rows, :RQ], shapes[rows, RQ:])
-        o, lse = prefix_attend(
-            work,
-            core_arg,
-            q.reshape(count * row_tok, HEAD),
-            prefix_keys,
-            pk_other,
-            prefix_values,
-            pv_other,
-            dtype,
+    def prefix(shape, q0, q1, dtype):
+        return prefix_attend(
+            core_arg, shape, q0, q1, prefix_keys, pk_other, prefix_values, pv_other, dtype
         )
-        return o.reshape(q.shape), lse.reshape(count, row_tok // BLK, BLK)
-
-    near_lengths = shapes[:2, :RQ]
-    suffix = suffix_attend(jnp.cumsum(near_lengths, axis=1) - near_lengths, q_two, k_two, v_two)
-    far = prefix(q_far, slice(2, 4), jnp.bfloat16)
+
+    suffix = suffix_attend(near_shape, mine, other)
+    far = prefix(far_shape, q_far0, q_far1, jnp.bfloat16)
     back = (x_swap(far[0]), x_swap(far[1]))
-    near = prefix(q_two, slice(0, 2), jnp.float32)
-    attended = merge_parts(
-        [[(*part, row) for part in (suffix, near, back)] for row in range(2)]
-    )
+    near = prefix(near_shape, mine[0], other[0], jnp.float32)
+    near_o, pick, give, gain = together(near[0], pick, give, norm_gain.reshape(1, -1))
+    attended = merge_parts([suffix, (near_o, near[1]), back])
     heads = lax.all_to_all(attended, "exp", split_axis=0, concat_axis=0, tiled=True)
     keep, send = project(heads, proj_rows)
-    stream, normed = norm_rows(keep, core_swap(send), residual, norm_gain)
+    stream, normed = norm_rows(keep, core_swap(send), residual, gain)
     rows = gather_rows(z, normed)
     picked = [
         jnp.dot(pick[i], part, preferred_element_type=jnp.float32).astype(jnp.bfloat16)
         for i, part in enumerate(rows)
     ]
     sums = run_experts(picked, give, w_gate, w_up, w_down)
-    parts = scatter_sums(z, sums)
-    return (stream + sum(parts[1:], parts[0])).astype(jnp.bfloat16)
+    return (stream + scatter_sums(z, sums)).astype(jnp.bfloat16)
 
 
 def solution(mesh):

time: 273 us -> 268 us (0.982)
  starting transfers between devices: 53.3 us -> 61.4 us
  waiting for transfers between devices: 73.7 us -> 69.3 us
  blocking collectives: 20.6 us -> 16.3 us
    ppermute x12 -> x16, waiting for transfers between devices: 24.3 us -> 58.2 us  [the longest x8 34.9 us: z_up(): lax.ppermute(array, 'exp', [(i, i + 2) for i in range(2 * first, 2 * last...]
    ppermute x3, waiting for transfers between devices: 19.3 us -> 1.86 us  [block_device(): lax.ppermute(tab, 'exp', [(i, i ^ step) for i in range(8)])]
    ppermute x8, waiting for transfers between devices: 22.7 us -> 7.01 us  [y_swap(): return lax.ppermute(array, 'exp', [(i, i ^ 1) for i in range(8)])]
    ppermute x12 -> x16, starting transfers between devices: 27.4 us -> 40.7 us  [the longest x8 32.2 us: z_up(): lax.ppermute(array, 'exp', [(i, i + 2) for i in range(2 * first, 2 * last...]
    ppermute x4 -> x5, waiting for transfers between devices: 5.77 us -> 0.01 us  [x_swap(): return lax.ppermute(array, 'req', [(i, i ^ 2) for i in range(4)])]
    all_to_all x1, blocking collectives: 20.6 us -> 16.3 us  [block_device(): lax.all_to_all(attended, 'exp', split_axis=0, concat_axis=0, tiled=True)]
    ppermute x8, starting transfers between devices: 9.43 us -> 6.66 us  [y_swap(): return lax.ppermute(array, 'exp', [(i, i ^ 1) for i in range(8)])]
    ppermute x4 -> x5, starting transfers between devices: 7.05 us -> 5.73 us  [x_swap(): return lax.ppermute(array, 'req', [(i, i ^ 2) for i in range(4)])]
  transfers between devices with their start and end apart: 33 -> 38, of which waited for: 16 -> 19; matrix products, arithmetic and copies ran while one was open for 10% -> 9% of each run, Pallas kernels for 17% -> 17%
where the time goes in v3:
time: 268 us; the launch traced here: 267 us
  Pallas kernels  73.7 us (28%)
  waiting for transfers between devices  69.3 us (26%)
  starting transfers between devices  61.4 us (23%)
  blocking collectives  16.3 us (6%)
  between operations  13.8 us (5%)
  other arithmetic  11.9 us (4%)
  local copies, waits for them, and re-layouts  10.7 us (4%)
  matrix products  9.74 us (4%)
    ppermute x8, waiting for transfers between devices, z_up(): lax.ppermute(array, 'exp', [(i, i + 2) for i in range(2 * first, 2 * last...  34.9 us
    ppermute x8, starting transfers between devices, z_up(): lax.ppermute(array, 'exp', [(i, i + 2) for i in range(2 * first, 2 * last...  32.2 us
    pallas_call x2, Pallas kernels, prefix_attend(): pl.pallas_call(prefix_kernel, in_specs=[smem, smem] + [anywhere] * 6, out...  29.9 us
    ppermute x8, waiting for transfers between devices, z_down(): lax.ppermute(array, 'exp', [(i, i - 2) for i in range(2 * last, 2 * first...  23.3 us
    pallas_call x1, Pallas kernels, run_experts(): pl.pallas_call(experts_kernel, grid=(EXP_DEV,), in_specs=[pl.BlockSpec((S...  20.5 us
    all_to_all x1, blocking collectives, block_device(): lax.all_to_all(attended, 'exp', split_axis=0, concat_axis=0, tiled=True)  16.3 us
    dot_general x8, matrix products, block_device(): jnp.dot(pick[i], part, preferred_element_type=jnp.float32)  9.74 us
    ppermute x8, starting transfers between devices, z_down(): lax.ppermute(array, 'exp', [(i, i - 2) for i in range(2 * last, 2 * first...  8.53 us
  transfers between devices with their start and end apart: 38, of which 19 were waited for; matrix products, arithmetic and copies ran while one was open for 9% of the time, Pallas kernels for 17%

profile of v3, /device:TPU:0, one launch (start us, length us, event | category | flops | bytes accessed | tf_op | source)
XLA Modules:
  0.0 266.9 jit_solution(1993945453674449090)
XLA Ops:
  6.5 1.2 copy-done
  9.8 2.4 split_tokens.1
  12.3 3.8 %split_prefix.1 = (bf16[4,1024,128]{2,1,0:T(8,128)(2,1)}, bf16[4,1024,128]{2,1,0:T(8,128)(2,1)}) custom-call(s32[1]{0:T(128)} %bitcast.sc_ref.core_ref, bf16[4,1024,256]{2,1,0:T(8,128)(2,1)} %pk.5, bf16[4,1024,256]{2,1,0:T(8,128)(2,1)} %pv.5), custom_call_target="tpu_custom_call" | custom-call | tf_op jit(solution)/shard_map/split_prefix/pallas_call | solution.py:308
  18.0 3.0 %collective-permute-start.4 = (bf16[1,8,128]{2,1,0:T(8,128)(2,1)S(1)}, bf16[1,8,128]{2,1,0:T(8,128)(2,1)S(1)}, u32[]{:S(2)}, u32[]{:S(2)}) collective-permute-start(bf16[1,8,128]{2,1,0:T(8,128)(2,1)S(1)} %maximum_bitcast_fusion), channel_id=1, source_target_pairs={{0,1},{1,0},{2,3},{3,2},{4,5},{5,4},{6,7},{7,6},{8,9},{9,8},{10,11... | collective-permute-start | bytes 6152 | tf_op jit(solution)/shard_map/ppermute | solution.py:892
  20.9 1.0 slice_bitcast_fusion.1.q0
  22.8 1.8 collective-permute-start.5
  25.2 1.3 reshape.19.gain
  26.7 1.5 collective-permute-start.8
  28.3 2.6 collective-permute-start.6
  31.6 1.7 collective-permute-done.6
  34.2 1.7 route.1
  35.9 1.8 collective-permute-start.9
  37.7 5.2 %suffix_attend.1 = (f32[2048,128]{1,0:T(8,128)}, f32[2,8,128]{2,1,0:T(8,128)}) custom-call(s32[2,16]{1,0:T(2,128)} %copy-done.11, bf16[3,1024,128]{2,1,0:T(8,128)(2,1)} %get-tuple-element.58.row0, bf16[3,1024,128]{2,1,0:T(8,128)(2,1)} %copy-done.9), custom_call_target="tpu_custom_call" | custom-call | flops 4294967296 | bytes 1048576 | tf_op jit(solution)/shard_map/suffix_attend/pallas_call | solution.py:576
  44.8 15.2 %prefix_attend.3 = (bf16[2048,128]{1,0:T(8,128)(2,1)}, f32[2,8,128]{2,1,0:T(8,128)}) custom-call(s32[1]{0:T(128)} %bitcast.sc_ref.core_ref, s32[2,16]{1,0:T(2,128)} %copy-done.15, bf16[1024,128]{1,0:T(8,128)(2,1)} %copy-done.13, bf16[1024,128]{1,0:T(8,128)(2,1)} %copy-done.14, bf16[4,1024,256]{2,1,0:T(8,128)(2,1)} %pk.5, bf16[4,1024,128]{2,1,0:T(8,128)(2,1)} %copy-done.12, ...), custom_call_target="tpu_custom_call" | custom-call | flops 8589934592 | bytes 4194304 | tf_op jit(solution)/shard_map/prefix_attend/pallas_call | solution.py:492
  60.7 1.3 collective-permute-start.11
  62.0 14.8 %prefix_attend.2 = (f32[2048,128]{1,0:T(8,128)}, f32[2,8,128]{2,1,0:T(8,128)}) custom-call(s32[1]{0:T(128)} %bitcast.sc_ref.core_ref, s32[2,16]{1,0:T(2,128)} %copy-done.11, bf16[1024,128]{1,0:T(8,128)(2,1)} %copy-done.7, bf16[1024,128]{1,0:T(8,128)(2,1)} %copy-done.8, bf16[4,1024,256]{2,1,0:T(8,128)(2,1)} %pk.5, bf16[4,1024,128]{2,1,0:T(8,128)(2,1)} %copy-done.12, ...), custom_call_target="tpu_custom_call" | custom-call | flops 8589934592 | bytes 4194304 | tf_op jit(solution)/shard_map/prefix_attend/pallas_call | solution.py:492
  77.7 3.1 %merge_parts.1 = bf16[8,256,128]{2,1,0:T(8,128)(2,1)} custom-call(f32[2048,128]{1,0:T(8,128)} %get-tuple-element.60.refs_0_.refs_6_, f32[2,8,128]{2,1,0:T(8,128)} %get-tuple-element.61.refs_1_.refs_7_, f32[2048,128]{1,0:T(8,128)} %get-tuple-element.67.refs_2_.refs_8_, f32[2,8,128]{2,1,0:T(8,128)} %get-tuple-element.68.refs_3_.refs_9_, ...), custom_call_target="tpu_custom_call" | custom-call | tf_op jit(solution)/shard_map/merge_parts/pallas_call | solution.py:629
  80.8 16.3 %all_to_all.5.a_ref = bf16[8,256,128]{2,1,0:T(8,128)(2,1)} all-to-all(bf16[8,256,128]{2,1,0:T(8,128)(2,1)} %merge_parts.1), channel_id=1, replica_groups=mesh['req'=4,'exp'=8] {'exp'}, dimensions={0} | all-to-all | bytes 1048576 | tf_op jit(solution)/shard_map/all_to_all | solution.py:912
  97.2 4.1 %project.1 = (f32[128,2048]{1,0:T(8,128)}, bf16[128,2048]{1,0:T(8,128)(2,1)}) custom-call(bf16[8,256,128]{2,1,0:T(8,128)(2,1)} %all_to_all.5.a_ref, bf16[1024,2048]{1,0:T(8,128)(2,1)} %all-gather.2.cloned.1.call-done.w_ref), custom_call_target="tpu_custom_call" | custom-call | tf_op jit(solution)/shard_map/project/pallas_call | solution.py:656
  101.3 2.1 collective-permute-done.12.got
  104.2 2.9 %norm_rows.1 = (f32[128,2048]{1,0:T(8,128)}, bf16[128,2048]{1,0:T(8,128)(2,1)}) custom-call(f32[128,2048]{1,0:T(8,128)} %get-tuple-element.71.keep, bf16[128,2048]{1,0:T(8,128)(2,1)} %copy-done.5, bf16[128,2048]{1,0:T(8,128)(2,1)} %residual.1, bf16[1,2048]{1,0:T(2,128)(2,1)} %reshape.19.gain), custom_call_target="tpu_custom_call" | custom-call | tf_op jit(solution)/shard_map/norm_rows/pallas_call | solution.py:683
  107.1 3.0 %collective-permute-start.13 = (bf16[128,2048]{1,0:T(8,128)(2,1)}, bf16[128,2048]{1,0:T(8,128)(2,1)S(1)}, u32[]{:S(2)}, u32[]{:S(2)}) collective-permute-start(bf16[128,2048]{1,0:T(8,128)(2,1)} %get-tuple-element.76), channel_id=1, source_target_pairs={{0,2},{1,3},{2,4},{3,5},{4,6},{5,7},{8,10},{9,11},{10,12},{11,13},... | collective-permute-start | bytes 1572872 | tf_op jit(solution)/shard_map/ppermute | solution.py:265
  110.1 1.3 collective-permute-start.14
  111.7 10.1 %collective-permute-done.13 = bf16[128,2048]{1,0:T(8,128)(2,1)S(1)} collective-permute-done((bf16[128,2048]{1,0:T(8,128)(2,1)}, bf16[128,2048]{1,0:T(8,128)(2,1)S(1)}, u32[]{:S(2)}, u32[]{:S(2)}) %collective-permute-start.13) | collective-permute-done | bytes 524320 | tf_op jit(solution)/shard_map/ppermute | solution.py:265
  121.8 4.0 %collective-permute-done.14 = bf16[128,2048]{1,0:T(8,128)(2,1)S(1)} collective-permute-done((bf16[128,2048]{1,0:T(8,128)(2,1)}, bf16[128,2048]{1,0:T(8,128)(2,1)S(1)}, u32[]{:S(2)}, u32[]{:S(2)}) %collective-permute-start.14) | collective-permute-done | bytes 524320 | tf_op jit(solution)/shard_map/ppermute | solution.py:269
  125.9 3.8 %collective-permute-start.16 = (bf16[128,2048]{1,0:T(8,128)(2,1)S(1)}, bf16[128,2048]{1,0:T(8,128)(2,1)S(1)}, u32[]{:S(2)}, u32[]{:S(2)}) collective-permute-start(bf16[128,2048]{1,0:T(8,128)(2,1)S(1)} %collective-permute-done.13), channel_id=1, source_target_pairs={{0,2},{1,3},{2,4},{3,5},{4,6},{5,7},{8,10},{9,11},{10,12},{11,13},... | collective-permute-start | bytes 1572872 | tf_op jit(solution)/shard_map/ppermute | solution.py:265
  129.6 1.3 collective-permute-start.17
  131.4 2.1 convolution_convert_fusion.7.refs_0_
  133.5 1.1 convolution_convert_fusion.6.refs_1_
  134.6 5.0 %collective-permute-done.16 = bf16[128,2048]{1,0:T(8,128)(2,1)S(1)} collective-permute-done((bf16[128,2048]{1,0:T(8,128)(2,1)S(1)}, bf16[128,2048]{1,0:T(8,128)(2,1)S(1)}, u32[]{:S(2)}, u32[]{:S(2)}) %collective-permute-start.16) | collective-permute-done | bytes 524320 | tf_op jit(solution)/shard_map/ppermute | solution.py:265
  139.6 4.1 %collective-permute-done.17 = bf16[128,2048]{1,0:T(8,128)(2,1)S(1)} collective-permute-done((bf16[128,2048]{1,0:T(8,128)(2,1)S(1)}, bf16[128,2048]{1,0:T(8,128)(2,1)S(1)}, u32[]{:S(2)}, u32[]{:S(2)}) %collective-permute-start.17) | collective-permute-done | bytes 524320 | tf_op jit(solution)/shard_map/ppermute | solution.py:269
  143.8 3.8 %collective-permute-start.19 = (bf16[128,2048]{1,0:T(8,128)(2,1)S(1)}, bf16[128,2048]{1,0:T(8,128)(2,1)S(1)}, u32[]{:S(2)}, u32[]{:S(2)}) collective-permute-start(bf16[128,2048]{1,0:T(8,128)(2,1)S(1)} %collective-permute-done.16), channel_id=1, source_target_pairs={{0,2},{1,3},{2,4},{3,5},{4,6},{5,7},{8,10},{9,11},{10,12},{11,13},... | collective-permute-start | bytes 1572872 | tf_op jit(solution)/shard_map/ppermute | solution.py:265
  147.7 1.3 collective-permute-start.20
  149.3 1.1 convolution_convert_fusion.3.refs_4_
  150.4 1.1 convolution_convert_fusion.5.refs_2_
  151.5 1.1 convolution_convert_fusion.2.refs_5_
  152.6 3.4 %collective-permute-done.19 = bf16[128,2048]{1,0:T(8,128)(2,1)S(1)} collective-permute-done((bf16[128,2048]{1,0:T(8,128)(2,1)S(1)}, bf16[128,2048]{1,0:T(8,128)(2,1)S(1)}, u32[]{:S(2)}, u32[]{:S(2)}) %collective-permute-start.19) | collective-permute-done | bytes 524320 | tf_op jit(solution)/shard_map/ppermute | solution.py:265
  156.1 4.2 %collective-permute-done.20 = bf16[128,2048]{1,0:T(8,128)(2,1)S(1)} collective-permute-done((bf16[128,2048]{1,0:T(8,128)(2,1)S(1)}, bf16[128,2048]{1,0:T(8,128)(2,1)S(1)}, u32[]{:S(2)}, u32[]{:S(2)}) %collective-permute-start.20) | collective-permute-done | bytes 524320 | tf_op jit(solution)/shard_map/ppermute | solution.py:269
  161.6 1.3 collective-permute-start.24
  162.9 1.1 convolution_convert_fusion.4.refs_3_
  164.0 1.1 convolution_convert_fusion.1.refs_6_
  165.1 1.8 collective-permute-done.22
  166.9 6.5 %collective-permute-done.24 = bf16[64,2048]{1,0:T(8,128)(2,1)S(1)} collective-permute-done((bf16[64,2048]{1,0:T(8,128)(2,1)S(1)}, bf16[64,2048]{1,0:T(8,128)(2,1)S(1)}, u32[]{:S(2)}, u32[]{:S(2)}) %collective-permute-start.24) | collective-permute-done | bytes 262176 | tf_op jit(solution)/shard_map/ppermute | solution.py:269
  173.4 1.1 convolution_convert_fusion.refs_7_
  174.5 20.5 %experts.1 = (bf16[128,2048]{1,0:T(8,128)(2,1)}, bf16[128,2048]{1,0:T(8,128)(2,1)}, bf16[128,2048]{1,0:T(8,128)(2,1)}, bf16[128,2048]{1,0:T(8,128)(2,1)}, bf16[1...) custom-call(bf16[128,2048]{1,0:T(8,128)(2,1)} %convolution_convert_f, ...), custom_call_target="tpu_custom_call" | custom-call | tf_op jit(solution)/shard_map/experts/pallas_call | solution.py:769
  195.1 1.1 collective-permute-start.25
  196.2 3.9 %collective-permute-start.26 = (bf16[64,2048]{1,0:T(8,128)(2,1)}, bf16[64,2048]{1,0:T(8,128)(2,1)S(1)}, u32[]{:S(2)}, u32[]{:S(2)}) collective-permute-start(bf16[64,2048]{1,0:T(8,128)(2,1)} %get-tuple-element.93), channel_id=1, source_target_pairs={{0,2},{1,3},{2,4},{3,5},{8,10},{9,11},{10,12},{11,13},{16,18},{17,... | collective-permute-start | bytes 786440 | tf_op jit(solution)/shard_map/ppermute | solution.py:265
  204.3 1.2 add_convert_fusion.4
  205.6 1.0 collective-permute-start.30
  206.6 1.0 add_convert_fusion.3
  207.7 6.2 %collective-permute-start.31 = (bf16[128,2048]{1,0:T(8,128)(2,1)S(1)}, bf16[128,2048]{1,0:T(8,128)(2,1)S(1)}, u32[]{:S(2)}, u32[]{:S(2)}) collective-permute-start(bf16[128,2048]{1,0:T(8,128)(2,1)S(1)} %pad_maximum_fusion.2), channel_id=1, source_target_pairs={{0,2},{1,3},{8,10},{9,11},{16,18},{17,19},{24,26},{25,27}} | collective-permute-start | bytes 1572872 | tf_op jit(solution)/shard_map/ppermute | solution.py:265
  214.6 1.1 collective-permute-start.29
  215.7 4.5 %collective-permute-done.30 = bf16[128,2048]{1,0:T(8,128)(2,1)S(1)} collective-permute-done((bf16[128,2048]{1,0:T(8,128)(2,1)S(1)}, bf16[128,2048]{1,0:T(8,128)(2,1)S(1)}, u32[]{:S(2)}, u32[]{:S(2)}) %collective-permute-start.30) | collective-permute-done | bytes 524320 | tf_op jit(solution)/shard_map/ppermute | solution.py:261
  220.2 3.4 %collective-permute-done.31 = bf16[128,2048]{1,0:T(8,128)(2,1)S(1)} collective-permute-done((bf16[128,2048]{1,0:T(8,128)(2,1)S(1)}, bf16[128,2048]{1,0:T(8,128)(2,1)S(1)}, u32[]{:S(2)}, u32[]{:S(2)}) %collective-permute-start.31) | collective-permute-done | bytes 524320 | tf_op jit(solution)/shard_map/ppermute | solution.py:265
  223.6 1.5 fusion.9
  225.1 4.4 %collective-permute-start.33 = (bf16[128,2048]{1,0:T(8,128)(2,1)S(1)}, bf16[128,2048]{1,0:T(8,128)(2,1)S(1)}, u32[]{:S(2)}, u32[]{:S(2)}) collective-permute-start(bf16[128,2048]{1,0:T(8,128)(2,1)S(1)} %get-tuple-element.114), channel_id=1, source_target_pairs={{0,2},{1,3},{2,4},{3,5},{8,10},{9,11},{10,12},{11,13},{16,18},{17,... | collective-permute-start | bytes 1572872 | tf_op jit(solution)/shard_map/ppermute | solution.py:265
  231.2 1.9 collective-permute-start.28
  233.2 6.7 %collective-permute-done.33 = bf16[128,2048]{1,0:T(8,128)(2,1)S(1)} collective-permute-done((bf16[128,2048]{1,0:T(8,128)(2,1)S(1)}, bf16[128,2048]{1,0:T(8,128)(2,1)S(1)}, u32[]{:S(2)}, u32[]{:S(2)}) %collective-permute-start.33) | collective-permute-done | bytes 524320 | tf_op jit(solution)/shard_map/ppermute | solution.py:265
  239.8 1.6 fusion.17
  241.5 6.3 %collective-permute-start.35 = (bf16[128,2048]{1,0:T(8,128)(2,1)S(1)}, bf16[128,2048]{1,0:T(8,128)(2,1)S(1)}, u32[]{:S(2)}, u32[]{:S(2)}) collective-permute-start(bf16[128,2048]{1,0:T(8,128)(2,1)S(1)} %get-tuple-element.112), channel_id=1, source_target_pairs={{0,2},{1,3},{2,4},{3,5},{4,6},{5,7},{8,10},{9,11},{10,12},{11,13},... | collective-permute-start | bytes 1572872 | tf_op jit(solution)/shard_map/ppermute | solution.py:265
  247.8 1.3 collective-permute-start.36
  249.1 5.3 %collective-permute-done.35 = bf16[128,2048]{1,0:T(8,128)(2,1)S(1)} collective-permute-done((bf16[128,2048]{1,0:T(8,128)(2,1)S(1)}, bf16[128,2048]{1,0:T(8,128)(2,1)S(1)}, u32[]{:S(2)}, u32[]{:S(2)}) %collective-permute-start.35) | collective-permute-done | bytes 524320 | tf_op jit(solution)/shard_map/ppermute | solution.py:265
  254.5 4.4 %collective-permute-done.36 = bf16[128,2048]{1,0:T(8,128)(2,1)S(1)} collective-permute-done((bf16[128,2048]{1,0:T(8,128)(2,1)S(1)}, bf16[128,2048]{1,0:T(8,128)(2,1)S(1)}, u32[]{:S(2)}, u32[]{:S(2)}) %collective-permute-start.36) | collective-permute-done | bytes 524320 | tf_op jit(solution)/shard_map/ppermute | solution.py:269
  258.9 1.2 add_convert_fusion
  (95 shorter events, 20.7 us)
Async XLA Ops:
  6.5 1.2 copy-start
  6.5 90.6 %all-gather.2.cloned.1.call-start = ((), (), s32[]{:S(2)}) async-start(), calls=%async_computation.1 | async-start | bytes 4718592 | tf_op jit(solution)/shard_map/all_gather | solution.py:887
  9.4 18.9 %collective-permute-start = (s32[1,16]{1,0:T(1,128)S(1)}, s32[1,16]{1,0:T(1,128)S(1)}, u32[]{:S(2)}, u32[]{:S(2)}) collective-permute-start(s32[1,16]{1,0:T(1,128)S(1)} %pad_add_fusion.1), channel_id=1, source_target_pairs={{0,8},{8,0},{16,24},{24,16},{1,9},{9,1},{17,25},{25,17},{2,10},{10... | collective-permute-start | bytes 200 | tf_op jit(solution)/shard_map/ppermute | solution.py:253
  12.2 23.7 %collective-permute-start.1 = (bf16[3,1024,128]{2,1,0:T(8,128)(2,1)}, bf16[3,1024,128]{2,1,0:T(8,128)(2,1)S(1)}, u32[]{:S(2)}, u32[]{:S(2)}) collective-permute-start(bf16[3,1024,128]{2,1,0:T(8,128)(2,1)} %get-tuple-element.59), channel_id=1, source_target_pairs={{0,8},{8,0},{16,24},{24,16},{1,9},{9,1},{17,25},{25,17},{2,10},{10... | collective-permute-start | bytes 2359304 | tf_op jit(solution)/shard_map/ppermute | solution.py:253
  16.1 26.8 %collective-permute-start.2 = (bf16[4,1024,128]{2,1,0:T(8,128)(2,1)}, bf16[4,1024,128]{2,1,0:T(8,128)(2,1)S(1)}, u32[]{:S(2)}, u32[]{:S(2)}) collective-permute-start(bf16[4,1024,128]{2,1,0:T(8,128)(2,1)} %get-tuple-element.62), channel_id=1, source_target_pairs={{0,8},{8,0},{16,24},{24,16},{1,9},{9,1},{17,25},{25,17},{2,10},{10... | collective-permute-start | bytes 3145736 | tf_op jit(solution)/shard_map/ppermute | solution.py:253
  16.5 26.4 %collective-permute-start.3 = (bf16[4,1024,128]{2,1,0:T(8,128)(2,1)}, bf16[4,1024,128]{2,1,0:T(8,128)(2,1)}, u32[]{:S(2)}, u32[]{:S(2)}) collective-permute-start(bf16[4,1024,128]{2,1,0:T(8,128)(2,1)} %get-tuple-element.63), channel_id=1, source_target_pairs={{0,8},{8,0},{16,24},{24,16},{1,9},{9,1},{17,25},{25,17},{2,10},{10... | collective-permute-start | bytes 3145736 | tf_op jit(solution)/shard_map/ppermute | solution.py:253
  18.0 4.8 %collective-permute-start.4 = (bf16[1,8,128]{2,1,0:T(8,128)(2,1)S(1)}, bf16[1,8,128]{2,1,0:T(8,128)(2,1)S(1)}, u32[]{:S(2)}, u32[]{:S(2)}) collective-permute-start(bf16[1,8,128]{2,1,0:T(8,128)(2,1)S(1)} %maximum_bitcast_fusion), channel_id=1, source_target_pairs={{0,1},{1,0},{2,3},{3,2},{4,5},{5,4},{6,7},{7,6},{8,9},{9,8},{10,11... | collective-permute-start | bytes 6152 | tf_op jit(solution)/shard_map/ppermute | solution.py:892
  21.9 38.0 %copy-start.7 = (bf16[1024,128]{1,0:T(8,128)(2,1)}, bf16[1024,128]{1,0:T(8,128)(2,1)S(1)}, u32[]{:S(2)}) copy-start(bf16[1024,128]{1,0:T(8,128)(2,1)S(1)} %slice_bitcast_fusion.1.q0) | copy-start | bytes 786436
  22.8 3.9 %collective-permute-start.5 = (bf16[2,8,128]{2,1,0:T(8,128)(2,1)S(1)}, bf16[2,8,128]{2,1,0:T(8,128)(2,1)S(1)}, u32[]{:S(2)}, u32[]{:S(2)}) collective-permute-start(bf16[2,8,128]{2,1,0:T(8,128)(2,1)S(1)} %pad_maximum_fusion.5), channel_id=1, source_target_pairs={{0,2},{1,3},{2,0},{3,1},{4,6},{5,7},{6,4},{7,5},{8,10},{9,11},{10,... | collective-permute-start | bytes 12296 | tf_op jit(solution)/shard_map/ppermute | solution.py:892
  26.7 16.2 %collective-permute-start.8 = (bf16[1024,128]{1,0:T(8,128)(2,1)S(1)}, bf16[1024,128]{1,0:T(8,128)(2,1)S(1)}, u32[]{:S(2)}, u32[]{:S(2)}) collective-permute-start(bf16[1024,128]{1,0:T(8,128)(2,1)S(1)} %slice_bitcast_fusion.1.q0), channel_id=1, source_target_pairs={{0,16},{8,24},{16,0},{24,8},{1,17},{9,25},{17,1},{25,9},{2,18},{10... | collective-permute-start | bytes 786440 | tf_op jit(solution)/shard_map/ppermute | solution.py:257
  28.3 5.0 %collective-permute-start.6 = (bf16[4,8,128]{2,1,0:T(8,128)(2,1)S(1)}, bf16[4,8,128]{2,1,0:T(8,128)(2,1)S(1)}, u32[]{:S(2)}, u32[]{:S(2)}) collective-permute-start(bf16[4,8,128]{2,1,0:T(8,128)(2,1)S(1)} %pad_maximum_fusion.4), channel_id=1, source_target_pairs={{0,4},{1,5},{2,6},{3,7},{4,0},{5,1},{6,2},{7,3},{8,12},{9,13},{10,... | collective-permute-start | bytes 24584 | tf_op jit(solution)/shard_map/ppermute | solution.py:892
  31.6 6.2 %copy-start.11 = (s32[2,16]{1,0:T(2,128)}, s32[2,16]{1,0:T(2,128)S(1)}, u32[]{:S(2)}) copy-start(s32[2,16]{1,0:T(2,128)S(1)} %pad_add_fusion.shape_ref) | copy-start | bytes 388
  33.3 9.6 %collective-permute-start.7 = (s32[2,16]{1,0:T(2,128)S(1)}, s32[2,16]{1,0:T(2,128)S(1)}, u32[]{:S(2)}, u32[]{:S(2)}) collective-permute-start(s32[2,16]{1,0:T(2,128)S(1)} %pad_add_fusion.shape_ref), channel_id=1, source_target_pairs={{0,16},{8,24},{16,0},{24,8},{1,17},{9,25},{17,1},{25,9},{2,18},{10... | collective-permute-start | bytes 392 | tf_op jit(solution)/shard_map/ppermute | solution.py:257
  35.9 1.8 copy-start.9
  35.9 24.0 %copy-start.8 = (bf16[1024,128]{1,0:T(8,128)(2,1)}, bf16[1024,128]{1,0:T(8,128)(2,1)S(1)}, u32[]{:S(2)}) copy-start(bf16[1024,128]{1,0:T(8,128)(2,1)S(1)} %slice_bitcast_fusion.q1) | copy-start | bytes 786436
  35.9 7.0 %collective-permute-start.9 = (bf16[1024,128]{1,0:T(8,128)(2,1)S(1)}, bf16[1024,128]{1,0:T(8,128)(2,1)S(1)}, u32[]{:S(2)}, u32[]{:S(2)}) collective-permute-start(bf16[1024,128]{1,0:T(8,128)(2,1)S(1)} %slice_bitcast_fusion.q1), channel_id=1, source_target_pairs={{0,16},{8,24},{16,0},{24,8},{1,17},{9,25},{17,1},{25,9},{2,18},{10... | collective-permute-start | bytes 786440 | tf_op jit(solution)/shard_map/ppermute | solution.py:257
  42.9 0.6 copy-start.15
  42.9 0.7 copy-start.13
  42.9 1.1 copy-start.12
  44.1 0.7 copy-start.14
  59.9 16.9 %collective-permute-start.10 = (bf16[2048,128]{1,0:T(8,128)(2,1)}, bf16[2048,128]{1,0:T(8,128)(2,1)S(1)}, u32[]{:S(2)}, u32[]{:S(2)}) collective-permute-start(bf16[2048,128]{1,0:T(8,128)(2,1)} %get-tuple-element.69), channel_id=1, source_target_pairs={{0,16},{8,24},{16,0},{24,8},{1,17},{9,25},{17,1},{25,9},{2,18},{10... | collective-permute-start | bytes 1572872 | tf_op jit(solution)/shard_map/ppermute | solution.py:257
  60.7 16.1 %collective-permute-start.11 = (f32[2,8,128]{2,1,0:T(8,128)}, f32[2,8,128]{2,1,0:T(8,128)S(1)}, u32[]{:S(2)}, u32[]{:S(2)}) collective-permute-start(f32[2,8,128]{2,1,0:T(8,128)} %get-tuple-element.70), channel_id=1, source_target_pairs={{0,16},{8,24},{16,0},{24,8},{1,17},{9,25},{17,1},{25,9},{2,18},{10... | collective-permute-start | bytes 24584 | tf_op jit(solution)/shard_map/ppermute | solution.py:257
  76.8 54.5 %copy-start.6 = (bf16[8,128,128]{2,1,0:T(8,128)(2,1)S(1)}, bf16[8,128,128]{2,1,0:T(8,128)(2,1)}, u32[]{:S(2)}) copy-start(bf16[8,128,128]{2,1,0:T(8,128)(2,1)} %get-tuple-element.75) | copy-start | bytes 786436
  76.8 0.6 copy-start.10
  76.9 0.8 copy-start.2
  101.3 2.1 collective-permute-start.12
  103.4 0.8 copy-start.5
  107.1 14.7 %collective-permute-start.13 = (bf16[128,2048]{1,0:T(8,128)(2,1)}, bf16[128,2048]{1,0:T(8,128)(2,1)S(1)}, u32[]{:S(2)}, u32[]{:S(2)}) collective-permute-start(bf16[128,2048]{1,0:T(8,128)(2,1)} %get-tuple-element.76), channel_id=1, source_target_pairs={{0,2},{1,3},{2,4},{3,5},{4,6},{5,7},{8,10},{9,11},{10,12},{11,13},... | collective-permute-start | bytes 1572872 | tf_op jit(solution)/shard_map/ppermute | solution.py:265
  110.1 15.8 %collective-permute-start.14 = (bf16[128,2048]{1,0:T(8,128)(2,1)}, bf16[128,2048]{1,0:T(8,128)(2,1)S(1)}, u32[]{:S(2)}, u32[]{:S(2)}) collective-permute-start(bf16[128,2048]{1,0:T(8,128)(2,1)} %get-tuple-element.76), channel_id=1, source_target_pairs={{2,0},{3,1},{4,2},{5,3},{6,4},{7,5},{10,8},{11,9},{12,10},{13,11},... | collective-permute-start | bytes 1572872 | tf_op jit(solution)/shard_map/ppermute | solution.py:269
  111.4 14.5 %collective-permute-start.15 = (bf16[128,2048]{1,0:T(8,128)(2,1)}, bf16[128,2048]{1,0:T(8,128)(2,1)S(1)}, u32[]{:S(2)}, u32[]{:S(2)}) collective-permute-start(bf16[128,2048]{1,0:T(8,128)(2,1)} %get-tuple-element.76), channel_id=1, source_target_pairs={{0,1},{1,0},{2,3},{3,2},{4,5},{5,4},{6,7},{7,6},{8,9},{9,8},{10,11... | collective-permute-start | bytes 1572872 | tf_op jit(solution)/shard_map/ppermute | solution.py:261
  125.9 13.7 %collective-permute-start.16 = (bf16[128,2048]{1,0:T(8,128)(2,1)S(1)}, bf16[128,2048]{1,0:T(8,128)(2,1)S(1)}, u32[]{:S(2)}, u32[]{:S(2)}) collective-permute-start(bf16[128,2048]{1,0:T(8,128)(2,1)S(1)} %collective-permute-done.13), channel_id=1, source_target_pairs={{0,2},{1,3},{2,4},{3,5},{4,6},{5,7},{8,10},{9,11},{10,12},{11,13},... | collective-permute-start | bytes 1572872 | tf_op jit(solution)/shard_map/ppermute | solution.py:265
  129.6 14.1 %collective-permute-start.17 = (bf16[128,2048]{1,0:T(8,128)(2,1)S(1)}, bf16[128,2048]{1,0:T(8,128)(2,1)S(1)}, u32[]{:S(2)}, u32[]{:S(2)}) collective-permute-start(bf16[128,2048]{1,0:T(8,128)(2,1)S(1)} %collective-permute-done.14), channel_id=1, source_target_pairs={{2,0},{3,1},{4,2},{5,3},{6,4},{7,5},{10,8},{11,9},{12,10},{13,11},... | collective-permute-start | bytes 1572872 | tf_op jit(solution)/shard_map/ppermute | solution.py:269
  131.0 12.7 %collective-permute-start.18 = (bf16[128,2048]{1,0:T(8,128)(2,1)S(1)}, bf16[128,2048]{1,0:T(8,128)(2,1)S(1)}, u32[]{:S(2)}, u32[]{:S(2)}) collective-permute-start(bf16[128,2048]{1,0:T(8,128)(2,1)S(1)} %fusion.12), channel_id=1, source_target_pairs={{0,1},{1,0},{2,3},{3,2},{4,5},{5,4},{6,7},{7,6},{8,9},{9,8},{10,11... | collective-permute-start | bytes 1572872 | tf_op jit(solution)/shard_map/ppermute | solution.py:261
  143.8 12.3 %collective-permute-start.19 = (bf16[128,2048]{1,0:T(8,128)(2,1)S(1)}, bf16[128,2048]{1,0:T(8,128)(2,1)S(1)}, u32[]{:S(2)}, u32[]{:S(2)}) collective-permute-start(bf16[128,2048]{1,0:T(8,128)(2,1)S(1)} %collective-permute-done.16), channel_id=1, source_target_pairs={{0,2},{1,3},{2,4},{3,5},{4,6},{5,7},{8,10},{9,11},{10,12},{11,13},... | collective-permute-start | bytes 1572872 | tf_op jit(solution)/shard_map/ppermute | solution.py:265
  147.7 12.6 %collective-permute-start.20 = (bf16[128,2048]{1,0:T(8,128)(2,1)S(1)}, bf16[128,2048]{1,0:T(8,128)(2,1)S(1)}, u32[]{:S(2)}, u32[]{:S(2)}) collective-permute-start(bf16[128,2048]{1,0:T(8,128)(2,1)S(1)} %collective-permute-done.17), channel_id=1, source_target_pairs={{2,0},{3,1},{4,2},{5,3},{6,4},{7,5},{10,8},{11,9},{12,10},{13,11},... | collective-permute-start | bytes 1572872 | tf_op jit(solution)/shard_map/ppermute | solution.py:269
  148.9 11.4 %collective-permute-start.21 = (bf16[128,2048]{1,0:T(8,128)(2,1)S(1)}, bf16[128,2048]{1,0:T(8,128)(2,1)S(1)}, u32[]{:S(2)}, u32[]{:S(2)}) collective-permute-start(bf16[128,2048]{1,0:T(8,128)(2,1)S(1)} %select_select_fusion), channel_id=1, source_target_pairs={{0,1},{1,0},{2,3},{3,2},{4,5},{5,4},{6,7},{7,6},{8,9},{9,8},{10,11... | collective-permute-start | bytes 1572872 | tf_op jit(solution)/shard_map/ppermute | solution.py:261
  160.5 6.4 %collective-permute-start.22 = (bf16[64,2048]{1,0:T(8,128)(2,1)S(1)}, bf16[64,2048]{1,0:T(8,128)(2,1)S(1)}, u32[]{:S(2)}, u32[]{:S(2)}) collective-permute-start(bf16[64,2048]{1,0:T(8,128)(2,1)S(1)} %slice.79), channel_id=1, source_target_pairs={{0,1},{1,0},{2,3},{3,2},{4,5},{5,4},{6,7},{7,6},{8,9},{9,8},{10,11... | collective-permute-start | bytes 786440 | tf_op jit(solution)/shard_map/ppermute | solution.py:261
  161.0 6.0 %collective-permute-start.23 = (bf16[64,2048]{1,0:T(8,128)(2,1)S(1)}, bf16[64,2048]{1,0:T(8,128)(2,1)S(1)}, u32[]{:S(2)}, u32[]{:S(2)}) collective-permute-start(bf16[64,2048]{1,0:T(8,128)(2,1)S(1)} %get-tuple-element.116), channel_id=1, source_target_pairs={{2,4},{3,5},{4,6},{5,7},{10,12},{11,13},{12,14},{13,15},{18,20},{1... | collective-permute-start | bytes 786440 | tf_op jit(solution)/shard_map/ppermute | solution.py:265
  161.6 11.8 %collective-permute-start.24 = (bf16[64,2048]{1,0:T(8,128)(2,1)S(1)}, bf16[64,2048]{1,0:T(8,128)(2,1)S(1)}, u32[]{:S(2)}, u32[]{:S(2)}) collective-permute-start(bf16[64,2048]{1,0:T(8,128)(2,1)S(1)} %get-tuple-element.115), channel_id=1, source_target_pairs={{2,0},{3,1},{4,2},{5,3},{10,8},{11,9},{12,10},{13,11},{18,16},{19,... | collective-permute-start | bytes 786440 | tf_op jit(solution)/shard_map/ppermute | solution.py:269
  174.5 85.6 %copy-start.1 = (bf16[256,2048]{1,0:T(8,128)(2,1)S(1)}, bf16[256,2048]{1,0:T(8,128)(2,1)}, u32[]{:S(2)}) copy-start(bf16[256,2048]{1,0:T(8,128)(2,1)} %param.24) | copy-start | bytes 3145732
  195.0 63.9 %copy-start.3 = (f32[128,2048]{1,0:T(8,128)S(1)}, f32[128,2048]{1,0:T(8,128)}, u32[]{:S(2)}) copy-start(f32[128,2048]{1,0:T(8,128)} %get-tuple-element.74) | copy-start | bytes 3145732
  195.1 63.9 %copy-start.4 = (bf16[128,2048]{1,0:T(8,128)(2,1)S(1)}, bf16[128,2048]{1,0:T(8,128)(2,1)}, u32[]{:S(2)}) copy-start(bf16[128,2048]{1,0:T(8,128)(2,1)} %get-tuple-element.90) | copy-start | bytes 1572868
  195.1 8.3 %collective-permute-start.25 = (bf16[64,2048]{1,0:T(8,128)(2,1)}, bf16[64,2048]{1,0:T(8,128)(2,1)S(1)}, u32[]{:S(2)}, u32[]{:S(2)}) collective-permute-start(bf16[64,2048]{1,0:T(8,128)(2,1)} %get-tuple-element.92), channel_id=1, source_target_pairs={{0,1},{1,0},{2,3},{3,2},{4,5},{5,4},{6,7},{7,6},{8,9},{9,8},{10,11... | collective-permute-start | bytes 786440 | tf_op jit(solution)/shard_map/ppermute | solution.py:261
  196.2 8.1 %collective-permute-start.26 = (bf16[64,2048]{1,0:T(8,128)(2,1)}, bf16[64,2048]{1,0:T(8,128)(2,1)S(1)}, u32[]{:S(2)}, u32[]{:S(2)}) collective-permute-start(bf16[64,2048]{1,0:T(8,128)(2,1)} %get-tuple-element.93), channel_id=1, source_target_pairs={{0,2},{1,3},{2,4},{3,5},{8,10},{9,11},{10,12},{11,13},{16,18},{17,... | collective-permute-start | bytes 786440 | tf_op jit(solution)/shard_map/ppermute | solution.py:265
  200.1 4.2 %collective-permute-start.27 = (bf16[64,2048]{1,0:T(8,128)(2,1)}, bf16[64,2048]{1,0:T(8,128)(2,1)S(1)}, u32[]{:S(2)}, u32[]{:S(2)}) collective-permute-start(bf16[64,2048]{1,0:T(8,128)(2,1)} %get-tuple-element.93), channel_id=1, source_target_pairs={{4,2},{5,3},{6,4},{7,5},{12,10},{13,11},{14,12},{15,13},{20,18},{2... | collective-permute-start | bytes 786440 | tf_op jit(solution)/shard_map/ppermute | solution.py:269
  205.6 14.6 %collective-permute-start.30 = (bf16[128,2048]{1,0:T(8,128)(2,1)S(1)}, bf16[128,2048]{1,0:T(8,128)(2,1)S(1)}, u32[]{:S(2)}, u32[]{:S(2)}) collective-permute-start(bf16[128,2048]{1,0:T(8,128)(2,1)S(1)} %pad_maximum_fusion.1), channel_id=1, source_target_pairs={{0,1},{1,0},{2,3},{3,2},{4,5},{5,4},{6,7},{7,6},{8,9},{9,8},{10,11... | collective-permute-start | bytes 1572872 | tf_op jit(solution)/shard_map/ppermute | solution.py:261
  207.7 15.9 %collective-permute-start.31 = (bf16[128,2048]{1,0:T(8,128)(2,1)S(1)}, bf16[128,2048]{1,0:T(8,128)(2,1)S(1)}, u32[]{:S(2)}, u32[]{:S(2)}) collective-permute-start(bf16[128,2048]{1,0:T(8,128)(2,1)S(1)} %pad_maximum_fusion.2), channel_id=1, source_target_pairs={{0,2},{1,3},{8,10},{9,11},{16,18},{17,19},{24,26},{25,27}} | collective-permute-start | bytes 1572872 | tf_op jit(solution)/shard_map/ppermute | solution.py:265
  213.9 9.7 %collective-permute-start.32 = (bf16[128,2048]{1,0:T(8,128)(2,1)S(1)}, bf16[128,2048]{1,0:T(8,128)(2,1)S(1)}, u32[]{:S(2)}, u32[]{:S(2)}) collective-permute-start(bf16[128,2048]{1,0:T(8,128)(2,1)S(1)} %pad_maximum_fusion.2), channel_id=1, source_target_pairs={{6,4},{7,5},{14,12},{15,13},{22,20},{23,21},{30,28},{31,29}} | collective-permute-start | bytes 1572872 | tf_op jit(solution)/shard_map/ppermute | solution.py:269
  214.6 18.6 %collective-permute-start.29 = (bf16[128,2048]{1,0:T(8,128)(2,1)}, bf16[128,2048]{1,0:T(8,128)(2,1)S(1)}, u32[]{:S(2)}, u32[]{:S(2)}) collective-permute-start(bf16[128,2048]{1,0:T(8,128)(2,1)} %get-tuple-element.97), channel_id=1, source_target_pairs={{0,1},{1,0},{2,3},{3,2},{4,5},{5,4},{6,7},{7,6},{8,9},{9,8},{10,11... | collective-permute-start | bytes 1572872 | tf_op jit(solution)/shard_map/ppermute | solution.py:261
  225.1 14.8 %collective-permute-start.33 = (bf16[128,2048]{1,0:T(8,128)(2,1)S(1)}, bf16[128,2048]{1,0:T(8,128)(2,1)S(1)}, u32[]{:S(2)}, u32[]{:S(2)}) collective-permute-start(bf16[128,2048]{1,0:T(8,128)(2,1)S(1)} %get-tuple-element.114), channel_id=1, source_target_pairs={{0,2},{1,3},{2,4},{3,5},{8,10},{9,11},{10,12},{11,13},{16,18},{17,... | collective-permute-start | bytes 1572872 | tf_op jit(solution)/shard_map/ppermute | solution.py:265
  229.5 10.3 %collective-permute-start.34 = (bf16[128,2048]{1,0:T(8,128)(2,1)S(1)}, bf16[128,2048]{1,0:T(8,128)(2,1)S(1)}, u32[]{:S(2)}, u32[]{:S(2)}) collective-permute-start(bf16[128,2048]{1,0:T(8,128)(2,1)S(1)} %get-tuple-element.113), channel_id=1, source_target_pairs={{4,2},{5,3},{6,4},{7,5},{12,10},{13,11},{14,12},{15,13},{20,18},{2... | collective-permute-start | bytes 1572872 | tf_op jit(solution)/shard_map/ppermute | solution.py:269
  231.2 17.9 %collective-permute-start.28 = (bf16[128,2048]{1,0:T(8,128)(2,1)S(1)}, bf16[128,2048]{1,0:T(8,128)(2,1)S(1)}, u32[]{:S(2)}, u32[]{:S(2)}) collective-permute-start(bf16[128,2048]{1,0:T(8,128)(2,1)S(1)} %pad_maximum_fusion), channel_id=1, source_target_pairs={{0,1},{1,0},{2,3},{3,2},{4,5},{5,4},{6,7},{7,6},{8,9},{9,8},{10,11... | collective-permute-start | bytes 1572872 | tf_op jit(solution)/shard_map/ppermute | solution.py:261
  241.5 13.0 %collective-permute-start.35 = (bf16[128,2048]{1,0:T(8,128)(2,1)S(1)}, bf16[128,2048]{1,0:T(8,128)(2,1)S(1)}, u32[]{:S(2)}, u32[]{:S(2)}) collective-permute-start(bf16[128,2048]{1,0:T(8,128)(2,1)S(1)} %get-tuple-element.112), channel_id=1, source_target_pairs={{0,2},{1,3},{2,4},{3,5},{4,6},{5,7},{8,10},{9,11},{10,12},{11,13},... | collective-permute-start | bytes 1572872 | tf_op jit(solution)/shard_map/ppermute | solution.py:265
  247.8 11.1 %collective-permute-start.36 = (bf16[128,2048]{1,0:T(8,128)(2,1)S(1)}, bf16[128,2048]{1,0:T(8,128)(2,1)S(1)}, u32[]{:S(2)}, u32[]{:S(2)}) collective-permute-start(bf16[128,2048]{1,0:T(8,128)(2,1)S(1)} %get-tuple-element.111), channel_id=1, source_target_pairs={{2,0},{3,1},{4,2},{5,3},{6,4},{7,5},{10,8},{11,9},{12,10},{13,11},... | collective-permute-start | bytes 1572872 | tf_op jit(solution)/shard_map/ppermute | solution.py:269
Sparse Core Ops, SparseCore 0:
  9.5 76.3 all-gather.1

commit v4 on v3

--- a/solution.py
+++ b/solution.py
@@ -1,3 +1,4 @@
+import functools
 import math
 
 import jax
@@ -261,58 +262,39 @@
     return lax.ppermute(array, "exp", [(i, i ^ 1) for i in range(8)])
 
 
-def z_up(array, first=0, last=2):
-    return lax.ppermute(array, "exp", [(i, i + 2) for i in range(2 * first, 2 * last + 2)])
-
-
-def z_down(array, first=3, last=1):
-    return lax.ppermute(array, "exp", [(i, i - 2) for i in range(2 * last, 2 * first + 2)])
-
-
-def split_tokens_kernel(sc_ref, *refs):
-    for i in range(3):
-        refs[6][i] = refs[i][...]
-        refs[7][i] = refs[3 + i][...]
-
-
-def split_tokens(core, q, k, v):
-    rows = q.shape[0]
-    part = rows // 2
-    mine = pl.BlockSpec((part, HEAD), lambda i, s: (i, s[0]))
-    theirs = pl.BlockSpec((part, HEAD), lambda i, s: (i, 1 - s[0]))
-    out = pl.BlockSpec((3, part, HEAD), lambda i, s: (0, i, 0))
-    shape = jax.ShapeDtypeStruct((3, rows, HEAD), q.dtype)
+def z_swap(array, distance):
+    return lax.ppermute(array, "exp", [(i, i ^ (2 * distance)) for i in range(8)])
+
+
+def split_kernel(sc_ref, q, k, v, pk, pv, out_tokens, out_prefix):
+    for i, part in enumerate((q, k, v)):
+        out_tokens[i] = part[...]
+    out_prefix[0] = pk[...]
+    out_prefix[1] = pv[...]
+
+
+def split_theirs(place, q, k, v, pk, pv):
+    rows, span = q.shape[0], pk.shape[1]
+    part = rows // G
+    tokens = pl.BlockSpec((part, HEAD), lambda i, s: (i, 1 - s[0]))
+    prefix = pl.BlockSpec((1, span, HEAD), lambda i, s: (i, 0, 1 - s[0]))
     return pl.pallas_call(
-        split_tokens_kernel,
+        split_kernel,
         grid_spec=pltpu.PrefetchScalarGridSpec(
             num_scalar_prefetch=1,
-            grid=(2,),
-            in_specs=[mine] * 3 + [theirs] * 3,
-            out_specs=[out, out],
-        ),
-        out_shape=(shape, shape),
-        name="split_tokens",
-    )(core, q, k, v, q, k, v)
-
-
-def split_prefix_kernel(sc_ref, pk, pv, out_pk, out_pv):
-    out_pk[...] = pk[...]
-    out_pv[...] = pv[...]
-
-
-def split_prefix(core, pk, pv):
-    span = pk.shape[1]
-    theirs = pl.BlockSpec((1, span, HEAD), lambda i, s: (i, 0, 1 - s[0]))
-    out = pl.BlockSpec((1, span, HEAD), lambda i, s: (i, 0, 0))
-    shape = jax.ShapeDtypeStruct((G, span, HEAD), pk.dtype)
-    return pl.pallas_call(
-        split_prefix_kernel,
-        grid_spec=pltpu.PrefetchScalarGridSpec(
-            num_scalar_prefetch=1, grid=(G,), in_specs=[theirs] * 2, out_specs=[out] * 2
-        ),
-        out_shape=(shape, shape),
-        name="split_prefix",
-    )(core, pk, pv)
+            grid=(G,),
+            in_specs=[tokens] * 3 + [prefix] * 2,
+            out_specs=[
+                pl.BlockSpec((3, part, HEAD), lambda i, s: (0, i, 0)),
+                pl.BlockSpec((2, 1, span, HEAD), lambda i, s: (0, i, 0, 0)),
+            ],
+        ),
+        out_shape=(
+            jax.ShapeDtypeStruct((3, rows, HEAD), q.dtype),
+            jax.ShapeDtypeStruct((2, G, span, HEAD), q.dtype),
+        ),
+        name="split_theirs",
+    )(place, q, k, v, pk, pv)
 
 
 def as_row(column):
@@ -325,15 +307,15 @@
 ITEMS = 16
 
 
-def build_work(shape_ref, rows, item_group, item_block):
+def build_work(shapes, item_group, item_block):
     per_row = ROW_TOK // SUB
     spans = []
-    for r in range(rows):
+    for r, (shape, at) in enumerate(shapes):
         start = 0
         for j in range(RQ):
-            end = start + shape_ref[r, j]
+            end = start + shape[at, j]
             first, last = r * per_row + start // SUB, r * per_row + (end - 1) // SUB
-            spans.append((first, last, shape_ref[r, RQ + j]))
+            spans.append((first, last, shape[at, RQ + j]))
             start = end
 
     def of_group(g, begin):
@@ -368,32 +350,32 @@
 
 
 def prefix_kernel(
-    core_ref, shape_ref, q0, q1, pk, pk_other, pv, pv_other, o_ref, lse_ref,
+    far, sc_ref, shape_a, shape_b, q0, q1, pk, pv, other, o_ref, lse_ref,
     q_ref, ka, kb, va, vb, grp, lse, sa, sb, ta, tb, item_group, item_block, sems,
 ):
     tokens = q_ref.shape[0]
-    rows = tokens // ROW_TOK
     span = ka.shape[1]
-    mine_cols = pl.ds(pl.multiple_of(core_ref[0] * HEAD, HEAD), HEAD)
+    shapes = ((shape_a, 0), (shape_b, far))
+    mine = pl.ds(pl.multiple_of(sc_ref[0] * HEAD, HEAD), HEAD)
     copies = [
-        pltpu.make_async_copy(q0, q_ref.at[:ROW_TOK, :], sems.at[0]),
+        pltpu.make_async_copy(q0.at[:, mine], q_ref.at[:ROW_TOK, :], sems.at[0]),
         pltpu.make_async_copy(q1, q_ref.at[ROW_TOK:, :], sems.at[1]),
-        pltpu.make_async_copy(pk.at[:, :, mine_cols], ka, sems.at[2]),
-        pltpu.make_async_copy(pk_other, kb, sems.at[3]),
-        pltpu.make_async_copy(pv.at[:, :, mine_cols], va, sems.at[4]),
-        pltpu.make_async_copy(pv_other, vb, sems.at[5]),
+        pltpu.make_async_copy(pk.at[:, :, mine], ka, sems.at[2]),
+        pltpu.make_async_copy(other.at[0], kb, sems.at[3]),
+        pltpu.make_async_copy(pv.at[:, :, mine], va, sems.at[4]),
+        pltpu.make_async_copy(other.at[1], vb, sems.at[5]),
     ]
     for copy in copies:
         copy.start()
-    for r in range(rows):
+    for r, (shape, at) in enumerate(shapes):
         token = lax.broadcasted_iota(jnp.int32, (ROW_TOK, HEAD), 0)
-        group = jnp.full((ROW_TOK, HEAD), shape_ref[r, RQ], jnp.int32)
+        group = jnp.full((ROW_TOK, HEAD), shape[at, RQ], jnp.int32)
         start = 0
         for j in range(1, RQ):
-            start = start + shape_ref[r, j - 1]
-            group = jnp.where(token >= start, shape_ref[r, RQ + j], group)
+            start = start + shape[at, j - 1]
+            group = jnp.where(token >= start, shape[at, RQ + j], group)
         grp[r * ROW_TOK : (r + 1) * ROW_TOK, :] = group
-    count = build_work(shape_ref, rows, item_group, item_block)
+    count = build_work(shapes, item_group, item_block)
     for copy in copies:
         copy.wait()
     step = 512
@@ -477,8 +459,8 @@
         ]
 
 
-def prefix_attend(core, shape, q0, q1, pk, pk_other, pv, pv_other, out_dtype):
-    rows = shape.shape[0]
+def prefix_attend(place, far, shape_a, shape_b, q0, q1, pk, pv, other, out_dtype):
+    rows = 2
     tokens = rows * ROW_TOK
     span = pk.shape[1]
     blocks = ROW_TOK // BLK
@@ -490,8 +472,8 @@
     scores = pltpu.VMEM((PER_ITEM * SUB, 2 * span), jnp.float32)
     tops = pltpu.VMEM((PER_ITEM * SUB, HEAD), jnp.float32)
     return pl.pallas_call(
-        prefix_kernel,
-        in_specs=[smem, smem] + [anywhere] * 6,
+        functools.partial(prefix_kernel, far),
+        in_specs=[smem] * 3 + [anywhere] * 5,
         out_specs=(vmem, vmem),
         out_shape=(
             jax.ShapeDtypeStruct((tokens, HEAD), out_dtype),
@@ -520,17 +502,18 @@
             transcendentals=0,
         ),
         name="prefix_attend",
-    )(core, shape, q0, q1, pk, pk_other, pv, pv_other)
-
-
-def suffix_kernel(shape_ref, row0, row1, o_ref, lse_ref):
+    )(place, shape_a, shape_b, q0, q1, pk, pv, other)
+
+
+def suffix_kernel(sc_ref, shape_a, shape_b, q, k, v, other_row, o_ref, lse_ref):
     count = ROW_TOK // SUF
-    for row, qkv in enumerate((row0, row1)):
+    rows = ((shape_a, (q, k, v)), (shape_b, [other_row.at[i] for i in range(3)]))
+    for row, (shape, qkv) in enumerate(rows):
         token = lax.broadcasted_iota(jnp.int32, (ROW_TOK, 1), 0)
         first = jnp.zeros((ROW_TOK, 1), jnp.int32)
         start = 0
         for j in range(1, RQ):
-            start = start + shape_ref[row, j - 1]
+            start = start + shape[0, j - 1]
             first = jnp.where(token >= start, start, first)
 
         def bounds(i):
@@ -540,8 +523,8 @@
         def score(i, qkv=qkv, first=first, token=token):
             low, here, seen = bounds(i)
             s = lax.dot_general(
-                qkv[0, here, :],
-                qkv[1, seen, :],
+                qkv[0][here, :],
+                qkv[1][seen, :],
                 (((1,), (1,)), ((), ())),
                 preferred_element_type=jnp.float32,
             )
@@ -554,7 +537,7 @@
             p = jnp.exp2((s - top) * SCORE_SCALE)
             total = jnp.sum(p, axis=1, keepdims=True)
             out = jnp.dot(
-                p.astype(jnp.bfloat16), qkv[2, seen, :], preferred_element_type=jnp.float32
+                p.astype(jnp.bfloat16), qkv[2][seen, :], preferred_element_type=jnp.float32
             )
             o_ref[row * ROW_TOK + i * SUF : row * ROW_TOK + (i + 1) * SUF, :] = out * (1.0 / total)
             lse = top * SCORE_SCALE + jnp.log2(total)
@@ -569,32 +552,44 @@
             held = later
 
 
-def suffix_attend(shape, row0, row1):
-    rows, tokens = shape.shape[0], row0.shape[1]
+def suffix_attend(place, shape_a, shape_b, q, k, v, other):
+    rows, tokens = 2, q.shape[0]
+    blocks = tokens // BLK
     smem = pl.BlockSpec(memory_space=pltpu.SMEM)
-    vmem = pl.BlockSpec(memory_space=pltpu.VMEM)
+    mine = pl.BlockSpec((tokens, HEAD), lambda i, s: (0, s[0]))
     return pl.pallas_call(
         suffix_kernel,
-        in_specs=[smem, vmem, vmem],
-        out_specs=(vmem, vmem),
+        grid_spec=pltpu.PrefetchScalarGridSpec(
+            num_scalar_prefetch=1,
+            grid=(1,),
+            in_specs=[smem, smem]
+            + [mine] * 3
+            + [pl.BlockSpec((3, tokens, HEAD), lambda i, s: (0, 0, 0))],
+            out_specs=[
+                pl.BlockSpec((rows * tokens, HEAD), lambda i, s: (0, 0)),
+                pl.BlockSpec((rows, blocks, BLK), lambda i, s: (0, 0, 0)),
+            ],
+        ),
         out_shape=(
             jax.ShapeDtypeStruct((rows * tokens, HEAD), jnp.float32),
-            jax.ShapeDtypeStruct((rows, tokens // BLK, BLK), jnp.float32),
+            jax.ShapeDtypeStruct((rows, blocks, BLK), jnp.float32),
         ),
         compiler_params=pltpu.CompilerParams(vmem_limit_bytes=VMEM_BIG),
         cost_estimate=pl.CostEstimate(
             flops=rows * tokens * tokens * HEAD * 4 * 4, bytes_accessed=1 << 20, transcendentals=0
         ),
         name="suffix_attend",
-    )(shape, row0, row1)
+    )(place, shape_a, shape_b, q, k, v, other)
 
 
 MERGE_BLOCKS = 4
 
 
 def merge_kernel(*refs):
-    parts, out_ref = refs[:-1], refs[-1]
+    parts, tab_ref, out_ref = refs[:-2], refs[-2], refs[-1]
     step = pl.program_id(0)
+    for block in range(MERGE_BLOCKS):
+        out_ref[block, 2 * BLK :, :] = tab_ref[...]
     half = len(parts) // 2
     for row in range(2):
         sources = parts[row * half : (row + 1) * half]
@@ -615,7 +610,8 @@
             out_ref[block, row * BLK : (row + 1) * BLK, :] = (summed / total).astype(out_ref.dtype)
 
 
-def merge_parts(parts):
+def merge_parts(parts, tab):
+    extra = tab.shape[0]
     blocks = ROW_TOK // BLK
     steps = blocks // MERGE_BLOCKS
     specs, operands = [], []
@@ -629,18 +625,18 @@
     return pl.pallas_call(
         merge_kernel,
         grid=(steps,),
-        in_specs=specs,
-        out_specs=pl.BlockSpec((MERGE_BLOCKS, 2 * BLK, HEAD), lambda b: (b, 0, 0)),
-        out_shape=jax.ShapeDtypeStruct((blocks, 2 * BLK, HEAD), jnp.bfloat16),
+        in_specs=specs + [pl.BlockSpec((extra, BLK), lambda b: (0, 0))],
+        out_specs=pl.BlockSpec((MERGE_BLOCKS, 2 * BLK + extra, HEAD), lambda b: (b, 0, 0)),
+        out_shape=jax.ShapeDtypeStruct((blocks, 2 * BLK + extra, HEAD), jnp.bfloat16),
         name="merge_parts",
-    )(*operands)
+    )(*operands, tab)
 
 
 def project_kernel(a_ref, w_ref, keep_ref, send_ref, lhs):
     @pl.when(pl.program_id(0) == 0)
     def first():
         for h in range(a_ref.shape[0]):
-            lhs[:, h * HEAD : (h + 1) * HEAD] = a_ref[h]
+            lhs[:, h * HEAD : (h + 1) * HEAD] = a_ref[h, : 2 * BLK, :]
 
     out = jnp.dot(lhs[...], w_ref[...], preferred_element_type=jnp.float32)
     rows = keep_ref.shape[0]
@@ -649,7 +645,8 @@
 
 
 def project(attended, weights):
-    heads, tokens, unused = attended.shape
+    heads, held, unused = attended.shape
+    tokens = 2 * BLK
     depth, width = weights.shape
     rows, tile = tokens // 2, 1024
     out_spec = pl.BlockSpec((rows, tile), lambda i: (0, i))
@@ -657,7 +654,7 @@
         project_kernel,
         grid=(width // tile,),
         in_specs=[
-            pl.BlockSpec((heads, tokens, HEAD), lambda i: (0, 0, 0)),
+            pl.BlockSpec((heads, held, HEAD), lambda i: (0, 0, 0)),
             pl.BlockSpec((depth, tile), lambda i: (0, i)),
         ],
         out_specs=[out_spec, out_spec],
@@ -692,6 +689,7 @@
 
 EXP_DEV = 4
 SLOTS = 32
+SLOTS_XOR = (0, 2, 4, 6, 1, 3, 5, 7)
 
 
 def route_kernel(sc_ref, tab_ref, pick_ref, give_ref):
@@ -700,12 +698,13 @@
         < lax.broadcasted_iota(jnp.int32, (BLK, BLK), 1)
     ).astype(jnp.bfloat16)
     place = lax.broadcasted_iota(jnp.int32, (SLOTS, BLK), 0).astype(jnp.float32)
-    for slot in range(8):
-        tab = tab_ref[sc_ref[slot]].astype(jnp.float32)
-        ids, gates = tab[:TOPK], tab[TOPK:]
+    place_here = sc_ref[1]
+    for slot, offset in enumerate(SLOTS_XOR):
+        tab = tab_ref[place_here ^ offset].astype(jnp.float32)
+        ids, gates = tab[:TOPK], tab[TOPK : 2 * TOPK]
         chosen, weights = [], []
         for j in range(EXP_DEV):
-            match = ids == (sc_ref[8] + j).astype(jnp.float32)
+            match = ids == (place_here * EXP_DEV + j).astype(jnp.float32)
             chosen.append(jnp.sum(match.astype(jnp.float32), axis=0, keepdims=True))
             weights.append(jnp.sum(jnp.where(match, gates, 0.0), axis=0, keepdims=True))
         held = jnp.concatenate(chosen + chosen, axis=0)
@@ -721,23 +720,26 @@
         give_ref[slot] = jnp.transpose(spread).astype(jnp.bfloat16)
 
 
-def route(scalars, tab):
+def route(place, heads):
+    extra = heads.shape[1] - 2 * BLK
     shape = jax.ShapeDtypeStruct((8, BLK, EXP_DEV * SLOTS), jnp.bfloat16)
     return pl.pallas_call(
         route_kernel,
+        grid=(1,),
         in_specs=[
             pl.BlockSpec(memory_space=pltpu.SMEM),
-            pl.BlockSpec(memory_space=pltpu.VMEM),
+            pl.BlockSpec((8, extra, BLK), lambda i: (0, 2 * BLK // extra, 0)),
         ],
+        out_specs=[pl.BlockSpec((8, BLK, BLK), lambda i: (0, 0, 0))] * 2,
         out_shape=(shape, shape),
         name="route",
-    )(scalars, tab)
+    )(place, heads)
 
 
 def experts_kernel(*refs):
     picked = refs[:8]
     give_ref, wg, wu, wd = refs[8:12]
-    outs, rows_out = refs[12:21], refs[21]
+    outs, rows_out = refs[12:-1], refs[-1]
     expert = pl.program_id(0)
     rows = jnp.concatenate([part[...] for part in picked], axis=0)
     contract = (((1,), (1,)), ((), ()))
@@ -754,18 +756,19 @@
         for slot in range(8):
             out = jnp.dot(give_ref[slot], rows_out[slot], preferred_element_type=jnp.float32)
             out = out.astype(jnp.bfloat16)
-            if slot < 7:
-                outs[slot][...] = out
+            at = slot + slot // 4
+            if slot % 4 < 3:
+                outs[at][...] = out
             else:
-                outs[7][...] = out[: BLK // 2]
-                outs[8][...] = out[BLK // 2 :]
+                outs[at][...] = out[: BLK // 2]
+                outs[at + 1][...] = out[BLK // 2 :]
 
 
 def run_experts(picked, give, w_gate, w_up, w_down):
     width = picked[0].shape[1]
     hidden = w_down.shape[1]
     once = pl.Buffered(1)
-    heights = [BLK] * 7 + [BLK // 2] * 2
+    heights = ([BLK] * 3 + [BLK // 2] * 2) * 2
     return pl.pallas_call(
         experts_kernel,
         grid=(EXP_DEV,),
@@ -780,72 +783,33 @@
     )(*picked, give, w_gate.transpose(0, 2, 1), w_up.transpose(0, 2, 1), w_down)
 
 
-def pick_by_z(z, *choices):
-    picked = choices[-1]
-    for i in range(len(choices) - 2, -1, -1):
-        if choices[i] is not picked:
-            picked = jnp.where(z == i, choices[i], picked)
-    return picked
-
-
-SLOT_Z = ((0, 1, 2, 3), (1, 0, 3, 2), (2, 3, 0, 1), (3, 2, 1, 0))
-
-
-def together(*arrays):
-    return lax.optimization_barrier(arrays)
-
-
-def gather_rows(z, own):
+def gather_rows(own):
     half = own.shape[0] // 2
-    up, down, there0 = together(z_up(own), z_down(own), y_swap(own))
-    first = pick_by_z(z, down, up, down, up)
-    up2, down2, there1 = together(z_up(up), z_down(down), y_swap(first))
-    second = pick_by_z(z, down2, down2, up2, up2)
-    up3, down3, there2 = together(z_up(up2), z_down(down2), y_swap(second))
-    third = pick_by_z(z, down3, down, up, up3)
-    late_up = z_up(pick_by_z(z, there0, there0, there2, there2)[half:], 1, 2)
-    late_down = z_down(pick_by_z(z, there2, there2, there0, there0)[half:], 2, 1)
-    late, late_up, late_down = together(y_swap(third[:half]), late_up, late_down)
-    there3 = jnp.concatenate([late, pick_by_z(z, late_down, late_down, late_up, late_up)], axis=0)
-    return [own, first, second, third, there0, there1, there2, there3]
-
-
-def plus(*parts):
-    return sum([part.astype(jnp.float32) for part in parts[1:]], parts[0].astype(jnp.float32))
-
-
-def plus16(*parts):
-    return plus(*parts).astype(jnp.bfloat16)
-
-
-def scatter_sums(z, sums):
-    half = sums[7].shape[0]
-    got, late_up, late_down = together(
-        y_swap(sums[7]), z_up(sums[8], 0, 1), z_down(sums[8], 3, 2)
-    )
-    s3 = jnp.concatenate([plus16(sums[3][:half], got), sums[3][half:]], axis=0)
-    fourth = plus16(sums[4][half:], pick_by_z(z, late_down, late_down, late_up, late_up))
-    sixth = plus16(sums[6][half:], pick_by_z(z, late_up, late_up, late_down, late_down))
-    fourth = jnp.concatenate([sums[4][:half], fourth], axis=0)
-    sixth = jnp.concatenate([sums[6][:half], sixth], axis=0)
-    got, up, down = together(y_swap(sixth), z_up(s3, 0, 0), z_down(s3, 3, 3))
-    s2 = plus16(sums[2], got)
-    got, up, down = together(
-        y_swap(sums[5]),
-        z_up(pick_by_z(z, s2, plus16(s2, up), s2, s2), 0, 1),
-        z_down(pick_by_z(z, s2, s2, plus16(s2, down), s2), 3, 2),
-    )
-    s1 = plus16(sums[1], got)
-    got, up, down = together(
-        y_swap(fourth),
-        z_up(pick_by_z(z, s1, plus16(s3, up), plus16(s1, up), s1)),
-        z_down(pick_by_z(z, s1, plus16(s1, down), plus16(s3, down), s1)),
-    )
-    return plus(sums[0], got, up, down)
-
-
-def tabled(values, index):
-    return jnp.asarray(values, jnp.int32)[index]
+    there = [y_swap(own)]
+    near = [z_swap(own, 1), z_swap(own, 2), z_swap(own[:half], 3), z_swap(own[half:], 3)]
+    there += [y_swap(part) for part in near]
+    return [own] + near, there
+
+
+def pick_rows(pick, parts):
+    half = parts[3].shape[0]
+    picked = [jnp.dot(pick[i], parts[i], preferred_element_type=jnp.float32) for i in range(3)]
+    picked.append(
+        jnp.dot(pick[3][:, :half], parts[3], preferred_element_type=jnp.float32)
+        + jnp.dot(pick[3][:, half:], parts[4], preferred_element_type=jnp.float32)
+    )
+    return [part.astype(jnp.bfloat16) for part in picked]
+
+
+def scatter_sums(stream, own, there):
+    def plus(a, b):
+        return (a.astype(jnp.float32) + b.astype(jnp.float32)).astype(jnp.bfloat16)
+
+    last = [z_swap(plus(own[i], y_swap(there[i])), 3) for i in (3, 4)]
+    total = stream + jnp.concatenate(last, axis=0).astype(jnp.float32)
+    for i in (2, 1):
+        total = total + z_swap(plus(own[i], y_swap(there[i])), i).astype(jnp.float32)
+    return total + own[0].astype(jnp.float32) + y_swap(there[0]).astype(jnp.float32)
 
 
 def block_device(
@@ -865,60 +829,42 @@
     w_up,
     w_down,
 ):
-    row_tok = queries.shape[0]
     core = lax.rem(lax.axis_index("req"), 2)
-    place = lax.axis_index("exp")
-    z = place // 2
-    core_arg = core.astype(jnp.int32).reshape(1)
-
-    mine, theirs = split_tokens(core_arg, queries, keys, values)
-    q_far0 = x_swap(mine[0])
-    other = core_swap(theirs)
-
+    place = jnp.stack([core, lax.axis_index("exp")]).astype(jnp.int32)
+
+    far_queries = x_swap(queries)
     shape = jnp.concatenate([lengths, groups], axis=1)
-    near_shape = jnp.concatenate([shape, core_swap(shape)], axis=0)
-    far_shape = x_swap(near_shape)
-
-    pk_theirs, pv_theirs = split_prefix(core_arg, prefix_keys, prefix_values)
-    pk_other, pv_other = core_swap(pk_theirs), core_swap(pv_theirs)
-    q_far1 = x_swap(other[0])
+    far_shape = x_swap(shape)
+    other_shapes = core_swap(jnp.concatenate([shape, far_shape], axis=0))
 
     proj_rows = lax.dynamic_slice_in_dim(out_proj, core * HEAD, HEAD, 0)
     proj_rows = lax.all_gather(proj_rows, "exp", axis=0, tiled=True)
 
-    tab = jnp.concatenate([expert_ids.T.astype(jnp.bfloat16), expert_gates.T], axis=0)[None]
-    for step in (1, 2, 4):
-        tab = jnp.concatenate(
-            [tab, lax.ppermute(tab, "exp", [(i, i ^ step) for i in range(8)])], axis=0
+    theirs, prefix_theirs = split_theirs(place, queries, keys, values, prefix_keys, prefix_values)
+    other, prefix_other = core_swap(theirs), core_swap(prefix_theirs)
+    far_other = core_swap(jnp.where(core == 0, far_queries[:, HEAD:], far_queries[:, :HEAD]))
+
+    def prefix(far, shape_a, q0, q1, dtype):
+        return prefix_attend(
+            place, far, shape_a, other_shapes, q0, q1, prefix_keys, prefix_values, prefix_other, dtype
         )
-    slot_z = tabled(SLOT_Z, z)
-    slot_place = jnp.concatenate(
-        [slot_z * 2 + lax.rem(place, 2), slot_z * 2 + 1 - lax.rem(place, 2)]
-    )
-    scalars = jnp.concatenate([slot_place ^ place, (place * EXP_DEV).reshape(1)])
-    pick, give = route(scalars.astype(jnp.int32), tab)
-
-    def prefix(shape, q0, q1, dtype):
-        return prefix_attend(
-            core_arg, shape, q0, q1, prefix_keys, pk_other, prefix_values, pv_other, dtype
-        )
-
-    suffix = suffix_attend(near_shape, mine, other)
-    far = prefix(far_shape, q_far0, q_far1, jnp.bfloat16)
+
+    tab = jnp.concatenate([expert_ids.T.astype(jnp.bfloat16), expert_gates.T], axis=0)
+    tab = jnp.pad(tab, ((0, 16 - tab.shape[0]), (0, 0)))
+    suffix = suffix_attend(place, shape, other_shapes, queries, keys, values, other)
+    far = prefix(1, far_shape, far_queries, far_other, jnp.bfloat16)
     back = (x_swap(far[0]), x_swap(far[1]))
-    near = prefix(near_shape, mine[0], other[0], jnp.float32)
-    near_o, pick, give, gain = together(near[0], pick, give, norm_gain.reshape(1, -1))
-    attended = merge_parts([suffix, (near_o, near[1]), back])
+    near = prefix(0, shape, queries, other[0], jnp.float32)
+    near_o, gain = lax.optimization_barrier((near[0], norm_gain.reshape(1, -1)))
+    attended = merge_parts([suffix, (near_o, near[1]), back], tab)
     heads = lax.all_to_all(attended, "exp", split_axis=0, concat_axis=0, tiled=True)
     keep, send = project(heads, proj_rows)
     stream, normed = norm_rows(keep, core_swap(send), residual, gain)
-    rows = gather_rows(z, normed)
-    picked = [
-        jnp.dot(pick[i], part, preferred_element_type=jnp.float32).astype(jnp.bfloat16)
-        for i, part in enumerate(rows)
-    ]
+    pick, give = route(place, heads)
+    here, there = gather_rows(normed)
+    picked = pick_rows(pick[:4], here) + pick_rows(pick[4:], there)
     sums = run_experts(picked, give, w_gate, w_up, w_down)
-    return (stream + scatter_sums(z, sums)).astype(jnp.bfloat16)
+    return scatter_sums(stream, sums[:5], sums[5:]).astype(jnp.bfloat16)
 
 
 def solution(mesh):

time: 268 us -> 270 us (level)
  waiting for transfers between devices: 69.3 us -> 110 us
  starting transfers between devices: 61.4 us -> 23.9 us
  blocking collectives: 16.3 us -> 22 us
  other arithmetic: 11.9 us -> 7.16 us
    ppermute x19 -> x8, starting transfers between devices: 48 us -> 8.98 us  [z_swap(): return lax.ppermute(array, 'exp', [(i, i ^ 2 * distance) for i in range(8)])]
    ppermute x8 -> x10, waiting for transfers between devices: 7.01 us -> 45.7 us  [y_swap(): return lax.ppermute(array, 'exp', [(i, i ^ 1) for i in range(8)])]
    ppermute x5 -> x4, waiting for transfers between devices: 0.01 us -> 10.8 us  [x_swap(): return lax.ppermute(array, 'req', [(i, i ^ 2) for i in range(4)])]
    ppermute x19 -> x8, waiting for transfers between devices: 60.1 us -> 52.6 us  [z_swap(): return lax.ppermute(array, 'exp', [(i, i ^ 2 * distance) for i in range(8)])]
    all_to_all x1, blocking collectives: 16.3 us -> 22 us  [block_device(): lax.all_to_all(attended, 'exp', split_axis=0, concat_axis=0, tiled=True)]
    select_n x7 -> x1, other arithmetic: 3.41 us -> 0.04 us  [block_device(): jnp.where(core == 0, far_queries[:, HEAD:], far_queries[:, :HEAD])]
    convert_element_type x3 -> x5, other arithmetic: 3.43 us -> 5.71 us  [the longest x4 4.45 us: plus(): return (a.astype(jnp.float32) + b.astype(jnp.float32)).astype(jnp.bfloat16)]
    ppermute x8 -> x10, starting transfers between devices: 6.66 us -> 8.81 us  [y_swap(): return lax.ppermute(array, 'exp', [(i, i ^ 1) for i in range(8)])]
  transfers between devices with their start and end apart: 38 -> 28, of which waited for: 19 -> 13; matrix products, arithmetic and copies ran while one was open for 9% -> 7% of each run, Pallas kernels for 17% -> 17%
where the time goes in v4:
time: 270 us; the launch traced here: 269 us
  waiting for transfers between devices  110 us (41%)
  Pallas kernels  72.3 us (27%)
  starting transfers between devices  23.9 us (9%)
  blocking collectives  22 us (8%)
  between operations  13.6 us (5%)
  matrix products  10.4 us (4%)
  local copies, waits for them, and re-layouts  9.87 us (4%)
  other arithmetic  7.16 us (3%)
    ppermute x8, waiting for transfers between devices, z_swap(): return lax.ppermute(array, 'exp', [(i, i ^ 2 * distance) for i in range(8)])  52.6 us
    ppermute x10, waiting for transfers between devices, y_swap(): return lax.ppermute(array, 'exp', [(i, i ^ 1) for i in range(8)])  45.7 us
    pallas_call x2, Pallas kernels, prefix_attend(): pl.pallas_call(functools.partial(prefix_kernel, far), in_specs=[smem] * 3...  29.4 us
    all_to_all x1, blocking collectives, block_device(): lax.all_to_all(attended, 'exp', split_axis=0, concat_axis=0, tiled=True)  22 us
    pallas_call x1, Pallas kernels, run_experts(): pl.pallas_call(experts_kernel, grid=(EXP_DEV,), in_specs=[pl.BlockSpec((S...  20.3 us
    ppermute x4, waiting for transfers between devices, x_swap(): return lax.ppermute(array, 'req', [(i, i ^ 2) for i in range(4)])  10.8 us
    ppermute x8, starting transfers between devices, z_swap(): return lax.ppermute(array, 'exp', [(i, i ^ 2 * distance) for i in range(8)])  8.98 us
    ppermute x10, starting transfers between devices, y_swap(): return lax.ppermute(array, 'exp', [(i, i ^ 1) for i in range(8)])  8.81 us
  transfers between devices with their start and end apart: 28, of which 13 were waited for; matrix products, arithmetic and copies ran while one was open for 7% of the time, Pallas kernels for 17%

profile of v4, /device:TPU:0, one launch (start us, length us, event | category | flops | bytes accessed | tf_op | source)
XLA Modules:
  0.0 269.4 jit_solution(13181648125734945521)
XLA Ops:
  6.6 1.1 copy-done
  7.8 0.8 constant_dynamic-slice_fusion
  8.6 0.7 pad_add_fusion.1.sc_ref
  9.3 4.8 %split_theirs.1 = (bf16[3,1024,128]{2,1,0:T(8,128)(2,1)}, bf16[2,4,1024,128]{3,2,1,0:T(8,128)(2,1)}) custom-call(s32[2]{0:T(128)} %pad_add_fusion.1.sc_ref, bf16[1024,256]{1,0:T(8,128)(2,1)} %q0.1, bf16[1024,256]{1,0:T(8,128)(2,1)} %k.3, bf16[1024,256]{1,0:T(8,128)(2,1)} %v.3, bf16[4,1024,256]{2,1,0:T(8,128)(2,1)} %pk.5, bf16[4,1024,256]{2,1,0:T(8,128)(2,1)} %pv.5), custom_call_target="tpu_custom_call" | custom-call | tf_op jit(solution)/shard_map/split_theirs/pallas_call | solution.py:281
  14.6 2.6 collective-permute-start.4
  17.7 0.6 fusion.22.refs_12_
  18.3 0.6 reshape.3.gain
  18.9 10.8 %collective-permute-done.shape_a = s32[1,16]{1,0:T(1,128)S(1)} collective-permute-done((s32[1,16]{1,0:T(1,128)S(1)}, s32[1,16]{1,0:T(1,128)S(1)}, u32[]{:S(2)}, u32[]{:S(2)}) %collective-permute-start) | collective-permute-done | bytes 96 | tf_op jit(solution)/shard_map/ppermute | solution.py:258
  31.0 0.6 copy-done.18
  31.5 0.9 copy-done.9
  32.4 5.8 %suffix_attend.1 = (f32[2048,128]{1,0:T(8,128)}, f32[2,8,128]{2,1,0:T(8,128)}) custom-call(s32[2]{0:T(128)} %pad_add_fusion.1.sc_ref, s32[1,16]{1,0:T(1,128)} %copy-done.19, s32[2,16]{1,0:T(2,128)} %copy-done.18, bf16[1024,256]{1,0:T(8,128)(2,1)} %q0.1, bf16[1024,256]{1,0:T(8,128)(2,1)} %k.3, bf16[1024,256]{1,0:T(8,128)(2,1)} %v.3, ...), custom_call_target="tpu_custom_call" | custom-call | flops 4294967296 | bytes 1048576 | tf_op jit(solution)/shard_map/suffix_attend/pallas_call | solution.py:560
  38.3 1.7 slice_bitcast_fusion.q1
  39.9 0.7 copy-done.17
  40.6 14.7 %prefix_attend.3 = (bf16[2048,128]{1,0:T(8,128)(2,1)}, f32[2,8,128]{2,1,0:T(8,128)}) custom-call(s32[2]{0:T(128)} %pad_add_fusion.1.sc_ref, s32[1,16]{1,0:T(1,128)} %copy-done.16, s32[2,16]{1,0:T(2,128)} %copy-done.18, bf16[1024,256]{1,0:T(8,128)(2,1)} %copy-done.5, bf16[1024,128]{1,0:T(8,128)(2,1)} %copy-done.17, bf16[4,1024,256]{2,1,0:T(8,128)(2,1)} %pk.5, ...), custom_call_target="tpu_custom_call" | custom-call | flops 8589934592 | bytes 4194304 | tf_op jit(solution)/shard_map/prefix_attend/pallas_call | solution.py:474
  55.3 1.8 collective-permute-start.6
  57.4 14.8 %prefix_attend.2 = (f32[2048,128]{1,0:T(8,128)}, f32[2,8,128]{2,1,0:T(8,128)}) custom-call(s32[2]{0:T(128)} %pad_add_fusion.1.sc_ref, s32[1,16]{1,0:T(1,128)} %copy-done.19, s32[2,16]{1,0:T(2,128)} %copy-done.18, bf16[1024,256]{1,0:T(8,128)(2,1)} %q0.1, bf16[1024,128]{1,0:T(8,128)(2,1)} %slice_bitcast_fusion.q1, bf16[4,1024,256]{2,1,0:T(8,128)(2,1)} %pk.5, ...), custom_call_target="tpu_custom_call" | custom-call | flops 8589934592 | bytes 4194304 | tf_op jit(solution)/shard_map/prefix_attend/pallas_call | solution.py:474
  72.2 0.6 copy-done.10
  73.0 3.1 %merge_parts.1 = bf16[8,272,128]{2,1,0:T(8,128)(2,1)} custom-call(f32[2048,128]{1,0:T(8,128)} %get-tuple-element.32.refs_0_.refs_6_, f32[2,8,128]{2,1,0:T(8,128)} %get-tuple-element.33.refs_1_.refs_7_, f32[2048,128]{1,0:T(8,128)} %get-tuple-element.36.refs_2_.refs_8_, f32[2,8,128]{2,1,0:T(8,128)} %get-tuple-element.37.refs_3_.refs_9_, ...), custom_call_target="tpu_custom_call" | custom-call | tf_op jit(solution)/shard_map/merge_parts/pallas_call | solution.py:625
  76.1 22.0 %all_to_all.5.a_ref.tab_ref = bf16[8,272,128]{2,1,0:T(8,128)(2,1)} all-to-all(bf16[8,272,128]{2,1,0:T(8,128)(2,1)} %merge_parts.1), channel_id=1, replica_groups=mesh['req'=4,'exp'=8] {'exp'}, dimensions={0} | all-to-all | bytes 1114112 | tf_op jit(solution)/shard_map/all_to_all | solution.py:860
  98.1 4.1 %project.1 = (f32[128,2048]{1,0:T(8,128)}, bf16[128,2048]{1,0:T(8,128)(2,1)}) custom-call(bf16[8,272,128]{2,1,0:T(8,128)(2,1)} %all_to_all.5.a_ref.tab_ref, bf16[1024,2048]{1,0:T(8,128)(2,1)} %all-gather.2.cloned.1.call-done.w_ref), custom_call_target="tpu_custom_call" | custom-call | tf_op jit(solution)/shard_map/project/pallas_call | solution.py:653
  102.2 1.8 route.1
  104.4 0.8 copy-done.6
  105.2 2.9 %norm_rows.1 = (f32[128,2048]{1,0:T(8,128)}, bf16[128,2048]{1,0:T(8,128)(2,1)}) custom-call(f32[128,2048]{1,0:T(8,128)} %get-tuple-element.40.keep, bf16[128,2048]{1,0:T(8,128)(2,1)} %copy-done.6, bf16[128,2048]{1,0:T(8,128)(2,1)} %residual.1, bf16[1,2048]{1,0:T(2,128)(2,1)} %reshape.3.gain), custom_call_target="tpu_custom_call" | custom-call | tf_op jit(solution)/shard_map/norm_rows/pallas_call | solution.py:680
  108.1 1.1 fusion.23
  109.1 1.5 collective-permute-start.12
  110.6 2.4 collective-permute-start.11
  113.0 0.8 slice_bitcast_fusion.1
  113.8 2.0 collective-permute-start.9
  115.8 0.7 collective-permute-start.13
  116.5 2.2 convolution_convert_fusion.5.refs_0_
  118.6 1.7 collective-permute-done.12
  120.3 0.7 collective-permute-start.17
  121.1 4.8 %collective-permute-done.11 = bf16[64,2048]{1,0:T(8,128)(2,1)S(1)} collective-permute-done((bf16[64,2048]{1,0:T(8,128)(2,1)S(1)}, bf16[64,2048]{1,0:T(8,128)(2,1)S(1)}, u32[]{:S(2)}, u32[]{:S(2)}) %collective-permute-start.11) | collective-permute-done | bytes 262176 | tf_op jit(solution)/shard_map/ppermute | solution.py:266
  125.9 0.7 collective-permute-start.16
  127.0 1.1 fusion.refs_3_
  128.0 29.0 %collective-permute-done.10 = bf16[128,2048]{1,0:T(8,128)(2,1)S(1)} collective-permute-done((bf16[128,2048]{1,0:T(8,128)(2,1)}, bf16[128,2048]{1,0:T(8,128)(2,1)S(1)}, u32[]{:S(2)}, u32[]{:S(2)}) %collective-permute-start.10) | collective-permute-done | bytes 524320 | tf_op jit(solution)/shard_map/ppermute | solution.py:266
  157.0 0.5 collective-permute-start.15
  157.5 1.1 convolution_convert_fusion.3.refs_2_
  158.6 1.5 collective-permute-start.14
  160.5 1.1 convolution_convert_fusion.4.refs_1_
  161.6 1.1 convolution_convert_fusion.2.refs_4_
  162.6 1.1 fusion.1.refs_7_
  163.7 8.1 %collective-permute-done.15 = bf16[128,2048]{1,0:T(8,128)(2,1)S(1)} collective-permute-done((bf16[128,2048]{1,0:T(8,128)(2,1)S(1)}, bf16[128,2048]{1,0:T(8,128)(2,1)S(1)}, u32[]{:S(2)}, u32[]{:S(2)}) %collective-permute-start.15) | collective-permute-done | bytes 524320 | tf_op jit(solution)/shard_map/ppermute | solution.py:262
  171.9 1.1 convolution_convert_fusion.refs_6_
  173.0 8.5 %collective-permute-done.14 = bf16[128,2048]{1,0:T(8,128)(2,1)S(1)} collective-permute-done((bf16[128,2048]{1,0:T(8,128)(2,1)S(1)}, bf16[128,2048]{1,0:T(8,128)(2,1)S(1)}, u32[]{:S(2)}, u32[]{:S(2)}) %collective-permute-start.14) | collective-permute-done | bytes 524320 | tf_op jit(solution)/shard_map/ppermute | solution.py:262
  181.4 1.1 convolution_convert_fusion.1.refs_5_
  182.5 20.3 %experts.1 = (bf16[128,2048]{1,0:T(8,128)(2,1)}, bf16[128,2048]{1,0:T(8,128)(2,1)}, bf16[128,2048]{1,0:T(8,128)(2,1)}, bf16[64,2048]{1,0:T(8,128)(2,1)}, bf16[64...) custom-call(bf16[128,2048]{1,0:T(8,128)(2,1)} %convolution_convert_f, ...), custom_call_target="tpu_custom_call" | custom-call | tf_op jit(solution)/shard_map/experts/pallas_call | solution.py:772
  202.8 0.6 collective-permute-start.18
  203.4 1.5 collective-permute-start.22
  204.9 0.5 collective-permute-start.20
  205.5 1.5 collective-permute-start.24
  206.9 0.5 collective-permute-start.26
  207.5 4.9 %collective-permute-done.18 = bf16[64,2048]{1,0:T(8,128)(2,1)S(1)} collective-permute-done((bf16[64,2048]{1,0:T(8,128)(2,1)}, bf16[64,2048]{1,0:T(8,128)(2,1)S(1)}, u32[]{:S(2)}, u32[]{:S(2)}) %collective-permute-start.18) | collective-permute-done | bytes 262176 | tf_op jit(solution)/shard_map/ppermute | solution.py:262
  212.4 1.1 add_convert_fusion.4
  213.5 1.5 collective-permute-start.19
  214.9 8.6 %collective-permute-done.22 = bf16[128,2048]{1,0:T(8,128)(2,1)S(1)} collective-permute-done((bf16[128,2048]{1,0:T(8,128)(2,1)}, bf16[128,2048]{1,0:T(8,128)(2,1)S(1)}, u32[]{:S(2)}, u32[]{:S(2)}) %collective-permute-start.22) | collective-permute-done | bytes 524320 | tf_op jit(solution)/shard_map/ppermute | solution.py:262
  223.6 1.2 add_convert_fusion.2
  224.8 15.6 %collective-permute-done.24 = bf16[128,2048]{1,0:T(8,128)(2,1)S(1)} collective-permute-done((bf16[128,2048]{1,0:T(8,128)(2,1)}, bf16[128,2048]{1,0:T(8,128)(2,1)S(1)}, u32[]{:S(2)}, u32[]{:S(2)}) %collective-permute-start.24) | collective-permute-done | bytes 524320 | tf_op jit(solution)/shard_map/ppermute | solution.py:262
  240.4 1.2 add_convert_fusion.1
  241.7 1.0 add_convert_fusion.3
  242.7 1.5 collective-permute-start.21
  244.2 11.6 %collective-permute-done.21 = bf16[64,2048]{1,0:T(8,128)(2,1)S(1)} collective-permute-done((bf16[64,2048]{1,0:T(8,128)(2,1)S(1)}, bf16[64,2048]{1,0:T(8,128)(2,1)S(1)}, u32[]{:S(2)}, u32[]{:S(2)}) %collective-permute-start.21) | collective-permute-done | bytes 262176 | tf_op jit(solution)/shard_map/ppermute | solution.py:266
  255.8 5.5 %collective-permute-done.25 = bf16[128,2048]{1,0:T(8,128)(2,1)S(1)} collective-permute-done((bf16[128,2048]{1,0:T(8,128)(2,1)S(1)}, bf16[128,2048]{1,0:T(8,128)(2,1)S(1)}, u32[]{:S(2)}, u32[]{:S(2)}) %collective-permute-start.25) | collective-permute-done | bytes 524320 | tf_op jit(solution)/shard_map/ppermute | solution.py:266
  261.3 1.3 add_convert_fusion
  (69 shorter events, 4.0 us)
Async XLA Ops:
  6.5 1.2 copy-start
  6.5 8.0 %copy-start.4 = (bf16[1024,256]{1,0:T(8,128)(2,1)S(1)}, bf16[1024,256]{1,0:T(8,128)(2,1)}, u32[]{:S(2)}) copy-start(bf16[1024,256]{1,0:T(8,128)(2,1)} %q0.1) | copy-start | bytes 1572868
  6.5 10.8 %copy-start.15 = (s32[1,8]{1,0:T(1,128)S(1)}, s32[1,8]{1,0:T(1,128)}, u32[]{:S(2)}) copy-start(s32[1,8]{1,0:T(1,128)} %param.20) | copy-start | bytes 100
  6.5 10.8 %copy-start.14 = (s32[1,8]{1,0:T(1,128)S(1)}, s32[1,8]{1,0:T(1,128)}, u32[]{:S(2)}) copy-start(s32[1,8]{1,0:T(1,128)} %param.21) | copy-start | bytes 100
  6.5 11.1 %copy-start.12 = (s32[128,4]{0,1:T(4,128)S(1)}, s32[128,4]{0,1:T(4,128)}, u32[]{:S(2)}) copy-start(s32[128,4]{0,1:T(4,128)} %param.25) | copy-start | bytes 6148
  6.5 11.1 %copy-start.13 = (bf16[128,4]{0,1:T(4,128)(2,1)S(1)}, bf16[128,4]{0,1:T(4,128)(2,1)}, u32[]{:S(2)}) copy-start(bf16[128,4]{0,1:T(4,128)(2,1)} %param.26) | copy-start | bytes 3076
  6.6 11.7 %copy-start.11 = (bf16[2048]{0:T(1024)(128)(2,1)S(1)}, bf16[2048]{0:T(1024)(128)(2,1)}, u32[]{:S(2)}) copy-start(bf16[2048]{0:T(1024)(128)(2,1)} %param.24) | copy-start | bytes 12292
  6.6 91.6 %all-gather.2.cloned.1.call-start = ((), (), s32[]{:S(2)}) async-start(), calls=%async_computation.1 | async-start | bytes 4718592 | tf_op jit(solution)/shard_map/all_gather | solution.py:841
  14.1 25.8 %collective-permute-start.3 = (bf16[2,4,1024,128]{3,2,1,0:T(8,128)(2,1)}, bf16[2,4,1024,128]{3,2,1,0:T(8,128)(2,1)}, u32[]{:S(2)}, u32[]{:S(2)}) collective-permute-start(bf16[2,4,1024,128]{3,2,1,0:T(8,128)(2,1)} %get-tuple-element.34), channel_id=1, source_target_pairs={{0,8},{8,0},{16,24},{24,16},{1,9},{9,1},{17,25},{25,17},{2,10},{10... | collective-permute-start | bytes 6291464 | tf_op jit(solution)/shard_map/ppermute | solution.py:254
  14.6 15.2 %collective-permute-start.4 = (bf16[1024,256]{1,0:T(8,128)(2,1)S(1)}, bf16[1024,256]{1,0:T(8,128)(2,1)S(1)}, u32[]{:S(2)}, u32[]{:S(2)}) collective-permute-start(bf16[1024,256]{1,0:T(8,128)(2,1)S(1)} %copy-done.4), channel_id=1, source_target_pairs={{0,16},{8,24},{16,0},{24,8},{1,17},{9,25},{17,1},{25,9},{2,18},{10... | collective-permute-start | bytes 1572872 | tf_op jit(solution)/shard_map/ppermute | solution.py:258
  17.1 13.8 %collective-permute-start.2 = (bf16[3,1024,128]{2,1,0:T(8,128)(2,1)}, bf16[3,1024,128]{2,1,0:T(8,128)(2,1)S(1)}, u32[]{:S(2)}, u32[]{:S(2)}) collective-permute-start(bf16[3,1024,128]{2,1,0:T(8,128)(2,1)} %get-tuple-element.31), channel_id=1, source_target_pairs={{0,8},{8,0},{16,24},{24,16},{1,9},{9,1},{17,25},{25,17},{2,10},{10... | collective-permute-start | bytes 2359304 | tf_op jit(solution)/shard_map/ppermute | solution.py:254
  17.4 13.6 %copy-start.19 = (s32[1,16]{1,0:T(1,128)}, s32[1,16]{1,0:T(1,128)S(1)}, u32[]{:S(2)}) copy-start(s32[1,16]{1,0:T(1,128)S(1)} %pad_add_fusion.2.shape_a) | copy-start | bytes 196
  17.4 12.3 %collective-permute-start = (s32[1,16]{1,0:T(1,128)S(1)}, s32[1,16]{1,0:T(1,128)S(1)}, u32[]{:S(2)}, u32[]{:S(2)}) collective-permute-start(s32[1,16]{1,0:T(1,128)S(1)} %pad_add_fusion.2.shape_a), channel_id=1, source_target_pairs={{0,16},{8,24},{16,0},{24,8},{1,17},{9,25},{17,1},{25,9},{2,18},{10... | collective-permute-start | bytes 200 | tf_op jit(solution)/shard_map/ppermute | solution.py:258
  29.7 8.5 %copy-start.16 = (s32[1,16]{1,0:T(1,128)}, s32[1,16]{1,0:T(1,128)S(1)}, u32[]{:S(2)}) copy-start(s32[1,16]{1,0:T(1,128)S(1)} %collective-permute-done.shape_a) | copy-start | bytes 196
  29.8 1.1 collective-permute-start.1
  29.8 8.4 %copy-start.5 = (bf16[1024,256]{1,0:T(8,128)(2,1)}, bf16[1024,256]{1,0:T(8,128)(2,1)S(1)}, u32[]{:S(2)}) copy-start(bf16[1024,256]{1,0:T(8,128)(2,1)S(1)} %collective-permute-done.4.q0) | copy-start | bytes 1572868
  29.9 10.0 %collective-permute-start.5 = (bf16[1024,128]{1,0:T(8,128)(2,1)S(1)}, bf16[1024,128]{1,0:T(8,128)(2,1)S(1)}, u32[]{:S(2)}, u32[]{:S(2)}) collective-permute-start(bf16[1024,128]{1,0:T(8,128)(2,1)S(1)} %slice_select_fusion), channel_id=1, source_target_pairs={{0,8},{8,0},{16,24},{24,16},{1,9},{9,1},{17,25},{25,17},{2,10},{10... | collective-permute-start | bytes 786440 | tf_op jit(solution)/shard_map/ppermute | solution.py:254
  30.9 0.6 copy-start.18
  31.5 0.9 copy-start.9
  39.9 0.7 copy-start.17
  55.3 16.9 %collective-permute-start.6 = (bf16[2048,128]{1,0:T(8,128)(2,1)}, bf16[2048,128]{1,0:T(8,128)(2,1)S(1)}, u32[]{:S(2)}, u32[]{:S(2)}) collective-permute-start(bf16[2048,128]{1,0:T(8,128)(2,1)} %get-tuple-element.38), channel_id=1, source_target_pairs={{0,16},{8,24},{16,0},{24,8},{1,17},{9,25},{17,1},{25,9},{2,18},{10... | collective-permute-start | bytes 1572872 | tf_op jit(solution)/shard_map/ppermute | solution.py:258
  57.2 15.0 %collective-permute-start.7 = (f32[2,8,128]{2,1,0:T(8,128)}, f32[2,8,128]{2,1,0:T(8,128)S(1)}, u32[]{:S(2)}, u32[]{:S(2)}) collective-permute-start(f32[2,8,128]{2,1,0:T(8,128)} %get-tuple-element.39), channel_id=1, source_target_pairs={{0,16},{8,24},{16,0},{24,8},{1,17},{9,25},{17,1},{25,9},{2,18},{10... | collective-permute-start | bytes 24584 | tf_op jit(solution)/shard_map/ppermute | solution.py:258
  72.2 0.6 copy-start.10
  72.2 0.8 copy-start.2
  102.2 2.1 collective-permute-start.8
  104.0 53.5 %copy-start.8 = (bf16[8,128,128]{2,1,0:T(8,128)(2,1)S(1)}, bf16[8,128,128]{2,1,0:T(8,128)(2,1)}, u32[]{:S(2)}) copy-start(bf16[8,128,128]{2,1,0:T(8,128)(2,1)} %get-tuple-element.44) | copy-start | bytes 786436
  104.4 0.8 copy-start.6
  109.1 11.2 %collective-permute-start.12 = (bf16[64,2048]{1,0:T(8,128)(2,1)S(1)}, bf16[64,2048]{1,0:T(8,128)(2,1)S(1)}, u32[]{:S(2)}, u32[]{:S(2)}) collective-permute-start(bf16[64,2048]{1,0:T(8,128)(2,1)S(1)} %get-tuple-element.58), channel_id=1, source_target_pairs={{0,6},{1,7},{2,4},{3,5},{4,2},{5,3},{6,0},{7,1},{8,14},{9,15},{10,... | collective-permute-start | bytes 786440 | tf_op jit(solution)/shard_map/ppermute | solution.py:266
  110.6 15.3 %collective-permute-start.11 = (bf16[64,2048]{1,0:T(8,128)(2,1)S(1)}, bf16[64,2048]{1,0:T(8,128)(2,1)S(1)}, u32[]{:S(2)}, u32[]{:S(2)}) collective-permute-start(bf16[64,2048]{1,0:T(8,128)(2,1)S(1)} %get-tuple-element.57), channel_id=1, source_target_pairs={{0,6},{1,7},{2,4},{3,5},{4,2},{5,3},{6,0},{7,1},{8,14},{9,15},{10,... | collective-permute-start | bytes 786440 | tf_op jit(solution)/shard_map/ppermute | solution.py:266
  113.8 43.2 %collective-permute-start.10 = (bf16[128,2048]{1,0:T(8,128)(2,1)}, bf16[128,2048]{1,0:T(8,128)(2,1)S(1)}, u32[]{:S(2)}, u32[]{:S(2)}) collective-permute-start(bf16[128,2048]{1,0:T(8,128)(2,1)} %get-tuple-element.45), channel_id=1, source_target_pairs={{0,4},{1,5},{2,6},{3,7},{4,0},{5,1},{6,2},{7,3},{8,12},{9,13},{10,... | collective-permute-start | bytes 1572872 | tf_op jit(solution)/shard_map/ppermute | solution.py:266
  113.8 44.8 %collective-permute-start.9 = (bf16[128,2048]{1,0:T(8,128)(2,1)}, bf16[128,2048]{1,0:T(8,128)(2,1)S(1)}, u32[]{:S(2)}, u32[]{:S(2)}) collective-permute-start(bf16[128,2048]{1,0:T(8,128)(2,1)} %get-tuple-element.45), channel_id=1, source_target_pairs={{0,2},{1,3},{2,0},{3,1},{4,6},{5,7},{6,4},{7,5},{8,10},{9,11},{10,... | collective-permute-start | bytes 1572872 | tf_op jit(solution)/shard_map/ppermute | solution.py:266
  115.8 45.8 %collective-permute-start.13 = (bf16[128,2048]{1,0:T(8,128)(2,1)}, bf16[128,2048]{1,0:T(8,128)(2,1)S(1)}, u32[]{:S(2)}, u32[]{:S(2)}) collective-permute-start(bf16[128,2048]{1,0:T(8,128)(2,1)} %get-tuple-element.45), channel_id=1, source_target_pairs={{0,1},{1,0},{2,3},{3,2},{4,5},{5,4},{6,7},{7,6},{8,9},{9,8},{10,11... | collective-permute-start | bytes 1572872 | tf_op jit(solution)/shard_map/ppermute | solution.py:262
  120.3 39.8 %collective-permute-start.17 = (bf16[64,2048]{1,0:T(8,128)(2,1)S(1)}, bf16[64,2048]{1,0:T(8,128)(2,1)S(1)}, u32[]{:S(2)}, u32[]{:S(2)}) collective-permute-start(bf16[64,2048]{1,0:T(8,128)(2,1)S(1)} %collective-permute-done.12), channel_id=1, source_target_pairs={{0,1},{1,0},{2,3},{3,2},{4,5},{5,4},{6,7},{7,6},{8,9},{9,8},{10,11... | collective-permute-start | bytes 786440 | tf_op jit(solution)/shard_map/ppermute | solution.py:262
  125.9 36.7 %collective-permute-start.16 = (bf16[64,2048]{1,0:T(8,128)(2,1)S(1)}, bf16[64,2048]{1,0:T(8,128)(2,1)S(1)}, u32[]{:S(2)}, u32[]{:S(2)}) collective-permute-start(bf16[64,2048]{1,0:T(8,128)(2,1)S(1)} %collective-permute-done.11), channel_id=1, source_target_pairs={{0,1},{1,0},{2,3},{3,2},{4,5},{5,4},{6,7},{7,6},{8,9},{9,8},{10,11... | collective-permute-start | bytes 786440 | tf_op jit(solution)/shard_map/ppermute | solution.py:262
  157.0 14.9 %collective-permute-start.15 = (bf16[128,2048]{1,0:T(8,128)(2,1)S(1)}, bf16[128,2048]{1,0:T(8,128)(2,1)S(1)}, u32[]{:S(2)}, u32[]{:S(2)}) collective-permute-start(bf16[128,2048]{1,0:T(8,128)(2,1)S(1)} %collective-permute-done.10), channel_id=1, source_target_pairs={{0,1},{1,0},{2,3},{3,2},{4,5},{5,4},{6,7},{7,6},{8,9},{9,8},{10,11... | collective-permute-start | bytes 1572872 | tf_op jit(solution)/shard_map/ppermute | solution.py:262
  158.6 22.8 %collective-permute-start.14 = (bf16[128,2048]{1,0:T(8,128)(2,1)S(1)}, bf16[128,2048]{1,0:T(8,128)(2,1)S(1)}, u32[]{:S(2)}, u32[]{:S(2)}) collective-permute-start(bf16[128,2048]{1,0:T(8,128)(2,1)S(1)} %collective-permute-done.9), channel_id=1, source_target_pairs={{0,1},{1,0},{2,3},{3,2},{4,5},{5,4},{6,7},{7,6},{8,9},{9,8},{10,11... | collective-permute-start | bytes 1572872 | tf_op jit(solution)/shard_map/ppermute | solution.py:262
  202.8 58.5 %copy-start.3 = (f32[128,2048]{1,0:T(8,128)S(1)}, f32[128,2048]{1,0:T(8,128)}, u32[]{:S(2)}) copy-start(f32[128,2048]{1,0:T(8,128)} %get-tuple-element.43) | copy-start | bytes 3145732
  202.8 58.5 %copy-start.7 = (bf16[128,2048]{1,0:T(8,128)(2,1)S(1)}, bf16[128,2048]{1,0:T(8,128)(2,1)}, u32[]{:S(2)}) copy-start(bf16[128,2048]{1,0:T(8,128)(2,1)} %get-tuple-element.55) | copy-start | bytes 1572868
  202.8 9.5 %collective-permute-start.18 = (bf16[64,2048]{1,0:T(8,128)(2,1)}, bf16[64,2048]{1,0:T(8,128)(2,1)S(1)}, u32[]{:S(2)}, u32[]{:S(2)}) collective-permute-start(bf16[64,2048]{1,0:T(8,128)(2,1)} %get-tuple-element.48), channel_id=1, source_target_pairs={{0,1},{1,0},{2,3},{3,2},{4,5},{5,4},{6,7},{7,6},{8,9},{9,8},{10,11... | collective-permute-start | bytes 786440 | tf_op jit(solution)/shard_map/ppermute | solution.py:262
  203.4 20.1 %collective-permute-start.22 = (bf16[128,2048]{1,0:T(8,128)(2,1)}, bf16[128,2048]{1,0:T(8,128)(2,1)S(1)}, u32[]{:S(2)}, u32[]{:S(2)}) collective-permute-start(bf16[128,2048]{1,0:T(8,128)(2,1)} %get-tuple-element.52), channel_id=1, source_target_pairs={{0,1},{1,0},{2,3},{3,2},{4,5},{5,4},{6,7},{7,6},{8,9},{9,8},{10,11... | collective-permute-start | bytes 1572872 | tf_op jit(solution)/shard_map/ppermute | solution.py:262
  204.9 36.8 %collective-permute-start.20 = (bf16[64,2048]{1,0:T(8,128)(2,1)}, bf16[64,2048]{1,0:T(8,128)(2,1)S(1)}, u32[]{:S(2)}, u32[]{:S(2)}) collective-permute-start(bf16[64,2048]{1,0:T(8,128)(2,1)} %get-tuple-element.50), channel_id=1, source_target_pairs={{0,1},{1,0},{2,3},{3,2},{4,5},{5,4},{6,7},{7,6},{8,9},{9,8},{10,11... | collective-permute-start | bytes 786440 | tf_op jit(solution)/shard_map/ppermute | solution.py:262
  205.5 35.0 %collective-permute-start.24 = (bf16[128,2048]{1,0:T(8,128)(2,1)}, bf16[128,2048]{1,0:T(8,128)(2,1)S(1)}, u32[]{:S(2)}, u32[]{:S(2)}) collective-permute-start(bf16[128,2048]{1,0:T(8,128)(2,1)} %get-tuple-element.54), channel_id=1, source_target_pairs={{0,1},{1,0},{2,3},{3,2},{4,5},{5,4},{6,7},{7,6},{8,9},{9,8},{10,11... | collective-permute-start | bytes 1572872 | tf_op jit(solution)/shard_map/ppermute | solution.py:262
  206.9 48.9 %collective-permute-start.26 = (bf16[128,2048]{1,0:T(8,128)(2,1)}, bf16[128,2048]{1,0:T(8,128)(2,1)S(1)}, u32[]{:S(2)}, u32[]{:S(2)}) collective-permute-start(bf16[128,2048]{1,0:T(8,128)(2,1)} %get-tuple-element.56), channel_id=1, source_target_pairs={{0,1},{1,0},{2,3},{3,2},{4,5},{5,4},{6,7},{7,6},{8,9},{9,8},{10,11... | collective-permute-start | bytes 1572872 | tf_op jit(solution)/shard_map/ppermute | solution.py:262
  212.4 50.3 %copy-start.1 = (bf16[256,2048]{1,0:T(8,128)(2,1)S(1)}, bf16[256,2048]{1,0:T(8,128)(2,1)}, u32[]{:S(2)}) copy-start(bf16[256,2048]{1,0:T(8,128)(2,1)} %param.23) | copy-start | bytes 3145732
  213.5 30.8 %collective-permute-start.19 = (bf16[64,2048]{1,0:T(8,128)(2,1)S(1)}, bf16[64,2048]{1,0:T(8,128)(2,1)S(1)}, u32[]{:S(2)}, u32[]{:S(2)}) collective-permute-start(bf16[64,2048]{1,0:T(8,128)(2,1)S(1)} %add_convert_fusion.4), channel_id=1, source_target_pairs={{0,6},{1,7},{2,4},{3,5},{4,2},{5,3},{6,0},{7,1},{8,14},{9,15},{10,... | collective-permute-start | bytes 786440 | tf_op jit(solution)/shard_map/ppermute | solution.py:266
  224.8 31.1 %collective-permute-start.23 = (bf16[128,2048]{1,0:T(8,128)(2,1)S(1)}, bf16[128,2048]{1,0:T(8,128)(2,1)S(1)}, u32[]{:S(2)}, u32[]{:S(2)}) collective-permute-start(bf16[128,2048]{1,0:T(8,128)(2,1)S(1)} %add_convert_fusion.2), channel_id=1, source_target_pairs={{0,4},{1,5},{2,6},{3,7},{4,0},{5,1},{6,2},{7,3},{8,12},{9,13},{10,... | collective-permute-start | bytes 1572872 | tf_op jit(solution)/shard_map/ppermute | solution.py:266
  241.6 19.7 %collective-permute-start.25 = (bf16[128,2048]{1,0:T(8,128)(2,1)S(1)}, bf16[128,2048]{1,0:T(8,128)(2,1)S(1)}, u32[]{:S(2)}, u32[]{:S(2)}) collective-permute-start(bf16[128,2048]{1,0:T(8,128)(2,1)S(1)} %add_convert_fusion.1), channel_id=1, source_target_pairs={{0,2},{1,3},{2,0},{3,1},{4,6},{5,7},{6,4},{7,5},{8,10},{9,11},{10,... | collective-permute-start | bytes 1572872 | tf_op jit(solution)/shard_map/ppermute | solution.py:266
  242.7 13.1 %collective-permute-start.21 = (bf16[64,2048]{1,0:T(8,128)(2,1)S(1)}, bf16[64,2048]{1,0:T(8,128)(2,1)S(1)}, u32[]{:S(2)}, u32[]{:S(2)}) collective-permute-start(bf16[64,2048]{1,0:T(8,128)(2,1)S(1)} %add_convert_fusion.3), channel_id=1, source_target_pairs={{0,6},{1,7},{2,4},{3,5},{4,2},{5,3},{6,0},{7,1},{8,14},{9,15},{10,... | collective-permute-start | bytes 786440 | tf_op jit(solution)/shard_map/ppermute | solution.py:266
Sparse Core Ops, SparseCore 0:
  9.5 76.0 all-gather.1

commit v5 on v4

--- a/solution.py
+++ b/solution.py
@@ -1,4 +1,3 @@
-import functools
 import math
 
 import jax
@@ -262,8 +261,12 @@
     return lax.ppermute(array, "exp", [(i, i ^ 1) for i in range(8)])
 
 
-def z_swap(array, distance):
-    return lax.ppermute(array, "exp", [(i, i ^ (2 * distance)) for i in range(8)])
+def outer_swap(array):
+    return lax.ppermute(array, "exp", [(i, i ^ 2) for i in range(8)])
+
+
+def middle_swap(array):
+    return lax.ppermute(array, "exp", [(2, 4), (3, 5), (4, 2), (5, 3)])
 
 
 def split_kernel(sc_ref, q, k, v, pk, pv, out_tokens, out_prefix):
@@ -350,16 +353,16 @@
 
 
 def prefix_kernel(
-    far, sc_ref, shape_a, shape_b, q0, q1, pk, pv, other, o_ref, lse_ref,
+    sc_ref, shape_a, shape_b, q0, q1, pk, pv, other, o_ref, lse_ref,
     q_ref, ka, kb, va, vb, grp, lse, sa, sb, ta, tb, item_group, item_block, sems,
 ):
     tokens = q_ref.shape[0]
     span = ka.shape[1]
-    shapes = ((shape_a, 0), (shape_b, far))
+    shapes = ((shape_a, 0), (shape_b, 0))
     mine = pl.ds(pl.multiple_of(sc_ref[0] * HEAD, HEAD), HEAD)
     copies = [
         pltpu.make_async_copy(q0.at[:, mine], q_ref.at[:ROW_TOK, :], sems.at[0]),
-        pltpu.make_async_copy(q1, q_ref.at[ROW_TOK:, :], sems.at[1]),
+        pltpu.make_async_copy(q1.at[0], q_ref.at[ROW_TOK:, :], sems.at[1]),
         pltpu.make_async_copy(pk.at[:, :, mine], ka, sems.at[2]),
         pltpu.make_async_copy(other.at[0], kb, sems.at[3]),
         pltpu.make_async_copy(pv.at[:, :, mine], va, sems.at[4]),
@@ -459,7 +462,7 @@
         ]
 
 
-def prefix_attend(place, far, shape_a, shape_b, q0, q1, pk, pv, other, out_dtype):
+def prefix_attend(place, shape_a, shape_b, q0, q1, pk, pv, other, out_dtype):
     rows = 2
     tokens = rows * ROW_TOK
     span = pk.shape[1]
@@ -472,7 +475,7 @@
     scores = pltpu.VMEM((PER_ITEM * SUB, 2 * span), jnp.float32)
     tops = pltpu.VMEM((PER_ITEM * SUB, HEAD), jnp.float32)
     return pl.pallas_call(
-        functools.partial(prefix_kernel, far),
+        prefix_kernel,
         in_specs=[smem] * 3 + [anywhere] * 5,
         out_specs=(vmem, vmem),
         out_shape=(
@@ -689,7 +692,7 @@
 
 EXP_DEV = 4
 SLOTS = 32
-SLOTS_XOR = (0, 2, 4, 6, 1, 3, 5, 7)
+SLOT_Z = ((0, 1, 2, 3), (1, 0, 3, 2), (2, 3, 0, 1), (3, 2, 1, 0))
 
 
 def route_kernel(sc_ref, tab_ref, pick_ref, give_ref):
@@ -699,8 +702,12 @@
     ).astype(jnp.bfloat16)
     place = lax.broadcasted_iota(jnp.int32, (SLOTS, BLK), 0).astype(jnp.float32)
     place_here = sc_ref[1]
-    for slot, offset in enumerate(SLOTS_XOR):
-        tab = tab_ref[place_here ^ offset].astype(jnp.float32)
+    here_z, here_y = place_here // 2, place_here % 2
+    for slot in range(8):
+        of = SLOT_Z[3][slot % 4]
+        for z in range(3):
+            of = jnp.where(here_z == z, SLOT_Z[z][slot % 4], of)
+        tab = tab_ref[of * 2 + (here_y if slot < 4 else 1 - here_y)].astype(jnp.float32)
         ids, gates = tab[:TOPK], tab[TOPK : 2 * TOPK]
         chosen, weights = [], []
         for j in range(EXP_DEV):
@@ -756,19 +763,18 @@
         for slot in range(8):
             out = jnp.dot(give_ref[slot], rows_out[slot], preferred_element_type=jnp.float32)
             out = out.astype(jnp.bfloat16)
-            at = slot + slot // 4
-            if slot % 4 < 3:
-                outs[at][...] = out
+            if slot < 7:
+                outs[slot][...] = out
             else:
-                outs[at][...] = out[: BLK // 2]
-                outs[at + 1][...] = out[BLK // 2 :]
+                outs[7][...] = out[: BLK // 2]
+                outs[8][...] = out[BLK // 2 :]
 
 
 def run_experts(picked, give, w_gate, w_up, w_down):
     width = picked[0].shape[1]
     hidden = w_down.shape[1]
     once = pl.Buffered(1)
-    heights = ([BLK] * 3 + [BLK // 2] * 2) * 2
+    heights = [BLK] * 7 + [BLK // 2] * 2
     return pl.pallas_call(
         experts_kernel,
         grid=(EXP_DEV,),
@@ -783,33 +789,73 @@
     )(*picked, give, w_gate.transpose(0, 2, 1), w_up.transpose(0, 2, 1), w_down)
 
 
-def gather_rows(own):
+def together(*arrays):
+    return lax.optimization_barrier(arrays)
+
+
+def gather_rows(middle, own):
     half = own.shape[0] // 2
-    there = [y_swap(own)]
-    near = [z_swap(own, 1), z_swap(own, 2), z_swap(own[:half], 3), z_swap(own[half:], 3)]
-    there += [y_swap(part) for part in near]
-    return [own] + near, there
+    outer0, middle0, there0 = together(outer_swap(own), middle_swap(own), y_swap(own))
+    outer1, middle1, there1 = together(
+        outer_swap(middle0), middle_swap(outer0), y_swap(outer0)
+    )
+    second = jnp.where(middle, middle1, outer1)
+    outer2, there2 = together(outer_swap(middle1), y_swap(second))
+    third = jnp.where(middle, middle0, outer2)
+    there3, late_outer, late_middle = together(
+        y_swap(third[:half]), outer_swap(there2[half:]), middle_swap(there0[half:])
+    )
+    late = jnp.where(middle, late_middle, late_outer)
+    return [own, outer0, second, third], [there0, there1, there2, there3, late]
 
 
 def pick_rows(pick, parts):
-    half = parts[3].shape[0]
-    picked = [jnp.dot(pick[i], parts[i], preferred_element_type=jnp.float32) for i in range(3)]
-    picked.append(
-        jnp.dot(pick[3][:, :half], parts[3], preferred_element_type=jnp.float32)
-        + jnp.dot(pick[3][:, half:], parts[4], preferred_element_type=jnp.float32)
-    )
+    picked = [
+        jnp.dot(matrix, part, preferred_element_type=jnp.float32)
+        for matrix, part in zip(pick, parts[:4])
+        if part.shape[0] == matrix.shape[1]
+    ]
+    if len(parts) == 5:
+        half = parts[3].shape[0]
+        picked.append(
+            jnp.dot(pick[3][:, :half], parts[3], preferred_element_type=jnp.float32)
+            + jnp.dot(pick[3][:, half:], parts[4], preferred_element_type=jnp.float32)
+        )
     return [part.astype(jnp.bfloat16) for part in picked]
 
 
-def scatter_sums(stream, own, there):
-    def plus(a, b):
-        return (a.astype(jnp.float32) + b.astype(jnp.float32)).astype(jnp.bfloat16)
-
-    last = [z_swap(plus(own[i], y_swap(there[i])), 3) for i in (3, 4)]
-    total = stream + jnp.concatenate(last, axis=0).astype(jnp.float32)
-    for i in (2, 1):
-        total = total + z_swap(plus(own[i], y_swap(there[i])), i).astype(jnp.float32)
-    return total + own[0].astype(jnp.float32) + y_swap(there[0]).astype(jnp.float32)
+def scatter_sums(middle, stream, own, there):
+    half = there[3].shape[0]
+
+    def plus(*parts):
+        total = parts[0].astype(jnp.float32)
+        for part in parts[1:]:
+            total = total + part.astype(jnp.float32)
+        return total
+
+    def plus16(*parts):
+        return plus(*parts).astype(jnp.bfloat16)
+
+    def in_middle(array):
+        return jnp.where(middle, array.astype(jnp.float32), 0.0)
+
+    got, late_outer, late_middle = together(
+        y_swap(there[3]), outer_swap(there[4]), middle_swap(there[4])
+    )
+    sum3 = jnp.concatenate([plus16(own[3][:half], got), own[3][half:]], axis=0)
+    there2 = jnp.concatenate(
+        [there[2][:half], plus16(there[2][half:], in_middle(late_outer))], axis=0
+    )
+    there0 = jnp.concatenate(
+        [there[0][:half], plus16(there[0][half:], in_middle(late_middle))], axis=0
+    )
+    got, outer = together(y_swap(there2), outer_swap(sum3))
+    sum2 = plus16(own[2], got, in_middle(outer))
+    got, outer, across = together(y_swap(there[1]), outer_swap(sum2), middle_swap(sum2))
+    sum1 = plus16(own[1], got, in_middle(across))
+    sum3 = plus16(sum3, in_middle(outer))
+    got, outer, across = together(y_swap(there0), outer_swap(sum1), middle_swap(sum3))
+    return plus(stream, own[0], got, outer, in_middle(across))
 
 
 def block_device(
@@ -830,41 +876,44 @@
     w_down,
 ):
     core = lax.rem(lax.axis_index("req"), 2)
+    z = lax.axis_index("exp") // 2
+    middle = (z == 1) | (z == 2)
     place = jnp.stack([core, lax.axis_index("exp")]).astype(jnp.int32)
 
+    shape = jnp.concatenate([lengths, groups], axis=1)
+    other_shape = core_swap(shape)
+    far_shape = x_swap(shape)
     far_queries = x_swap(queries)
-    shape = jnp.concatenate([lengths, groups], axis=1)
-    far_shape = x_swap(shape)
-    other_shapes = core_swap(jnp.concatenate([shape, far_shape], axis=0))
+    far_other_shape = core_swap(far_shape)
 
     proj_rows = lax.dynamic_slice_in_dim(out_proj, core * HEAD, HEAD, 0)
     proj_rows = lax.all_gather(proj_rows, "exp", axis=0, tiled=True)
 
     theirs, prefix_theirs = split_theirs(place, queries, keys, values, prefix_keys, prefix_values)
     other, prefix_other = core_swap(theirs), core_swap(prefix_theirs)
-    far_other = core_swap(jnp.where(core == 0, far_queries[:, HEAD:], far_queries[:, :HEAD]))
-
-    def prefix(far, shape_a, q0, q1, dtype):
+    far_other = core_swap(jnp.where(core == 0, far_queries[:, HEAD:], far_queries[:, :HEAD])[None])
+
+    def prefix(shape_a, shape_b, q0, q1, dtype):
         return prefix_attend(
-            place, far, shape_a, other_shapes, q0, q1, prefix_keys, prefix_values, prefix_other, dtype
+            place, shape_a, shape_b, q0, q1, prefix_keys, prefix_values, prefix_other, dtype
         )
 
     tab = jnp.concatenate([expert_ids.T.astype(jnp.bfloat16), expert_gates.T], axis=0)
     tab = jnp.pad(tab, ((0, 16 - tab.shape[0]), (0, 0)))
-    suffix = suffix_attend(place, shape, other_shapes, queries, keys, values, other)
-    far = prefix(1, far_shape, far_queries, far_other, jnp.bfloat16)
+    suffix = suffix_attend(place, shape, other_shape, queries, keys, values, other)
+    far = prefix(far_shape, far_other_shape, far_queries, far_other, jnp.bfloat16)
     back = (x_swap(far[0]), x_swap(far[1]))
-    near = prefix(0, shape, queries, other[0], jnp.float32)
+    near = prefix(shape, other_shape, queries, other, jnp.float32)
     near_o, gain = lax.optimization_barrier((near[0], norm_gain.reshape(1, -1)))
     attended = merge_parts([suffix, (near_o, near[1]), back], tab)
     heads = lax.all_to_all(attended, "exp", split_axis=0, concat_axis=0, tiled=True)
     keep, send = project(heads, proj_rows)
     stream, normed = norm_rows(keep, core_swap(send), residual, gain)
     pick, give = route(place, heads)
-    here, there = gather_rows(normed)
+    here, there = gather_rows(middle, normed)
     picked = pick_rows(pick[:4], here) + pick_rows(pick[4:], there)
     sums = run_experts(picked, give, w_gate, w_up, w_down)
-    return scatter_sums(stream, sums[:5], sums[5:]).astype(jnp.bfloat16)
+    return scatter_sums(middle, stream, sums[:4], sums[4:]).astype(jnp.bfloat16)
 
 
 def solution(mesh):

time: 270 us -> 247 us (0.915)
  waiting for transfers between devices: 110 us -> 77.8 us
  starting transfers between devices: 23.9 us -> 31.9 us
    ppermute x10 -> x8, waiting for transfers between devices: 45.7 us -> 22.2 us  [y_swap(): return lax.ppermute(array, 'exp', [(i, i ^ 1) for i in range(8)])]
    ppermute x8 -> x14, waiting for transfers between devices: 52.6 us -> 42.6 us  [the longest x8 42.6 us: outer_swap(): return lax.ppermute(array, 'exp', [(i, i ^ 2) for i in range(8)])]
    ppermute x8 -> x14, starting transfers between devices: 8.98 us -> 17.7 us  [the longest x8 13.7 us: outer_swap(): return lax.ppermute(array, 'exp', [(i, i ^ 2) for i in range(8)])]
    dot_general x6 -> x7, matrix products: 7.59 us -> 10.2 us  [pick_rows(): jnp.dot(matrix, part, preferred_element_type=jnp.float32)]
    convert_element_type x5 -> x7, other arithmetic: 5.71 us -> 3.99 us  [the longest x6 2.79 us: plus16(): return plus(*parts).astype(jnp.bfloat16)]
    ppermute x10 -> x8, starting transfers between devices: 8.81 us -> 7.88 us  [y_swap(): return lax.ppermute(array, 'exp', [(i, i ^ 1) for i in range(8)])]
  transfers between devices with their start and end apart: 28 -> 33, of which waited for: 13 -> 15; matrix products, arithmetic and copies ran while one was open for 7% -> 7% of each run, Pallas kernels for 17% -> 18%
where the time goes in v5:
time: 247 us; the launch traced here: 246 us
  waiting for transfers between devices  77.8 us (31%)
  Pallas kernels  72.5 us (29%)
  starting transfers between devices  31.9 us (13%)
  blocking collectives  23.4 us (9%)
  between operations  13.9 us (6%)
  matrix products  11.6 us (5%)
  local copies, waits for them, and re-layouts  9.12 us (4%)
  other arithmetic  5.59 us (2%)
    ppermute x8, waiting for transfers between devices, outer_swap(): return lax.ppermute(array, 'exp', [(i, i ^ 2) for i in range(8)])  42.6 us
    pallas_call x2, Pallas kernels, prefix_attend(): pl.pallas_call(prefix_kernel, in_specs=[smem] * 3 + [anywhere] * 5, out_s...  29.4 us
    all_to_all x1, blocking collectives, block_device(): lax.all_to_all(attended, 'exp', split_axis=0, concat_axis=0, tiled=True)  23.4 us
    ppermute x8, waiting for transfers between devices, y_swap(): return lax.ppermute(array, 'exp', [(i, i ^ 1) for i in range(8)])  22.2 us
    pallas_call x1, Pallas kernels, run_experts(): pl.pallas_call(experts_kernel, grid=(EXP_DEV,), in_specs=[pl.BlockSpec((S...  20.4 us
    ppermute x8, starting transfers between devices, outer_swap(): return lax.ppermute(array, 'exp', [(i, i ^ 2) for i in range(8)])  13.7 us
    ppermute x4, waiting for transfers between devices, x_swap(): return lax.ppermute(array, 'req', [(i, i ^ 2) for i in range(4)])  10.8 us
    dot_general x7, matrix products, pick_rows(): jnp.dot(matrix, part, preferred_element_type=jnp.float32)  10.2 us
  transfers between devices with their start and end apart: 33, of which 15 were waited for; matrix products, arithmetic and copies ran while one was open for 7% of the time, Pallas kernels for 18%

profile of v5, /device:TPU:0, one launch (start us, length us, event | category | flops | bytes accessed | tf_op | source)
XLA Modules:
  0.0 245.6 jit_solution(3000055401980914006)
XLA Ops:
  6.6 1.1 copy-done
  7.8 0.8 constant_dynamic-slice_fusion
  8.6 0.7 pad_add_fusion.sc_ref
  9.3 4.8 %split_theirs.1 = (bf16[3,1024,128]{2,1,0:T(8,128)(2,1)}, bf16[2,4,1024,128]{3,2,1,0:T(8,128)(2,1)}) custom-call(s32[2]{0:T(128)} %pad_add_fusion.sc_ref, bf16[1024,256]{1,0:T(8,128)(2,1)} %q0.1, bf16[1024,256]{1,0:T(8,128)(2,1)} %k.3, bf16[1024,256]{1,0:T(8,128)(2,1)} %v.3, bf16[4,1024,256]{2,1,0:T(8,128)(2,1)} %pk.5, bf16[4,1024,256]{2,1,0:T(8,128)(2,1)} %pv.5), custom_call_target="tpu_custom_call" | custom-call | tf_op jit(solution)/shard_map/split_theirs/pallas_call | solution.py:284
  14.6 2.9 %collective-permute-start.5 = (bf16[1024,256]{1,0:T(8,128)(2,1)S(1)}, bf16[1024,256]{1,0:T(8,128)(2,1)S(1)}, u32[]{:S(2)}, u32[]{:S(2)}) collective-permute-start(bf16[1024,256]{1,0:T(8,128)(2,1)S(1)} %copy-done.4), channel_id=1, source_target_pairs={{0,16},{8,24},{16,0},{24,8},{1,17},{9,25},{17,1},{25,9},{2,18},{10... | collective-permute-start | bytes 1572872 | tf_op jit(solution)/shard_map/ppermute | solution.py:257
  19.0 10.8 %collective-permute-done.3.shape_a = s32[1,16]{1,0:T(1,128)S(1)} collective-permute-done((s32[1,16]{1,0:T(1,128)S(1)}, s32[1,16]{1,0:T(1,128)S(1)}, u32[]{:S(2)}, u32[]{:S(2)}) %collective-permute-start.3) | collective-permute-done | bytes 96 | tf_op jit(solution)/shard_map/ppermute | solution.py:257
  31.0 0.9 copy-done.16
  31.9 5.8 %suffix_attend.1 = (f32[2048,128]{1,0:T(8,128)}, f32[2,8,128]{2,1,0:T(8,128)}) custom-call(s32[2]{0:T(128)} %pad_add_fusion.sc_ref, s32[1,16]{1,0:T(1,128)} %copy-done.21, s32[1,16]{1,0:T(1,128)} %copy-done.22, bf16[1024,256]{1,0:T(8,128)(2,1)} %q0.1, bf16[1024,256]{1,0:T(8,128)(2,1)} %k.3, bf16[1024,256]{1,0:T(8,128)(2,1)} %v.3, ...), custom_call_target="tpu_custom_call" | custom-call | flops 4294967296 | bytes 1048576 | tf_op jit(solution)/shard_map/suffix_attend/pallas_call | solution.py:563
  38.4 14.7 %prefix_attend.3 = (bf16[2048,128]{1,0:T(8,128)(2,1)}, f32[2,8,128]{2,1,0:T(8,128)}) custom-call(s32[2]{0:T(128)} %pad_add_fusion.sc_ref, s32[1,16]{1,0:T(1,128)} %copy-done.23, s32[1,16]{1,0:T(1,128)} %copy-done.24, bf16[1024,256]{1,0:T(8,128)(2,1)} %copy-done.7, bf16[1,1024,128]{2,1,0:T(8,128)(2,1)} %copy-done.18, bf16[4,1024,256]{2,1,0:T(8,128)(2,1)} %pk.5, ...), custom_call_target="tpu_custom_call" | custom-call | flops 8589934592 | bytes 4194304 | tf_op jit(solution)/shard_map/prefix_attend/pallas_call | solution.py:477
  53.1 1.8 collective-permute-start.7
  55.2 14.7 %prefix_attend.2 = (f32[2048,128]{1,0:T(8,128)}, f32[2,8,128]{2,1,0:T(8,128)}) custom-call(s32[2]{0:T(128)} %pad_add_fusion.sc_ref, s32[1,16]{1,0:T(1,128)} %copy-done.21, s32[1,16]{1,0:T(1,128)} %copy-done.22, bf16[1024,256]{1,0:T(8,128)(2,1)} %q0.1, bf16[3,1024,128]{2,1,0:T(8,128)(2,1)} %copy-done.16, bf16[4,1024,256]{2,1,0:T(8,128)(2,1)} %pk.5, ...), custom_call_target="tpu_custom_call" | custom-call | flops 8589934592 | bytes 4194304 | tf_op jit(solution)/shard_map/prefix_attend/pallas_call | solution.py:477
  70.8 3.2 %merge_parts.1 = bf16[8,272,128]{2,1,0:T(8,128)(2,1)} custom-call(f32[2048,128]{1,0:T(8,128)} %get-tuple-element.53.refs_0_.refs_6_, f32[2,8,128]{2,1,0:T(8,128)} %get-tuple-element.54.refs_1_.refs_7_, f32[2048,128]{1,0:T(8,128)} %get-tuple-element.57.refs_2_.refs_8_, f32[2,8,128]{2,1,0:T(8,128)} %get-tuple-element.58.refs_3_.refs_9_, ...), custom_call_target="tpu_custom_call" | custom-call | tf_op jit(solution)/shard_map/merge_parts/pallas_call | solution.py:628
  73.9 23.4 %all_to_all.5.a_ref.tab_ref = bf16[8,272,128]{2,1,0:T(8,128)(2,1)} all-to-all(bf16[8,272,128]{2,1,0:T(8,128)(2,1)} %merge_parts.1), channel_id=1, replica_groups=mesh['req'=4,'exp'=8] {'exp'}, dimensions={0} | all-to-all | bytes 1114112 | tf_op jit(solution)/shard_map/all_to_all | solution.py:909
  97.3 4.1 %project.1 = (f32[128,2048]{1,0:T(8,128)}, bf16[128,2048]{1,0:T(8,128)(2,1)}) custom-call(bf16[8,272,128]{2,1,0:T(8,128)(2,1)} %all_to_all.5.a_ref.tab_ref, bf16[1024,2048]{1,0:T(8,128)(2,1)} %all-gather.2.cloned.1.call-done.w_ref), custom_call_target="tpu_custom_call" | custom-call | tf_op jit(solution)/shard_map/project/pallas_call | solution.py:656
  101.4 2.1 collective-permute-done.9.got
  103.6 0.8 copy-done.10
  104.3 2.9 %norm_rows.1 = (f32[128,2048]{1,0:T(8,128)}, bf16[128,2048]{1,0:T(8,128)(2,1)}) custom-call(f32[128,2048]{1,0:T(8,128)} %get-tuple-element.61.keep, bf16[128,2048]{1,0:T(8,128)(2,1)} %copy-done.10, bf16[128,2048]{1,0:T(8,128)(2,1)} %residual.1, bf16[1,2048]{1,0:T(2,128)(2,1)} %reshape.3.gain), custom_call_target="tpu_custom_call" | custom-call | tf_op jit(solution)/shard_map/norm_rows/pallas_call | solution.py:683
  107.8 0.7 collective-permute-start.11
  108.5 1.5 collective-permute-start.12
  109.9 1.8 route.1
  111.7 9.7 %collective-permute-done.10 = bf16[128,2048]{1,0:T(8,128)(2,1)S(1)} collective-permute-done((bf16[128,2048]{1,0:T(8,128)(2,1)}, bf16[128,2048]{1,0:T(8,128)(2,1)S(1)}, u32[]{:S(2)}, u32[]{:S(2)}) %collective-permute-start.10) | collective-permute-done | bytes 524320 | tf_op jit(solution)/shard_map/ppermute | solution.py:265
  121.4 1.0 collective-permute-done.12
  122.4 0.7 collective-permute-start.14
  123.1 1.5 collective-permute-start.15
  124.6 5.7 %collective-permute-start.13 = (bf16[128,2048]{1,0:T(8,128)(2,1)S(1)}, bf16[128,2048]{1,0:T(8,128)(2,1)S(1)}, u32[]{:S(2)}, u32[]{:S(2)}) collective-permute-start(bf16[128,2048]{1,0:T(8,128)(2,1)S(1)} %collective-permute-done.11), channel_id=1, source_target_pairs={{0,2},{1,3},{2,0},{3,1},{4,6},{5,7},{6,4},{7,5},{8,10},{9,11},{10,... | collective-permute-start | bytes 1572872 | tf_op jit(solution)/shard_map/ppermute | solution.py:265
  130.3 0.8 slice_bitcast_fusion
  131.0 2.1 convolution_convert_fusion.6.refs_0_
  133.2 1.8 convolution_convert_fusion.5.refs_1_
  135.0 5.4 %collective-permute-done.13 = bf16[128,2048]{1,0:T(8,128)(2,1)S(1)} collective-permute-done((bf16[128,2048]{1,0:T(8,128)(2,1)S(1)}, bf16[128,2048]{1,0:T(8,128)(2,1)S(1)}, u32[]{:S(2)}, u32[]{:S(2)}) %collective-permute-start.13) | collective-permute-done | bytes 524320 | tf_op jit(solution)/shard_map/ppermute | solution.py:265
  140.5 1.9 collective-permute-start.16
  142.4 0.7 collective-permute-start.17
  143.1 1.9 convolution_convert_fusion.2.refs_4_
  145.0 0.7 collective-permute-start.20
  145.7 1.1 convolution_convert_fusion.4.refs_2_
  146.8 1.1 convolution_convert_fusion.1.refs_5_
  147.9 6.6 %collective-permute-done.17 = bf16[128,2048]{1,0:T(8,128)(2,1)S(1)} collective-permute-done((bf16[128,2048]{1,0:T(8,128)(2,1)S(1)}, bf16[128,2048]{1,0:T(8,128)(2,1)S(1)}, u32[]{:S(2)}, u32[]{:S(2)}) %collective-permute-start.17) | collective-permute-done | bytes 524320 | tf_op jit(solution)/shard_map/ppermute | solution.py:261
  154.5 0.7 collective-permute-start.18
  155.4 1.1 convolution_convert_fusion.refs_6_
  156.5 1.1 convolution_convert_fusion.3.refs_3_
  157.6 3.3 %collective-permute-done.18 = bf16[64,2048]{1,0:T(8,128)(2,1)S(1)} collective-permute-done((bf16[64,2048]{1,0:T(8,128)(2,1)S(1)}, bf16[64,2048]{1,0:T(8,128)(2,1)S(1)}, u32[]{:S(2)}, u32[]{:S(2)}) %collective-permute-start.18) | collective-permute-done | bytes 262176 | tf_op jit(solution)/shard_map/ppermute | solution.py:261
  161.0 0.7 collective-permute-done.19
  162.0 1.1 fusion.refs_7_
  163.1 20.4 %experts.1 = (bf16[128,2048]{1,0:T(8,128)(2,1)}, bf16[128,2048]{1,0:T(8,128)(2,1)}, bf16[128,2048]{1,0:T(8,128)(2,1)}, bf16[128,2048]{1,0:T(8,128)(2,1)}, bf16[1...) custom-call(bf16[128,2048]{1,0:T(8,128)(2,1)} %convolution_convert_f, ...), custom_call_target="tpu_custom_call" | custom-call | tf_op jit(solution)/shard_map/experts/pallas_call | solution.py:778
  183.5 1.5 collective-permute-start.21
  185.1 0.7 collective-permute-start.23
  185.8 1.0 slice.66
  186.8 1.0 slice.63
  187.7 2.4 collective-permute-done.21
  190.2 4.0 %collective-permute-done.22 = bf16[64,2048]{1,0:T(8,128)(2,1)S(1)} collective-permute-done((bf16[64,2048]{1,0:T(8,128)(2,1)}, bf16[64,2048]{1,0:T(8,128)(2,1)S(1)}, u32[]{:S(2)}, u32[]{:S(2)}) %collective-permute-start.22) | collective-permute-done | bytes 262176 | tf_op jit(solution)/shard_map/ppermute | solution.py:265
  194.1 1.0 add_convert_fusion.4
  195.2 1.4 collective-permute-start.27
  196.6 1.0 add_convert_fusion.5
  197.7 0.7 collective-permute-start.26
  198.4 1.4 collective-permute-start.25
  199.8 9.1 %collective-permute-done.27 = bf16[128,2048]{1,0:T(8,128)(2,1)S(1)} collective-permute-done((bf16[128,2048]{1,0:T(8,128)(2,1)S(1)}, bf16[128,2048]{1,0:T(8,128)(2,1)S(1)}, u32[]{:S(2)}, u32[]{:S(2)}) %collective-permute-start.27) | collective-permute-done | bytes 524320 | tf_op jit(solution)/shard_map/ppermute | solution.py:265
  208.9 3.8 %collective-permute-done.26 = bf16[128,2048]{1,0:T(8,128)(2,1)S(1)} collective-permute-done((bf16[128,2048]{1,0:T(8,128)(2,1)S(1)}, bf16[128,2048]{1,0:T(8,128)(2,1)S(1)}, u32[]{:S(2)}, u32[]{:S(2)}) %collective-permute-start.26) | collective-permute-done | bytes 524320 | tf_op jit(solution)/shard_map/ppermute | solution.py:261
  212.9 0.8 collective-permute-start.28
  213.6 0.7 collective-permute-start.29
  214.6 5.2 %collective-permute-done.25 = bf16[128,2048]{1,0:T(8,128)(2,1)S(1)} collective-permute-done((bf16[128,2048]{1,0:T(8,128)(2,1)S(1)}, bf16[128,2048]{1,0:T(8,128)(2,1)S(1)}, u32[]{:S(2)}, u32[]{:S(2)}) %collective-permute-start.25) | collective-permute-done | bytes 524320 | tf_op jit(solution)/shard_map/ppermute | solution.py:261
  219.7 6.5 %collective-permute-done.28 = bf16[128,2048]{1,0:T(8,128)(2,1)S(1)} collective-permute-done((bf16[128,2048]{1,0:T(8,128)(2,1)S(1)}, bf16[128,2048]{1,0:T(8,128)(2,1)S(1)}, u32[]{:S(2)}, u32[]{:S(2)}) %collective-permute-start.28) | collective-permute-done | bytes 524320 | tf_op jit(solution)/shard_map/ppermute | solution.py:265
  226.4 0.7 collective-permute-start.31
  227.4 3.0 %collective-permute-start.30 = (bf16[128,2048]{1,0:T(8,128)(2,1)S(1)}, bf16[128,2048]{1,0:T(8,128)(2,1)S(1)}, u32[]{:S(2)}, u32[]{:S(2)}) collective-permute-start(bf16[128,2048]{1,0:T(8,128)(2,1)S(1)} %add_convert_fusion.2), channel_id=1, source_target_pairs={{0,2},{1,3},{2,0},{3,1},{4,6},{5,7},{6,4},{7,5},{8,10},{9,11},{10,... | collective-permute-start | bytes 1572872 | tf_op jit(solution)/shard_map/ppermute | solution.py:265
  230.4 7.2 %collective-permute-done.30 = bf16[128,2048]{1,0:T(8,128)(2,1)S(1)} collective-permute-done((bf16[128,2048]{1,0:T(8,128)(2,1)S(1)}, bf16[128,2048]{1,0:T(8,128)(2,1)S(1)}, u32[]{:S(2)}, u32[]{:S(2)}) %collective-permute-start.30) | collective-permute-done | bytes 524320 | tf_op jit(solution)/shard_map/ppermute | solution.py:265
  237.6 1.2 add_convert_fusion
  (98 shorter events, 7.3 us)
Async XLA Ops:
  6.5 1.2 copy-start
  6.5 8.1 %copy-start.4 = (bf16[1024,256]{1,0:T(8,128)(2,1)S(1)}, bf16[1024,256]{1,0:T(8,128)(2,1)}, u32[]{:S(2)}) copy-start(bf16[1024,256]{1,0:T(8,128)(2,1)} %q0.1) | copy-start | bytes 1572868
  6.5 11.0 %copy-start.20 = (s32[1,8]{1,0:T(1,128)S(1)}, s32[1,8]{1,0:T(1,128)}, u32[]{:S(2)}) copy-start(s32[1,8]{1,0:T(1,128)} %param.20) | copy-start | bytes 100
  6.5 11.0 %copy-start.19 = (s32[1,8]{1,0:T(1,128)S(1)}, s32[1,8]{1,0:T(1,128)}, u32[]{:S(2)}) copy-start(s32[1,8]{1,0:T(1,128)} %param.21) | copy-start | bytes 100
  6.5 11.2 %copy-start.14 = (s32[128,4]{0,1:T(4,128)S(1)}, s32[128,4]{0,1:T(4,128)}, u32[]{:S(2)}) copy-start(s32[128,4]{0,1:T(4,128)} %param.25) | copy-start | bytes 6148
  6.5 11.2 %copy-start.15 = (bf16[128,4]{0,1:T(4,128)(2,1)S(1)}, bf16[128,4]{0,1:T(4,128)(2,1)}, u32[]{:S(2)}) copy-start(bf16[128,4]{0,1:T(4,128)(2,1)} %param.26) | copy-start | bytes 3076
  6.6 11.8 %copy-start.13 = (bf16[2048]{0:T(1024)(128)(2,1)S(1)}, bf16[2048]{0:T(1024)(128)(2,1)}, u32[]{:S(2)}) copy-start(bf16[2048]{0:T(1024)(128)(2,1)} %param.24) | copy-start | bytes 12292
  6.6 90.7 %all-gather.2.cloned.1.call-start = ((), (), s32[]{:S(2)}) async-start(), calls=%async_computation.1 | async-start | bytes 4718592 | tf_op jit(solution)/shard_map/all_gather | solution.py:890
  14.1 23.6 %collective-permute-start.2 = (bf16[2,4,1024,128]{3,2,1,0:T(8,128)(2,1)}, bf16[2,4,1024,128]{3,2,1,0:T(8,128)(2,1)}, u32[]{:S(2)}, u32[]{:S(2)}) collective-permute-start(bf16[2,4,1024,128]{3,2,1,0:T(8,128)(2,1)} %get-tuple-element.55), channel_id=1, source_target_pairs={{0,8},{8,0},{16,24},{24,16},{1,9},{9,1},{17,25},{25,17},{2,10},{10... | collective-permute-start | bytes 6291464 | tf_op jit(solution)/shard_map/ppermute | solution.py:253
  14.6 15.8 %collective-permute-start.1 = (bf16[3,1024,128]{2,1,0:T(8,128)(2,1)}, bf16[3,1024,128]{2,1,0:T(8,128)(2,1)S(1)}, u32[]{:S(2)}, u32[]{:S(2)}) collective-permute-start(bf16[3,1024,128]{2,1,0:T(8,128)(2,1)} %get-tuple-element.52), channel_id=1, source_target_pairs={{0,8},{8,0},{16,24},{24,16},{1,9},{9,1},{17,25},{25,17},{2,10},{10... | collective-permute-start | bytes 2359304 | tf_op jit(solution)/shard_map/ppermute | solution.py:253
  14.6 15.2 %collective-permute-start.5 = (bf16[1024,256]{1,0:T(8,128)(2,1)S(1)}, bf16[1024,256]{1,0:T(8,128)(2,1)S(1)}, u32[]{:S(2)}, u32[]{:S(2)}) collective-permute-start(bf16[1024,256]{1,0:T(8,128)(2,1)S(1)} %copy-done.4), channel_id=1, source_target_pairs={{0,16},{8,24},{16,0},{24,8},{1,17},{9,25},{17,1},{25,9},{2,18},{10... | collective-permute-start | bytes 1572872 | tf_op jit(solution)/shard_map/ppermute | solution.py:257
  17.7 12.8 %copy-start.21 = (s32[1,16]{1,0:T(1,128)}, s32[1,16]{1,0:T(1,128)S(1)}, u32[]{:S(2)}) copy-start(s32[1,16]{1,0:T(1,128)S(1)} %pad_add_fusion.1.shape_a) | copy-start | bytes 196
  17.7 12.8 %collective-permute-start = (s32[1,16]{1,0:T(1,128)S(1)}, s32[1,16]{1,0:T(1,128)S(1)}, u32[]{:S(2)}, u32[]{:S(2)}) collective-permute-start(s32[1,16]{1,0:T(1,128)S(1)} %pad_add_fusion.1.shape_a), channel_id=1, source_target_pairs={{0,8},{8,0},{16,24},{24,16},{1,9},{9,1},{17,25},{25,17},{2,10},{10... | collective-permute-start | bytes 200 | tf_op jit(solution)/shard_map/ppermute | solution.py:253
  17.7 12.1 %collective-permute-start.3 = (s32[1,16]{1,0:T(1,128)S(1)}, s32[1,16]{1,0:T(1,128)S(1)}, u32[]{:S(2)}, u32[]{:S(2)}) collective-permute-start(s32[1,16]{1,0:T(1,128)S(1)} %pad_add_fusion.1.shape_a), channel_id=1, source_target_pairs={{0,16},{8,24},{16,0},{24,8},{1,17},{9,25},{17,1},{25,9},{2,18},{10... | collective-permute-start | bytes 200 | tf_op jit(solution)/shard_map/ppermute | solution.py:257
  29.8 7.9 %copy-start.23 = (s32[1,16]{1,0:T(1,128)}, s32[1,16]{1,0:T(1,128)S(1)}, u32[]{:S(2)}) copy-start(s32[1,16]{1,0:T(1,128)S(1)} %collective-permute-done.3.shape_a) | copy-start | bytes 196
  29.8 7.9 %collective-permute-start.4 = (s32[1,16]{1,0:T(1,128)S(1)}, s32[1,16]{1,0:T(1,128)S(1)}, u32[]{:S(2)}, u32[]{:S(2)}) collective-permute-start(s32[1,16]{1,0:T(1,128)S(1)} %collective-permute-done.3.shape_a), channel_id=1, source_target_pairs={{0,8},{8,0},{16,24},{24,16},{1,9},{9,1},{17,25},{25,17},{2,10},{10... | collective-permute-start | bytes 200 | tf_op jit(solution)/shard_map/ppermute | solution.py:253
  29.8 7.9 %copy-start.7 = (bf16[1024,256]{1,0:T(8,128)(2,1)}, bf16[1024,256]{1,0:T(8,128)(2,1)S(1)}, u32[]{:S(2)}) copy-start(bf16[1024,256]{1,0:T(8,128)(2,1)S(1)} %collective-permute-done.5.q0) | copy-start | bytes 1572868
  29.9 7.9 %collective-permute-start.6 = (bf16[1,1024,128]{2,1,0:T(8,128)(2,1)S(1)}, bf16[1,1024,128]{2,1,0:T(8,128)(2,1)S(1)}, u32[]{:S(2)}, u32[]{:S(2)}) collective-permute-start(bf16[1,1024,128]{2,1,0:T(8,128)(2,1)S(1)} %fusion.1), channel_id=1, source_target_pairs={{0,8},{8,0},{16,24},{24,16},{1,9},{9,1},{17,25},{25,17},{2,10},{10... | collective-permute-start | bytes 786440 | tf_op jit(solution)/shard_map/ppermute | solution.py:253
  30.4 0.6 copy-start.22
  31.0 0.9 copy-start.16
  37.7 0.6 copy-start.24
  37.7 0.7 copy-start.18
  53.1 16.9 %collective-permute-start.7 = (bf16[2048,128]{1,0:T(8,128)(2,1)}, bf16[2048,128]{1,0:T(8,128)(2,1)S(1)}, u32[]{:S(2)}, u32[]{:S(2)}) collective-permute-start(bf16[2048,128]{1,0:T(8,128)(2,1)} %get-tuple-element.59), channel_id=1, source_target_pairs={{0,16},{8,24},{16,0},{24,8},{1,17},{9,25},{17,1},{25,9},{2,18},{10... | collective-permute-start | bytes 1572872 | tf_op jit(solution)/shard_map/ppermute | solution.py:257
  54.9 15.1 %collective-permute-start.8 = (f32[2,8,128]{2,1,0:T(8,128)}, f32[2,8,128]{2,1,0:T(8,128)S(1)}, u32[]{:S(2)}, u32[]{:S(2)}) collective-permute-start(f32[2,8,128]{2,1,0:T(8,128)} %get-tuple-element.60), channel_id=1, source_target_pairs={{0,16},{8,24},{16,0},{24,8},{1,17},{9,25},{17,1},{25,9},{2,18},{10... | collective-permute-start | bytes 24584 | tf_op jit(solution)/shard_map/ppermute | solution.py:257
  70.0 0.6 copy-start.12
  70.0 0.8 copy-start.2
  101.4 2.1 collective-permute-start.9
  103.6 0.8 copy-start.10
  107.3 14.2 %collective-permute-start.10 = (bf16[128,2048]{1,0:T(8,128)(2,1)}, bf16[128,2048]{1,0:T(8,128)(2,1)S(1)}, u32[]{:S(2)}, u32[]{:S(2)}) collective-permute-start(bf16[128,2048]{1,0:T(8,128)(2,1)} %get-tuple-element.66), channel_id=1, source_target_pairs={{0,2},{1,3},{2,0},{3,1},{4,6},{5,7},{6,4},{7,5},{8,10},{9,11},{10,... | collective-permute-start | bytes 1572872 | tf_op jit(solution)/shard_map/ppermute | solution.py:265
  107.8 13.7 %collective-permute-start.11 = (bf16[128,2048]{1,0:T(8,128)(2,1)}, bf16[128,2048]{1,0:T(8,128)(2,1)S(1)}, u32[]{:S(2)}, u32[]{:S(2)}) collective-permute-start(bf16[128,2048]{1,0:T(8,128)(2,1)} %get-tuple-element.66), channel_id=1, source_target_pairs={{2,4},{3,5},{4,2},{5,3},{10,12},{11,13},{12,10},{13,11},{18,20},{1... | collective-permute-start | bytes 1572872 | tf_op jit(solution)/shard_map/ppermute | solution.py:269
  108.5 14.0 %collective-permute-start.12 = (bf16[128,2048]{1,0:T(8,128)(2,1)}, bf16[128,2048]{1,0:T(8,128)(2,1)S(1)}, u32[]{:S(2)}, u32[]{:S(2)}) collective-permute-start(bf16[128,2048]{1,0:T(8,128)(2,1)} %get-tuple-element.66), channel_id=1, source_target_pairs={{0,1},{1,0},{2,3},{3,2},{4,5},{5,4},{6,7},{7,6},{8,9},{9,8},{10,11... | collective-permute-start | bytes 1572872 | tf_op jit(solution)/shard_map/ppermute | solution.py:261
  111.7 34.0 %copy-start.11 = (bf16[8,128,128]{2,1,0:T(8,128)(2,1)S(1)}, bf16[8,128,128]{2,1,0:T(8,128)(2,1)}, u32[]{:S(2)}) copy-start(bf16[8,128,128]{2,1,0:T(8,128)(2,1)} %get-tuple-element.65) | copy-start | bytes 786436
  122.4 18.1 %collective-permute-start.14 = (bf16[128,2048]{1,0:T(8,128)(2,1)S(1)}, bf16[128,2048]{1,0:T(8,128)(2,1)S(1)}, u32[]{:S(2)}, u32[]{:S(2)}) collective-permute-start(bf16[128,2048]{1,0:T(8,128)(2,1)S(1)} %collective-permute-done.10), channel_id=1, source_target_pairs={{2,4},{3,5},{4,2},{5,3},{10,12},{11,13},{12,10},{13,11},{18,20},{1... | collective-permute-start | bytes 1572872 | tf_op jit(solution)/shard_map/ppermute | solution.py:269
  123.1 17.4 %collective-permute-start.15 = (bf16[128,2048]{1,0:T(8,128)(2,1)S(1)}, bf16[128,2048]{1,0:T(8,128)(2,1)S(1)}, u32[]{:S(2)}, u32[]{:S(2)}) collective-permute-start(bf16[128,2048]{1,0:T(8,128)(2,1)S(1)} %collective-permute-done.10), channel_id=1, source_target_pairs={{0,1},{1,0},{2,3},{3,2},{4,5},{5,4},{6,7},{7,6},{8,9},{9,8},{10,11... | collective-permute-start | bytes 1572872 | tf_op jit(solution)/shard_map/ppermute | solution.py:261
  124.6 15.9 %collective-permute-start.13 = (bf16[128,2048]{1,0:T(8,128)(2,1)S(1)}, bf16[128,2048]{1,0:T(8,128)(2,1)S(1)}, u32[]{:S(2)}, u32[]{:S(2)}) collective-permute-start(bf16[128,2048]{1,0:T(8,128)(2,1)S(1)} %collective-permute-done.11), channel_id=1, source_target_pairs={{0,2},{1,3},{2,0},{3,1},{4,6},{5,7},{6,4},{7,5},{8,10},{9,11},{10,... | collective-permute-start | bytes 1572872 | tf_op jit(solution)/shard_map/ppermute | solution.py:265
  140.5 14.0 %collective-permute-start.16 = (bf16[128,2048]{1,0:T(8,128)(2,1)S(1)}, bf16[128,2048]{1,0:T(8,128)(2,1)S(1)}, u32[]{:S(2)}, u32[]{:S(2)}) collective-permute-start(bf16[128,2048]{1,0:T(8,128)(2,1)S(1)} %collective-permute-done.14), channel_id=1, source_target_pairs={{0,2},{1,3},{2,0},{3,1},{4,6},{5,7},{6,4},{7,5},{8,10},{9,11},{10,... | collective-permute-start | bytes 1572872 | tf_op jit(solution)/shard_map/ppermute | solution.py:265
  142.4 12.0 %collective-permute-start.17 = (bf16[128,2048]{1,0:T(8,128)(2,1)S(1)}, bf16[128,2048]{1,0:T(8,128)(2,1)S(1)}, u32[]{:S(2)}, u32[]{:S(2)}) collective-permute-start(bf16[128,2048]{1,0:T(8,128)(2,1)S(1)} %broadcast_select_fusion.1), channel_id=1, source_target_pairs={{0,1},{1,0},{2,3},{3,2},{4,5},{5,4},{6,7},{7,6},{8,9},{9,8},{10,11... | collective-permute-start | bytes 1572872 | tf_op jit(solution)/shard_map/ppermute | solution.py:261
  145.0 12.6 %collective-permute-start.20 = (bf16[64,2048]{1,0:T(8,128)(2,1)S(1)}, bf16[64,2048]{1,0:T(8,128)(2,1)S(1)}, u32[]{:S(2)}, u32[]{:S(2)}) collective-permute-start(bf16[64,2048]{1,0:T(8,128)(2,1)S(1)} %slice.59), channel_id=1, source_target_pairs={{2,4},{3,5},{4,2},{5,3},{10,12},{11,13},{12,10},{13,11},{18,20},{1... | collective-permute-start | bytes 786440 | tf_op jit(solution)/shard_map/ppermute | solution.py:269
  154.5 6.4 %collective-permute-start.18 = (bf16[64,2048]{1,0:T(8,128)(2,1)S(1)}, bf16[64,2048]{1,0:T(8,128)(2,1)S(1)}, u32[]{:S(2)}, u32[]{:S(2)}) collective-permute-start(bf16[64,2048]{1,0:T(8,128)(2,1)S(1)} %slice.70), channel_id=1, source_target_pairs={{0,1},{1,0},{2,3},{3,2},{4,5},{5,4},{6,7},{7,6},{8,9},{9,8},{10,11... | collective-permute-start | bytes 786440 | tf_op jit(solution)/shard_map/ppermute | solution.py:261
  155.2 6.4 %collective-permute-start.19 = (bf16[64,2048]{1,0:T(8,128)(2,1)S(1)}, bf16[64,2048]{1,0:T(8,128)(2,1)S(1)}, u32[]{:S(2)}, u32[]{:S(2)}) collective-permute-start(bf16[64,2048]{1,0:T(8,128)(2,1)S(1)} %slice.58), channel_id=1, source_target_pairs={{0,2},{1,3},{2,0},{3,1},{4,6},{5,7},{6,4},{7,5},{8,10},{9,11},{10,... | collective-permute-start | bytes 786440 | tf_op jit(solution)/shard_map/ppermute | solution.py:265
  183.5 14.9 %copy-start.17 = (bf16[128,2048]{1,0:T(8,128)(2,1)S(1)}, bf16[128,2048]{1,0:T(8,128)(2,1)}, u32[]{:S(2)}) copy-start(bf16[128,2048]{1,0:T(8,128)(2,1)} %get-tuple-element.85) | copy-start | bytes 1572868
  183.5 16.3 %copy-start.8 = (bf16[128,2048]{1,0:T(8,128)(2,1)S(1)}, bf16[128,2048]{1,0:T(8,128)(2,1)}, u32[]{:S(2)}) copy-start(bf16[128,2048]{1,0:T(8,128)(2,1)} %get-tuple-element.80) | copy-start | bytes 1572868
  183.5 29.1 %copy-start.6 = (bf16[128,2048]{1,0:T(8,128)(2,1)S(1)}, bf16[128,2048]{1,0:T(8,128)(2,1)}, u32[]{:S(2)}) copy-start(bf16[128,2048]{1,0:T(8,128)(2,1)} %get-tuple-element.86) | copy-start | bytes 1572868
  183.5 6.6 %collective-permute-start.21 = (bf16[64,2048]{1,0:T(8,128)(2,1)}, bf16[64,2048]{1,0:T(8,128)(2,1)S(1)}, u32[]{:S(2)}, u32[]{:S(2)}) collective-permute-start(bf16[64,2048]{1,0:T(8,128)(2,1)} %get-tuple-element.81), channel_id=1, source_target_pairs={{0,1},{1,0},{2,3},{3,2},{4,5},{5,4},{6,7},{7,6},{8,9},{9,8},{10,11... | collective-permute-start | bytes 786440 | tf_op jit(solution)/shard_map/ppermute | solution.py:261
  185.0 9.1 %collective-permute-start.22 = (bf16[64,2048]{1,0:T(8,128)(2,1)}, bf16[64,2048]{1,0:T(8,128)(2,1)S(1)}, u32[]{:S(2)}, u32[]{:S(2)}) collective-permute-start(bf16[64,2048]{1,0:T(8,128)(2,1)} %get-tuple-element.82), channel_id=1, source_target_pairs={{0,2},{1,3},{2,0},{3,1},{4,6},{5,7},{6,4},{7,5},{8,10},{9,11},{10,... | collective-permute-start | bytes 786440 | tf_op jit(solution)/shard_map/ppermute | solution.py:265
  185.1 9.0 %collective-permute-start.23 = (bf16[64,2048]{1,0:T(8,128)(2,1)}, bf16[64,2048]{1,0:T(8,128)(2,1)S(1)}, u32[]{:S(2)}, u32[]{:S(2)}) collective-permute-start(bf16[64,2048]{1,0:T(8,128)(2,1)} %get-tuple-element.82), channel_id=1, source_target_pairs={{2,4},{3,5},{4,2},{5,3},{10,12},{11,13},{12,10},{13,11},{18,20},{1... | collective-permute-start | bytes 786440 | tf_op jit(solution)/shard_map/ppermute | solution.py:269
  195.2 31.9 %copy-start.5 = (bf16[128,2048]{1,0:T(8,128)(2,1)S(1)}, bf16[128,2048]{1,0:T(8,128)(2,1)}, u32[]{:S(2)}) copy-start(bf16[128,2048]{1,0:T(8,128)(2,1)} %get-tuple-element.84) | copy-start | bytes 1572868
  195.2 13.7 %collective-permute-start.27 = (bf16[128,2048]{1,0:T(8,128)(2,1)S(1)}, bf16[128,2048]{1,0:T(8,128)(2,1)S(1)}, u32[]{:S(2)}, u32[]{:S(2)}) collective-permute-start(bf16[128,2048]{1,0:T(8,128)(2,1)S(1)} %pad_maximum_fusion.2), channel_id=1, source_target_pairs={{0,2},{1,3},{2,0},{3,1},{4,6},{5,7},{6,4},{7,5},{8,10},{9,11},{10,... | collective-permute-start | bytes 1572872 | tf_op jit(solution)/shard_map/ppermute | solution.py:265
  197.7 39.9 %copy-start.3 = (f32[128,2048]{1,0:T(8,128)S(1)}, f32[128,2048]{1,0:T(8,128)}, u32[]{:S(2)}) copy-start(f32[128,2048]{1,0:T(8,128)} %get-tuple-element.64) | copy-start | bytes 3145732
  197.7 39.9 %copy-start.9 = (bf16[128,2048]{1,0:T(8,128)(2,1)S(1)}, bf16[128,2048]{1,0:T(8,128)(2,1)}, u32[]{:S(2)}) copy-start(bf16[128,2048]{1,0:T(8,128)(2,1)} %get-tuple-element.79) | copy-start | bytes 1572868
  197.7 14.9 %collective-permute-start.26 = (bf16[128,2048]{1,0:T(8,128)(2,1)S(1)}, bf16[128,2048]{1,0:T(8,128)(2,1)S(1)}, u32[]{:S(2)}, u32[]{:S(2)}) collective-permute-start(bf16[128,2048]{1,0:T(8,128)(2,1)S(1)} %pad_maximum_fusion.1), channel_id=1, source_target_pairs={{0,1},{1,0},{2,3},{3,2},{4,5},{5,4},{6,7},{7,6},{8,9},{9,8},{10,11... | collective-permute-start | bytes 1572872 | tf_op jit(solution)/shard_map/ppermute | solution.py:261
  198.4 21.3 %collective-permute-start.25 = (bf16[128,2048]{1,0:T(8,128)(2,1)S(1)}, bf16[128,2048]{1,0:T(8,128)(2,1)S(1)}, u32[]{:S(2)}, u32[]{:S(2)}) collective-permute-start(bf16[128,2048]{1,0:T(8,128)(2,1)S(1)} %copy-done.17), channel_id=1, source_target_pairs={{0,1},{1,0},{2,3},{3,2},{4,5},{5,4},{6,7},{7,6},{8,9},{9,8},{10,11... | collective-permute-start | bytes 1572872 | tf_op jit(solution)/shard_map/ppermute | solution.py:261
  212.9 13.4 %collective-permute-start.28 = (bf16[128,2048]{1,0:T(8,128)(2,1)S(1)}, bf16[128,2048]{1,0:T(8,128)(2,1)S(1)}, u32[]{:S(2)}, u32[]{:S(2)}) collective-permute-start(bf16[128,2048]{1,0:T(8,128)(2,1)S(1)} %add_convert_fusion.3), channel_id=1, source_target_pairs={{0,2},{1,3},{2,0},{3,1},{4,6},{5,7},{6,4},{7,5},{8,10},{9,11},{10,... | collective-permute-start | bytes 1572872 | tf_op jit(solution)/shard_map/ppermute | solution.py:265
  213.6 12.6 %collective-permute-start.29 = (bf16[128,2048]{1,0:T(8,128)(2,1)S(1)}, bf16[128,2048]{1,0:T(8,128)(2,1)S(1)}, u32[]{:S(2)}, u32[]{:S(2)}) collective-permute-start(bf16[128,2048]{1,0:T(8,128)(2,1)S(1)} %add_convert_fusion.3), channel_id=1, source_target_pairs={{2,4},{3,5},{4,2},{5,3},{10,12},{11,13},{12,10},{13,11},{18,20},{1... | collective-permute-start | bytes 1572872 | tf_op jit(solution)/shard_map/ppermute | solution.py:269
  214.3 24.5 %copy-start.1 = (bf16[256,2048]{1,0:T(8,128)(2,1)S(1)}, bf16[256,2048]{1,0:T(8,128)(2,1)}, u32[]{:S(2)}) copy-start(bf16[256,2048]{1,0:T(8,128)(2,1)} %param.23) | copy-start | bytes 3145732
  214.5 15.9 %collective-permute-start.24 = (bf16[128,2048]{1,0:T(8,128)(2,1)S(1)}, bf16[128,2048]{1,0:T(8,128)(2,1)S(1)}, u32[]{:S(2)}, u32[]{:S(2)}) collective-permute-start(bf16[128,2048]{1,0:T(8,128)(2,1)S(1)} %pad_maximum_fusion), channel_id=1, source_target_pairs={{0,1},{1,0},{2,3},{3,2},{4,5},{5,4},{6,7},{7,6},{8,9},{9,8},{10,11... | collective-permute-start | bytes 1572872 | tf_op jit(solution)/shard_map/ppermute | solution.py:261
  226.4 4.0 %collective-permute-start.31 = (bf16[128,2048]{1,0:T(8,128)(2,1)S(1)}, bf16[128,2048]{1,0:T(8,128)(2,1)S(1)}, u32[]{:S(2)}, u32[]{:S(2)}) collective-permute-start(bf16[128,2048]{1,0:T(8,128)(2,1)S(1)} %add_convert_fusion.1), channel_id=1, source_target_pairs={{2,4},{3,5},{4,2},{5,3},{10,12},{11,13},{12,10},{13,11},{18,20},{1... | collective-permute-start | bytes 1572872 | tf_op jit(solution)/shard_map/ppermute | solution.py:269
  227.4 10.2 %collective-permute-start.30 = (bf16[128,2048]{1,0:T(8,128)(2,1)S(1)}, bf16[128,2048]{1,0:T(8,128)(2,1)S(1)}, u32[]{:S(2)}, u32[]{:S(2)}) collective-permute-start(bf16[128,2048]{1,0:T(8,128)(2,1)S(1)} %add_convert_fusion.2), channel_id=1, source_target_pairs={{0,2},{1,3},{2,0},{3,1},{4,6},{5,7},{6,4},{7,5},{8,10},{9,11},{10,... | collective-permute-start | bytes 1572872 | tf_op jit(solution)/shard_map/ppermute | solution.py:265
Sparse Core Ops, SparseCore 0:
  9.5 78.0 all-gather.1

commit v6 on v5

--- a/solution.py
+++ b/solution.py
@@ -247,6 +247,7 @@
 LOG2E = 1.4426950408889634
 SCORE_SCALE = LOG2E / math.sqrt(HEAD)
 VMEM_BIG = 56 * 1024 * 1024
+VMEM_SMALL = 12 * 1024 * 1024
 
 
 def core_swap(array):
@@ -631,6 +632,7 @@
         in_specs=specs + [pl.BlockSpec((extra, BLK), lambda b: (0, 0))],
         out_specs=pl.BlockSpec((MERGE_BLOCKS, 2 * BLK + extra, HEAD), lambda b: (b, 0, 0)),
         out_shape=jax.ShapeDtypeStruct((blocks, 2 * BLK + extra, HEAD), jnp.bfloat16),
+        compiler_params=pltpu.CompilerParams(vmem_limit_bytes=VMEM_SMALL),
         name="merge_parts",
     )(*operands, tab)
 
@@ -666,7 +668,7 @@
             jax.ShapeDtypeStruct((rows, width), jnp.bfloat16),
         ),
         scratch_shapes=[pltpu.VMEM((tokens, depth), jnp.bfloat16)],
-        compiler_params=pltpu.CompilerParams(vmem_limit_bytes=VMEM_BIG),
+        compiler_params=pltpu.CompilerParams(vmem_limit_bytes=VMEM_SMALL),
         name="project",
     )(attended, weights)
 
@@ -686,11 +688,14 @@
             jax.ShapeDtypeStruct(keep.shape, jnp.float32),
             jax.ShapeDtypeStruct(keep.shape, jnp.bfloat16),
         ),
+        compiler_params=pltpu.CompilerParams(vmem_limit_bytes=VMEM_SMALL),
         name="norm_rows",
     )(keep, got, residual, gain)
 
 
 EXP_DEV = 4
+VMEM_STAGE = 2 * 1024 * 1024
+EXPERT_VMEM = 8 * 1024 * 1024
 SLOTS = 32
 SLOT_Z = ((0, 1, 2, 3), (1, 0, 3, 2), (2, 3, 0, 1), (3, 2, 1, 0))
 
@@ -739,65 +744,87 @@
         ],
         out_specs=[pl.BlockSpec((8, BLK, BLK), lambda i: (0, 0, 0))] * 2,
         out_shape=(shape, shape),
+        compiler_params=pltpu.CompilerParams(vmem_limit_bytes=VMEM_SMALL),
         name="route",
     )(place, heads)
+
+
+def stage_kernel(source, held, sems):
+    copies = [pltpu.make_async_copy(source.at[i], held.at[i], sems.at[i]) for i in range(EXP_DEV)]
+    for copy in copies:
+        copy.start()
+    for copy in copies:
+        copy.wait()
+
+
+def stage(weights):
+    return pl.pallas_call(
+        stage_kernel,
+        in_specs=[pl.BlockSpec(memory_space=pltpu.HBM)],
+        out_specs=pl.BlockSpec(memory_space=pltpu.VMEM),
+        out_shape=jax.ShapeDtypeStruct(weights.shape, weights.dtype),
+        scratch_shapes=[pltpu.SemaphoreType.DMA((EXP_DEV,))],
+        compiler_params=pltpu.CompilerParams(vmem_limit_bytes=VMEM_STAGE),
+        cost_estimate=pl.CostEstimate(flops=0, bytes_accessed=2 * weights.size, transcendentals=0),
+        name="stage",
+    )(weights)
 
 
 def experts_kernel(*refs):
     picked = refs[:8]
     give_ref, wg, wu, wd = refs[8:12]
     outs, rows_out = refs[12:-1], refs[-1]
-    expert = pl.program_id(0)
-    rows = jnp.concatenate([part[...] for part in picked], axis=0)
     contract = (((1,), (1,)), ((), ()))
-    gate_h = lax.dot_general(rows, wg[0], contract, preferred_element_type=jnp.float32)
-    up_h = lax.dot_general(rows, wu[0], contract, preferred_element_type=jnp.float32)
-    hidden = (gate_h / (1.0 + jnp.exp(-gate_h)) * up_h).astype(jnp.bfloat16)
-    out = jnp.dot(hidden, wd[0], preferred_element_type=jnp.float32).astype(jnp.bfloat16)
-    here = pl.ds(pl.multiple_of(expert * SLOTS, SLOTS), SLOTS)
+
+    def run(expert, carry):
+        here = pl.ds(pl.multiple_of(expert * SLOTS, SLOTS), SLOTS)
+        rows = jnp.concatenate([part[here, :] for part in picked], axis=0)
+        gate_h = lax.dot_general(wg[expert], rows, contract, preferred_element_type=jnp.float32)
+        up_h = lax.dot_general(wu[expert], rows, contract, preferred_element_type=jnp.float32)
+        hidden = jnp.transpose((gate_h / (1.0 + jnp.exp(-gate_h)) * up_h).astype(jnp.bfloat16))
+        out = jnp.dot(hidden, wd[expert], preferred_element_type=jnp.float32).astype(jnp.bfloat16)
+        for slot in range(8):
+            rows_out[slot, here, :] = out[slot * SLOTS : (slot + 1) * SLOTS]
+        return carry
+
+    lax.fori_loop(0, EXP_DEV, run, 0)
     for slot in range(8):
-        rows_out[slot, here, :] = out[slot * SLOTS : (slot + 1) * SLOTS]
-
-    @pl.when(expert == EXP_DEV - 1)
-    def last():
-        for slot in range(8):
-            out = jnp.dot(give_ref[slot], rows_out[slot], preferred_element_type=jnp.float32)
-            out = out.astype(jnp.bfloat16)
-            if slot < 7:
-                outs[slot][...] = out
-            else:
-                outs[7][...] = out[: BLK // 2]
-                outs[8][...] = out[BLK // 2 :]
+        out = jnp.dot(give_ref[slot], rows_out[slot], preferred_element_type=jnp.float32)
+        out = out.astype(jnp.bfloat16)
+        if slot < 7:
+            outs[slot][...] = out
+        else:
+            outs[7][...] = out[: BLK // 2]
+            outs[8][...] = out[BLK // 2 :]
 
 
 def run_experts(picked, give, w_gate, w_up, w_down):
     width = picked[0].shape[1]
-    hidden = w_down.shape[1]
-    once = pl.Buffered(1)
     heights = [BLK] * 7 + [BLK // 2] * 2
+    vmem = pl.BlockSpec(memory_space=pltpu.VMEM)
     return pl.pallas_call(
         experts_kernel,
-        grid=(EXP_DEV,),
-        in_specs=[pl.BlockSpec((SLOTS, width), lambda j: (j, 0))] * 8
-        + [pl.BlockSpec((8, BLK, BLK), lambda j: (0, 0, 0))]
-        + [pl.BlockSpec((1, hidden, width), lambda j: (j, 0, 0))] * 3,
-        out_specs=[pl.BlockSpec((n, width), lambda j: (0, 0), pipeline_mode=once) for n in heights],
+        in_specs=[vmem] * 12,
+        out_specs=[vmem] * 9,
         out_shape=[jax.ShapeDtypeStruct((n, width), jnp.bfloat16) for n in heights],
         scratch_shapes=[pltpu.VMEM((8, EXP_DEV * SLOTS, width), jnp.bfloat16)],
-        compiler_params=pltpu.CompilerParams(vmem_limit_bytes=VMEM_BIG),
+        compiler_params=pltpu.CompilerParams(vmem_limit_bytes=EXPERT_VMEM),
         name="experts",
-    )(*picked, give, w_gate.transpose(0, 2, 1), w_up.transpose(0, 2, 1), w_down)
+    )(*picked, give, w_gate, w_up, w_down)
 
 
 def together(*arrays):
     return lax.optimization_barrier(arrays)
 
 
-def gather_rows(middle, own):
+def gather_rows(middle, own, weights):
     half = own.shape[0] // 2
-    outer0, middle0, there0 = together(outer_swap(own), middle_swap(own), y_swap(own))
-    outer1, middle1, there1 = together(
-        outer_swap(middle0), middle_swap(outer0), y_swap(outer0)
+    own, *weights = together(own, *weights)
+    outer0, middle0, there0, gate = together(
+        outer_swap(own), middle_swap(own), y_swap(own), stage(weights[0])
+    )
+    outer1, middle1, there1, down = together(
+        outer_swap(middle0), middle_swap(outer0), y_swap(outer0), stage(weights[2])
     )
     second = jnp.where(middle, middle1, outer1)
     outer2, there2 = together(outer_swap(middle1), y_swap(second))
@@ -806,7 +833,7 @@
         y_swap(third[:half]), outer_swap(there2[half:]), middle_swap(there0[half:])
     )
     late = jnp.where(middle, late_middle, late_outer)
-    return [own, outer0, second, third], [there0, there1, there2, there3, late]
+    return [own, outer0, second, third], [there0, there1, there2, there3, late], (gate, weights[1], down)
 
 
 def pick_rows(pick, parts):
@@ -884,14 +911,12 @@
     other_shape = core_swap(shape)
     far_shape = x_swap(shape)
     far_queries = x_swap(queries)
-    far_other_shape = core_swap(far_shape)
 
     proj_rows = lax.dynamic_slice_in_dim(out_proj, core * HEAD, HEAD, 0)
     proj_rows = lax.all_gather(proj_rows, "exp", axis=0, tiled=True)
 
     theirs, prefix_theirs = split_theirs(place, queries, keys, values, prefix_keys, prefix_values)
     other, prefix_other = core_swap(theirs), core_swap(prefix_theirs)
-    far_other = core_swap(jnp.where(core == 0, far_queries[:, HEAD:], far_queries[:, :HEAD])[None])
 
     def prefix(shape_a, shape_b, q0, q1, dtype):
         return prefix_attend(
@@ -901,6 +926,9 @@
     tab = jnp.concatenate([expert_ids.T.astype(jnp.bfloat16), expert_gates.T], axis=0)
     tab = jnp.pad(tab, ((0, 16 - tab.shape[0]), (0, 0)))
     suffix = suffix_attend(place, shape, other_shape, queries, keys, values, other)
+    unused, far_queries, far_shape = together(suffix[1], far_queries, far_shape)
+    far_send = jnp.where(core == 0, far_queries[:, HEAD:], far_queries[:, :HEAD])[None]
+    far_other, far_other_shape = core_swap(far_send), core_swap(far_shape)
     far = prefix(far_shape, far_other_shape, far_queries, far_other, jnp.bfloat16)
     back = (x_swap(far[0]), x_swap(far[1]))
     near = prefix(shape, other_shape, queries, other, jnp.float32)
@@ -910,9 +938,10 @@
     keep, send = project(heads, proj_rows)
     stream, normed = norm_rows(keep, core_swap(send), residual, gain)
     pick, give = route(place, heads)
-    here, there = gather_rows(middle, normed)
+    weights = (w_gate.transpose(0, 2, 1), w_up.transpose(0, 2, 1), w_down)
+    here, there, weights = gather_rows(middle, normed, weights)
     picked = pick_rows(pick[:4], here) + pick_rows(pick[4:], there)
-    sums = run_experts(picked, give, w_gate, w_up, w_down)
+    sums = run_experts(picked, give, *weights)
     return scatter_sums(middle, stream, sums[:4], sums[4:]).astype(jnp.bfloat16)
 
 

time: 247 us -> 231 us (0.935)
  waiting for transfers between devices: 77.8 us -> 61.3 us
  Pallas kernels: 72.5 us -> 57.8 us
  local copies, waits for them, and re-layouts: 9.12 us -> 18.3 us
  starting transfers between devices: 31.9 us -> 40.5 us
  matrix products: 11.6 us -> 4.17 us
  blocking collectives: 23.4 us -> 28.6 us
    unnamed x50, local copies, waits for them, and re-layouts: 4.92 us -> 17.3 us
    ppermute x8, waiting for transfers between devices: 42.6 us -> 33.6 us  [outer_swap(): return lax.ppermute(array, 'exp', [(i, i ^ 2) for i in range(8)])]
    ppermute x4, waiting for transfers between devices: 10.8 us -> 3.17 us  [x_swap(): return lax.ppermute(array, 'req', [(i, i ^ 2) for i in range(4)])]
    pallas_call x1 -> x3, Pallas kernels: 20.4 us -> 13.3 us  [the longest x1 11.6 us: run_experts(): pl.pallas_call(experts_kernel, in_specs=[vmem] * 12, out_specs=[vmem] * 9...]
    dot_general x7, matrix products: 10.2 us -> 3.55 us  [pick_rows(): jnp.dot(matrix, part, preferred_element_type=jnp.float32)]
    ppermute x8, starting transfers between devices: 13.7 us -> 20.1 us  [outer_swap(): return lax.ppermute(array, 'exp', [(i, i ^ 2) for i in range(8)])]
    all_to_all x1, blocking collectives: 23.4 us -> 28.6 us  [block_device(): lax.all_to_all(attended, 'exp', split_axis=0, concat_axis=0, tiled=True)]
    pallas_call x1, Pallas kernels: 2.91 us -> 0.42 us  [norm_rows(): pl.pallas_call(norm_kernel, out_shape=(jax.ShapeDtypeStruct(keep.shape, j...]
  transfers between devices with their start and end apart: 33 -> 33, of which waited for: 15 -> 18; matrix products, arithmetic and copies ran while one was open for 7% -> 3% of each run, Pallas kernels for 18% -> 19%
where the time goes in v6:
time: 231 us; the launch traced here: 228 us
  waiting for transfers between devices  61.3 us (27%)
  Pallas kernels  57.8 us (25%)
  starting transfers between devices  40.5 us (18%)
  blocking collectives  28.6 us (12%)
  local copies, waits for them, and re-layouts  18.3 us (8%)
  between operations  13.9 us (6%)
  matrix products  4.17 us (2%)
  other arithmetic  3.76 us (2%)
    ppermute x8, waiting for transfers between devices, outer_swap(): return lax.ppermute(array, 'exp', [(i, i ^ 2) for i in range(8)])  33.6 us
    pallas_call x2, Pallas kernels, prefix_attend(): pl.pallas_call(prefix_kernel, in_specs=[smem] * 3 + [anywhere] * 5, out_s...  29.6 us
    all_to_all x1, blocking collectives, block_device(): lax.all_to_all(attended, 'exp', split_axis=0, concat_axis=0, tiled=True)  28.6 us
    ppermute x8, waiting for transfers between devices, y_swap(): return lax.ppermute(array, 'exp', [(i, i ^ 1) for i in range(8)])  20.4 us
    ppermute x8, starting transfers between devices, outer_swap(): return lax.ppermute(array, 'exp', [(i, i ^ 2) for i in range(8)])  20.1 us
    unnamed x50, local copies, waits for them, and re-layouts  17.3 us
    pallas_call x1, Pallas kernels, run_experts(): pl.pallas_call(experts_kernel, in_specs=[vmem] * 12, out_specs=[vmem] * 9...  11.6 us
    ppermute x8, starting transfers between devices, y_swap(): return lax.ppermute(array, 'exp', [(i, i ^ 1) for i in range(8)])  9.2 us
  transfers between devices with their start and end apart: 33, of which 18 were waited for; matrix products, arithmetic and copies ran while one was open for 3% of the time, Pallas kernels for 19%

profile of v6, /device:TPU:0, one launch (start us, length us, event | category | flops | bytes accessed | tf_op | source)
XLA Modules:
  0.0 228.4 jit_solution(8023904184598408726)
XLA Ops:
  6.5 1.2 copy-done
  7.8 0.9 constant_dynamic-slice_fusion
  8.7 0.7 pad_add_fusion.sc_ref
  9.3 4.9 %split_theirs.1 = (bf16[3,1024,128]{2,1,0:T(8,128)(2,1)}, bf16[2,4,1024,128]{3,2,1,0:T(8,128)(2,1)}) custom-call(s32[2]{0:T(128)} %pad_add_fusion.sc_ref, bf16[1024,256]{1,0:T(8,128)(2,1)} %q0.1, bf16[1024,256]{1,0:T(8,128)(2,1)} %k.3, bf16[1024,256]{1,0:T(8,128)(2,1)} %v.3, bf16[4,1024,256]{2,1,0:T(8,128)(2,1)} %pk.5, bf16[4,1024,256]{2,1,0:T(8,128)(2,1)} %pv.5), custom_call_target="tpu_custom_call" | custom-call | tf_op jit(solution)/shard_map/split_theirs/pallas_call | solution.py:285
  14.7 2.9 %collective-permute-start.3 = (bf16[1024,256]{1,0:T(8,128)(2,1)}, bf16[1024,256]{1,0:T(8,128)(2,1)S(1)}, u32[]{:S(2)}, u32[]{:S(2)}) collective-permute-start(bf16[1024,256]{1,0:T(8,128)(2,1)} %q0.1), channel_id=1, source_target_pairs={{0,16},{8,24},{16,0},{24,8},{1,17},{9,25},{17,1},{25,9},{2,18},{10... | collective-permute-start | bytes 1572872 | tf_op jit(solution)/shard_map/ppermute | solution.py:258
  17.6 0.7 pad_add_fusion.1.shape_a
  18.5 1.1 collective-permute-done.shape_b
  20.1 0.9 copy-done.16
  21.0 5.9 %suffix_attend.1 = (f32[2048,128]{1,0:T(8,128)}, f32[2,8,128]{2,1,0:T(8,128)}) custom-call(s32[2]{0:T(128)} %pad_add_fusion.sc_ref, s32[1,16]{1,0:T(1,128)} %copy-done.18, s32[1,16]{1,0:T(1,128)} %copy-done.19, bf16[1024,256]{1,0:T(8,128)(2,1)} %q0.1, bf16[1024,256]{1,0:T(8,128)(2,1)} %k.3, bf16[1024,256]{1,0:T(8,128)(2,1)} %v.3, ...), custom_call_target="tpu_custom_call" | custom-call | flops 4294967296 | bytes 1048576 | tf_op jit(solution)/shard_map/suffix_attend/pallas_call | solution.py:564
  26.9 3.2 %collective-permute-done.4.shape_a = s32[1,16]{1,0:T(1,128)S(1)} collective-permute-done((s32[1,16]{1,0:T(1,128)S(1)}, s32[1,16]{1,0:T(1,128)S(1)}, u32[]{:S(2)}, u32[]{:S(2)}) %collective-permute-start.4) | collective-permute-done | bytes 96 | tf_op jit(solution)/shard_map/ppermute | solution.py:258
  30.8 0.9 collective-permute-done.5.shape_b
  32.4 1.4 copy-done.15
  33.8 14.7 %prefix_attend.3 = (bf16[2048,128]{1,0:T(8,128)(2,1)}, f32[2,8,128]{2,1,0:T(8,128)}) custom-call(s32[2]{0:T(128)} %pad_add_fusion.sc_ref, s32[1,16]{1,0:T(1,128)} %copy-done.20, s32[1,16]{1,0:T(1,128)} %copy-done.21, bf16[1024,256]{1,0:T(8,128)(2,1)} %copy-done.11, bf16[1,1024,128]{2,1,0:T(8,128)(2,1)} %copy-done.17, bf16[4,1024,256]{2,1,0:T(8,128)(2,1)} %pk.5, ...), custom_call_target="tpu_custom_call" | custom-call | flops 8589934592 | bytes 4194304 | tf_op jit(solution)/shard_map/prefix_attend/pallas_call | solution.py:478
  48.5 1.8 collective-permute-start.8
  50.6 14.9 %prefix_attend.2 = (f32[2048,128]{1,0:T(8,128)}, f32[2,8,128]{2,1,0:T(8,128)}) custom-call(s32[2]{0:T(128)} %pad_add_fusion.sc_ref, s32[1,16]{1,0:T(1,128)} %copy-done.18, s32[1,16]{1,0:T(1,128)} %copy-done.19, bf16[1024,256]{1,0:T(8,128)(2,1)} %q0.1, bf16[3,1024,128]{2,1,0:T(8,128)(2,1)} %copy-done.16, bf16[4,1024,256]{2,1,0:T(8,128)(2,1)} %pk.5, ...), custom_call_target="tpu_custom_call" | custom-call | flops 8589934592 | bytes 4194304 | tf_op jit(solution)/shard_map/prefix_attend/pallas_call | solution.py:478
  65.6 1.2 copy-done.5
  66.8 0.7 copy-done.9
  67.5 1.0 merge_parts.1
  68.5 28.6 %all_to_all.5.a_ref.tab_ref = bf16[8,272,128]{2,1,0:T(8,128)(2,1)S(1)} all-to-all(bf16[8,272,128]{2,1,0:T(8,128)(2,1)S(1)} %merge_parts.1), channel_id=1, replica_groups=mesh['req'=4,'exp'=8] {'exp'}, dimensions={0} | all-to-all | bytes 1114112 | tf_op jit(solution)/shard_map/all_to_all | solution.py:937
  97.2 2.2 copy-done.6
  99.4 2.0 project.1
  101.4 1.9 collective-permute-done.9.got
  103.7 1.5 collective-permute-start.12
  105.2 1.5 collective-permute-start.11
  106.7 1.5 collective-permute-start.10
  108.2 0.8 route.1
  109.0 4.3 %copy-done.2 = bf16[4,2048,704]{1,2,0:T(8,128)(2,1)S(1)} copy-done((bf16[4,2048,704]{1,2,0:T(8,128)(2,1)S(1)}, bf16[4,2048,704]{1,2,0:T(8,128)(2,1)}, u32[]{:S(2)}) %copy-start.2) | copy-done | bytes 11534360
  113.3 0.8 stage.2.refs_9_
  114.1 3.7 %collective-permute-done.12 = bf16[128,2048]{1,0:T(8,128)(2,1)S(1)} collective-permute-done((bf16[128,2048]{1,0:T(8,128)(2,1)S(1)}, bf16[128,2048]{1,0:T(8,128)(2,1)S(1)}, u32[]{:S(2)}, u32[]{:S(2)}) %collective-permute-start.12) | collective-permute-done | bytes 524320 | tf_op jit(solution)/shard_map/ppermute | solution.py:262
  117.8 2.7 %collective-permute-done.10 = bf16[128,2048]{1,0:T(8,128)(2,1)} collective-permute-done((bf16[128,2048]{1,0:T(8,128)(2,1)S(1)}, bf16[128,2048]{1,0:T(8,128)(2,1)}, u32[]{:S(2)}, u32[]{:S(2)}) %collective-permute-start.10) | collective-permute-done | bytes 524320 | tf_op jit(solution)/shard_map/ppermute | solution.py:266
  121.1 0.7 collective-permute-start.14
  121.8 4.0 %collective-permute-start.13 = (bf16[128,2048]{1,0:T(8,128)(2,1)}, bf16[128,2048]{1,0:T(8,128)(2,1)S(1)}, u32[]{:S(2)}, u32[]{:S(2)}) collective-permute-start(bf16[128,2048]{1,0:T(8,128)(2,1)} %collective-permute-done.11), channel_id=1, source_target_pairs={{0,2},{1,3},{2,0},{3,1},{4,6},{5,7},{6,4},{7,5},{8,10},{9,11},{10,... | collective-permute-start | bytes 1572872 | tf_op jit(solution)/shard_map/ppermute | solution.py:266
  125.8 4.3 %copy-done.3 = bf16[4,704,2048]{2,1,0:T(8,128)(2,1)S(1)} copy-done((bf16[4,704,2048]{2,1,0:T(8,128)(2,1)S(1)}, bf16[4,704,2048]{2,1,0:T(8,128)(2,1)}, u32[]{:S(2)}) %copy-start.3) | copy-done | bytes 11534360
  130.1 0.8 stage.3.refs_11_
  131.2 1.8 convolution_convert_fusion.5.refs_1_
  133.1 3.1 %collective-permute-done.13 = bf16[128,2048]{1,0:T(8,128)(2,1)S(1)} collective-permute-done((bf16[128,2048]{1,0:T(8,128)(2,1)}, bf16[128,2048]{1,0:T(8,128)(2,1)S(1)}, u32[]{:S(2)}, u32[]{:S(2)}) %collective-permute-start.13) | collective-permute-done | bytes 524320 | tf_op jit(solution)/shard_map/ppermute | solution.py:266
  136.2 1.9 collective-permute-start.16
  138.2 1.5 collective-permute-start.17
  139.9 0.7 collective-permute-start.20
  141.2 7.6 %collective-permute-done.17 = bf16[128,2048]{1,0:T(8,128)(2,1)S(1)} collective-permute-done((bf16[128,2048]{1,0:T(8,128)(2,1)S(1)}, bf16[128,2048]{1,0:T(8,128)(2,1)S(1)}, u32[]{:S(2)}, u32[]{:S(2)}) %collective-permute-start.17) | collective-permute-done | bytes 524320 | tf_op jit(solution)/shard_map/ppermute | solution.py:262
  148.9 1.7 collective-permute-start.19
  150.6 1.4 collective-permute-start.18
  152.6 2.8 %collective-permute-done.19 = bf16[64,2048]{1,0:T(8,128)(2,1)S(1)} collective-permute-done((bf16[64,2048]{1,0:T(8,128)(2,1)S(1)}, bf16[64,2048]{1,0:T(8,128)(2,1)S(1)}, u32[]{:S(2)}, u32[]{:S(2)}) %collective-permute-start.19) | collective-permute-done | bytes 262176 | tf_op jit(solution)/shard_map/ppermute | solution.py:266
  155.4 1.6 collective-permute-done.18
  157.6 11.6 %experts.1 = (bf16[128,2048]{1,0:T(8,128)(2,1)S(1)}, bf16[128,2048]{1,0:T(8,128)(2,1)S(1)}, bf16[128,2048]{1,0:T(8,128)(2,1)S(1)}, bf16[128,2048]{1,0:T(8,128)(2...) custom-call(bf16[128,2048]{1,0:T(8,128)(2,1)S(1)} %convolution_conve, ...), custom_call_target="tpu_custom_call" | custom-call | tf_op jit(solution)/shard_map/experts/pallas_call | solution.py:805
  169.3 1.5 collective-permute-start.21
  170.7 0.7 collective-permute-start.23
  171.4 2.3 collective-permute-start.22
  173.7 2.0 collective-permute-done.21
  175.7 5.1 %collective-permute-done.22 = bf16[64,2048]{1,0:T(8,128)(2,1)S(1)} collective-permute-done((bf16[64,2048]{1,0:T(8,128)(2,1)S(1)}, bf16[64,2048]{1,0:T(8,128)(2,1)S(1)}, u32[]{:S(2)}, u32[]{:S(2)}) %collective-permute-start.22) | collective-permute-done | bytes 262176 | tf_op jit(solution)/shard_map/ppermute | solution.py:266
  181.0 2.1 collective-permute-start.27
  183.2 0.7 collective-permute-start.26
  183.9 1.4 collective-permute-start.25
  185.4 6.4 %collective-permute-done.27 = bf16[128,2048]{1,0:T(8,128)(2,1)S(1)} collective-permute-done((bf16[128,2048]{1,0:T(8,128)(2,1)S(1)}, bf16[128,2048]{1,0:T(8,128)(2,1)S(1)}, u32[]{:S(2)}, u32[]{:S(2)}) %collective-permute-start.27) | collective-permute-done | bytes 524320 | tf_op jit(solution)/shard_map/ppermute | solution.py:266
  191.8 3.0 %collective-permute-done.26 = bf16[128,2048]{1,0:T(8,128)(2,1)S(1)} collective-permute-done((bf16[128,2048]{1,0:T(8,128)(2,1)S(1)}, bf16[128,2048]{1,0:T(8,128)(2,1)S(1)}, u32[]{:S(2)}, u32[]{:S(2)}) %collective-permute-start.26) | collective-permute-done | bytes 524320 | tf_op jit(solution)/shard_map/ppermute | solution.py:262
  195.0 0.7 collective-permute-start.29
  195.8 4.8 %collective-permute-start.28 = (bf16[128,2048]{1,0:T(8,128)(2,1)S(1)}, bf16[128,2048]{1,0:T(8,128)(2,1)S(1)}, u32[]{:S(2)}, u32[]{:S(2)}) collective-permute-start(bf16[128,2048]{1,0:T(8,128)(2,1)S(1)} %add_convert_fusion.3), channel_id=1, source_target_pairs={{0,2},{1,3},{2,0},{3,1},{4,6},{5,7},{6,4},{7,5},{8,10},{9,11},{10,... | collective-permute-start | bytes 1572872 | tf_op jit(solution)/shard_map/ppermute | solution.py:266
  200.7 0.7 collective-permute-start.24
  201.4 2.5 %collective-permute-done.25 = bf16[128,2048]{1,0:T(8,128)(2,1)S(1)} collective-permute-done((bf16[128,2048]{1,0:T(8,128)(2,1)S(1)}, bf16[128,2048]{1,0:T(8,128)(2,1)S(1)}, u32[]{:S(2)}, u32[]{:S(2)}) %collective-permute-start.25) | collective-permute-done | bytes 524320 | tf_op jit(solution)/shard_map/ppermute | solution.py:262
  203.9 6.8 %collective-permute-done.28 = bf16[128,2048]{1,0:T(8,128)(2,1)S(1)} collective-permute-done((bf16[128,2048]{1,0:T(8,128)(2,1)S(1)}, bf16[128,2048]{1,0:T(8,128)(2,1)S(1)}, u32[]{:S(2)}, u32[]{:S(2)}) %collective-permute-start.28) | collective-permute-done | bytes 524320 | tf_op jit(solution)/shard_map/ppermute | solution.py:266
  211.1 1.8 collective-permute-start.30
  212.9 0.7 collective-permute-start.31
  213.6 6.7 %collective-permute-done.30 = bf16[128,2048]{1,0:T(8,128)(2,1)S(1)} collective-permute-done((bf16[128,2048]{1,0:T(8,128)(2,1)S(1)}, bf16[128,2048]{1,0:T(8,128)(2,1)S(1)}, u32[]{:S(2)}, u32[]{:S(2)}) %collective-permute-start.30) | collective-permute-done | bytes 524320 | tf_op jit(solution)/shard_map/ppermute | solution.py:266
  220.3 1.2 add_convert_fusion
  (101 shorter events, 7.6 us)
Async XLA Ops:
  6.5 1.2 copy-start
  6.5 90.6 %all-gather.2.cloned.1.call-start = ((), (), s32[]{:S(2)}) async-start(), calls=%async_computation.1 | async-start | bytes 4718592 | tf_op jit(solution)/shard_map/all_gather | solution.py:916
  8.6 21.5 %copy-start.13 = (s32[128,4]{0,1:T(4,128)S(1)}, s32[128,4]{0,1:T(4,128)}, u32[]{:S(2)}) copy-start(s32[128,4]{0,1:T(4,128)} %param.25) | copy-start | bytes 6148
  8.6 21.6 %copy-start.14 = (bf16[128,4]{0,1:T(4,128)(2,1)S(1)}, bf16[128,4]{0,1:T(4,128)(2,1)}, u32[]{:S(2)}) copy-start(bf16[128,4]{0,1:T(4,128)(2,1)} %param.26) | copy-start | bytes 3076
  8.6 22.1 %copy-start.12 = (bf16[2048]{0:T(1024)(128)(2,1)S(1)}, bf16[2048]{0:T(1024)(128)(2,1)}, u32[]{:S(2)}) copy-start(bf16[2048]{0:T(1024)(128)(2,1)} %param.24) | copy-start | bytes 12292
  14.2 17.5 %collective-permute-start.2 = (bf16[2,4,1024,128]{3,2,1,0:T(8,128)(2,1)}, bf16[2,4,1024,128]{3,2,1,0:T(8,128)(2,1)S(1)}, u32[]{:S(2)}, u32[]{:S(2)}) collective-permute-start(bf16[2,4,1024,128]{3,2,1,0:T(8,128)(2,1)} %get-tuple-element.63), channel_id=1, source_target_pairs={{0,8},{8,0},{16,24},{24,16},{1,9},{9,1},{17,25},{25,17},{2,10},{10... | collective-permute-start | bytes 6291464 | tf_op jit(solution)/shard_map/ppermute | solution.py:254
  14.6 5.1 %collective-permute-start.1 = (bf16[3,1024,128]{2,1,0:T(8,128)(2,1)}, bf16[3,1024,128]{2,1,0:T(8,128)(2,1)S(1)}, u32[]{:S(2)}, u32[]{:S(2)}) collective-permute-start(bf16[3,1024,128]{2,1,0:T(8,128)(2,1)} %get-tuple-element.60), channel_id=1, source_target_pairs={{0,8},{8,0},{16,24},{24,16},{1,9},{9,1},{17,25},{25,17},{2,10},{10... | collective-permute-start | bytes 2359304 | tf_op jit(solution)/shard_map/ppermute | solution.py:254
  14.7 15.4 %collective-permute-start.3 = (bf16[1024,256]{1,0:T(8,128)(2,1)}, bf16[1024,256]{1,0:T(8,128)(2,1)S(1)}, u32[]{:S(2)}, u32[]{:S(2)}) collective-permute-start(bf16[1024,256]{1,0:T(8,128)(2,1)} %q0.1), channel_id=1, source_target_pairs={{0,16},{8,24},{16,0},{24,8},{1,17},{9,25},{17,1},{25,9},{2,18},{10... | collective-permute-start | bytes 1572872 | tf_op jit(solution)/shard_map/ppermute | solution.py:258
  18.4 1.4 copy-start.18
  18.4 11.7 %collective-permute-start.4 = (s32[1,16]{1,0:T(1,128)S(1)}, s32[1,16]{1,0:T(1,128)S(1)}, u32[]{:S(2)}, u32[]{:S(2)}) collective-permute-start(s32[1,16]{1,0:T(1,128)S(1)} %pad_add_fusion.1.shape_a), channel_id=1, source_target_pairs={{0,16},{8,24},{16,0},{24,8},{1,17},{9,25},{17,1},{25,9},{2,18},{10... | collective-permute-start | bytes 200 | tf_op jit(solution)/shard_map/ppermute | solution.py:258
  18.4 1.2 collective-permute-start
  19.6 0.6 copy-start.19
  20.1 0.9 copy-start.16
  30.0 1.7 copy-start.20
  30.1 1.7 copy-start.11
  30.1 1.6 collective-permute-start.6
  30.2 1.5 collective-permute-start.5
  31.7 0.5 copy-start.21
  31.7 0.7 copy-start.17
  32.4 1.4 copy-start.15
  48.5 17.1 %collective-permute-start.8 = (f32[2,8,128]{2,1,0:T(8,128)}, f32[2,8,128]{2,1,0:T(8,128)S(1)}, u32[]{:S(2)}, u32[]{:S(2)}) collective-permute-start(f32[2,8,128]{2,1,0:T(8,128)} %get-tuple-element.70), channel_id=1, source_target_pairs={{0,16},{8,24},{16,0},{24,8},{1,17},{9,25},{17,1},{25,9},{2,18},{10... | collective-permute-start | bytes 24584 | tf_op jit(solution)/shard_map/ppermute | solution.py:258
  50.3 15.3 %copy-start.4 = (f32[2048,128]{1,0:T(8,128)S(1)}, f32[2048,128]{1,0:T(8,128)}, u32[]{:S(2)}) copy-start(f32[2048,128]{1,0:T(8,128)} %get-tuple-element.61.refs_0_.refs_6_) | copy-start | bytes 3145732
  50.3 15.3 %copy-start.8 = (f32[2,8,128]{2,1,0:T(8,128)S(1)}, f32[2,8,128]{2,1,0:T(8,128)}, u32[]{:S(2)}) copy-start(f32[2,8,128]{2,1,0:T(8,128)} %get-tuple-element.62.refs_1_.refs_7_) | copy-start | bytes 24580
  50.3 15.3 %collective-permute-start.7 = (bf16[2048,128]{1,0:T(8,128)(2,1)}, bf16[2048,128]{1,0:T(8,128)(2,1)S(1)}, u32[]{:S(2)}, u32[]{:S(2)}) collective-permute-start(bf16[2048,128]{1,0:T(8,128)(2,1)} %get-tuple-element.69), channel_id=1, source_target_pairs={{0,16},{8,24},{16,0},{24,8},{1,17},{9,25},{17,1},{25,9},{2,18},{10... | collective-permute-start | bytes 1572872 | tf_op jit(solution)/shard_map/ppermute | solution.py:258
  50.6 52.7 %copy-start.7 = (bf16[128,2048]{1,0:T(8,128)(2,1)S(1)}, bf16[128,2048]{1,0:T(8,128)(2,1)}, u32[]{:S(2)}) copy-start(bf16[128,2048]{1,0:T(8,128)(2,1)} %residual.1) | copy-start | bytes 1572868
  65.5 42.6 %copy-start.10 = (s32[2]{0:T(128)S(1)}, s32[2]{0:T(128)}, u32[]{:S(2)}) copy-start(s32[2]{0:T(128)} %pad_add_fusion.sc_ref) | copy-start | bytes 28
  65.6 1.2 copy-start.5
  66.8 0.7 copy-start.9
  97.2 2.2 copy-start.6
  101.3 2.0 collective-permute-start.9
  103.7 14.0 %collective-permute-start.12 = (bf16[128,2048]{1,0:T(8,128)(2,1)S(1)}, bf16[128,2048]{1,0:T(8,128)(2,1)S(1)}, u32[]{:S(2)}, u32[]{:S(2)}) collective-permute-start(bf16[128,2048]{1,0:T(8,128)(2,1)S(1)} %get-tuple-element.77), channel_id=1, source_target_pairs={{0,1},{1,0},{2,3},{3,2},{4,5},{5,4},{6,7},{7,6},{8,9},{9,8},{10,11... | collective-permute-start | bytes 1572872 | tf_op jit(solution)/shard_map/ppermute | solution.py:262
  105.2 12.5 %collective-permute-start.11 = (bf16[128,2048]{1,0:T(8,128)(2,1)S(1)}, bf16[128,2048]{1,0:T(8,128)(2,1)}, u32[]{:S(2)}, u32[]{:S(2)}) collective-permute-start(bf16[128,2048]{1,0:T(8,128)(2,1)S(1)} %get-tuple-element.77), channel_id=1, source_target_pairs={{2,4},{3,5},{4,2},{5,3},{10,12},{11,13},{12,10},{13,11},{18,20},{1... | collective-permute-start | bytes 1572872 | tf_op jit(solution)/shard_map/ppermute | solution.py:270
  106.7 13.8 %collective-permute-start.10 = (bf16[128,2048]{1,0:T(8,128)(2,1)S(1)}, bf16[128,2048]{1,0:T(8,128)(2,1)}, u32[]{:S(2)}, u32[]{:S(2)}) collective-permute-start(bf16[128,2048]{1,0:T(8,128)(2,1)S(1)} %get-tuple-element.77), channel_id=1, source_target_pairs={{0,2},{1,3},{2,0},{3,1},{4,6},{5,7},{6,4},{7,5},{8,10},{9,11},{10,... | collective-permute-start | bytes 1572872 | tf_op jit(solution)/shard_map/ppermute | solution.py:266
  109.0 4.3 %copy-start.2 = (bf16[4,2048,704]{1,2,0:T(8,128)(2,1)S(1)}, bf16[4,2048,704]{1,2,0:T(8,128)(2,1)}, u32[]{:S(2)}) copy-start(bf16[4,2048,704]{1,2,0:T(8,128)(2,1)} %param.27) | copy-start | bytes 34603012
  120.5 15.7 %collective-permute-start.15 = (bf16[128,2048]{1,0:T(8,128)(2,1)}, bf16[128,2048]{1,0:T(8,128)(2,1)S(1)}, u32[]{:S(2)}, u32[]{:S(2)}) collective-permute-start(bf16[128,2048]{1,0:T(8,128)(2,1)} %collective-permute-done.10), channel_id=1, source_target_pairs={{0,1},{1,0},{2,3},{3,2},{4,5},{5,4},{6,7},{7,6},{8,9},{9,8},{10,11... | collective-permute-start | bytes 1572872 | tf_op jit(solution)/shard_map/ppermute | solution.py:262
  121.1 15.1 %collective-permute-start.14 = (bf16[128,2048]{1,0:T(8,128)(2,1)}, bf16[128,2048]{1,0:T(8,128)(2,1)S(1)}, u32[]{:S(2)}, u32[]{:S(2)}) collective-permute-start(bf16[128,2048]{1,0:T(8,128)(2,1)} %collective-permute-done.10), channel_id=1, source_target_pairs={{2,4},{3,5},{4,2},{5,3},{10,12},{11,13},{12,10},{13,11},{18,20},{1... | collective-permute-start | bytes 1572872 | tf_op jit(solution)/shard_map/ppermute | solution.py:270
  121.8 14.4 %collective-permute-start.13 = (bf16[128,2048]{1,0:T(8,128)(2,1)}, bf16[128,2048]{1,0:T(8,128)(2,1)S(1)}, u32[]{:S(2)}, u32[]{:S(2)}) collective-permute-start(bf16[128,2048]{1,0:T(8,128)(2,1)} %collective-permute-done.11), channel_id=1, source_target_pairs={{0,2},{1,3},{2,0},{3,1},{4,6},{5,7},{6,4},{7,5},{8,10},{9,11},{10,... | collective-permute-start | bytes 1572872 | tf_op jit(solution)/shard_map/ppermute | solution.py:266
  125.8 4.3 %copy-start.3 = (bf16[4,704,2048]{2,1,0:T(8,128)(2,1)S(1)}, bf16[4,704,2048]{2,1,0:T(8,128)(2,1)}, u32[]{:S(2)}) copy-start(bf16[4,704,2048]{2,1,0:T(8,128)(2,1)} %source) | copy-start | bytes 34603012
  130.1 27.5 %slice-start = ((s8[11534336]{0:T(1024)(128)(4,1)}), s8[4194304]{0:T(1024)(128)(4,1)S(1)}, s32[]{:S(2)}) async-start(s8[11534336]{0:T(1024)(128)(4,1)} %bitcast.40), calls=%async_computation.2 | async-start | bytes 8388608
  130.1 27.5 %slice-start.1 = ((s8[11534336]{0:T(1024)(128)(4,1)}), s8[4194304]{0:T(1024)(128)(4,1)S(1)}, s32[]{:S(2)}) async-start(s8[11534336]{0:T(1024)(128)(4,1)} %bitcast.40), calls=%async_computation.3 | async-start | bytes 8388608
  133.1 24.6 %slice-start.2 = ((s8[11534336]{0:T(1024)(128)(4,1)}), s8[3145728]{0:T(1024)(128)(4,1)S(1)}, s32[]{:S(2)}) async-start(s8[11534336]{0:T(1024)(128)(4,1)} %bitcast.40), calls=%async_computation.4 | async-start | bytes 6291456
  136.2 12.6 %collective-permute-start.16 = (bf16[128,2048]{1,0:T(8,128)(2,1)S(1)}, bf16[128,2048]{1,0:T(8,128)(2,1)S(1)}, u32[]{:S(2)}, u32[]{:S(2)}) collective-permute-start(bf16[128,2048]{1,0:T(8,128)(2,1)S(1)} %collective-permute-done.14), channel_id=1, source_target_pairs={{0,2},{1,3},{2,0},{3,1},{4,6},{5,7},{6,4},{7,5},{8,10},{9,11},{10,... | collective-permute-start | bytes 1572872 | tf_op jit(solution)/shard_map/ppermute | solution.py:266
  138.2 10.6 %collective-permute-start.17 = (bf16[128,2048]{1,0:T(8,128)(2,1)S(1)}, bf16[128,2048]{1,0:T(8,128)(2,1)S(1)}, u32[]{:S(2)}, u32[]{:S(2)}) collective-permute-start(bf16[128,2048]{1,0:T(8,128)(2,1)S(1)} %broadcast_select_fusion.1), channel_id=1, source_target_pairs={{0,1},{1,0},{2,3},{3,2},{4,5},{5,4},{6,7},{7,6},{8,9},{9,8},{10,11... | collective-permute-start | bytes 1572872 | tf_op jit(solution)/shard_map/ppermute | solution.py:262
  139.9 12.6 %collective-permute-start.20 = (bf16[64,2048]{1,0:T(8,128)(2,1)S(1)}, bf16[64,2048]{1,0:T(8,128)(2,1)S(1)}, u32[]{:S(2)}, u32[]{:S(2)}) collective-permute-start(bf16[64,2048]{1,0:T(8,128)(2,1)S(1)} %slice.59), channel_id=1, source_target_pairs={{2,4},{3,5},{4,2},{5,3},{10,12},{11,13},{12,10},{13,11},{18,20},{1... | collective-permute-start | bytes 786440 | tf_op jit(solution)/shard_map/ppermute | solution.py:270
  148.9 6.4 %collective-permute-start.19 = (bf16[64,2048]{1,0:T(8,128)(2,1)S(1)}, bf16[64,2048]{1,0:T(8,128)(2,1)S(1)}, u32[]{:S(2)}, u32[]{:S(2)}) collective-permute-start(bf16[64,2048]{1,0:T(8,128)(2,1)S(1)} %slice.58), channel_id=1, source_target_pairs={{0,2},{1,3},{2,0},{3,1},{4,6},{5,7},{6,4},{7,5},{8,10},{9,11},{10,... | collective-permute-start | bytes 786440 | tf_op jit(solution)/shard_map/ppermute | solution.py:266
  150.6 6.4 %collective-permute-start.18 = (bf16[64,2048]{1,0:T(8,128)(2,1)S(1)}, bf16[64,2048]{1,0:T(8,128)(2,1)S(1)}, u32[]{:S(2)}, u32[]{:S(2)}) collective-permute-start(bf16[64,2048]{1,0:T(8,128)(2,1)S(1)} %slice.68), channel_id=1, source_target_pairs={{0,1},{1,0},{2,3},{3,2},{4,5},{5,4},{6,7},{7,6},{8,9},{9,8},{10,11... | collective-permute-start | bytes 786440 | tf_op jit(solution)/shard_map/ppermute | solution.py:262
  157.6 63.9 %copy-start.1 = (bf16[256,2048]{1,0:T(8,128)(2,1)S(1)}, bf16[256,2048]{1,0:T(8,128)(2,1)}, u32[]{:S(2)}) copy-start(bf16[256,2048]{1,0:T(8,128)(2,1)} %param.23) | copy-start | bytes 3145732
  169.3 6.4 %collective-permute-start.21 = (bf16[64,2048]{1,0:T(8,128)(2,1)S(1)}, bf16[64,2048]{1,0:T(8,128)(2,1)S(1)}, u32[]{:S(2)}, u32[]{:S(2)}) collective-permute-start(bf16[64,2048]{1,0:T(8,128)(2,1)S(1)} %get-tuple-element.97), channel_id=1, source_target_pairs={{0,1},{1,0},{2,3},{3,2},{4,5},{5,4},{6,7},{7,6},{8,9},{9,8},{10,11... | collective-permute-start | bytes 786440 | tf_op jit(solution)/shard_map/ppermute | solution.py:262
  170.7 5.0 %collective-permute-start.23 = (bf16[64,2048]{1,0:T(8,128)(2,1)S(1)}, bf16[64,2048]{1,0:T(8,128)(2,1)S(1)}, u32[]{:S(2)}, u32[]{:S(2)}) collective-permute-start(bf16[64,2048]{1,0:T(8,128)(2,1)S(1)} %get-tuple-element.98), channel_id=1, source_target_pairs={{2,4},{3,5},{4,2},{5,3},{10,12},{11,13},{12,10},{13,11},{18,20},{1... | collective-permute-start | bytes 786440 | tf_op jit(solution)/shard_map/ppermute | solution.py:270
  171.4 9.4 %collective-permute-start.22 = (bf16[64,2048]{1,0:T(8,128)(2,1)S(1)}, bf16[64,2048]{1,0:T(8,128)(2,1)S(1)}, u32[]{:S(2)}, u32[]{:S(2)}) collective-permute-start(bf16[64,2048]{1,0:T(8,128)(2,1)S(1)} %get-tuple-element.98), channel_id=1, source_target_pairs={{0,2},{1,3},{2,0},{3,1},{4,6},{5,7},{6,4},{7,5},{8,10},{9,11},{10,... | collective-permute-start | bytes 786440 | tf_op jit(solution)/shard_map/ppermute | solution.py:266
  181.0 10.7 %collective-permute-start.27 = (bf16[128,2048]{1,0:T(8,128)(2,1)S(1)}, bf16[128,2048]{1,0:T(8,128)(2,1)S(1)}, u32[]{:S(2)}, u32[]{:S(2)}) collective-permute-start(bf16[128,2048]{1,0:T(8,128)(2,1)S(1)} %pad_maximum_fusion.2), channel_id=1, source_target_pairs={{0,2},{1,3},{2,0},{3,1},{4,6},{5,7},{6,4},{7,5},{8,10},{9,11},{10,... | collective-permute-start | bytes 1572872 | tf_op jit(solution)/shard_map/ppermute | solution.py:266
  183.2 11.6 %collective-permute-start.26 = (bf16[128,2048]{1,0:T(8,128)(2,1)S(1)}, bf16[128,2048]{1,0:T(8,128)(2,1)S(1)}, u32[]{:S(2)}, u32[]{:S(2)}) collective-permute-start(bf16[128,2048]{1,0:T(8,128)(2,1)S(1)} %pad_maximum_fusion.1), channel_id=1, source_target_pairs={{0,1},{1,0},{2,3},{3,2},{4,5},{5,4},{6,7},{7,6},{8,9},{9,8},{10,11... | collective-permute-start | bytes 1572872 | tf_op jit(solution)/shard_map/ppermute | solution.py:262
  183.9 20.0 %collective-permute-start.25 = (bf16[128,2048]{1,0:T(8,128)(2,1)S(1)}, bf16[128,2048]{1,0:T(8,128)(2,1)S(1)}, u32[]{:S(2)}, u32[]{:S(2)}) collective-permute-start(bf16[128,2048]{1,0:T(8,128)(2,1)S(1)} %get-tuple-element.101), channel_id=1, source_target_pairs={{0,1},{1,0},{2,3},{3,2},{4,5},{5,4},{6,7},{7,6},{8,9},{9,8},{10,11... | collective-permute-start | bytes 1572872 | tf_op jit(solution)/shard_map/ppermute | solution.py:262
  195.0 8.9 %collective-permute-start.29 = (bf16[128,2048]{1,0:T(8,128)(2,1)S(1)}, bf16[128,2048]{1,0:T(8,128)(2,1)S(1)}, u32[]{:S(2)}, u32[]{:S(2)}) collective-permute-start(bf16[128,2048]{1,0:T(8,128)(2,1)S(1)} %add_convert_fusion.3), channel_id=1, source_target_pairs={{2,4},{3,5},{4,2},{5,3},{10,12},{11,13},{12,10},{13,11},{18,20},{1... | collective-permute-start | bytes 1572872 | tf_op jit(solution)/shard_map/ppermute | solution.py:270
  195.8 14.9 %collective-permute-start.28 = (bf16[128,2048]{1,0:T(8,128)(2,1)S(1)}, bf16[128,2048]{1,0:T(8,128)(2,1)S(1)}, u32[]{:S(2)}, u32[]{:S(2)}) collective-permute-start(bf16[128,2048]{1,0:T(8,128)(2,1)S(1)} %add_convert_fusion.3), channel_id=1, source_target_pairs={{0,2},{1,3},{2,0},{3,1},{4,6},{5,7},{6,4},{7,5},{8,10},{9,11},{10,... | collective-permute-start | bytes 1572872 | tf_op jit(solution)/shard_map/ppermute | solution.py:266
  200.7 12.9 %collective-permute-start.24 = (bf16[128,2048]{1,0:T(8,128)(2,1)S(1)}, bf16[128,2048]{1,0:T(8,128)(2,1)S(1)}, u32[]{:S(2)}, u32[]{:S(2)}) collective-permute-start(bf16[128,2048]{1,0:T(8,128)(2,1)S(1)} %pad_maximum_fusion), channel_id=1, source_target_pairs={{0,1},{1,0},{2,3},{3,2},{4,5},{5,4},{6,7},{7,6},{8,9},{9,8},{10,11... | collective-permute-start | bytes 1572872 | tf_op jit(solution)/shard_map/ppermute | solution.py:262
  211.1 9.2 %collective-permute-start.30 = (bf16[128,2048]{1,0:T(8,128)(2,1)S(1)}, bf16[128,2048]{1,0:T(8,128)(2,1)S(1)}, u32[]{:S(2)}, u32[]{:S(2)}) collective-permute-start(bf16[128,2048]{1,0:T(8,128)(2,1)S(1)} %add_convert_fusion.2), channel_id=1, source_target_pairs={{0,2},{1,3},{2,0},{3,1},{4,6},{5,7},{6,4},{7,5},{8,10},{9,11},{10,... | collective-permute-start | bytes 1572872 | tf_op jit(solution)/shard_map/ppermute | solution.py:266
  212.9 7.4 %collective-permute-start.31 = (bf16[128,2048]{1,0:T(8,128)(2,1)S(1)}, bf16[128,2048]{1,0:T(8,128)(2,1)S(1)}, u32[]{:S(2)}, u32[]{:S(2)}) collective-permute-start(bf16[128,2048]{1,0:T(8,128)(2,1)S(1)} %add_convert_fusion.1), channel_id=1, source_target_pairs={{2,4},{3,5},{4,2},{5,3},{10,12},{11,13},{12,10},{13,11},{18,20},{1... | collective-permute-start | bytes 1572872 | tf_op jit(solution)/shard_map/ppermute | solution.py:270
Sparse Core Ops, SparseCore 0:
  9.5 86.3 all-gather.1

commit v7 on v6

--- a/solution.py
+++ b/solution.py
@@ -246,7 +246,7 @@
 BLK = 128
 LOG2E = 1.4426950408889634
 SCORE_SCALE = LOG2E / math.sqrt(HEAD)
-VMEM_BIG = 56 * 1024 * 1024
+VMEM_BIG = 28 * 1024 * 1024
 VMEM_SMALL = 12 * 1024 * 1024
 
 
@@ -264,6 +264,12 @@
 
 def outer_swap(array):
     return lax.ppermute(array, "exp", [(i, i ^ 2) for i in range(8)])
+
+
+def gather_z(array):
+    return lax.all_gather(
+        array, "exp", axis=0, axis_index_groups=[[0, 2, 4, 6], [1, 3, 5, 7]], tiled=True
+    )
 
 
 def middle_swap(array):
@@ -452,8 +458,12 @@
     def pair(i, carry):
         score(2 * i + 1, sb, tb)
         weigh(2 * i, sa, ta)
-        score(2 * i + 2, sa, ta)
-        weigh(2 * i + 1, sb, tb)
+
+        @pl.when(2 * i + 1 < count)
+        def second():
+            score(2 * i + 2, sa, ta)
+            weigh(2 * i + 1, sb, tb)
+
         return carry
 
     lax.fori_loop(0, (count + 1) // 2, pair, 0)
@@ -586,102 +596,110 @@
     )(place, shape_a, shape_b, q, k, v, other)
 
 
-MERGE_BLOCKS = 4
-
-
-def merge_kernel(*refs):
+def merge_kernel(sc_ref, *refs):
     parts, tab_ref, out_ref = refs[:-2], refs[-2], refs[-1]
-    step = pl.program_id(0)
-    for block in range(MERGE_BLOCKS):
-        out_ref[block, 2 * BLK :, :] = tab_ref[...]
+    block = pl.program_id(0)
+    out_ref[0, 2 * BLK :, :] = tab_ref[...]
     half = len(parts) // 2
     for row in range(2):
         sources = parts[row * half : (row + 1) * half]
-        for block in range(MERGE_BLOCKS):
-            here = slice(block * BLK, (block + 1) * BLK)
-            at = pl.ds(step * MERGE_BLOCKS + block, 1)
-            lses = [
-                jnp.transpose(jnp.broadcast_to(lse[0, at, :], (BLK, BLK))) for lse in sources[1::2]
-            ]
-            top = lses[0]
-            for lse in lses[1:]:
-                top = jnp.maximum(top, lse)
-            total, summed = 0.0, 0.0
-            for lse, o in zip(lses, sources[0::2]):
-                weight = jnp.exp2(lse - top)
-                total = total + weight
-                summed = summed + weight * o[here, :].astype(jnp.float32)
-            out_ref[block, row * BLK : (row + 1) * BLK, :] = (summed / total).astype(out_ref.dtype)
-
-
-def merge_parts(parts, tab):
+        lses = [
+            jnp.transpose(jnp.broadcast_to(lse[0, pl.ds(block, 1), :], (BLK, BLK)))
+            for lse in sources[1::2]
+        ]
+        top = lses[0]
+        for lse in lses[1:]:
+            top = jnp.maximum(top, lse)
+        total, summed = 0.0, 0.0
+        for lse, o in zip(lses, sources[0::2]):
+            weight = jnp.exp2(lse - top)
+            total = total + weight
+            summed = summed + weight * o[...].astype(jnp.float32)
+        out_ref[0, row * BLK : (row + 1) * BLK, :] = (summed / total).astype(out_ref.dtype)
+
+
+def merge_parts(place, parts, tab):
     extra = tab.shape[0]
     blocks = ROW_TOK // BLK
-    steps = blocks // MERGE_BLOCKS
     specs, operands = [], []
     for row in range(2):
         for o, lse in parts:
             operands += [o, lse]
             specs += [
-                pl.BlockSpec((MERGE_BLOCKS * BLK, HEAD), lambda b, row=row: (row * steps + b, 0)),
-                pl.BlockSpec((1, blocks, BLK), lambda b, row=row: (row, 0, 0)),
+                pl.BlockSpec((BLK, HEAD), lambda b, s, row=row: (row * blocks + b, 0)),
+                pl.BlockSpec((1, blocks, BLK), lambda b, s, row=row: (row, 0, 0)),
             ]
     return pl.pallas_call(
         merge_kernel,
-        grid=(steps,),
-        in_specs=specs + [pl.BlockSpec((extra, BLK), lambda b: (0, 0))],
-        out_specs=pl.BlockSpec((MERGE_BLOCKS, 2 * BLK + extra, HEAD), lambda b: (b, 0, 0)),
+        grid_spec=pltpu.PrefetchScalarGridSpec(
+            num_scalar_prefetch=1,
+            grid=(blocks,),
+            in_specs=specs + [pl.BlockSpec((extra, BLK), lambda b, s: (0, 0))],
+            out_specs=pl.BlockSpec((1, 2 * BLK + extra, HEAD), lambda b, s: (b ^ s[1], 0, 0)),
+        ),
         out_shape=jax.ShapeDtypeStruct((blocks, 2 * BLK + extra, HEAD), jnp.bfloat16),
         compiler_params=pltpu.CompilerParams(vmem_limit_bytes=VMEM_SMALL),
         name="merge_parts",
-    )(*operands, tab)
-
-
-def project_kernel(a_ref, w_ref, keep_ref, send_ref, lhs):
-    @pl.when(pl.program_id(0) == 0)
-    def first():
-        for h in range(a_ref.shape[0]):
-            lhs[:, h * HEAD : (h + 1) * HEAD] = a_ref[h, : 2 * BLK, :]
-
-    out = jnp.dot(lhs[...], w_ref[...], preferred_element_type=jnp.float32)
-    rows = keep_ref.shape[0]
-    keep_ref[...] = out[:rows]
-    send_ref[...] = out[rows:].astype(send_ref.dtype)
-
-
-def project(attended, weights):
-    heads, held, unused = attended.shape
-    tokens = 2 * BLK
+    )(place, *operands, tab)
+
+
+def exchange_heads(attended):
+    heads = [attended[:2]]
+    for d in range(1, attended.shape[0] // 2):
+        heads.append(
+            lax.ppermute(
+                attended[2 * d : 2 * d + 2], "exp", [(i, i ^ (2 * d)) for i in range(8)]
+            )
+        )
+    return heads
+
+
+def project_kernel(sc_ref, *refs):
+    heads, weights, outs, lhs = refs[:4], refs[4], refs[5:9], refs[9]
+    z_here = sc_ref[1] // 2
+    for d, part in enumerate(heads):
+        columns = pl.ds(pl.multiple_of((z_here ^ d) * HEAD, HEAD), HEAD)
+        for row in range(2):
+            for chunk in range(2):
+                to = (2 * row + chunk) * BLK
+                lhs[to : to + BLK, columns] = part[chunk, row * BLK : (row + 1) * BLK, :]
+    tile = 512
+    for low in range(0, weights.shape[1], tile):
+        here = slice(low, low + tile)
+        out = jnp.dot(lhs[...], weights[:, here], preferred_element_type=jnp.float32)
+        for i, out_ref in enumerate(outs):
+            out_ref[:, here] = out[i * BLK : (i + 1) * BLK].astype(out_ref.dtype)
+
+
+def project(place, heads, weights):
     depth, width = weights.shape
-    rows, tile = tokens // 2, 1024
-    out_spec = pl.BlockSpec((rows, tile), lambda i: (0, i))
+    smem = pl.BlockSpec(memory_space=pltpu.SMEM)
+    vmem = pl.BlockSpec(memory_space=pltpu.VMEM)
     return pl.pallas_call(
         project_kernel,
-        grid=(width // tile,),
-        in_specs=[
-            pl.BlockSpec((heads, held, HEAD), lambda i: (0, 0, 0)),
-            pl.BlockSpec((depth, tile), lambda i: (0, i)),
+        in_specs=[smem] + [vmem] * 5,
+        out_specs=[vmem] * 4,
+        out_shape=[
+            jax.ShapeDtypeStruct((BLK, width), dtype)
+            for dtype in (jnp.float32, jnp.bfloat16, jnp.bfloat16, jnp.bfloat16)
         ],
-        out_specs=[out_spec, out_spec],
-        out_shape=(
-            jax.ShapeDtypeStruct((rows, width), jnp.float32),
-            jax.ShapeDtypeStruct((rows, width), jnp.bfloat16),
-        ),
-        scratch_shapes=[pltpu.VMEM((tokens, depth), jnp.bfloat16)],
+        scratch_shapes=[pltpu.VMEM((4 * BLK, depth), jnp.bfloat16)],
         compiler_params=pltpu.CompilerParams(vmem_limit_bytes=VMEM_SMALL),
         name="project",
-    )(attended, weights)
-
-
-def norm_kernel(keep, got, residual, gain, stream_ref, normed_ref):
-    stream = residual[...].astype(jnp.float32) + (keep[...] + got[...].astype(jnp.float32))
+    )(place, *heads, weights)
+
+
+def norm_kernel(keep, got, late, residual, gain, stream_ref, normed_ref):
+    stream = residual[...].astype(jnp.float32) + (
+        keep[...] + got[...].astype(jnp.float32) + late[...].astype(jnp.float32)
+    )
     meansq = jnp.mean(stream * stream, axis=-1, keepdims=True)
     stream_ref[...] = stream
     normed = stream * lax.rsqrt(meansq + 1e-06) * gain[...].astype(jnp.float32)
     normed_ref[...] = normed.astype(normed_ref.dtype)
 
 
-def norm_rows(keep, got, residual, gain):
+def norm_rows(keep, got, late, residual, gain):
     return pl.pallas_call(
         norm_kernel,
         out_shape=(
@@ -690,29 +708,26 @@
         ),
         compiler_params=pltpu.CompilerParams(vmem_limit_bytes=VMEM_SMALL),
         name="norm_rows",
-    )(keep, got, residual, gain)
+    )(keep, got, late, residual, gain)
 
 
 EXP_DEV = 4
 VMEM_STAGE = 2 * 1024 * 1024
 EXPERT_VMEM = 8 * 1024 * 1024
 SLOTS = 32
-SLOT_Z = ((0, 1, 2, 3), (1, 0, 3, 2), (2, 3, 0, 1), (3, 2, 1, 0))
-
-
-def route_kernel(sc_ref, tab_ref, pick_ref, give_ref):
+SLOTS_XOR = (0, 2, 4, 6, 1, 3, 5, 7)
+
+
+def route_kernel(sc_ref, *refs):
+    own, other, pick_ref, give_ref = refs
     before = (
         lax.broadcasted_iota(jnp.int32, (BLK, BLK), 0)
         < lax.broadcasted_iota(jnp.int32, (BLK, BLK), 1)
     ).astype(jnp.bfloat16)
     place = lax.broadcasted_iota(jnp.int32, (SLOTS, BLK), 0).astype(jnp.float32)
     place_here = sc_ref[1]
-    here_z, here_y = place_here // 2, place_here % 2
-    for slot in range(8):
-        of = SLOT_Z[3][slot % 4]
-        for z in range(3):
-            of = jnp.where(here_z == z, SLOT_Z[z][slot % 4], of)
-        tab = tab_ref[of * 2 + (here_y if slot < 4 else 1 - here_y)].astype(jnp.float32)
+    for slot, offset in enumerate(SLOTS_XOR):
+        tab = (own if offset % 2 == 0 else other)[offset // 2].astype(jnp.float32)
         ids, gates = tab[:TOPK], tab[TOPK : 2 * TOPK]
         chosen, weights = [], []
         for j in range(EXP_DEV):
@@ -732,21 +747,17 @@
         give_ref[slot] = jnp.transpose(spread).astype(jnp.bfloat16)
 
 
-def route(place, heads):
-    extra = heads.shape[1] - 2 * BLK
+def route(place, own, other):
     shape = jax.ShapeDtypeStruct((8, BLK, EXP_DEV * SLOTS), jnp.bfloat16)
+    vmem = pl.BlockSpec(memory_space=pltpu.VMEM)
     return pl.pallas_call(
         route_kernel,
-        grid=(1,),
-        in_specs=[
-            pl.BlockSpec(memory_space=pltpu.SMEM),
-            pl.BlockSpec((8, extra, BLK), lambda i: (0, 2 * BLK // extra, 0)),
-        ],
-        out_specs=[pl.BlockSpec((8, BLK, BLK), lambda i: (0, 0, 0))] * 2,
+        in_specs=[pl.BlockSpec(memory_space=pltpu.SMEM), vmem, vmem],
+        out_specs=[vmem, vmem],
         out_shape=(shape, shape),
         compiler_params=pltpu.CompilerParams(vmem_limit_bytes=VMEM_SMALL),
         name="route",
-    )(place, heads)
+    )(place, own, other)
 
 
 def stage_kernel(source, held, sems):
@@ -912,8 +923,7 @@
     far_shape = x_swap(shape)
     far_queries = x_swap(queries)
 
-    proj_rows = lax.dynamic_slice_in_dim(out_proj, core * HEAD, HEAD, 0)
-    proj_rows = lax.all_gather(proj_rows, "exp", axis=0, tiled=True)
+    proj_rows = gather_z(lax.dynamic_slice_in_dim(out_proj, core * HEAD, HEAD, 0))
 
     theirs, prefix_theirs = split_theirs(place, queries, keys, values, prefix_keys, prefix_values)
     other, prefix_other = core_swap(theirs), core_swap(prefix_theirs)
@@ -932,12 +942,16 @@
     far = prefix(far_shape, far_other_shape, far_queries, far_other, jnp.bfloat16)
     back = (x_swap(far[0]), x_swap(far[1]))
     near = prefix(shape, other_shape, queries, other, jnp.float32)
-    near_o, gain = lax.optimization_barrier((near[0], norm_gain.reshape(1, -1)))
-    attended = merge_parts([suffix, (near_o, near[1]), back], tab)
-    heads = lax.all_to_all(attended, "exp", split_axis=0, concat_axis=0, tiled=True)
-    keep, send = project(heads, proj_rows)
-    stream, normed = norm_rows(keep, core_swap(send), residual, gain)
-    pick, give = route(place, heads)
+    near_o, gain = together(near[0], norm_gain.reshape(1, -1))
+    attended = merge_parts(place, [suffix, (near_o, near[1]), back], tab)
+    heads = exchange_heads(attended)
+    tabs = jnp.stack([part[0, 2 * BLK :, :] for part in heads])
+    keep, pair, send, send_pair = project(place, heads, proj_rows)
+    send_pair, tabs, other_tabs = together(send_pair, tabs, y_swap(tabs))
+    pair = pair.astype(jnp.float32) + core_swap(send_pair).astype(jnp.float32)
+    late = y_swap(pair.astype(jnp.bfloat16))
+    stream, normed = norm_rows(keep, core_swap(send), late, residual, gain)
+    pick, give = route(place, tabs, other_tabs)
     weights = (w_gate.transpose(0, 2, 1), w_up.transpose(0, 2, 1), w_down)
     here, there, weights = gather_rows(middle, normed, weights)
     picked = pick_rows(pick[:4], here) + pick_rows(pick[4:], there)

time: 231 us -> 225 us (0.974)
  blocking collectives: 28.6 us -> 0 us
  waiting for transfers between devices: 61.3 us -> 83.5 us
  starting transfers between devices: 40.5 us -> 43.7 us
  local copies, waits for them, and re-layouts: 18.3 us -> 15.9 us
    all_to_all x1 -> x0, blocking collectives: 28.6 us -> none  [block_device(): lax.all_to_all(attended, 'exp', split_axis=0, concat_axis=0, tiled=True)]
    ppermute x8 -> x10, waiting for transfers between devices: 20.4 us -> 36.6 us  [y_swap(): return lax.ppermute(array, 'exp', [(i, i ^ 1) for i in range(8)])]
    ppermute x0 -> x3, waiting for transfers between devices: none -> 10.9 us  [exchange_heads(): lax.ppermute(attended[2 * d:2 * d + 2], 'exp', [(i, i ^ 2 * d) for i in r...]
    ppermute x0 -> x3, starting transfers between devices: none -> 4.56 us  [exchange_heads(): lax.ppermute(attended[2 * d:2 * d + 2], 'exp', [(i, i ^ 2 * d) for i in r...]
    unnamed x50 -> x42, local copies, waits for them, and re-layouts: 17.3 us -> 13.9 us
    ppermute x8, waiting for transfers between devices: 33.6 us -> 31.1 us  [outer_swap(): return lax.ppermute(array, 'exp', [(i, i ^ 2) for i in range(8)])]
    ppermute x8 -> x10, starting transfers between devices: 9.2 us -> 8.68 us  [y_swap(): return lax.ppermute(array, 'exp', [(i, i ^ 1) for i in range(8)])]
  transfers between devices with their start and end apart: 33 -> 39, of which waited for: 18 -> 20; matrix products, arithmetic and copies ran while one was open for 3% -> 4% of each run, Pallas kernels for 19% -> 18%
where the time goes in v7:
time: 225 us; the launch traced here: 223 us
  waiting for transfers between devices  83.5 us (37%)
  Pallas kernels  56.3 us (25%)
  starting transfers between devices  43.7 us (19%)
  local copies, waits for them, and re-layouts  15.9 us (7%)
  between operations  13.9 us (6%)
  matrix products  5.21 us (2%)
  other arithmetic  4.84 us (2%)
    ppermute x10, waiting for transfers between devices, y_swap(): return lax.ppermute(array, 'exp', [(i, i ^ 1) for i in range(8)])  36.6 us
    ppermute x8, waiting for transfers between devices, outer_swap(): return lax.ppermute(array, 'exp', [(i, i ^ 2) for i in range(8)])  31.1 us
    pallas_call x2, Pallas kernels, prefix_attend(): pl.pallas_call(prefix_kernel, in_specs=[smem] * 3 + [anywhere] * 5, out_s...  28.1 us
    ppermute x8, starting transfers between devices, outer_swap(): return lax.ppermute(array, 'exp', [(i, i ^ 2) for i in range(8)])  18.8 us
    unnamed x42, local copies, waits for them, and re-layouts  13.9 us
    pallas_call x1, Pallas kernels, run_experts(): pl.pallas_call(experts_kernel, in_specs=[vmem] * 12, out_specs=[vmem] * 9...  11.6 us
    ppermute x3, waiting for transfers between devices, exchange_heads(): lax.ppermute(attended[2 * d:2 * d + 2], 'exp', [(i, i ^ 2 * d) for i in r...  10.9 us
    ppermute x10, starting transfers between devices, y_swap(): return lax.ppermute(array, 'exp', [(i, i ^ 1) for i in range(8)])  8.68 us
  transfers between devices with their start and end apart: 39, of which 20 were waited for; matrix products, arithmetic and copies ran while one was open for 4% of the time, Pallas kernels for 18%

profile of v7, /device:TPU:0, one launch (start us, length us, event | category | flops | bytes accessed | tf_op | source)
XLA Modules:
  0.0 223.3 jit_solution(14365506567793840065)
XLA Ops:
  7.1 4.9 %split_theirs.1 = (bf16[3,1024,128]{2,1,0:T(8,128)(2,1)}, bf16[2,4,1024,128]{3,2,1,0:T(8,128)(2,1)}) custom-call(s32[2]{0:T(128)} %pad_add_fusion.sc_ref, bf16[1024,256]{1,0:T(8,128)(2,1)} %q0.1, bf16[1024,256]{1,0:T(8,128)(2,1)} %k.3, bf16[1024,256]{1,0:T(8,128)(2,1)} %v.3, bf16[4,1024,256]{2,1,0:T(8,128)(2,1)} %pk.5, bf16[4,1024,256]{2,1,0:T(8,128)(2,1)} %pv.5), custom_call_target="tpu_custom_call" | custom-call | tf_op jit(solution)/shard_map/split_theirs/pallas_call | solution.py:291
  12.6 2.9 %collective-permute-start.3 = (bf16[1024,256]{1,0:T(8,128)(2,1)}, bf16[1024,256]{1,0:T(8,128)(2,1)}, u32[]{:S(2)}, u32[]{:S(2)}) collective-permute-start(bf16[1024,256]{1,0:T(8,128)(2,1)} %q0.1), channel_id=1, source_target_pairs={{0,16},{8,24},{16,0},{24,8},{1,17},{9,25},{17,1},{25,9},{2,18},{10... | collective-permute-start | bytes 1572872 | tf_op jit(solution)/shard_map/ppermute | solution.py:258
  15.5 0.8 constant_dynamic-slice_fusion
  16.4 0.7 pad_add_fusion.1.shape_a
  17.2 1.1 collective-permute-done.shape_b
  18.3 1.0 copy-done.7
  19.3 1.0 copy-done.8
  20.4 1.0 copy-done.9
  22.0 4.7 %suffix_attend.1 = (f32[2048,128]{1,0:T(8,128)S(1)}, f32[2,8,128]{2,1,0:T(8,128)S(1)}) custom-call(s32[2]{0:T(128)S(1)} %copy-done.12, s32[1,16]{1,0:T(1,128)S(1)} %pad_add_fusion.1.shape_a, s32[1,16]{1,0:T(1,128)S(1)} %collective-permute-done.shape_b, bf16[1024,256]{1,0:T(8,128)(2,1)S(1)} %copy-done.9, bf16[1024,256]{1,0:T(8,128)(2,1)S(1)} %copy-done.7, ...), custom_call_target="tpu_custom_call" | custom-call | flops 4294967296 | bytes 1048576 | tf_op jit(solution)/shard_map/suffix_attend/pallas_call | solution.py:574
  26.7 1.3 collective-permute-done.4.shape_a
  28.0 1.1 select_bitcast_fusion
  29.8 0.9 collective-permute-done.5.shape_b
  30.7 13.9 %prefix_attend.3 = (bf16[2048,128]{1,0:T(8,128)(2,1)S(1)}, f32[2,8,128]{2,1,0:T(8,128)S(1)}) custom-call(s32[2]{0:T(128)S(1)} %copy-done.13, s32[1,16]{1,0:T(1,128)S(1)} %collective-permute-done.4.shape_a, s32[1,16]{1,0:T(1,128)S(1)} %collective-permute-done.5.shape_b, bf16[1024,256]{1,0:T(8,128)(2,1)} %collective-permute-done.3.q0, ...), custom_call_target="tpu_custom_call" | custom-call | flops 8589934592 | bytes 4194304 | tf_op jit(solution)/shard_map/prefix_attend/pallas_call | solution.py:488
  44.6 1.8 collective-permute-start.8
  46.7 14.1 %prefix_attend.2 = (f32[2048,128]{1,0:T(8,128)S(1)}, f32[2,8,128]{2,1,0:T(8,128)S(1)}) custom-call(s32[2]{0:T(128)S(1)} %copy-done.13, s32[1,16]{1,0:T(1,128)S(1)} %pad_add_fusion.1.shape_a, s32[1,16]{1,0:T(1,128)S(1)} %collective-permute-done.shape_b, bf16[1024,256]{1,0:T(8,128)(2,1)S(1)} %copy-done.10, ...), custom_call_target="tpu_custom_call" | custom-call | flops 8589934592 | bytes 4194304 | tf_op jit(solution)/shard_map/prefix_attend/pallas_call | solution.py:488
  60.9 2.1 merge_parts.1
  63.1 3.9 %collective-permute-start.11 = (bf16[2,272,128]{2,1,0:T(8,128)(2,1)S(1)}, bf16[2,272,128]{2,1,0:T(8,128)(2,1)S(1)}, u32[]{:S(2)}, u32[]{:S(2)}) collective-permute-start(bf16[2,272,128]{2,1,0:T(8,128)(2,1)S(1)} %get-tuple-element.125), channel_id=1, source_target_pairs={{0,6},{1,7},{2,4},{3,5},{4,2},{5,3},{6,0},{7,1},{8,14},{9,15},{10,... | collective-permute-start | bytes 417800 | tf_op jit(solution)/shard_map/ppermute | solution.py:650
  67.0 0.6 collective-permute-start.9
  67.7 3.9 %collective-permute-done.11.refs_3_ = bf16[2,272,128]{2,1,0:T(8,128)(2,1)S(1)} collective-permute-done((bf16[2,272,128]{2,1,0:T(8,128)(2,1)S(1)}, bf16[2,272,128]{2,1,0:T(8,128)(2,1)S(1)}, u32[]{:S(2)}, u32[]{:S(2)}) %collective-permute-start.11) | collective-permute-done | bytes 139296 | tf_op jit(solution)/shard_map/ppermute | solution.py:650
  71.6 7.0 %collective-permute-done.10.refs_2_ = bf16[2,272,128]{2,1,0:T(8,128)(2,1)S(1)} collective-permute-done((bf16[2,272,128]{2,1,0:T(8,128)(2,1)S(1)}, bf16[2,272,128]{2,1,0:T(8,128)(2,1)S(1)}, u32[]{:S(2)}, u32[]{:S(2)}) %collective-permute-start.10) | collective-permute-done | bytes 139296 | tf_op jit(solution)/shard_map/ppermute | solution.py:650
  78.6 1.6 collective-permute-start.13
  80.2 1.6 copy-done.6
  81.8 1.9 project.1
  84.3 1.4 collective-permute-done.14
  86.4 13.4 %collective-permute-done.15.late = bf16[128,2048]{1,0:T(8,128)(2,1)S(1)} collective-permute-done((bf16[128,2048]{1,0:T(8,128)(2,1)S(1)}, bf16[128,2048]{1,0:T(8,128)(2,1)S(1)}, u32[]{:S(2)}, u32[]{:S(2)}) %collective-permute-start.15) | collective-permute-done | bytes 524320 | tf_op jit(solution)/shard_map/ppermute | solution.py:262
  100.9 1.5 collective-permute-start.17
  102.4 1.1 collective-permute-start.16
  103.4 0.8 route.1
  104.3 4.3 %copy-done.2 = bf16[4,2048,704]{1,2,0:T(8,128)(2,1)S(1)} copy-done((bf16[4,2048,704]{1,2,0:T(8,128)(2,1)S(1)}, bf16[4,2048,704]{1,2,0:T(8,128)(2,1)}, u32[]{:S(2)}) %copy-start.2) | copy-done | bytes 11534360
  108.6 0.8 stage.2.refs_9_
  109.4 4.2 %collective-permute-done.18 = bf16[128,2048]{1,0:T(8,128)(2,1)S(1)} collective-permute-done((bf16[128,2048]{1,0:T(8,128)(2,1)S(1)}, bf16[128,2048]{1,0:T(8,128)(2,1)S(1)}, u32[]{:S(2)}, u32[]{:S(2)}) %collective-permute-start.18) | collective-permute-done | bytes 524320 | tf_op jit(solution)/shard_map/ppermute | solution.py:262
  113.6 1.8 collective-permute-done.16
  115.4 1.5 collective-permute-start.21
  116.9 0.7 collective-permute-start.20
  117.6 3.2 %collective-permute-start.19 = (bf16[128,2048]{1,0:T(8,128)(2,1)}, bf16[128,2048]{1,0:T(8,128)(2,1)S(1)}, u32[]{:S(2)}, u32[]{:S(2)}) collective-permute-start(bf16[128,2048]{1,0:T(8,128)(2,1)} %collective-permute-done.17), channel_id=1, source_target_pairs={{0,2},{1,3},{2,0},{3,1},{4,6},{5,7},{6,4},{7,5},{8,10},{9,11},{10,... | collective-permute-start | bytes 1572872 | tf_op jit(solution)/shard_map/ppermute | solution.py:266
  120.7 4.3 %copy-done.3 = bf16[4,704,2048]{2,1,0:T(8,128)(2,1)S(1)} copy-done((bf16[4,704,2048]{2,1,0:T(8,128)(2,1)S(1)}, bf16[4,704,2048]{2,1,0:T(8,128)(2,1)}, u32[]{:S(2)}) %copy-start.3) | copy-done | bytes 11534360
  125.0 0.8 stage.3.refs_11_
  126.1 1.8 convolution_convert_fusion.5.refs_1_
  128.0 2.9 %collective-permute-done.19 = bf16[128,2048]{1,0:T(8,128)(2,1)S(1)} collective-permute-done((bf16[128,2048]{1,0:T(8,128)(2,1)}, bf16[128,2048]{1,0:T(8,128)(2,1)S(1)}, u32[]{:S(2)}, u32[]{:S(2)}) %collective-permute-start.19) | collective-permute-done | bytes 524320 | tf_op jit(solution)/shard_map/ppermute | solution.py:266
  131.0 2.1 collective-permute-start.22
  133.7 1.3 convolution_convert_fusion.2.refs_4_
  135.0 1.0 slice.92
  136.0 0.7 collective-permute-start.26
  137.2 5.1 %collective-permute-done.23 = bf16[128,2048]{1,0:T(8,128)(2,1)S(1)} collective-permute-done((bf16[128,2048]{1,0:T(8,128)(2,1)S(1)}, bf16[128,2048]{1,0:T(8,128)(2,1)S(1)}, u32[]{:S(2)}, u32[]{:S(2)}) %collective-permute-start.23) | collective-permute-done | bytes 524320 | tf_op jit(solution)/shard_map/ppermute | solution.py:262
  142.5 2.7 %collective-permute-start.25 = (bf16[64,2048]{1,0:T(8,128)(2,1)S(1)}, bf16[64,2048]{1,0:T(8,128)(2,1)S(1)}, u32[]{:S(2)}, u32[]{:S(2)}) collective-permute-start(bf16[64,2048]{1,0:T(8,128)(2,1)S(1)} %slice.91), channel_id=1, source_target_pairs={{0,2},{1,3},{2,0},{3,1},{4,6},{5,7},{6,4},{7,5},{8,10},{9,11},{10,... | collective-permute-start | bytes 786440 | tf_op jit(solution)/shard_map/ppermute | solution.py:266
  146.2 3.2 %collective-permute-done.25 = bf16[64,2048]{1,0:T(8,128)(2,1)S(1)} collective-permute-done((bf16[64,2048]{1,0:T(8,128)(2,1)S(1)}, bf16[64,2048]{1,0:T(8,128)(2,1)S(1)}, u32[]{:S(2)}, u32[]{:S(2)}) %collective-permute-start.25) | collective-permute-done | bytes 262176 | tf_op jit(solution)/shard_map/ppermute | solution.py:266
  149.5 2.0 collective-permute-done.24
  152.2 11.6 %experts.1 = (bf16[128,2048]{1,0:T(8,128)(2,1)S(1)}, bf16[128,2048]{1,0:T(8,128)(2,1)S(1)}, bf16[128,2048]{1,0:T(8,128)(2,1)S(1)}, bf16[128,2048]{1,0:T(8,128)(2...) custom-call(bf16[128,2048]{1,0:T(8,128)(2,1)S(1)} %convolution_conve, ...), custom_call_target="tpu_custom_call" | custom-call | tf_op jit(solution)/shard_map/experts/pallas_call | solution.py:816
  164.4 0.7 collective-permute-start.29
  165.1 2.3 %collective-permute-start.28 = (bf16[64,2048]{1,0:T(8,128)(2,1)S(1)}, bf16[64,2048]{1,0:T(8,128)(2,1)S(1)}, u32[]{:S(2)}, u32[]{:S(2)}) collective-permute-start(bf16[64,2048]{1,0:T(8,128)(2,1)S(1)} %get-tuple-element.108), channel_id=1, source_target_pairs={{0,2},{1,3},{2,0},{3,1},{4,6},{5,7},{6,4},{7,5},{8,10},{9,11},{10,... | collective-permute-start | bytes 786440 | tf_op jit(solution)/shard_map/ppermute | solution.py:266
  167.4 4.0 %collective-permute-done.27 = bf16[64,2048]{1,0:T(8,128)(2,1)S(1)} collective-permute-done((bf16[64,2048]{1,0:T(8,128)(2,1)S(1)}, bf16[64,2048]{1,0:T(8,128)(2,1)S(1)}, u32[]{:S(2)}, u32[]{:S(2)}) %collective-permute-start.27) | collective-permute-done | bytes 262176 | tf_op jit(solution)/shard_map/ppermute | solution.py:262
  171.4 3.2 %collective-permute-done.28 = bf16[64,2048]{1,0:T(8,128)(2,1)S(1)} collective-permute-done((bf16[64,2048]{1,0:T(8,128)(2,1)S(1)}, bf16[64,2048]{1,0:T(8,128)(2,1)S(1)}, u32[]{:S(2)}, u32[]{:S(2)}) %collective-permute-start.28) | collective-permute-done | bytes 262176 | tf_op jit(solution)/shard_map/ppermute | solution.py:266
  174.8 2.1 collective-permute-start.33
  176.9 1.6 collective-permute-start.32
  179.1 7.5 %collective-permute-done.33 = bf16[128,2048]{1,0:T(8,128)(2,1)S(1)} collective-permute-done((bf16[128,2048]{1,0:T(8,128)(2,1)S(1)}, bf16[128,2048]{1,0:T(8,128)(2,1)S(1)}, u32[]{:S(2)}, u32[]{:S(2)}) %collective-permute-start.33) | collective-permute-done | bytes 524320 | tf_op jit(solution)/shard_map/ppermute | solution.py:266
  186.6 4.4 %collective-permute-done.32 = bf16[128,2048]{1,0:T(8,128)(2,1)S(1)} collective-permute-done((bf16[128,2048]{1,0:T(8,128)(2,1)S(1)}, bf16[128,2048]{1,0:T(8,128)(2,1)S(1)}, u32[]{:S(2)}, u32[]{:S(2)}) %collective-permute-start.32) | collective-permute-done | bytes 524320 | tf_op jit(solution)/shard_map/ppermute | solution.py:262
  191.3 0.7 collective-permute-start.35
  192.0 2.1 collective-permute-start.34
  194.9 3.5 %collective-permute-done.31 = bf16[128,2048]{1,0:T(8,128)(2,1)S(1)} collective-permute-done((bf16[128,2048]{1,0:T(8,128)(2,1)S(1)}, bf16[128,2048]{1,0:T(8,128)(2,1)S(1)}, u32[]{:S(2)}, u32[]{:S(2)}) %collective-permute-start.31) | collective-permute-done | bytes 524320 | tf_op jit(solution)/shard_map/ppermute | solution.py:262
  198.4 6.0 %collective-permute-done.34 = bf16[128,2048]{1,0:T(8,128)(2,1)S(1)} collective-permute-done((bf16[128,2048]{1,0:T(8,128)(2,1)S(1)}, bf16[128,2048]{1,0:T(8,128)(2,1)S(1)}, u32[]{:S(2)}, u32[]{:S(2)}) %collective-permute-start.34) | collective-permute-done | bytes 524320 | tf_op jit(solution)/shard_map/ppermute | solution.py:266
  204.8 3.3 %collective-permute-start.36 = (bf16[128,2048]{1,0:T(8,128)(2,1)S(1)}, bf16[128,2048]{1,0:T(8,128)(2,1)S(1)}, u32[]{:S(2)}, u32[]{:S(2)}) collective-permute-start(bf16[128,2048]{1,0:T(8,128)(2,1)S(1)} %add_convert_fusion.2), channel_id=1, source_target_pairs={{0,2},{1,3},{2,0},{3,1},{4,6},{5,7},{6,4},{7,5},{8,10},{9,11},{10,... | collective-permute-start | bytes 1572872 | tf_op jit(solution)/shard_map/ppermute | solution.py:266
  208.1 0.7 collective-permute-start.37
  208.8 6.5 %collective-permute-done.36 = bf16[128,2048]{1,0:T(8,128)(2,1)S(1)} collective-permute-done((bf16[128,2048]{1,0:T(8,128)(2,1)S(1)}, bf16[128,2048]{1,0:T(8,128)(2,1)S(1)}, u32[]{:S(2)}, u32[]{:S(2)}) %collective-permute-start.36) | collective-permute-done | bytes 524320 | tf_op jit(solution)/shard_map/ppermute | solution.py:266
  215.3 1.2 add_convert_fusion
  (111 shorter events, 11.3 us)
Async XLA Ops:
  6.5 9.0 %copy-start = (bf16[256,2048]{1,0:T(8,128)(2,1)S(1)}, bf16[256,2048]{1,0:T(8,128)(2,1)}, u32[]{:S(2)}) copy-start(bf16[256,2048]{1,0:T(8,128)(2,1)} %param.23) | copy-start | bytes 3145732
  6.5 73.7 %all-gather.2.cloned.1.call-start = ((), (), s32[]{:S(2)}) async-start(), calls=%async_computation | async-start | bytes 2621440 | tf_op jit(solution)/shard_map/all_gather | solution.py:270
  7.1 22.0 %copy-start.16 = (s32[128,4]{0,1:T(4,128)S(1)}, s32[128,4]{0,1:T(4,128)}, u32[]{:S(2)}) copy-start(s32[128,4]{0,1:T(4,128)} %param.25) | copy-start | bytes 6148
  7.1 22.1 %copy-start.17 = (bf16[128,4]{0,1:T(4,128)(2,1)S(1)}, bf16[128,4]{0,1:T(4,128)(2,1)}, u32[]{:S(2)}) copy-start(bf16[128,4]{0,1:T(4,128)(2,1)} %param.26) | copy-start | bytes 3076
  7.1 22.6 %copy-start.15 = (bf16[2048]{0:T(1024)(128)(2,1)S(1)}, bf16[2048]{0:T(1024)(128)(2,1)}, u32[]{:S(2)}) copy-start(bf16[2048]{0:T(1024)(128)(2,1)} %param.24) | copy-start | bytes 12292
  7.1 23.6 %copy-start.4 = (bf16[4,1024,256]{2,1,0:T(8,128)(2,1)S(1)}, bf16[4,1024,256]{2,1,0:T(8,128)(2,1)}, u32[]{:S(2)}) copy-start(bf16[4,1024,256]{2,1,0:T(8,128)(2,1)} %pk.5) | copy-start | bytes 6291460
  7.1 23.6 %copy-start.13 = (s32[2]{0:T(128)S(1)}, s32[2]{0:T(128)}, u32[]{:S(2)}) copy-start(s32[2]{0:T(128)} %pad_add_fusion.sc_ref) | copy-start | bytes 28
  12.1 18.6 %collective-permute-start.2 = (bf16[2,4,1024,128]{3,2,1,0:T(8,128)(2,1)}, bf16[2,4,1024,128]{3,2,1,0:T(8,128)(2,1)}, u32[]{:S(2)}, u32[]{:S(2)}) collective-permute-start(bf16[2,4,1024,128]{3,2,1,0:T(8,128)(2,1)} %get-tuple-element.68), channel_id=1, source_target_pairs={{0,8},{8,0},{16,24},{24,16},{1,9},{9,1},{17,25},{25,17},{2,10},{10... | collective-permute-start | bytes 6291464 | tf_op jit(solution)/shard_map/ppermute | solution.py:254
  12.5 5.7 %collective-permute-start.1 = (bf16[3,1024,128]{2,1,0:T(8,128)(2,1)}, bf16[3,1024,128]{2,1,0:T(8,128)(2,1)}, u32[]{:S(2)}, u32[]{:S(2)}) collective-permute-start(bf16[3,1024,128]{2,1,0:T(8,128)(2,1)} %get-tuple-element.65), channel_id=1, source_target_pairs={{0,8},{8,0},{16,24},{24,16},{1,9},{9,1},{17,25},{25,17},{2,10},{10... | collective-permute-start | bytes 2359304 | tf_op jit(solution)/shard_map/ppermute | solution.py:254
  12.6 15.4 %collective-permute-start.3 = (bf16[1024,256]{1,0:T(8,128)(2,1)}, bf16[1024,256]{1,0:T(8,128)(2,1)}, u32[]{:S(2)}, u32[]{:S(2)}) collective-permute-start(bf16[1024,256]{1,0:T(8,128)(2,1)} %q0.1), channel_id=1, source_target_pairs={{0,16},{8,24},{16,0},{24,8},{1,17},{9,25},{17,1},{25,9},{2,18},{10... | collective-permute-start | bytes 1572872 | tf_op jit(solution)/shard_map/ppermute | solution.py:258
  17.2 10.9 %collective-permute-start.4 = (s32[1,16]{1,0:T(1,128)S(1)}, s32[1,16]{1,0:T(1,128)S(1)}, u32[]{:S(2)}, u32[]{:S(2)}) collective-permute-start(s32[1,16]{1,0:T(1,128)S(1)} %pad_add_fusion.1.shape_a), channel_id=1, source_target_pairs={{0,16},{8,24},{16,0},{24,8},{1,17},{9,25},{17,1},{25,9},{2,18},{10... | collective-permute-start | bytes 200 | tf_op jit(solution)/shard_map/ppermute | solution.py:258
  17.2 1.1 collective-permute-start
  17.2 13.5 %copy-start.5 = (bf16[4,1024,256]{2,1,0:T(8,128)(2,1)S(1)}, bf16[4,1024,256]{2,1,0:T(8,128)(2,1)}, u32[]{:S(2)}) copy-start(bf16[4,1024,256]{2,1,0:T(8,128)(2,1)} %pv.5) | copy-start | bytes 6291460
  18.3 1.0 copy-start.7
  19.3 1.0 copy-start.8
  20.4 1.0 copy-start.9
  21.4 0.6 copy-start.12
  29.1 1.6 collective-permute-start.6
  29.2 1.5 collective-permute-start.5
  29.8 17.0 %copy-start.10 = (bf16[1024,256]{1,0:T(8,128)(2,1)S(1)}, bf16[1024,256]{1,0:T(8,128)(2,1)}, u32[]{:S(2)}) copy-start(bf16[1024,256]{1,0:T(8,128)(2,1)} %q0.1) | copy-start | bytes 1572868
  44.6 16.3 %collective-permute-start.8 = (f32[2,8,128]{2,1,0:T(8,128)S(1)}, f32[2,8,128]{2,1,0:T(8,128)S(1)}, u32[]{:S(2)}, u32[]{:S(2)}) collective-permute-start(f32[2,8,128]{2,1,0:T(8,128)S(1)} %get-tuple-element.75), channel_id=1, source_target_pairs={{0,16},{8,24},{16,0},{24,8},{1,17},{9,25},{17,1},{25,9},{2,18},{10... | collective-permute-start | bytes 24584 | tf_op jit(solution)/shard_map/ppermute | solution.py:258
  46.5 14.4 %collective-permute-start.7 = (bf16[2048,128]{1,0:T(8,128)(2,1)S(1)}, bf16[2048,128]{1,0:T(8,128)(2,1)S(1)}, u32[]{:S(2)}, u32[]{:S(2)}) collective-permute-start(bf16[2048,128]{1,0:T(8,128)(2,1)S(1)} %get-tuple-element.74), channel_id=1, source_target_pairs={{0,16},{8,24},{16,0},{24,8},{1,17},{9,25},{17,1},{25,9},{2,18},{10... | collective-permute-start | bytes 1572872 | tf_op jit(solution)/shard_map/ppermute | solution.py:258
  60.9 38.9 %copy-start.11 = (bf16[128,2048]{1,0:T(8,128)(2,1)S(1)}, bf16[128,2048]{1,0:T(8,128)(2,1)}, u32[]{:S(2)}) copy-start(bf16[128,2048]{1,0:T(8,128)(2,1)} %residual.1) | copy-start | bytes 1572868
  63.1 8.5 %collective-permute-start.11 = (bf16[2,272,128]{2,1,0:T(8,128)(2,1)S(1)}, bf16[2,272,128]{2,1,0:T(8,128)(2,1)S(1)}, u32[]{:S(2)}, u32[]{:S(2)}) collective-permute-start(bf16[2,272,128]{2,1,0:T(8,128)(2,1)S(1)} %get-tuple-element.125), channel_id=1, source_target_pairs={{0,6},{1,7},{2,4},{3,5},{4,2},{5,3},{6,0},{7,1},{8,14},{9,15},{10,... | collective-permute-start | bytes 417800 | tf_op jit(solution)/shard_map/ppermute | solution.py:650
  67.0 11.6 %collective-permute-start.10 = (bf16[2,272,128]{2,1,0:T(8,128)(2,1)S(1)}, bf16[2,272,128]{2,1,0:T(8,128)(2,1)S(1)}, u32[]{:S(2)}, u32[]{:S(2)}) collective-permute-start(bf16[2,272,128]{2,1,0:T(8,128)(2,1)S(1)} %get-tuple-element.126), channel_id=1, source_target_pairs={{0,4},{1,5},{2,6},{3,7},{4,0},{5,1},{6,2},{7,3},{8,12},{9,13},{10,... | collective-permute-start | bytes 417800 | tf_op jit(solution)/shard_map/ppermute | solution.py:650
  67.0 11.6 %collective-permute-start.9 = (bf16[2,272,128]{2,1,0:T(8,128)(2,1)S(1)}, bf16[2,272,128]{2,1,0:T(8,128)(2,1)S(1)}, u32[]{:S(2)}, u32[]{:S(2)}) collective-permute-start(bf16[2,272,128]{2,1,0:T(8,128)(2,1)S(1)} %get-tuple-element.127), channel_id=1, source_target_pairs={{0,2},{1,3},{2,0},{3,1},{4,6},{5,7},{6,4},{7,5},{8,10},{9,11},{10,... | collective-permute-start | bytes 417800 | tf_op jit(solution)/shard_map/ppermute | solution.py:650
  78.6 5.0 %collective-permute-start.13 = (bf16[4,16,128]{2,1,0:T(8,128)(2,1)S(1)}, bf16[4,16,128]{2,1,0:T(8,128)(2,1)S(1)}, u32[]{:S(2)}, u32[]{:S(2)}) collective-permute-start(bf16[4,16,128]{2,1,0:T(8,128)(2,1)S(1)} %pad_maximum_fusion.3.refs_0_), channel_id=1, source_target_pairs={{0,1},{1,0},{2,3},{3,2},{4,5},{5,4},{6,7},{7,6},{8,9},{9,8},{10,11... | collective-permute-start | bytes 49160 | tf_op jit(solution)/shard_map/ppermute | solution.py:262
  80.2 1.6 copy-start.6
  83.7 2.0 collective-permute-start.14
  83.8 2.6 %collective-permute-start.12 = (bf16[128,2048]{1,0:T(8,128)(2,1)S(1)}, bf16[128,2048]{1,0:T(8,128)(2,1)S(1)}, u32[]{:S(2)}, u32[]{:S(2)}) collective-permute-start(bf16[128,2048]{1,0:T(8,128)(2,1)S(1)} %get-tuple-element.77), channel_id=1, source_target_pairs={{0,8},{8,0},{16,24},{24,16},{1,9},{9,1},{17,25},{25,17},{2,10},{10... | collective-permute-start | bytes 1572872 | tf_op jit(solution)/shard_map/ppermute | solution.py:254
  85.8 14.0 %collective-permute-start.15 = (bf16[128,2048]{1,0:T(8,128)(2,1)S(1)}, bf16[128,2048]{1,0:T(8,128)(2,1)S(1)}, u32[]{:S(2)}, u32[]{:S(2)}) collective-permute-start(bf16[128,2048]{1,0:T(8,128)(2,1)S(1)} %add_convert_fusion.4), channel_id=1, source_target_pairs={{0,1},{1,0},{2,3},{3,2},{4,5},{5,4},{6,7},{7,6},{8,9},{9,8},{10,11... | collective-permute-start | bytes 1572872 | tf_op jit(solution)/shard_map/ppermute | solution.py:262
  100.3 13.2 %collective-permute-start.18 = (bf16[128,2048]{1,0:T(8,128)(2,1)S(1)}, bf16[128,2048]{1,0:T(8,128)(2,1)S(1)}, u32[]{:S(2)}, u32[]{:S(2)}) collective-permute-start(bf16[128,2048]{1,0:T(8,128)(2,1)S(1)} %get-tuple-element.87), channel_id=1, source_target_pairs={{0,1},{1,0},{2,3},{3,2},{4,5},{5,4},{6,7},{7,6},{8,9},{9,8},{10,11... | collective-permute-start | bytes 1572872 | tf_op jit(solution)/shard_map/ppermute | solution.py:262
  100.9 12.6 %collective-permute-start.17 = (bf16[128,2048]{1,0:T(8,128)(2,1)S(1)}, bf16[128,2048]{1,0:T(8,128)(2,1)}, u32[]{:S(2)}, u32[]{:S(2)}) collective-permute-start(bf16[128,2048]{1,0:T(8,128)(2,1)S(1)} %get-tuple-element.87), channel_id=1, source_target_pairs={{2,4},{3,5},{4,2},{5,3},{10,12},{11,13},{12,10},{13,11},{18,20},{1... | collective-permute-start | bytes 1572872 | tf_op jit(solution)/shard_map/ppermute | solution.py:276
  102.4 13.0 %collective-permute-start.16 = (bf16[128,2048]{1,0:T(8,128)(2,1)S(1)}, bf16[128,2048]{1,0:T(8,128)(2,1)}, u32[]{:S(2)}, u32[]{:S(2)}) collective-permute-start(bf16[128,2048]{1,0:T(8,128)(2,1)S(1)} %get-tuple-element.87), channel_id=1, source_target_pairs={{0,2},{1,3},{2,0},{3,1},{4,6},{5,7},{6,4},{7,5},{8,10},{9,11},{10,... | collective-permute-start | bytes 1572872 | tf_op jit(solution)/shard_map/ppermute | solution.py:266
  104.3 4.3 %copy-start.2 = (bf16[4,2048,704]{1,2,0:T(8,128)(2,1)S(1)}, bf16[4,2048,704]{1,2,0:T(8,128)(2,1)}, u32[]{:S(2)}) copy-start(bf16[4,2048,704]{1,2,0:T(8,128)(2,1)} %param.27) | copy-start | bytes 34603012
  113.5 17.4 %copy-start.14 = (bf16[128,2048]{1,0:T(8,128)(2,1)}, bf16[128,2048]{1,0:T(8,128)(2,1)S(1)}, u32[]{:S(2)}) copy-start(bf16[128,2048]{1,0:T(8,128)(2,1)S(1)} %collective-permute-done.18) | copy-start | bytes 1572868
  115.4 15.6 %collective-permute-start.21 = (bf16[128,2048]{1,0:T(8,128)(2,1)}, bf16[128,2048]{1,0:T(8,128)(2,1)S(1)}, u32[]{:S(2)}, u32[]{:S(2)}) collective-permute-start(bf16[128,2048]{1,0:T(8,128)(2,1)} %collective-permute-done.16), channel_id=1, source_target_pairs={{0,1},{1,0},{2,3},{3,2},{4,5},{5,4},{6,7},{7,6},{8,9},{9,8},{10,11... | collective-permute-start | bytes 1572872 | tf_op jit(solution)/shard_map/ppermute | solution.py:262
  116.9 14.1 %collective-permute-start.20 = (bf16[128,2048]{1,0:T(8,128)(2,1)}, bf16[128,2048]{1,0:T(8,128)(2,1)S(1)}, u32[]{:S(2)}, u32[]{:S(2)}) collective-permute-start(bf16[128,2048]{1,0:T(8,128)(2,1)} %collective-permute-done.16), channel_id=1, source_target_pairs={{2,4},{3,5},{4,2},{5,3},{10,12},{11,13},{12,10},{13,11},{18,20},{1... | collective-permute-start | bytes 1572872 | tf_op jit(solution)/shard_map/ppermute | solution.py:276
  117.6 13.4 %collective-permute-start.19 = (bf16[128,2048]{1,0:T(8,128)(2,1)}, bf16[128,2048]{1,0:T(8,128)(2,1)S(1)}, u32[]{:S(2)}, u32[]{:S(2)}) collective-permute-start(bf16[128,2048]{1,0:T(8,128)(2,1)} %collective-permute-done.17), channel_id=1, source_target_pairs={{0,2},{1,3},{2,0},{3,1},{4,6},{5,7},{6,4},{7,5},{8,10},{9,11},{10,... | collective-permute-start | bytes 1572872 | tf_op jit(solution)/shard_map/ppermute | solution.py:266
  120.7 4.3 %copy-start.3 = (bf16[4,704,2048]{2,1,0:T(8,128)(2,1)S(1)}, bf16[4,704,2048]{2,1,0:T(8,128)(2,1)}, u32[]{:S(2)}) copy-start(bf16[4,704,2048]{2,1,0:T(8,128)(2,1)} %source) | copy-start | bytes 34603012
  125.0 27.1 %slice-start = ((s8[11534336]{0:T(1024)(128)(4,1)}), s8[4194304]{0:T(1024)(128)(4,1)S(1)}, s32[]{:S(2)}) async-start(s8[11534336]{0:T(1024)(128)(4,1)} %bitcast.40), calls=%async_computation.1 | async-start | bytes 8388608
  125.0 27.1 %slice-start.1 = ((s8[11534336]{0:T(1024)(128)(4,1)}), s8[4194304]{0:T(1024)(128)(4,1)S(1)}, s32[]{:S(2)}) async-start(s8[11534336]{0:T(1024)(128)(4,1)} %bitcast.40), calls=%async_computation.2 | async-start | bytes 8388608
  128.0 24.2 %slice-start.2 = ((s8[11534336]{0:T(1024)(128)(4,1)}), s8[3145728]{0:T(1024)(128)(4,1)S(1)}, s32[]{:S(2)}) async-start(s8[11534336]{0:T(1024)(128)(4,1)} %bitcast.40), calls=%async_computation.3 | async-start | bytes 6291456
  131.0 11.4 %collective-permute-start.22 = (bf16[128,2048]{1,0:T(8,128)(2,1)S(1)}, bf16[128,2048]{1,0:T(8,128)(2,1)S(1)}, u32[]{:S(2)}, u32[]{:S(2)}) collective-permute-start(bf16[128,2048]{1,0:T(8,128)(2,1)S(1)} %collective-permute-done.20), channel_id=1, source_target_pairs={{0,2},{1,3},{2,0},{3,1},{4,6},{5,7},{6,4},{7,5},{8,10},{9,11},{10,... | collective-permute-start | bytes 1572872 | tf_op jit(solution)/shard_map/ppermute | solution.py:266
  133.1 9.2 %collective-permute-start.23 = (bf16[128,2048]{1,0:T(8,128)(2,1)S(1)}, bf16[128,2048]{1,0:T(8,128)(2,1)S(1)}, u32[]{:S(2)}, u32[]{:S(2)}) collective-permute-start(bf16[128,2048]{1,0:T(8,128)(2,1)S(1)} %broadcast_select_fusion.1), channel_id=1, source_target_pairs={{0,1},{1,0},{2,3},{3,2},{4,5},{5,4},{6,7},{7,6},{8,9},{9,8},{10,11... | collective-permute-start | bytes 1572872 | tf_op jit(solution)/shard_map/ppermute | solution.py:262
  136.0 10.2 %collective-permute-start.26 = (bf16[64,2048]{1,0:T(8,128)(2,1)S(1)}, bf16[64,2048]{1,0:T(8,128)(2,1)S(1)}, u32[]{:S(2)}, u32[]{:S(2)}) collective-permute-start(bf16[64,2048]{1,0:T(8,128)(2,1)S(1)} %slice.92), channel_id=1, source_target_pairs={{2,4},{3,5},{4,2},{5,3},{10,12},{11,13},{12,10},{13,11},{18,20},{1... | collective-permute-start | bytes 786440 | tf_op jit(solution)/shard_map/ppermute | solution.py:276
  142.5 7.0 %collective-permute-start.25 = (bf16[64,2048]{1,0:T(8,128)(2,1)S(1)}, bf16[64,2048]{1,0:T(8,128)(2,1)S(1)}, u32[]{:S(2)}, u32[]{:S(2)}) collective-permute-start(bf16[64,2048]{1,0:T(8,128)(2,1)S(1)} %slice.91), channel_id=1, source_target_pairs={{0,2},{1,3},{2,0},{3,1},{4,6},{5,7},{6,4},{7,5},{8,10},{9,11},{10,... | collective-permute-start | bytes 786440 | tf_op jit(solution)/shard_map/ppermute | solution.py:266
  145.1 6.4 %collective-permute-start.24 = (bf16[64,2048]{1,0:T(8,128)(2,1)S(1)}, bf16[64,2048]{1,0:T(8,128)(2,1)S(1)}, u32[]{:S(2)}, u32[]{:S(2)}) collective-permute-start(bf16[64,2048]{1,0:T(8,128)(2,1)S(1)} %slice.109), channel_id=1, source_target_pairs={{0,1},{1,0},{2,3},{3,2},{4,5},{5,4},{6,7},{7,6},{8,9},{9,8},{10,11... | collective-permute-start | bytes 786440 | tf_op jit(solution)/shard_map/ppermute | solution.py:262
  152.2 64.3 %copy-start.1 = (bf16[256,2048]{1,0:T(8,128)(2,1)S(1)}, bf16[256,2048]{1,0:T(8,128)(2,1)}, u32[]{:S(2)}) copy-start(bf16[256,2048]{1,0:T(8,128)(2,1)} %param.23) | copy-start | bytes 3145732
  163.8 7.6 %collective-permute-start.27 = (bf16[64,2048]{1,0:T(8,128)(2,1)S(1)}, bf16[64,2048]{1,0:T(8,128)(2,1)S(1)}, u32[]{:S(2)}, u32[]{:S(2)}) collective-permute-start(bf16[64,2048]{1,0:T(8,128)(2,1)S(1)} %get-tuple-element.107), channel_id=1, source_target_pairs={{0,1},{1,0},{2,3},{3,2},{4,5},{5,4},{6,7},{7,6},{8,9},{9,8},{10,11... | collective-permute-start | bytes 786440 | tf_op jit(solution)/shard_map/ppermute | solution.py:262
  164.4 7.0 %collective-permute-start.29 = (bf16[64,2048]{1,0:T(8,128)(2,1)S(1)}, bf16[64,2048]{1,0:T(8,128)(2,1)S(1)}, u32[]{:S(2)}, u32[]{:S(2)}) collective-permute-start(bf16[64,2048]{1,0:T(8,128)(2,1)S(1)} %get-tuple-element.108), channel_id=1, source_target_pairs={{2,4},{3,5},{4,2},{5,3},{10,12},{11,13},{12,10},{13,11},{18,20},{1... | collective-permute-start | bytes 786440 | tf_op jit(solution)/shard_map/ppermute | solution.py:276
  165.1 9.5 %collective-permute-start.28 = (bf16[64,2048]{1,0:T(8,128)(2,1)S(1)}, bf16[64,2048]{1,0:T(8,128)(2,1)S(1)}, u32[]{:S(2)}, u32[]{:S(2)}) collective-permute-start(bf16[64,2048]{1,0:T(8,128)(2,1)S(1)} %get-tuple-element.108), channel_id=1, source_target_pairs={{0,2},{1,3},{2,0},{3,1},{4,6},{5,7},{6,4},{7,5},{8,10},{9,11},{10,... | collective-permute-start | bytes 786440 | tf_op jit(solution)/shard_map/ppermute | solution.py:266
  174.8 11.8 %collective-permute-start.33 = (bf16[128,2048]{1,0:T(8,128)(2,1)S(1)}, bf16[128,2048]{1,0:T(8,128)(2,1)S(1)}, u32[]{:S(2)}, u32[]{:S(2)}) collective-permute-start(bf16[128,2048]{1,0:T(8,128)(2,1)S(1)} %pad_maximum_fusion.2), channel_id=1, source_target_pairs={{0,2},{1,3},{2,0},{3,1},{4,6},{5,7},{6,4},{7,5},{8,10},{9,11},{10,... | collective-permute-start | bytes 1572872 | tf_op jit(solution)/shard_map/ppermute | solution.py:266
  176.9 14.1 %collective-permute-start.32 = (bf16[128,2048]{1,0:T(8,128)(2,1)S(1)}, bf16[128,2048]{1,0:T(8,128)(2,1)S(1)}, u32[]{:S(2)}, u32[]{:S(2)}) collective-permute-start(bf16[128,2048]{1,0:T(8,128)(2,1)S(1)} %pad_maximum_fusion.1), channel_id=1, source_target_pairs={{0,1},{1,0},{2,3},{3,2},{4,5},{5,4},{6,7},{7,6},{8,9},{9,8},{10,11... | collective-permute-start | bytes 1572872 | tf_op jit(solution)/shard_map/ppermute | solution.py:262
  178.5 19.8 %collective-permute-start.31 = (bf16[128,2048]{1,0:T(8,128)(2,1)S(1)}, bf16[128,2048]{1,0:T(8,128)(2,1)S(1)}, u32[]{:S(2)}, u32[]{:S(2)}) collective-permute-start(bf16[128,2048]{1,0:T(8,128)(2,1)S(1)} %get-tuple-element.111), channel_id=1, source_target_pairs={{0,1},{1,0},{2,3},{3,2},{4,5},{5,4},{6,7},{7,6},{8,9},{9,8},{10,11... | collective-permute-start | bytes 1572872 | tf_op jit(solution)/shard_map/ppermute | solution.py:262
  191.3 7.1 %collective-permute-start.35 = (bf16[128,2048]{1,0:T(8,128)(2,1)S(1)}, bf16[128,2048]{1,0:T(8,128)(2,1)S(1)}, u32[]{:S(2)}, u32[]{:S(2)}) collective-permute-start(bf16[128,2048]{1,0:T(8,128)(2,1)S(1)} %add_convert_fusion.3), channel_id=1, source_target_pairs={{2,4},{3,5},{4,2},{5,3},{10,12},{11,13},{12,10},{13,11},{18,20},{1... | collective-permute-start | bytes 1572872 | tf_op jit(solution)/shard_map/ppermute | solution.py:276
  192.0 12.4 %collective-permute-start.34 = (bf16[128,2048]{1,0:T(8,128)(2,1)S(1)}, bf16[128,2048]{1,0:T(8,128)(2,1)S(1)}, u32[]{:S(2)}, u32[]{:S(2)}) collective-permute-start(bf16[128,2048]{1,0:T(8,128)(2,1)S(1)} %add_convert_fusion.3), channel_id=1, source_target_pairs={{0,2},{1,3},{2,0},{3,1},{4,6},{5,7},{6,4},{7,5},{8,10},{9,11},{10,... | collective-permute-start | bytes 1572872 | tf_op jit(solution)/shard_map/ppermute | solution.py:266
  194.3 14.5 %collective-permute-start.30 = (bf16[128,2048]{1,0:T(8,128)(2,1)S(1)}, bf16[128,2048]{1,0:T(8,128)(2,1)S(1)}, u32[]{:S(2)}, u32[]{:S(2)}) collective-permute-start(bf16[128,2048]{1,0:T(8,128)(2,1)S(1)} %pad_maximum_fusion), channel_id=1, source_target_pairs={{0,1},{1,0},{2,3},{3,2},{4,5},{5,4},{6,7},{7,6},{8,9},{9,8},{10,11... | collective-permute-start | bytes 1572872 | tf_op jit(solution)/shard_map/ppermute | solution.py:262
  204.8 10.5 %collective-permute-start.36 = (bf16[128,2048]{1,0:T(8,128)(2,1)S(1)}, bf16[128,2048]{1,0:T(8,128)(2,1)S(1)}, u32[]{:S(2)}, u32[]{:S(2)}) collective-permute-start(bf16[128,2048]{1,0:T(8,128)(2,1)S(1)} %add_convert_fusion.2), channel_id=1, source_target_pairs={{0,2},{1,3},{2,0},{3,1},{4,6},{5,7},{6,4},{7,5},{8,10},{9,11},{10,... | collective-permute-start | bytes 1572872 | tf_op jit(solution)/shard_map/ppermute | solution.py:266
  208.1 7.2 %collective-permute-start.37 = (bf16[128,2048]{1,0:T(8,128)(2,1)S(1)}, bf16[128,2048]{1,0:T(8,128)(2,1)S(1)}, u32[]{:S(2)}, u32[]{:S(2)}) collective-permute-start(bf16[128,2048]{1,0:T(8,128)(2,1)S(1)} %add_convert_fusion.1), channel_id=1, source_target_pairs={{2,4},{3,5},{4,2},{5,3},{10,12},{11,13},{12,10},{13,11},{18,20},{1... | collective-permute-start | bytes 1572872 | tf_op jit(solution)/shard_map/ppermute | solution.py:276
Sparse Core Ops, SparseCore 0:
  16.5 46.2 all-gather.1

commit v8 on v7

--- a/solution.py
+++ b/solution.py
@@ -247,6 +247,7 @@
 LOG2E = 1.4426950408889634
 SCORE_SCALE = LOG2E / math.sqrt(HEAD)
 VMEM_BIG = 28 * 1024 * 1024
+VMEM_MOST = 56 * 1024 * 1024
 VMEM_SMALL = 12 * 1024 * 1024
 
 
@@ -276,33 +277,39 @@
     return lax.ppermute(array, "exp", [(2, 4), (3, 5), (4, 2), (5, 3)])
 
 
-def split_kernel(sc_ref, q, k, v, pk, pv, out_tokens, out_prefix):
-    for i, part in enumerate((q, k, v)):
-        out_tokens[i] = part[...]
-    out_prefix[0] = pk[...]
-    out_prefix[1] = pv[...]
+def split_kernel(sc_ref, q, k, v, pk, pv, out_tokens, out_prefix, sems):
+    theirs = pl.ds(pl.multiple_of((1 - sc_ref[0]) * HEAD, HEAD), HEAD)
+    copies = [
+        pltpu.make_async_copy(part.at[:, theirs], out_tokens.at[i], sems.at[i])
+        for i, part in enumerate((q, k, v))
+    ]
+    for i, part in enumerate((pk, pv)):
+        for g in range(G):
+            copies.append(
+                pltpu.make_async_copy(
+                    part.at[g, :, theirs], out_prefix.at[i, g], sems.at[3 + i * G + g]
+                )
+            )
+    for copy in copies:
+        copy.start()
+    for copy in copies:
+        copy.wait()
 
 
 def split_theirs(place, q, k, v, pk, pv):
     rows, span = q.shape[0], pk.shape[1]
-    part = rows // G
-    tokens = pl.BlockSpec((part, HEAD), lambda i, s: (i, 1 - s[0]))
-    prefix = pl.BlockSpec((1, span, HEAD), lambda i, s: (i, 0, 1 - s[0]))
+    vmem = pl.BlockSpec(memory_space=pltpu.VMEM)
     return pl.pallas_call(
         split_kernel,
-        grid_spec=pltpu.PrefetchScalarGridSpec(
-            num_scalar_prefetch=1,
-            grid=(G,),
-            in_specs=[tokens] * 3 + [prefix] * 2,
-            out_specs=[
-                pl.BlockSpec((3, part, HEAD), lambda i, s: (0, i, 0)),
-                pl.BlockSpec((2, 1, span, HEAD), lambda i, s: (0, i, 0, 0)),
-            ],
-        ),
+        in_specs=[pl.BlockSpec(memory_space=pltpu.SMEM)]
+        + [pl.BlockSpec(memory_space=pl.ANY)] * 5,
+        out_specs=[vmem, vmem],
         out_shape=(
             jax.ShapeDtypeStruct((3, rows, HEAD), q.dtype),
             jax.ShapeDtypeStruct((2, G, span, HEAD), q.dtype),
         ),
+        scratch_shapes=[pltpu.SemaphoreType.DMA((3 + 2 * G,))],
+        compiler_params=pltpu.CompilerParams(vmem_limit_bytes=VMEM_MOST),
         name="split_theirs",
     )(place, q, k, v, pk, pv)
 
@@ -588,7 +595,7 @@
             jax.ShapeDtypeStruct((rows * tokens, HEAD), jnp.float32),
             jax.ShapeDtypeStruct((rows, blocks, BLK), jnp.float32),
         ),
-        compiler_params=pltpu.CompilerParams(vmem_limit_bytes=VMEM_BIG),
+        compiler_params=pltpu.CompilerParams(vmem_limit_bytes=VMEM_MOST),
         cost_estimate=pl.CostEstimate(
             flops=rows * tokens * tokens * HEAD * 4 * 4, bytes_accessed=1 << 20, transcendentals=0
         ),

time: 225 us -> 225 us (level)
  local copies, waits for them, and re-layouts: 15.9 us -> 12.7 us
    unnamed x42 -> x46, local copies, waits for them, and re-layouts: 13.9 us -> 10.7 us
where the time goes in v8:
time: 225 us; the launch traced here: 222 us
  waiting for transfers between devices  85.5 us (38%)
  Pallas kernels  55.7 us (25%)
  starting transfers between devices  43.9 us (20%)
  between operations  14 us (6%)
  local copies, waits for them, and re-layouts  12.7 us (6%)
  matrix products  5.2 us (2%)
  other arithmetic  4.91 us (2%)
    ppermute x10, waiting for transfers between devices, y_swap(): return lax.ppermute(array, 'exp', [(i, i ^ 1) for i in range(8)])  36.9 us
    ppermute x8, waiting for transfers between devices, outer_swap(): return lax.ppermute(array, 'exp', [(i, i ^ 2) for i in range(8)])  30.9 us
    pallas_call x2, Pallas kernels, prefix_attend(): pl.pallas_call(prefix_kernel, in_specs=[smem] * 3 + [anywhere] * 5, out_s...  27 us
    ppermute x8, starting transfers between devices, outer_swap(): return lax.ppermute(array, 'exp', [(i, i ^ 2) for i in range(8)])  18.8 us
    pallas_call x1, Pallas kernels, run_experts(): pl.pallas_call(experts_kernel, in_specs=[vmem] * 12, out_specs=[vmem] * 9...  11.6 us
    ppermute x3, waiting for transfers between devices, exchange_heads(): lax.ppermute(attended[2 * d:2 * d + 2], 'exp', [(i, i ^ 2 * d) for i in r...  11 us
    unnamed x46, local copies, waits for them, and re-layouts  10.7 us
    ppermute x10, starting transfers between devices, y_swap(): return lax.ppermute(array, 'exp', [(i, i ^ 1) for i in range(8)])  8.81 us
  transfers between devices with their start and end apart: 39, of which 20 were waited for; matrix products, arithmetic and copies ran while one was open for 4% of the time, Pallas kernels for 18%

profile of v8, /device:TPU:0, one launch (start us, length us, event | category | flops | bytes accessed | tf_op | source)
XLA Modules:
  0.0 221.9 jit_solution(12583196355631337214)
XLA Ops:
  6.5 0.6 pad_add_fusion.sc_ref
  7.2 4.2 %split_theirs.1 = (bf16[3,1024,128]{2,1,0:T(8,128)(2,1)}, bf16[2,4,1024,128]{3,2,1,0:T(8,128)(2,1)}) custom-call(s32[2]{0:T(128)} %pad_add_fusion.sc_ref, bf16[1024,256]{1,0:T(8,128)(2,1)} %q0.1, bf16[1024,256]{1,0:T(8,128)(2,1)} %k.3, bf16[1024,256]{1,0:T(8,128)(2,1)} %v.3, bf16[4,1024,256]{2,1,0:T(8,128)(2,1)} %pk.5, bf16[4,1024,256]{2,1,0:T(8,128)(2,1)} %pv.5), custom_call_target="tpu_custom_call" | custom-call | tf_op jit(solution)/shard_map/split_theirs/pallas_call | solution.py:302
  12.0 2.9 %collective-permute-start.3 = (bf16[1024,256]{1,0:T(8,128)(2,1)}, bf16[1024,256]{1,0:T(8,128)(2,1)}, u32[]{:S(2)}, u32[]{:S(2)}) collective-permute-start(bf16[1024,256]{1,0:T(8,128)(2,1)} %q0.1), channel_id=1, source_target_pairs={{0,16},{8,24},{16,0},{24,8},{1,17},{9,25},{17,1},{25,9},{2,18},{10... | collective-permute-start | bytes 1572872 | tf_op jit(solution)/shard_map/ppermute | solution.py:259
  15.0 0.8 constant_dynamic-slice_fusion
  15.8 0.7 pad_add_fusion.1.shape_a
  16.7 1.1 collective-permute-done.shape_b
  18.3 5.9 %suffix_attend.1 = (f32[2048,128]{1,0:T(8,128)}, f32[2,8,128]{2,1,0:T(8,128)}) custom-call(s32[2]{0:T(128)} %pad_add_fusion.sc_ref, s32[1,16]{1,0:T(1,128)} %copy-done.12, s32[1,16]{1,0:T(1,128)} %copy-done.14, bf16[1024,256]{1,0:T(8,128)(2,1)} %q0.1, bf16[1024,256]{1,0:T(8,128)(2,1)} %k.3, bf16[1024,256]{1,0:T(8,128)(2,1)} %v.3, ...), custom_call_target="tpu_custom_call" | custom-call | flops 4294967296 | bytes 1048576 | tf_op jit(solution)/shard_map/suffix_attend/pallas_call | solution.py:581
  24.1 3.3 %collective-permute-done.4.shape_a = s32[1,16]{1,0:T(1,128)S(1)} collective-permute-done((s32[1,16]{1,0:T(1,128)S(1)}, s32[1,16]{1,0:T(1,128)S(1)}, u32[]{:S(2)}, u32[]{:S(2)}) %collective-permute-start.4) | collective-permute-done | bytes 96 | tf_op jit(solution)/shard_map/ppermute | solution.py:259
  27.4 1.1 select_bitcast_fusion
  29.2 0.9 collective-permute-done.5.shape_b
  30.1 13.9 %prefix_attend.3 = (bf16[2048,128]{1,0:T(8,128)(2,1)S(1)}, f32[2,8,128]{2,1,0:T(8,128)S(1)}) custom-call(s32[2]{0:T(128)S(1)} %copy-done.11, s32[1,16]{1,0:T(1,128)S(1)} %collective-permute-done.4.shape_a, s32[1,16]{1,0:T(1,128)S(1)} %collective-permute-done.5.shape_b, bf16[1024,256]{1,0:T(8,128)(2,1)} %collective-permute-done.3.q0, ...), custom_call_target="tpu_custom_call" | custom-call | flops 8589934592 | bytes 4194304 | tf_op jit(solution)/shard_map/prefix_attend/pallas_call | solution.py:495
  44.1 0.8 collective-permute-start.8
  44.9 1.3 collective-permute-start.7
  46.2 13.1 %prefix_attend.2 = (f32[2048,128]{1,0:T(8,128)S(1)}, f32[2,8,128]{2,1,0:T(8,128)S(1)}) custom-call(s32[2]{0:T(128)S(1)} %copy-done.11, s32[1,16]{1,0:T(1,128)S(1)} %copy-done.13, s32[1,16]{1,0:T(1,128)S(1)} %copy-done.15, bf16[1024,256]{1,0:T(8,128)(2,1)S(1)} %copy-done.8, bf16[3,1024,128]{2,1,0:T(8,128)(2,1)} %collective-permute-done.1.other_row.q1, ...), custom_call_target="tpu_custom_call" | custom-call | flops 8589934592 | bytes 4194304 | tf_op jit(solution)/shard_map/prefix_attend/pallas_call | solution.py:495
  59.3 2.1 merge_parts.1
  61.5 3.9 %collective-permute-start.11 = (bf16[2,272,128]{2,1,0:T(8,128)(2,1)S(1)}, bf16[2,272,128]{2,1,0:T(8,128)(2,1)S(1)}, u32[]{:S(2)}, u32[]{:S(2)}) collective-permute-start(bf16[2,272,128]{2,1,0:T(8,128)(2,1)S(1)} %get-tuple-element.125), channel_id=1, source_target_pairs={{0,6},{1,7},{2,4},{3,5},{4,2},{5,3},{6,0},{7,1},{8,14},{9,15},{10,... | collective-permute-start | bytes 417800 | tf_op jit(solution)/shard_map/ppermute | solution.py:657
  65.5 0.6 collective-permute-start.9
  66.1 3.9 %collective-permute-done.11.refs_3_ = bf16[2,272,128]{2,1,0:T(8,128)(2,1)S(1)} collective-permute-done((bf16[2,272,128]{2,1,0:T(8,128)(2,1)S(1)}, bf16[2,272,128]{2,1,0:T(8,128)(2,1)S(1)}, u32[]{:S(2)}, u32[]{:S(2)}) %collective-permute-start.11) | collective-permute-done | bytes 139296 | tf_op jit(solution)/shard_map/ppermute | solution.py:657
  70.0 7.0 %collective-permute-done.10.refs_2_ = bf16[2,272,128]{2,1,0:T(8,128)(2,1)S(1)} collective-permute-done((bf16[2,272,128]{2,1,0:T(8,128)(2,1)S(1)}, bf16[2,272,128]{2,1,0:T(8,128)(2,1)S(1)}, u32[]{:S(2)}, u32[]{:S(2)}) %collective-permute-start.10) | collective-permute-done | bytes 139296 | tf_op jit(solution)/shard_map/ppermute | solution.py:657
  77.1 1.6 collective-permute-start.13
  78.7 1.6 copy-done.7
  80.3 1.9 project.1
  82.7 1.4 collective-permute-done.14
  84.9 13.4 %collective-permute-done.15.late = bf16[128,2048]{1,0:T(8,128)(2,1)S(1)} collective-permute-done((bf16[128,2048]{1,0:T(8,128)(2,1)S(1)}, bf16[128,2048]{1,0:T(8,128)(2,1)S(1)}, u32[]{:S(2)}, u32[]{:S(2)}) %collective-permute-start.15) | collective-permute-done | bytes 524320 | tf_op jit(solution)/shard_map/ppermute | solution.py:263
  99.4 1.5 collective-permute-start.17
  100.9 1.0 collective-permute-start.16
  101.8 0.8 route.1
  102.7 4.3 %copy-done.2 = bf16[4,2048,704]{1,2,0:T(8,128)(2,1)S(1)} copy-done((bf16[4,2048,704]{1,2,0:T(8,128)(2,1)S(1)}, bf16[4,2048,704]{1,2,0:T(8,128)(2,1)}, u32[]{:S(2)}) %copy-start.2) | copy-done | bytes 11534360
  107.0 0.8 stage.2.refs_9_
  107.8 4.2 %collective-permute-done.18 = bf16[128,2048]{1,0:T(8,128)(2,1)S(1)} collective-permute-done((bf16[128,2048]{1,0:T(8,128)(2,1)S(1)}, bf16[128,2048]{1,0:T(8,128)(2,1)S(1)}, u32[]{:S(2)}, u32[]{:S(2)}) %collective-permute-start.18) | collective-permute-done | bytes 524320 | tf_op jit(solution)/shard_map/ppermute | solution.py:263
  112.0 1.8 collective-permute-done.16
  113.8 1.5 collective-permute-start.21
  115.3 0.7 collective-permute-start.20
  116.0 3.2 %collective-permute-start.19 = (bf16[128,2048]{1,0:T(8,128)(2,1)}, bf16[128,2048]{1,0:T(8,128)(2,1)S(1)}, u32[]{:S(2)}, u32[]{:S(2)}) collective-permute-start(bf16[128,2048]{1,0:T(8,128)(2,1)} %collective-permute-done.17), channel_id=1, source_target_pairs={{0,2},{1,3},{2,0},{3,1},{4,6},{5,7},{6,4},{7,5},{8,10},{9,11},{10,... | collective-permute-start | bytes 1572872 | tf_op jit(solution)/shard_map/ppermute | solution.py:267
  119.2 4.3 %copy-done.3 = bf16[4,704,2048]{2,1,0:T(8,128)(2,1)S(1)} copy-done((bf16[4,704,2048]{2,1,0:T(8,128)(2,1)S(1)}, bf16[4,704,2048]{2,1,0:T(8,128)(2,1)}, u32[]{:S(2)}) %copy-start.3) | copy-done | bytes 11534360
  123.5 0.8 stage.3.refs_11_
  124.6 1.8 convolution_convert_fusion.5.refs_1_
  126.5 2.9 %collective-permute-done.19 = bf16[128,2048]{1,0:T(8,128)(2,1)S(1)} collective-permute-done((bf16[128,2048]{1,0:T(8,128)(2,1)}, bf16[128,2048]{1,0:T(8,128)(2,1)S(1)}, u32[]{:S(2)}, u32[]{:S(2)}) %collective-permute-start.19) | collective-permute-done | bytes 524320 | tf_op jit(solution)/shard_map/ppermute | solution.py:267
  129.4 2.1 collective-permute-start.22
  132.1 1.3 convolution_convert_fusion.2.refs_4_
  133.5 1.0 slice.92
  134.5 0.7 collective-permute-start.26
  135.7 5.1 %collective-permute-done.23 = bf16[128,2048]{1,0:T(8,128)(2,1)S(1)} collective-permute-done((bf16[128,2048]{1,0:T(8,128)(2,1)S(1)}, bf16[128,2048]{1,0:T(8,128)(2,1)S(1)}, u32[]{:S(2)}, u32[]{:S(2)}) %collective-permute-start.23) | collective-permute-done | bytes 524320 | tf_op jit(solution)/shard_map/ppermute | solution.py:263
  140.9 2.7 %collective-permute-start.25 = (bf16[64,2048]{1,0:T(8,128)(2,1)S(1)}, bf16[64,2048]{1,0:T(8,128)(2,1)S(1)}, u32[]{:S(2)}, u32[]{:S(2)}) collective-permute-start(bf16[64,2048]{1,0:T(8,128)(2,1)S(1)} %slice.91), channel_id=1, source_target_pairs={{0,2},{1,3},{2,0},{3,1},{4,6},{5,7},{6,4},{7,5},{8,10},{9,11},{10,... | collective-permute-start | bytes 786440 | tf_op jit(solution)/shard_map/ppermute | solution.py:267
  144.7 3.2 %collective-permute-done.25 = bf16[64,2048]{1,0:T(8,128)(2,1)S(1)} collective-permute-done((bf16[64,2048]{1,0:T(8,128)(2,1)S(1)}, bf16[64,2048]{1,0:T(8,128)(2,1)S(1)}, u32[]{:S(2)}, u32[]{:S(2)}) %collective-permute-start.25) | collective-permute-done | bytes 262176 | tf_op jit(solution)/shard_map/ppermute | solution.py:267
  148.0 2.0 collective-permute-done.24
  150.6 11.6 %experts.1 = (bf16[128,2048]{1,0:T(8,128)(2,1)S(1)}, bf16[128,2048]{1,0:T(8,128)(2,1)S(1)}, bf16[128,2048]{1,0:T(8,128)(2,1)S(1)}, bf16[128,2048]{1,0:T(8,128)(2...) custom-call(bf16[128,2048]{1,0:T(8,128)(2,1)S(1)} %convolution_conve, ...), custom_call_target="tpu_custom_call" | custom-call | tf_op jit(solution)/shard_map/experts/pallas_call | solution.py:823
  162.9 0.7 collective-permute-start.29
  163.5 2.2 %collective-permute-start.28 = (bf16[64,2048]{1,0:T(8,128)(2,1)S(1)}, bf16[64,2048]{1,0:T(8,128)(2,1)S(1)}, u32[]{:S(2)}, u32[]{:S(2)}) collective-permute-start(bf16[64,2048]{1,0:T(8,128)(2,1)S(1)} %get-tuple-element.108), channel_id=1, source_target_pairs={{0,2},{1,3},{2,0},{3,1},{4,6},{5,7},{6,4},{7,5},{8,10},{9,11},{10,... | collective-permute-start | bytes 786440 | tf_op jit(solution)/shard_map/ppermute | solution.py:267
  165.8 4.1 %collective-permute-done.27 = bf16[64,2048]{1,0:T(8,128)(2,1)S(1)} collective-permute-done((bf16[64,2048]{1,0:T(8,128)(2,1)S(1)}, bf16[64,2048]{1,0:T(8,128)(2,1)S(1)}, u32[]{:S(2)}, u32[]{:S(2)}) %collective-permute-start.27) | collective-permute-done | bytes 262176 | tf_op jit(solution)/shard_map/ppermute | solution.py:263
  169.9 3.0 %collective-permute-done.28 = bf16[64,2048]{1,0:T(8,128)(2,1)S(1)} collective-permute-done((bf16[64,2048]{1,0:T(8,128)(2,1)S(1)}, bf16[64,2048]{1,0:T(8,128)(2,1)S(1)}, u32[]{:S(2)}, u32[]{:S(2)}) %collective-permute-start.28) | collective-permute-done | bytes 262176 | tf_op jit(solution)/shard_map/ppermute | solution.py:267
  173.2 2.1 collective-permute-start.33
  175.3 1.6 collective-permute-start.32
  177.5 7.4 %collective-permute-done.33 = bf16[128,2048]{1,0:T(8,128)(2,1)S(1)} collective-permute-done((bf16[128,2048]{1,0:T(8,128)(2,1)S(1)}, bf16[128,2048]{1,0:T(8,128)(2,1)S(1)}, u32[]{:S(2)}, u32[]{:S(2)}) %collective-permute-start.33) | collective-permute-done | bytes 524320 | tf_op jit(solution)/shard_map/ppermute | solution.py:267
  184.9 4.6 %collective-permute-done.32 = bf16[128,2048]{1,0:T(8,128)(2,1)S(1)} collective-permute-done((bf16[128,2048]{1,0:T(8,128)(2,1)S(1)}, bf16[128,2048]{1,0:T(8,128)(2,1)S(1)}, u32[]{:S(2)}, u32[]{:S(2)}) %collective-permute-start.32) | collective-permute-done | bytes 524320 | tf_op jit(solution)/shard_map/ppermute | solution.py:263
  189.8 0.7 collective-permute-start.35
  190.5 2.0 collective-permute-start.34
  192.6 0.8 collective-permute-start.30
  193.4 3.4 %collective-permute-done.31 = bf16[128,2048]{1,0:T(8,128)(2,1)S(1)} collective-permute-done((bf16[128,2048]{1,0:T(8,128)(2,1)S(1)}, bf16[128,2048]{1,0:T(8,128)(2,1)S(1)}, u32[]{:S(2)}, u32[]{:S(2)}) %collective-permute-start.31) | collective-permute-done | bytes 524320 | tf_op jit(solution)/shard_map/ppermute | solution.py:263
  196.8 6.0 %collective-permute-done.34 = bf16[128,2048]{1,0:T(8,128)(2,1)S(1)} collective-permute-done((bf16[128,2048]{1,0:T(8,128)(2,1)S(1)}, bf16[128,2048]{1,0:T(8,128)(2,1)S(1)}, u32[]{:S(2)}, u32[]{:S(2)}) %collective-permute-start.34) | collective-permute-done | bytes 524320 | tf_op jit(solution)/shard_map/ppermute | solution.py:267
  203.2 3.5 %collective-permute-start.36 = (bf16[128,2048]{1,0:T(8,128)(2,1)S(1)}, bf16[128,2048]{1,0:T(8,128)(2,1)S(1)}, u32[]{:S(2)}, u32[]{:S(2)}) collective-permute-start(bf16[128,2048]{1,0:T(8,128)(2,1)S(1)} %add_convert_fusion.2), channel_id=1, source_target_pairs={{0,2},{1,3},{2,0},{3,1},{4,6},{5,7},{6,4},{7,5},{8,10},{9,11},{10,... | collective-permute-start | bytes 1572872 | tf_op jit(solution)/shard_map/ppermute | solution.py:267
  206.7 0.7 collective-permute-start.37
  207.4 6.5 %collective-permute-done.36 = bf16[128,2048]{1,0:T(8,128)(2,1)S(1)} collective-permute-done((bf16[128,2048]{1,0:T(8,128)(2,1)S(1)}, bf16[128,2048]{1,0:T(8,128)(2,1)S(1)}, u32[]{:S(2)}, u32[]{:S(2)}) %collective-permute-start.36) | collective-permute-done | bytes 524320 | tf_op jit(solution)/shard_map/ppermute | solution.py:267
  213.8 1.2 add_convert_fusion
  (115 shorter events, 9.9 us)
Async XLA Ops:
  6.5 8.4 %copy-start = (bf16[256,2048]{1,0:T(8,128)(2,1)S(1)}, bf16[256,2048]{1,0:T(8,128)(2,1)}, u32[]{:S(2)}) copy-start(bf16[256,2048]{1,0:T(8,128)(2,1)} %param.23) | copy-start | bytes 3145732
  6.5 72.2 %all-gather.2.cloned.1.call-start = ((), (), s32[]{:S(2)}) async-start(), calls=%async_computation | async-start | bytes 2621440 | tf_op jit(solution)/shard_map/all_gather | solution.py:271
  7.2 21.4 %copy-start.18 = (s32[128,4]{0,1:T(4,128)S(1)}, s32[128,4]{0,1:T(4,128)}, u32[]{:S(2)}) copy-start(s32[128,4]{0,1:T(4,128)} %param.25) | copy-start | bytes 6148
  7.2 21.4 %copy-start.19 = (bf16[128,4]{0,1:T(4,128)(2,1)S(1)}, bf16[128,4]{0,1:T(4,128)(2,1)}, u32[]{:S(2)}) copy-start(bf16[128,4]{0,1:T(4,128)(2,1)} %param.26) | copy-start | bytes 3076
  7.2 22.0 %copy-start.17 = (bf16[2048]{0:T(1024)(128)(2,1)S(1)}, bf16[2048]{0:T(1024)(128)(2,1)}, u32[]{:S(2)}) copy-start(bf16[2048]{0:T(1024)(128)(2,1)} %param.24) | copy-start | bytes 12292
  7.2 22.9 %copy-start.5 = (bf16[4,1024,256]{2,1,0:T(8,128)(2,1)S(1)}, bf16[4,1024,256]{2,1,0:T(8,128)(2,1)}, u32[]{:S(2)}) copy-start(bf16[4,1024,256]{2,1,0:T(8,128)(2,1)} %pk.5) | copy-start | bytes 6291460
  7.2 22.9 %copy-start.11 = (s32[2]{0:T(128)S(1)}, s32[2]{0:T(128)}, u32[]{:S(2)}) copy-start(s32[2]{0:T(128)} %pad_add_fusion.sc_ref) | copy-start | bytes 28
  11.4 18.7 %collective-permute-start.2 = (bf16[2,4,1024,128]{3,2,1,0:T(8,128)(2,1)}, bf16[2,4,1024,128]{3,2,1,0:T(8,128)(2,1)}, u32[]{:S(2)}, u32[]{:S(2)}) collective-permute-start(bf16[2,4,1024,128]{3,2,1,0:T(8,128)(2,1)} %get-tuple-element.68), channel_id=1, source_target_pairs={{0,8},{8,0},{16,24},{24,16},{1,9},{9,1},{17,25},{25,17},{2,10},{10... | collective-permute-start | bytes 6291464 | tf_op jit(solution)/shard_map/ppermute | solution.py:255
  12.0 5.8 %collective-permute-start.1 = (bf16[3,1024,128]{2,1,0:T(8,128)(2,1)}, bf16[3,1024,128]{2,1,0:T(8,128)(2,1)}, u32[]{:S(2)}, u32[]{:S(2)}) collective-permute-start(bf16[3,1024,128]{2,1,0:T(8,128)(2,1)} %get-tuple-element.65), channel_id=1, source_target_pairs={{0,8},{8,0},{16,24},{24,16},{1,9},{9,1},{17,25},{25,17},{2,10},{10... | collective-permute-start | bytes 2359304 | tf_op jit(solution)/shard_map/ppermute | solution.py:255
  12.0 15.4 %collective-permute-start.3 = (bf16[1024,256]{1,0:T(8,128)(2,1)}, bf16[1024,256]{1,0:T(8,128)(2,1)}, u32[]{:S(2)}, u32[]{:S(2)}) collective-permute-start(bf16[1024,256]{1,0:T(8,128)(2,1)} %q0.1), channel_id=1, source_target_pairs={{0,16},{8,24},{16,0},{24,8},{1,17},{9,25},{17,1},{25,9},{2,18},{10... | collective-permute-start | bytes 1572872 | tf_op jit(solution)/shard_map/ppermute | solution.py:259
  16.6 1.2 copy-start.12
  16.6 10.9 %collective-permute-start.4 = (s32[1,16]{1,0:T(1,128)S(1)}, s32[1,16]{1,0:T(1,128)S(1)}, u32[]{:S(2)}, u32[]{:S(2)}) collective-permute-start(s32[1,16]{1,0:T(1,128)S(1)} %pad_add_fusion.1.shape_a), channel_id=1, source_target_pairs={{0,16},{8,24},{16,0},{24,8},{1,17},{9,25},{17,1},{25,9},{2,18},{10... | collective-permute-start | bytes 200 | tf_op jit(solution)/shard_map/ppermute | solution.py:259
  16.6 1.2 collective-permute-start
  16.7 13.5 %copy-start.6 = (bf16[4,1024,256]{2,1,0:T(8,128)(2,1)S(1)}, bf16[4,1024,256]{2,1,0:T(8,128)(2,1)}, u32[]{:S(2)}) copy-start(bf16[4,1024,256]{2,1,0:T(8,128)(2,1)} %pv.5) | copy-start | bytes 6291460
  17.8 0.5 copy-start.14
  28.5 1.6 collective-permute-start.6
  28.6 1.5 collective-permute-start.5
  29.2 17.0 %copy-start.8 = (bf16[1024,256]{1,0:T(8,128)(2,1)S(1)}, bf16[1024,256]{1,0:T(8,128)(2,1)}, u32[]{:S(2)}) copy-start(bf16[1024,256]{1,0:T(8,128)(2,1)} %q0.1) | copy-start | bytes 1572868
  29.2 17.0 %copy-start.13 = (s32[1,16]{1,0:T(1,128)S(1)}, s32[1,16]{1,0:T(1,128)}, u32[]{:S(2)}) copy-start(s32[1,16]{1,0:T(1,128)} %copy-done.12) | copy-start | bytes 196
  29.2 17.0 %copy-start.15 = (s32[1,16]{1,0:T(1,128)S(1)}, s32[1,16]{1,0:T(1,128)}, u32[]{:S(2)}) copy-start(s32[1,16]{1,0:T(1,128)} %copy-done.14) | copy-start | bytes 196
  44.1 15.2 %collective-permute-start.8 = (f32[2,8,128]{2,1,0:T(8,128)S(1)}, f32[2,8,128]{2,1,0:T(8,128)S(1)}, u32[]{:S(2)}, u32[]{:S(2)}) collective-permute-start(f32[2,8,128]{2,1,0:T(8,128)S(1)} %get-tuple-element.75), channel_id=1, source_target_pairs={{0,16},{8,24},{16,0},{24,8},{1,17},{9,25},{17,1},{25,9},{2,18},{10... | collective-permute-start | bytes 24584 | tf_op jit(solution)/shard_map/ppermute | solution.py:259
  44.9 14.4 %copy-start.4 = (f32[2048,128]{1,0:T(8,128)S(1)}, f32[2048,128]{1,0:T(8,128)}, u32[]{:S(2)}) copy-start(f32[2048,128]{1,0:T(8,128)} %get-tuple-element.66.refs_0_.refs_6_) | copy-start | bytes 3145732
  44.9 14.4 %copy-start.10 = (f32[2,8,128]{2,1,0:T(8,128)S(1)}, f32[2,8,128]{2,1,0:T(8,128)}, u32[]{:S(2)}) copy-start(f32[2,8,128]{2,1,0:T(8,128)} %get-tuple-element.67.refs_1_.refs_7_) | copy-start | bytes 24580
  44.9 14.4 %collective-permute-start.7 = (bf16[2048,128]{1,0:T(8,128)(2,1)S(1)}, bf16[2048,128]{1,0:T(8,128)(2,1)S(1)}, u32[]{:S(2)}, u32[]{:S(2)}) collective-permute-start(bf16[2048,128]{1,0:T(8,128)(2,1)S(1)} %get-tuple-element.74), channel_id=1, source_target_pairs={{0,16},{8,24},{16,0},{24,8},{1,17},{9,25},{17,1},{25,9},{2,18},{10... | collective-permute-start | bytes 1572872 | tf_op jit(solution)/shard_map/ppermute | solution.py:259
  59.3 39.0 %copy-start.9 = (bf16[128,2048]{1,0:T(8,128)(2,1)S(1)}, bf16[128,2048]{1,0:T(8,128)(2,1)}, u32[]{:S(2)}) copy-start(bf16[128,2048]{1,0:T(8,128)(2,1)} %residual.1) | copy-start | bytes 1572868
  61.5 8.5 %collective-permute-start.11 = (bf16[2,272,128]{2,1,0:T(8,128)(2,1)S(1)}, bf16[2,272,128]{2,1,0:T(8,128)(2,1)S(1)}, u32[]{:S(2)}, u32[]{:S(2)}) collective-permute-start(bf16[2,272,128]{2,1,0:T(8,128)(2,1)S(1)} %get-tuple-element.125), channel_id=1, source_target_pairs={{0,6},{1,7},{2,4},{3,5},{4,2},{5,3},{6,0},{7,1},{8,14},{9,15},{10,... | collective-permute-start | bytes 417800 | tf_op jit(solution)/shard_map/ppermute | solution.py:657
  65.5 11.6 %collective-permute-start.10 = (bf16[2,272,128]{2,1,0:T(8,128)(2,1)S(1)}, bf16[2,272,128]{2,1,0:T(8,128)(2,1)S(1)}, u32[]{:S(2)}, u32[]{:S(2)}) collective-permute-start(bf16[2,272,128]{2,1,0:T(8,128)(2,1)S(1)} %get-tuple-element.126), channel_id=1, source_target_pairs={{0,4},{1,5},{2,6},{3,7},{4,0},{5,1},{6,2},{7,3},{8,12},{9,13},{10,... | collective-permute-start | bytes 417800 | tf_op jit(solution)/shard_map/ppermute | solution.py:657
  65.5 11.6 %collective-permute-start.9 = (bf16[2,272,128]{2,1,0:T(8,128)(2,1)S(1)}, bf16[2,272,128]{2,1,0:T(8,128)(2,1)S(1)}, u32[]{:S(2)}, u32[]{:S(2)}) collective-permute-start(bf16[2,272,128]{2,1,0:T(8,128)(2,1)S(1)} %get-tuple-element.127), channel_id=1, source_target_pairs={{0,2},{1,3},{2,0},{3,1},{4,6},{5,7},{6,4},{7,5},{8,10},{9,11},{10,... | collective-permute-start | bytes 417800 | tf_op jit(solution)/shard_map/ppermute | solution.py:657
  77.1 5.0 %collective-permute-start.13 = (bf16[4,16,128]{2,1,0:T(8,128)(2,1)S(1)}, bf16[4,16,128]{2,1,0:T(8,128)(2,1)S(1)}, u32[]{:S(2)}, u32[]{:S(2)}) collective-permute-start(bf16[4,16,128]{2,1,0:T(8,128)(2,1)S(1)} %pad_maximum_fusion.3.refs_0_), channel_id=1, source_target_pairs={{0,1},{1,0},{2,3},{3,2},{4,5},{5,4},{6,7},{7,6},{8,9},{9,8},{10,11... | collective-permute-start | bytes 49160 | tf_op jit(solution)/shard_map/ppermute | solution.py:263
  78.7 1.6 copy-start.7
  82.2 2.0 collective-permute-start.14
  82.2 2.6 %collective-permute-start.12 = (bf16[128,2048]{1,0:T(8,128)(2,1)S(1)}, bf16[128,2048]{1,0:T(8,128)(2,1)S(1)}, u32[]{:S(2)}, u32[]{:S(2)}) collective-permute-start(bf16[128,2048]{1,0:T(8,128)(2,1)S(1)} %get-tuple-element.77), channel_id=1, source_target_pairs={{0,8},{8,0},{16,24},{24,16},{1,9},{9,1},{17,25},{25,17},{2,10},{10... | collective-permute-start | bytes 1572872 | tf_op jit(solution)/shard_map/ppermute | solution.py:255
  84.3 14.0 %collective-permute-start.15 = (bf16[128,2048]{1,0:T(8,128)(2,1)S(1)}, bf16[128,2048]{1,0:T(8,128)(2,1)S(1)}, u32[]{:S(2)}, u32[]{:S(2)}) collective-permute-start(bf16[128,2048]{1,0:T(8,128)(2,1)S(1)} %add_convert_fusion.4), channel_id=1, source_target_pairs={{0,1},{1,0},{2,3},{3,2},{4,5},{5,4},{6,7},{7,6},{8,9},{9,8},{10,11... | collective-permute-start | bytes 1572872 | tf_op jit(solution)/shard_map/ppermute | solution.py:263
  98.8 13.2 %collective-permute-start.18 = (bf16[128,2048]{1,0:T(8,128)(2,1)S(1)}, bf16[128,2048]{1,0:T(8,128)(2,1)S(1)}, u32[]{:S(2)}, u32[]{:S(2)}) collective-permute-start(bf16[128,2048]{1,0:T(8,128)(2,1)S(1)} %get-tuple-element.87), channel_id=1, source_target_pairs={{0,1},{1,0},{2,3},{3,2},{4,5},{5,4},{6,7},{7,6},{8,9},{9,8},{10,11... | collective-permute-start | bytes 1572872 | tf_op jit(solution)/shard_map/ppermute | solution.py:263
  99.4 12.6 %collective-permute-start.17 = (bf16[128,2048]{1,0:T(8,128)(2,1)S(1)}, bf16[128,2048]{1,0:T(8,128)(2,1)}, u32[]{:S(2)}, u32[]{:S(2)}) collective-permute-start(bf16[128,2048]{1,0:T(8,128)(2,1)S(1)} %get-tuple-element.87), channel_id=1, source_target_pairs={{2,4},{3,5},{4,2},{5,3},{10,12},{11,13},{12,10},{13,11},{18,20},{1... | collective-permute-start | bytes 1572872 | tf_op jit(solution)/shard_map/ppermute | solution.py:277
  100.9 13.0 %collective-permute-start.16 = (bf16[128,2048]{1,0:T(8,128)(2,1)S(1)}, bf16[128,2048]{1,0:T(8,128)(2,1)}, u32[]{:S(2)}, u32[]{:S(2)}) collective-permute-start(bf16[128,2048]{1,0:T(8,128)(2,1)S(1)} %get-tuple-element.87), channel_id=1, source_target_pairs={{0,2},{1,3},{2,0},{3,1},{4,6},{5,7},{6,4},{7,5},{8,10},{9,11},{10,... | collective-permute-start | bytes 1572872 | tf_op jit(solution)/shard_map/ppermute | solution.py:267
  102.7 4.3 %copy-start.2 = (bf16[4,2048,704]{1,2,0:T(8,128)(2,1)S(1)}, bf16[4,2048,704]{1,2,0:T(8,128)(2,1)}, u32[]{:S(2)}) copy-start(bf16[4,2048,704]{1,2,0:T(8,128)(2,1)} %param.27) | copy-start | bytes 34603012
  112.0 17.4 %copy-start.16 = (bf16[128,2048]{1,0:T(8,128)(2,1)}, bf16[128,2048]{1,0:T(8,128)(2,1)S(1)}, u32[]{:S(2)}) copy-start(bf16[128,2048]{1,0:T(8,128)(2,1)S(1)} %collective-permute-done.18) | copy-start | bytes 1572868
  113.8 15.6 %collective-permute-start.21 = (bf16[128,2048]{1,0:T(8,128)(2,1)}, bf16[128,2048]{1,0:T(8,128)(2,1)S(1)}, u32[]{:S(2)}, u32[]{:S(2)}) collective-permute-start(bf16[128,2048]{1,0:T(8,128)(2,1)} %collective-permute-done.16), channel_id=1, source_target_pairs={{0,1},{1,0},{2,3},{3,2},{4,5},{5,4},{6,7},{7,6},{8,9},{9,8},{10,11... | collective-permute-start | bytes 1572872 | tf_op jit(solution)/shard_map/ppermute | solution.py:263
  115.3 14.1 %collective-permute-start.20 = (bf16[128,2048]{1,0:T(8,128)(2,1)}, bf16[128,2048]{1,0:T(8,128)(2,1)S(1)}, u32[]{:S(2)}, u32[]{:S(2)}) collective-permute-start(bf16[128,2048]{1,0:T(8,128)(2,1)} %collective-permute-done.16), channel_id=1, source_target_pairs={{2,4},{3,5},{4,2},{5,3},{10,12},{11,13},{12,10},{13,11},{18,20},{1... | collective-permute-start | bytes 1572872 | tf_op jit(solution)/shard_map/ppermute | solution.py:277
  116.0 13.4 %collective-permute-start.19 = (bf16[128,2048]{1,0:T(8,128)(2,1)}, bf16[128,2048]{1,0:T(8,128)(2,1)S(1)}, u32[]{:S(2)}, u32[]{:S(2)}) collective-permute-start(bf16[128,2048]{1,0:T(8,128)(2,1)} %collective-permute-done.17), channel_id=1, source_target_pairs={{0,2},{1,3},{2,0},{3,1},{4,6},{5,7},{6,4},{7,5},{8,10},{9,11},{10,... | collective-permute-start | bytes 1572872 | tf_op jit(solution)/shard_map/ppermute | solution.py:267
  119.2 4.3 %copy-start.3 = (bf16[4,704,2048]{2,1,0:T(8,128)(2,1)S(1)}, bf16[4,704,2048]{2,1,0:T(8,128)(2,1)}, u32[]{:S(2)}) copy-start(bf16[4,704,2048]{2,1,0:T(8,128)(2,1)} %source) | copy-start | bytes 34603012
  123.5 27.1 %slice-start = ((s8[11534336]{0:T(1024)(128)(4,1)}), s8[4194304]{0:T(1024)(128)(4,1)S(1)}, s32[]{:S(2)}) async-start(s8[11534336]{0:T(1024)(128)(4,1)} %bitcast.40), calls=%async_computation.1 | async-start | bytes 8388608
  123.5 27.1 %slice-start.1 = ((s8[11534336]{0:T(1024)(128)(4,1)}), s8[4194304]{0:T(1024)(128)(4,1)S(1)}, s32[]{:S(2)}) async-start(s8[11534336]{0:T(1024)(128)(4,1)} %bitcast.40), calls=%async_computation.2 | async-start | bytes 8388608
  126.5 24.2 %slice-start.2 = ((s8[11534336]{0:T(1024)(128)(4,1)}), s8[3145728]{0:T(1024)(128)(4,1)S(1)}, s32[]{:S(2)}) async-start(s8[11534336]{0:T(1024)(128)(4,1)} %bitcast.40), calls=%async_computation.3 | async-start | bytes 6291456
  129.4 11.4 %collective-permute-start.22 = (bf16[128,2048]{1,0:T(8,128)(2,1)S(1)}, bf16[128,2048]{1,0:T(8,128)(2,1)S(1)}, u32[]{:S(2)}, u32[]{:S(2)}) collective-permute-start(bf16[128,2048]{1,0:T(8,128)(2,1)S(1)} %collective-permute-done.20), channel_id=1, source_target_pairs={{0,2},{1,3},{2,0},{3,1},{4,6},{5,7},{6,4},{7,5},{8,10},{9,11},{10,... | collective-permute-start | bytes 1572872 | tf_op jit(solution)/shard_map/ppermute | solution.py:267
  131.6 9.2 %collective-permute-start.23 = (bf16[128,2048]{1,0:T(8,128)(2,1)S(1)}, bf16[128,2048]{1,0:T(8,128)(2,1)S(1)}, u32[]{:S(2)}, u32[]{:S(2)}) collective-permute-start(bf16[128,2048]{1,0:T(8,128)(2,1)S(1)} %broadcast_select_fusion.1), channel_id=1, source_target_pairs={{0,1},{1,0},{2,3},{3,2},{4,5},{5,4},{6,7},{7,6},{8,9},{9,8},{10,11... | collective-permute-start | bytes 1572872 | tf_op jit(solution)/shard_map/ppermute | solution.py:263
  134.5 10.2 %collective-permute-start.26 = (bf16[64,2048]{1,0:T(8,128)(2,1)S(1)}, bf16[64,2048]{1,0:T(8,128)(2,1)S(1)}, u32[]{:S(2)}, u32[]{:S(2)}) collective-permute-start(bf16[64,2048]{1,0:T(8,128)(2,1)S(1)} %slice.92), channel_id=1, source_target_pairs={{2,4},{3,5},{4,2},{5,3},{10,12},{11,13},{12,10},{13,11},{18,20},{1... | collective-permute-start | bytes 786440 | tf_op jit(solution)/shard_map/ppermute | solution.py:277
  140.9 7.0 %collective-permute-start.25 = (bf16[64,2048]{1,0:T(8,128)(2,1)S(1)}, bf16[64,2048]{1,0:T(8,128)(2,1)S(1)}, u32[]{:S(2)}, u32[]{:S(2)}) collective-permute-start(bf16[64,2048]{1,0:T(8,128)(2,1)S(1)} %slice.91), channel_id=1, source_target_pairs={{0,2},{1,3},{2,0},{3,1},{4,6},{5,7},{6,4},{7,5},{8,10},{9,11},{10,... | collective-permute-start | bytes 786440 | tf_op jit(solution)/shard_map/ppermute | solution.py:267
  143.6 6.4 %collective-permute-start.24 = (bf16[64,2048]{1,0:T(8,128)(2,1)S(1)}, bf16[64,2048]{1,0:T(8,128)(2,1)S(1)}, u32[]{:S(2)}, u32[]{:S(2)}) collective-permute-start(bf16[64,2048]{1,0:T(8,128)(2,1)S(1)} %slice.109), channel_id=1, source_target_pairs={{0,1},{1,0},{2,3},{3,2},{4,5},{5,4},{6,7},{7,6},{8,9},{9,8},{10,11... | collective-permute-start | bytes 786440 | tf_op jit(solution)/shard_map/ppermute | solution.py:263
  150.6 64.4 %copy-start.1 = (bf16[256,2048]{1,0:T(8,128)(2,1)S(1)}, bf16[256,2048]{1,0:T(8,128)(2,1)}, u32[]{:S(2)}) copy-start(bf16[256,2048]{1,0:T(8,128)(2,1)} %param.23) | copy-start | bytes 3145732
  162.3 7.6 %collective-permute-start.27 = (bf16[64,2048]{1,0:T(8,128)(2,1)S(1)}, bf16[64,2048]{1,0:T(8,128)(2,1)S(1)}, u32[]{:S(2)}, u32[]{:S(2)}) collective-permute-start(bf16[64,2048]{1,0:T(8,128)(2,1)S(1)} %get-tuple-element.107), channel_id=1, source_target_pairs={{0,1},{1,0},{2,3},{3,2},{4,5},{5,4},{6,7},{7,6},{8,9},{9,8},{10,11... | collective-permute-start | bytes 786440 | tf_op jit(solution)/shard_map/ppermute | solution.py:263
  162.9 7.1 %collective-permute-start.29 = (bf16[64,2048]{1,0:T(8,128)(2,1)S(1)}, bf16[64,2048]{1,0:T(8,128)(2,1)S(1)}, u32[]{:S(2)}, u32[]{:S(2)}) collective-permute-start(bf16[64,2048]{1,0:T(8,128)(2,1)S(1)} %get-tuple-element.108), channel_id=1, source_target_pairs={{2,4},{3,5},{4,2},{5,3},{10,12},{11,13},{12,10},{13,11},{18,20},{1... | collective-permute-start | bytes 786440 | tf_op jit(solution)/shard_map/ppermute | solution.py:277
  163.5 9.4 %collective-permute-start.28 = (bf16[64,2048]{1,0:T(8,128)(2,1)S(1)}, bf16[64,2048]{1,0:T(8,128)(2,1)S(1)}, u32[]{:S(2)}, u32[]{:S(2)}) collective-permute-start(bf16[64,2048]{1,0:T(8,128)(2,1)S(1)} %get-tuple-element.108), channel_id=1, source_target_pairs={{0,2},{1,3},{2,0},{3,1},{4,6},{5,7},{6,4},{7,5},{8,10},{9,11},{10,... | collective-permute-start | bytes 786440 | tf_op jit(solution)/shard_map/ppermute | solution.py:267
  173.2 11.8 %collective-permute-start.33 = (bf16[128,2048]{1,0:T(8,128)(2,1)S(1)}, bf16[128,2048]{1,0:T(8,128)(2,1)S(1)}, u32[]{:S(2)}, u32[]{:S(2)}) collective-permute-start(bf16[128,2048]{1,0:T(8,128)(2,1)S(1)} %pad_maximum_fusion.2), channel_id=1, source_target_pairs={{0,2},{1,3},{2,0},{3,1},{4,6},{5,7},{6,4},{7,5},{8,10},{9,11},{10,... | collective-permute-start | bytes 1572872 | tf_op jit(solution)/shard_map/ppermute | solution.py:267
  175.3 14.2 %collective-permute-start.32 = (bf16[128,2048]{1,0:T(8,128)(2,1)S(1)}, bf16[128,2048]{1,0:T(8,128)(2,1)S(1)}, u32[]{:S(2)}, u32[]{:S(2)}) collective-permute-start(bf16[128,2048]{1,0:T(8,128)(2,1)S(1)} %pad_maximum_fusion.1), channel_id=1, source_target_pairs={{0,1},{1,0},{2,3},{3,2},{4,5},{5,4},{6,7},{7,6},{8,9},{9,8},{10,11... | collective-permute-start | bytes 1572872 | tf_op jit(solution)/shard_map/ppermute | solution.py:263
  176.9 19.9 %collective-permute-start.31 = (bf16[128,2048]{1,0:T(8,128)(2,1)S(1)}, bf16[128,2048]{1,0:T(8,128)(2,1)S(1)}, u32[]{:S(2)}, u32[]{:S(2)}) collective-permute-start(bf16[128,2048]{1,0:T(8,128)(2,1)S(1)} %get-tuple-element.111), channel_id=1, source_target_pairs={{0,1},{1,0},{2,3},{3,2},{4,5},{5,4},{6,7},{7,6},{8,9},{9,8},{10,11... | collective-permute-start | bytes 1572872 | tf_op jit(solution)/shard_map/ppermute | solution.py:263
  189.8 7.1 %collective-permute-start.35 = (bf16[128,2048]{1,0:T(8,128)(2,1)S(1)}, bf16[128,2048]{1,0:T(8,128)(2,1)S(1)}, u32[]{:S(2)}, u32[]{:S(2)}) collective-permute-start(bf16[128,2048]{1,0:T(8,128)(2,1)S(1)} %add_convert_fusion.3), channel_id=1, source_target_pairs={{2,4},{3,5},{4,2},{5,3},{10,12},{11,13},{12,10},{13,11},{18,20},{1... | collective-permute-start | bytes 1572872 | tf_op jit(solution)/shard_map/ppermute | solution.py:277
  190.5 12.3 %collective-permute-start.34 = (bf16[128,2048]{1,0:T(8,128)(2,1)S(1)}, bf16[128,2048]{1,0:T(8,128)(2,1)S(1)}, u32[]{:S(2)}, u32[]{:S(2)}) collective-permute-start(bf16[128,2048]{1,0:T(8,128)(2,1)S(1)} %add_convert_fusion.3), channel_id=1, source_target_pairs={{0,2},{1,3},{2,0},{3,1},{4,6},{5,7},{6,4},{7,5},{8,10},{9,11},{10,... | collective-permute-start | bytes 1572872 | tf_op jit(solution)/shard_map/ppermute | solution.py:267
  192.6 14.7 %collective-permute-start.30 = (bf16[128,2048]{1,0:T(8,128)(2,1)S(1)}, bf16[128,2048]{1,0:T(8,128)(2,1)S(1)}, u32[]{:S(2)}, u32[]{:S(2)}) collective-permute-start(bf16[128,2048]{1,0:T(8,128)(2,1)S(1)} %pad_maximum_fusion), channel_id=1, source_target_pairs={{0,1},{1,0},{2,3},{3,2},{4,5},{5,4},{6,7},{7,6},{8,9},{9,8},{10,11... | collective-permute-start | bytes 1572872 | tf_op jit(solution)/shard_map/ppermute | solution.py:263
  203.2 10.6 %collective-permute-start.36 = (bf16[128,2048]{1,0:T(8,128)(2,1)S(1)}, bf16[128,2048]{1,0:T(8,128)(2,1)S(1)}, u32[]{:S(2)}, u32[]{:S(2)}) collective-permute-start(bf16[128,2048]{1,0:T(8,128)(2,1)S(1)} %add_convert_fusion.2), channel_id=1, source_target_pairs={{0,2},{1,3},{2,0},{3,1},{4,6},{5,7},{6,4},{7,5},{8,10},{9,11},{10,... | collective-permute-start | bytes 1572872 | tf_op jit(solution)/shard_map/ppermute | solution.py:267
  206.7 7.2 %collective-permute-start.37 = (bf16[128,2048]{1,0:T(8,128)(2,1)S(1)}, bf16[128,2048]{1,0:T(8,128)(2,1)S(1)}, u32[]{:S(2)}, u32[]{:S(2)}) collective-permute-start(bf16[128,2048]{1,0:T(8,128)(2,1)S(1)} %add_convert_fusion.1), channel_id=1, source_target_pairs={{2,4},{3,5},{4,2},{5,3},{10,12},{11,13},{12,10},{13,11},{18,20},{1... | collective-permute-start | bytes 1572872 | tf_op jit(solution)/shard_map/ppermute | solution.py:277
Sparse Core Ops, SparseCore 0:
  15.9 46.2 all-gather.1

commit v9 on v8

--- a/solution.py
+++ b/solution.py
@@ -662,17 +662,24 @@
 
 
 def project_kernel(sc_ref, *refs):
-    heads, weights, outs, lhs = refs[:4], refs[4], refs[5:9], refs[9]
+    heads, source, outs, (lhs, weights, sems) = refs[:4], refs[4], refs[5:9], refs[9:]
     z_here = sc_ref[1] // 2
+    tile = 512
+    slices = [slice(low, low + tile) for low in range(0, weights.shape[1], tile)]
+    copies = [
+        pltpu.make_async_copy(source.at[:, here], weights.at[:, here], sems.at[i])
+        for i, here in enumerate(slices)
+    ]
+    for copy in copies:
+        copy.start()
     for d, part in enumerate(heads):
         columns = pl.ds(pl.multiple_of((z_here ^ d) * HEAD, HEAD), HEAD)
         for row in range(2):
             for chunk in range(2):
                 to = (2 * row + chunk) * BLK
                 lhs[to : to + BLK, columns] = part[chunk, row * BLK : (row + 1) * BLK, :]
-    tile = 512
-    for low in range(0, weights.shape[1], tile):
-        here = slice(low, low + tile)
+    for here, copy in zip(slices, copies):
+        copy.wait()
         out = jnp.dot(lhs[...], weights[:, here], preferred_element_type=jnp.float32)
         for i, out_ref in enumerate(outs):
             out_ref[:, here] = out[i * BLK : (i + 1) * BLK].astype(out_ref.dtype)
@@ -684,14 +691,18 @@
     vmem = pl.BlockSpec(memory_space=pltpu.VMEM)
     return pl.pallas_call(
         project_kernel,
-        in_specs=[smem] + [vmem] * 5,
+        in_specs=[smem] + [vmem] * 4 + [pl.BlockSpec(memory_space=pl.ANY)],
         out_specs=[vmem] * 4,
         out_shape=[
             jax.ShapeDtypeStruct((BLK, width), dtype)
             for dtype in (jnp.float32, jnp.bfloat16, jnp.bfloat16, jnp.bfloat16)
         ],
-        scratch_shapes=[pltpu.VMEM((4 * BLK, depth), jnp.bfloat16)],
-        compiler_params=pltpu.CompilerParams(vmem_limit_bytes=VMEM_SMALL),
+        scratch_shapes=[
+            pltpu.VMEM((4 * BLK, depth), jnp.bfloat16),
+            pltpu.VMEM((depth, width), weights.dtype),
+            pltpu.SemaphoreType.DMA((width // 512,)),
+        ],
+        compiler_params=pltpu.CompilerParams(vmem_limit_bytes=VMEM_MOST),
         name="project",
     )(place, *heads, weights)
 

time: 225 us -> 229 us (1.018)
  Pallas kernels: 55.7 us -> 59.4 us
    pallas_call x1, Pallas kernels: 1.86 us -> 5.35 us  [project(): pl.pallas_call(project_kernel, in_specs=[smem] + [vmem] * 4 + [pl.BlockSp...]
    unnamed x46 -> x52, local copies, waits for them, and re-layouts: 10.7 us -> 10.4 us
  transfers between devices with their start and end apart: 39 -> 39, of which waited for: 20 -> 20; matrix products, arithmetic and copies ran while one was open for 4% -> 4% of each run, Pallas kernels for 18% -> 19%
where the time goes in v9:
time: 229 us; the launch traced here: 228 us
  waiting for transfers between devices  87.4 us (38%)
  Pallas kernels  59.4 us (26%)
  starting transfers between devices  44.6 us (19%)
  between operations  14 us (6%)
  local copies, waits for them, and re-layouts  12.1 us (5%)
  other arithmetic  5.91 us (3%)
  matrix products  4.18 us (2%)
    ppermute x10, waiting for transfers between devices, y_swap(): return lax.ppermute(array, 'exp', [(i, i ^ 1) for i in range(8)])  37.3 us
    ppermute x8, waiting for transfers between devices, outer_swap(): return lax.ppermute(array, 'exp', [(i, i ^ 2) for i in range(8)])  32.2 us
    pallas_call x2, Pallas kernels, prefix_attend(): pl.pallas_call(prefix_kernel, in_specs=[smem] * 3 + [anywhere] * 5, out_s...  27.1 us
    ppermute x8, starting transfers between devices, outer_swap(): return lax.ppermute(array, 'exp', [(i, i ^ 2) for i in range(8)])  20.7 us
    pallas_call x1, Pallas kernels, run_experts(): pl.pallas_call(experts_kernel, in_specs=[vmem] * 12, out_specs=[vmem] * 9...  11.7 us
    ppermute x3, waiting for transfers between devices, exchange_heads(): lax.ppermute(attended[2 * d:2 * d + 2], 'exp', [(i, i ^ 2 * d) for i in r...  11 us
    unnamed x52, local copies, waits for them, and re-layouts  10.4 us
    ppermute x10, starting transfers between devices, y_swap(): return lax.ppermute(array, 'exp', [(i, i ^ 1) for i in range(8)])  8.48 us
  transfers between devices with their start and end apart: 39, of which 20 were waited for; matrix products, arithmetic and copies ran while one was open for 4% of the time, Pallas kernels for 19%

profile of v9, /device:TPU:0, one launch (start us, length us, event | category | flops | bytes accessed | tf_op | source)
XLA Modules:
  0.0 227.5 jit_solution(2628618948418895001)
XLA Ops:
  7.2 4.3 %split_theirs.1 = (bf16[3,1024,128]{2,1,0:T(8,128)(2,1)}, bf16[2,4,1024,128]{3,2,1,0:T(8,128)(2,1)}) custom-call(s32[2]{0:T(128)} %pad_add_fusion.sc_ref, bf16[1024,256]{1,0:T(8,128)(2,1)} %q0.1, bf16[1024,256]{1,0:T(8,128)(2,1)} %k.3, bf16[1024,256]{1,0:T(8,128)(2,1)} %v.3, bf16[4,1024,256]{2,1,0:T(8,128)(2,1)} %pk.5, bf16[4,1024,256]{2,1,0:T(8,128)(2,1)} %pv.5), custom_call_target="tpu_custom_call" | custom-call | tf_op jit(solution)/shard_map/split_theirs/pallas_call | solution.py:302
  12.0 2.9 %collective-permute-start.3 = (bf16[1024,256]{1,0:T(8,128)(2,1)}, bf16[1024,256]{1,0:T(8,128)(2,1)}, u32[]{:S(2)}, u32[]{:S(2)}) collective-permute-start(bf16[1024,256]{1,0:T(8,128)(2,1)} %q0.1), channel_id=1, source_target_pairs={{0,16},{8,24},{16,0},{24,8},{1,17},{9,25},{17,1},{25,9},{2,18},{10... | collective-permute-start | bytes 1572872 | tf_op jit(solution)/shard_map/ppermute | solution.py:259
  14.9 0.8 constant_dynamic-slice_fusion
  15.8 0.7 pad_add_fusion.1.shape_a
  16.7 1.1 collective-permute-done.shape_b
  18.3 5.9 %suffix_attend.1 = (f32[2048,128]{1,0:T(8,128)}, f32[2,8,128]{2,1,0:T(8,128)}) custom-call(s32[2]{0:T(128)} %pad_add_fusion.sc_ref, s32[1,16]{1,0:T(1,128)} %copy-done.13, s32[1,16]{1,0:T(1,128)} %copy-done.15, bf16[1024,256]{1,0:T(8,128)(2,1)} %q0.1, bf16[1024,256]{1,0:T(8,128)(2,1)} %k.3, bf16[1024,256]{1,0:T(8,128)(2,1)} %v.3, ...), custom_call_target="tpu_custom_call" | custom-call | flops 4294967296 | bytes 1048576 | tf_op jit(solution)/shard_map/suffix_attend/pallas_call | solution.py:581
  24.2 3.3 %collective-permute-done.4.shape_a = s32[1,16]{1,0:T(1,128)S(1)} collective-permute-done((s32[1,16]{1,0:T(1,128)S(1)}, s32[1,16]{1,0:T(1,128)S(1)}, u32[]{:S(2)}, u32[]{:S(2)}) %collective-permute-start.4) | collective-permute-done | bytes 96 | tf_op jit(solution)/shard_map/ppermute | solution.py:259
  27.4 1.1 select_bitcast_fusion
  29.2 0.9 collective-permute-done.5.shape_b
  30.1 13.9 %prefix_attend.3 = (bf16[2048,128]{1,0:T(8,128)(2,1)S(1)}, f32[2,8,128]{2,1,0:T(8,128)S(1)}) custom-call(s32[2]{0:T(128)S(1)} %copy-done.11, s32[1,16]{1,0:T(1,128)S(1)} %collective-permute-done.4.shape_a, s32[1,16]{1,0:T(1,128)S(1)} %collective-permute-done.5.shape_b, bf16[1024,256]{1,0:T(8,128)(2,1)} %collective-permute-done.3.q0, ...), custom_call_target="tpu_custom_call" | custom-call | flops 8589934592 | bytes 4194304 | tf_op jit(solution)/shard_map/prefix_attend/pallas_call | solution.py:495
  44.1 0.8 collective-permute-start.8
  44.9 1.3 collective-permute-start.7
  46.2 13.1 %prefix_attend.2 = (f32[2048,128]{1,0:T(8,128)S(1)}, f32[2,8,128]{2,1,0:T(8,128)S(1)}) custom-call(s32[2]{0:T(128)S(1)} %copy-done.11, s32[1,16]{1,0:T(1,128)S(1)} %copy-done.14, s32[1,16]{1,0:T(1,128)S(1)} %copy-done.16, bf16[1024,256]{1,0:T(8,128)(2,1)S(1)} %copy-done.8, bf16[3,1024,128]{2,1,0:T(8,128)(2,1)} %collective-permute-done.1.other_row.q1, ...), custom_call_target="tpu_custom_call" | custom-call | flops 8589934592 | bytes 4194304 | tf_op jit(solution)/shard_map/prefix_attend/pallas_call | solution.py:495
  59.4 2.1 merge_parts.1
  61.5 0.7 fusion.23
  62.3 3.9 %collective-permute-start.11 = (bf16[2,272,128]{2,1,0:T(8,128)(2,1)S(1)}, bf16[2,272,128]{2,1,0:T(8,128)(2,1)S(1)}, u32[]{:S(2)}, u32[]{:S(2)}) collective-permute-start(bf16[2,272,128]{2,1,0:T(8,128)(2,1)S(1)} %get-tuple-element.125), channel_id=1, source_target_pairs={{0,6},{1,7},{2,4},{3,5},{4,2},{5,3},{6,0},{7,1},{8,14},{9,15},{10,... | collective-permute-start | bytes 417800 | tf_op jit(solution)/shard_map/ppermute | solution.py:657
  66.7 4.0 %collective-permute-done.11.refs_3_ = bf16[2,272,128]{2,1,0:T(8,128)(2,1)S(1)} collective-permute-done((bf16[2,272,128]{2,1,0:T(8,128)(2,1)S(1)}, bf16[2,272,128]{2,1,0:T(8,128)(2,1)S(1)}, u32[]{:S(2)}, u32[]{:S(2)}) %collective-permute-start.11) | collective-permute-done | bytes 139296 | tf_op jit(solution)/shard_map/ppermute | solution.py:657
  70.7 7.0 %collective-permute-done.10.refs_2_ = bf16[2,272,128]{2,1,0:T(8,128)(2,1)S(1)} collective-permute-done((bf16[2,272,128]{2,1,0:T(8,128)(2,1)S(1)}, bf16[2,272,128]{2,1,0:T(8,128)(2,1)S(1)}, u32[]{:S(2)}, u32[]{:S(2)}) %collective-permute-start.10) | collective-permute-done | bytes 139296 | tf_op jit(solution)/shard_map/ppermute | solution.py:657
  77.7 1.6 collective-permute-start.13
  79.3 5.3 %project.1 = (f32[128,2048]{1,0:T(8,128)}, bf16[128,2048]{1,0:T(8,128)(2,1)}, bf16[128,2048]{1,0:T(8,128)(2,1)}, bf16[128,2048]{1,0:T(8,128)(2,1)}) custom-call(s32[2]{0:T(128)} %pad_add_fusion.sc_ref, bf16[2,272,128]{2,1,0:T(8,128)(2,1)} %get-tuple-element.128.refs_0_, bf16[2,272,128]{2,1,0:T(8,128)(2,1)} %copy-done.19, bf16[2,272,128]{2,1,0:T(8,128)(2,1)} %copy-done.18, ...), custom_call_target="tpu_custom_call" | custom-call | tf_op jit(solution)/shard_map/project/pallas_call | solution.py:692
  85.2 1.6 collective-permute-done.14
  86.9 1.2 add_convert_fusion.4
  88.7 13.4 %collective-permute-done.15.late = bf16[128,2048]{1,0:T(8,128)(2,1)S(1)} collective-permute-done((bf16[128,2048]{1,0:T(8,128)(2,1)S(1)}, bf16[128,2048]{1,0:T(8,128)(2,1)S(1)}, u32[]{:S(2)}, u32[]{:S(2)}) %collective-permute-start.15) | collective-permute-done | bytes 524320 | tf_op jit(solution)/shard_map/ppermute | solution.py:263
  102.1 1.2 copy-done.7
  104.4 0.7 collective-permute-start.17
  105.1 1.9 collective-permute-start.16
  107.0 0.8 route.1
  107.9 4.3 %copy-done.2 = bf16[4,2048,704]{1,2,0:T(8,128)(2,1)S(1)} copy-done((bf16[4,2048,704]{1,2,0:T(8,128)(2,1)S(1)}, bf16[4,2048,704]{1,2,0:T(8,128)(2,1)}, u32[]{:S(2)}) %copy-start.2) | copy-done | bytes 11534360
  112.2 0.8 stage.2.refs_9_
  113.0 4.0 %collective-permute-done.18 = bf16[128,2048]{1,0:T(8,128)(2,1)S(1)} collective-permute-done((bf16[128,2048]{1,0:T(8,128)(2,1)S(1)}, bf16[128,2048]{1,0:T(8,128)(2,1)S(1)}, u32[]{:S(2)}, u32[]{:S(2)}) %collective-permute-start.18) | collective-permute-done | bytes 524320 | tf_op jit(solution)/shard_map/ppermute | solution.py:263
  117.0 1.2 collective-permute-done.16
  118.2 1.4 collective-permute-start.21
  119.6 0.7 collective-permute-start.20
  120.3 3.9 %collective-permute-start.19 = (bf16[128,2048]{1,0:T(8,128)(2,1)S(1)}, bf16[128,2048]{1,0:T(8,128)(2,1)S(1)}, u32[]{:S(2)}, u32[]{:S(2)}) collective-permute-start(bf16[128,2048]{1,0:T(8,128)(2,1)S(1)} %collective-permute-done.17), channel_id=1, source_target_pairs={{0,2},{1,3},{2,0},{3,1},{4,6},{5,7},{6,4},{7,5},{8,10},{9,11},{10,... | collective-permute-start | bytes 1572872 | tf_op jit(solution)/shard_map/ppermute | solution.py:267
  124.2 4.3 %copy-done.3 = bf16[4,704,2048]{2,1,0:T(8,128)(2,1)S(1)} copy-done((bf16[4,704,2048]{2,1,0:T(8,128)(2,1)S(1)}, bf16[4,704,2048]{2,1,0:T(8,128)(2,1)}, u32[]{:S(2)}) %copy-start.3) | copy-done | bytes 11534360
  128.5 0.8 stage.3.refs_11_
  129.6 1.8 convolution_convert_fusion.5.refs_1_
  131.5 2.8 %collective-permute-done.19 = bf16[128,2048]{1,0:T(8,128)(2,1)S(1)} collective-permute-done((bf16[128,2048]{1,0:T(8,128)(2,1)S(1)}, bf16[128,2048]{1,0:T(8,128)(2,1)S(1)}, u32[]{:S(2)}, u32[]{:S(2)}) %collective-permute-start.19) | collective-permute-done | bytes 524320 | tf_op jit(solution)/shard_map/ppermute | solution.py:267
  134.3 2.0 collective-permute-start.22
  136.3 0.7 collective-permute-start.23
  137.3 0.7 collective-permute-start.26
  138.6 8.0 %collective-permute-done.23 = bf16[128,2048]{1,0:T(8,128)(2,1)S(1)} collective-permute-done((bf16[128,2048]{1,0:T(8,128)(2,1)S(1)}, bf16[128,2048]{1,0:T(8,128)(2,1)S(1)}, u32[]{:S(2)}, u32[]{:S(2)}) %collective-permute-start.23) | collective-permute-done | bytes 524320 | tf_op jit(solution)/shard_map/ppermute | solution.py:263
  146.7 1.7 collective-permute-start.25
  149.6 3.6 %collective-permute-done.25 = bf16[64,2048]{1,0:T(8,128)(2,1)S(1)} collective-permute-done((bf16[64,2048]{1,0:T(8,128)(2,1)S(1)}, bf16[64,2048]{1,0:T(8,128)(2,1)S(1)}, u32[]{:S(2)}, u32[]{:S(2)}) %collective-permute-start.25) | collective-permute-done | bytes 262176 | tf_op jit(solution)/shard_map/ppermute | solution.py:267
  153.2 1.6 collective-permute-done.24
  155.4 11.7 %experts.1 = (bf16[128,2048]{1,0:T(8,128)(2,1)S(1)}, bf16[128,2048]{1,0:T(8,128)(2,1)S(1)}, bf16[128,2048]{1,0:T(8,128)(2,1)S(1)}, bf16[128,2048]{1,0:T(8,128)(2...) custom-call(bf16[128,2048]{1,0:T(8,128)(2,1)S(1)} %convolution_conve, ...), custom_call_target="tpu_custom_call" | custom-call | tf_op jit(solution)/shard_map/experts/pallas_call | solution.py:834
  167.1 0.7 collective-permute-start.27
  167.8 0.7 collective-permute-start.29
  168.5 2.7 %collective-permute-start.28 = (bf16[64,2048]{1,0:T(8,128)(2,1)S(1)}, bf16[64,2048]{1,0:T(8,128)(2,1)S(1)}, u32[]{:S(2)}, u32[]{:S(2)}) collective-permute-start(bf16[64,2048]{1,0:T(8,128)(2,1)S(1)} %get-tuple-element.108), channel_id=1, source_target_pairs={{0,2},{1,3},{2,0},{3,1},{4,6},{5,7},{6,4},{7,5},{8,10},{9,11},{10,... | collective-permute-start | bytes 786440 | tf_op jit(solution)/shard_map/ppermute | solution.py:267
  171.2 3.4 %collective-permute-done.27 = bf16[64,2048]{1,0:T(8,128)(2,1)S(1)} collective-permute-done((bf16[64,2048]{1,0:T(8,128)(2,1)S(1)}, bf16[64,2048]{1,0:T(8,128)(2,1)S(1)}, u32[]{:S(2)}, u32[]{:S(2)}) %collective-permute-start.27) | collective-permute-done | bytes 262176 | tf_op jit(solution)/shard_map/ppermute | solution.py:263
  174.6 3.8 %collective-permute-done.28 = bf16[64,2048]{1,0:T(8,128)(2,1)S(1)} collective-permute-done((bf16[64,2048]{1,0:T(8,128)(2,1)S(1)}, bf16[64,2048]{1,0:T(8,128)(2,1)S(1)}, u32[]{:S(2)}, u32[]{:S(2)}) %collective-permute-start.28) | collective-permute-done | bytes 262176 | tf_op jit(solution)/shard_map/ppermute | solution.py:267
  178.6 2.1 collective-permute-start.33
  180.7 1.5 collective-permute-start.32
  182.2 0.7 collective-permute-start.31
  182.9 7.9 %collective-permute-done.33 = bf16[128,2048]{1,0:T(8,128)(2,1)S(1)} collective-permute-done((bf16[128,2048]{1,0:T(8,128)(2,1)S(1)}, bf16[128,2048]{1,0:T(8,128)(2,1)S(1)}, u32[]{:S(2)}, u32[]{:S(2)}) %collective-permute-start.33) | collective-permute-done | bytes 524320 | tf_op jit(solution)/shard_map/ppermute | solution.py:267
  190.8 3.6 %collective-permute-done.32 = bf16[128,2048]{1,0:T(8,128)(2,1)S(1)} collective-permute-done((bf16[128,2048]{1,0:T(8,128)(2,1)S(1)}, bf16[128,2048]{1,0:T(8,128)(2,1)S(1)}, u32[]{:S(2)}, u32[]{:S(2)}) %collective-permute-start.32) | collective-permute-done | bytes 524320 | tf_op jit(solution)/shard_map/ppermute | solution.py:263
  194.6 0.7 collective-permute-start.35
  195.3 2.8 %collective-permute-start.34 = (bf16[128,2048]{1,0:T(8,128)(2,1)S(1)}, bf16[128,2048]{1,0:T(8,128)(2,1)S(1)}, u32[]{:S(2)}, u32[]{:S(2)}) collective-permute-start(bf16[128,2048]{1,0:T(8,128)(2,1)S(1)} %add_convert_fusion.3), channel_id=1, source_target_pairs={{0,2},{1,3},{2,0},{3,1},{4,6},{5,7},{6,4},{7,5},{8,10},{9,11},{10,... | collective-permute-start | bytes 1572872 | tf_op jit(solution)/shard_map/ppermute | solution.py:267
  198.3 3.4 %collective-permute-done.31 = bf16[128,2048]{1,0:T(8,128)(2,1)S(1)} collective-permute-done((bf16[128,2048]{1,0:T(8,128)(2,1)S(1)}, bf16[128,2048]{1,0:T(8,128)(2,1)S(1)}, u32[]{:S(2)}, u32[]{:S(2)}) %collective-permute-start.31) | collective-permute-done | bytes 524320 | tf_op jit(solution)/shard_map/ppermute | solution.py:263
  201.7 6.5 %collective-permute-done.34 = bf16[128,2048]{1,0:T(8,128)(2,1)S(1)} collective-permute-done((bf16[128,2048]{1,0:T(8,128)(2,1)S(1)}, bf16[128,2048]{1,0:T(8,128)(2,1)S(1)}, u32[]{:S(2)}, u32[]{:S(2)}) %collective-permute-start.34) | collective-permute-done | bytes 524320 | tf_op jit(solution)/shard_map/ppermute | solution.py:267
  208.6 3.7 %collective-permute-start.36 = (bf16[128,2048]{1,0:T(8,128)(2,1)S(1)}, bf16[128,2048]{1,0:T(8,128)(2,1)S(1)}, u32[]{:S(2)}, u32[]{:S(2)}) collective-permute-start(bf16[128,2048]{1,0:T(8,128)(2,1)S(1)} %add_convert_fusion.2), channel_id=1, source_target_pairs={{0,2},{1,3},{2,0},{3,1},{4,6},{5,7},{6,4},{7,5},{8,10},{9,11},{10,... | collective-permute-start | bytes 1572872 | tf_op jit(solution)/shard_map/ppermute | solution.py:267
  212.3 0.7 collective-permute-start.37
  213.0 6.5 %collective-permute-done.36 = bf16[128,2048]{1,0:T(8,128)(2,1)S(1)} collective-permute-done((bf16[128,2048]{1,0:T(8,128)(2,1)S(1)}, bf16[128,2048]{1,0:T(8,128)(2,1)S(1)}, u32[]{:S(2)}, u32[]{:S(2)}) %collective-permute-start.36) | collective-permute-done | bytes 524320 | tf_op jit(solution)/shard_map/ppermute | solution.py:267
  219.5 1.2 add_convert_fusion
  (121 shorter events, 9.8 us)
Async XLA Ops:
  6.5 8.4 %copy-start = (bf16[256,2048]{1,0:T(8,128)(2,1)S(1)}, bf16[256,2048]{1,0:T(8,128)(2,1)}, u32[]{:S(2)}) copy-start(bf16[256,2048]{1,0:T(8,128)(2,1)} %param.23) | copy-start | bytes 3145732
  6.5 72.8 %all-gather.2.cloned.1.call-start = ((), (), s32[]{:S(2)}) async-start(), calls=%async_computation | async-start | bytes 2621440 | tf_op jit(solution)/shard_map/all_gather | solution.py:271
  7.1 21.4 %copy-start.21 = (s32[128,4]{0,1:T(4,128)S(1)}, s32[128,4]{0,1:T(4,128)}, u32[]{:S(2)}) copy-start(s32[128,4]{0,1:T(4,128)} %param.25) | copy-start | bytes 6148
  7.1 21.5 %copy-start.22 = (bf16[128,4]{0,1:T(4,128)(2,1)S(1)}, bf16[128,4]{0,1:T(4,128)(2,1)}, u32[]{:S(2)}) copy-start(bf16[128,4]{0,1:T(4,128)(2,1)} %param.26) | copy-start | bytes 3076
  7.1 22.0 %copy-start.20 = (bf16[2048]{0:T(1024)(128)(2,1)S(1)}, bf16[2048]{0:T(1024)(128)(2,1)}, u32[]{:S(2)}) copy-start(bf16[2048]{0:T(1024)(128)(2,1)} %param.24) | copy-start | bytes 12292
  7.1 23.0 %copy-start.5 = (bf16[4,1024,256]{2,1,0:T(8,128)(2,1)S(1)}, bf16[4,1024,256]{2,1,0:T(8,128)(2,1)}, u32[]{:S(2)}) copy-start(bf16[4,1024,256]{2,1,0:T(8,128)(2,1)} %pk.5) | copy-start | bytes 6291460
  7.1 23.0 %copy-start.11 = (s32[2]{0:T(128)S(1)}, s32[2]{0:T(128)}, u32[]{:S(2)}) copy-start(s32[2]{0:T(128)} %pad_add_fusion.sc_ref) | copy-start | bytes 28
  11.4 18.7 %collective-permute-start.2 = (bf16[2,4,1024,128]{3,2,1,0:T(8,128)(2,1)}, bf16[2,4,1024,128]{3,2,1,0:T(8,128)(2,1)}, u32[]{:S(2)}, u32[]{:S(2)}) collective-permute-start(bf16[2,4,1024,128]{3,2,1,0:T(8,128)(2,1)} %get-tuple-element.68), channel_id=1, source_target_pairs={{0,8},{8,0},{16,24},{24,16},{1,9},{9,1},{17,25},{25,17},{2,10},{10... | collective-permute-start | bytes 6291464 | tf_op jit(solution)/shard_map/ppermute | solution.py:255
  11.9 5.8 %collective-permute-start.1 = (bf16[3,1024,128]{2,1,0:T(8,128)(2,1)}, bf16[3,1024,128]{2,1,0:T(8,128)(2,1)}, u32[]{:S(2)}, u32[]{:S(2)}) collective-permute-start(bf16[3,1024,128]{2,1,0:T(8,128)(2,1)} %get-tuple-element.65), channel_id=1, source_target_pairs={{0,8},{8,0},{16,24},{24,16},{1,9},{9,1},{17,25},{25,17},{2,10},{10... | collective-permute-start | bytes 2359304 | tf_op jit(solution)/shard_map/ppermute | solution.py:255
  12.0 15.4 %collective-permute-start.3 = (bf16[1024,256]{1,0:T(8,128)(2,1)}, bf16[1024,256]{1,0:T(8,128)(2,1)}, u32[]{:S(2)}, u32[]{:S(2)}) collective-permute-start(bf16[1024,256]{1,0:T(8,128)(2,1)} %q0.1), channel_id=1, source_target_pairs={{0,16},{8,24},{16,0},{24,8},{1,17},{9,25},{17,1},{25,9},{2,18},{10... | collective-permute-start | bytes 1572872 | tf_op jit(solution)/shard_map/ppermute | solution.py:259
  16.6 1.2 copy-start.13
  16.6 10.9 %collective-permute-start.4 = (s32[1,16]{1,0:T(1,128)S(1)}, s32[1,16]{1,0:T(1,128)S(1)}, u32[]{:S(2)}, u32[]{:S(2)}) collective-permute-start(s32[1,16]{1,0:T(1,128)S(1)} %pad_add_fusion.1.shape_a), channel_id=1, source_target_pairs={{0,16},{8,24},{16,0},{24,8},{1,17},{9,25},{17,1},{25,9},{2,18},{10... | collective-permute-start | bytes 200 | tf_op jit(solution)/shard_map/ppermute | solution.py:259
  16.6 1.2 collective-permute-start
  16.7 13.5 %copy-start.6 = (bf16[4,1024,256]{2,1,0:T(8,128)(2,1)S(1)}, bf16[4,1024,256]{2,1,0:T(8,128)(2,1)}, u32[]{:S(2)}) copy-start(bf16[4,1024,256]{2,1,0:T(8,128)(2,1)} %pv.5) | copy-start | bytes 6291460
  28.5 1.6 collective-permute-start.6
  28.6 1.5 collective-permute-start.5
  29.2 17.0 %copy-start.8 = (bf16[1024,256]{1,0:T(8,128)(2,1)S(1)}, bf16[1024,256]{1,0:T(8,128)(2,1)}, u32[]{:S(2)}) copy-start(bf16[1024,256]{1,0:T(8,128)(2,1)} %q0.1) | copy-start | bytes 1572868
  29.2 17.0 %copy-start.14 = (s32[1,16]{1,0:T(1,128)S(1)}, s32[1,16]{1,0:T(1,128)}, u32[]{:S(2)}) copy-start(s32[1,16]{1,0:T(1,128)} %copy-done.13) | copy-start | bytes 196
  29.2 17.0 %copy-start.16 = (s32[1,16]{1,0:T(1,128)S(1)}, s32[1,16]{1,0:T(1,128)}, u32[]{:S(2)}) copy-start(s32[1,16]{1,0:T(1,128)} %copy-done.15) | copy-start | bytes 196
  44.1 15.3 %collective-permute-start.8 = (f32[2,8,128]{2,1,0:T(8,128)S(1)}, f32[2,8,128]{2,1,0:T(8,128)S(1)}, u32[]{:S(2)}, u32[]{:S(2)}) collective-permute-start(f32[2,8,128]{2,1,0:T(8,128)S(1)} %get-tuple-element.75), channel_id=1, source_target_pairs={{0,16},{8,24},{16,0},{24,8},{1,17},{9,25},{17,1},{25,9},{2,18},{10... | collective-permute-start | bytes 24584 | tf_op jit(solution)/shard_map/ppermute | solution.py:259
  44.9 14.5 %copy-start.4 = (f32[2048,128]{1,0:T(8,128)S(1)}, f32[2048,128]{1,0:T(8,128)}, u32[]{:S(2)}) copy-start(f32[2048,128]{1,0:T(8,128)} %get-tuple-element.66.refs_0_.refs_6_) | copy-start | bytes 3145732
  44.9 14.5 %copy-start.10 = (f32[2,8,128]{2,1,0:T(8,128)S(1)}, f32[2,8,128]{2,1,0:T(8,128)}, u32[]{:S(2)}) copy-start(f32[2,8,128]{2,1,0:T(8,128)} %get-tuple-element.67.refs_1_.refs_7_) | copy-start | bytes 24580
  44.9 14.5 %collective-permute-start.7 = (bf16[2048,128]{1,0:T(8,128)(2,1)S(1)}, bf16[2048,128]{1,0:T(8,128)(2,1)S(1)}, u32[]{:S(2)}, u32[]{:S(2)}) collective-permute-start(bf16[2048,128]{1,0:T(8,128)(2,1)S(1)} %get-tuple-element.74), channel_id=1, source_target_pairs={{0,16},{8,24},{16,0},{24,8},{1,17},{9,25},{17,1},{25,9},{2,18},{10... | collective-permute-start | bytes 1572872 | tf_op jit(solution)/shard_map/ppermute | solution.py:259
  59.3 42.7 %copy-start.9 = (bf16[128,2048]{1,0:T(8,128)(2,1)S(1)}, bf16[128,2048]{1,0:T(8,128)(2,1)}, u32[]{:S(2)}) copy-start(bf16[128,2048]{1,0:T(8,128)(2,1)} %residual.1) | copy-start | bytes 1572868
  59.3 47.7 %copy-start.12 = (s32[2]{0:T(128)S(1)}, s32[2]{0:T(128)}, u32[]{:S(2)}) copy-start(s32[2]{0:T(128)} %pad_add_fusion.sc_ref) | copy-start | bytes 28
  62.3 8.4 %collective-permute-start.11 = (bf16[2,272,128]{2,1,0:T(8,128)(2,1)S(1)}, bf16[2,272,128]{2,1,0:T(8,128)(2,1)S(1)}, u32[]{:S(2)}, u32[]{:S(2)}) collective-permute-start(bf16[2,272,128]{2,1,0:T(8,128)(2,1)S(1)} %get-tuple-element.125), channel_id=1, source_target_pairs={{0,6},{1,7},{2,4},{3,5},{4,2},{5,3},{6,0},{7,1},{8,14},{9,15},{10,... | collective-permute-start | bytes 417800 | tf_op jit(solution)/shard_map/ppermute | solution.py:657
  66.1 11.6 %collective-permute-start.10 = (bf16[2,272,128]{2,1,0:T(8,128)(2,1)S(1)}, bf16[2,272,128]{2,1,0:T(8,128)(2,1)S(1)}, u32[]{:S(2)}, u32[]{:S(2)}) collective-permute-start(bf16[2,272,128]{2,1,0:T(8,128)(2,1)S(1)} %get-tuple-element.126), channel_id=1, source_target_pairs={{0,4},{1,5},{2,6},{3,7},{4,0},{5,1},{6,2},{7,3},{8,12},{9,13},{10,... | collective-permute-start | bytes 417800 | tf_op jit(solution)/shard_map/ppermute | solution.py:657
  66.1 11.6 %collective-permute-start.9 = (bf16[2,272,128]{2,1,0:T(8,128)(2,1)S(1)}, bf16[2,272,128]{2,1,0:T(8,128)(2,1)S(1)}, u32[]{:S(2)}, u32[]{:S(2)}) collective-permute-start(bf16[2,272,128]{2,1,0:T(8,128)(2,1)S(1)} %get-tuple-element.127), channel_id=1, source_target_pairs={{0,2},{1,3},{2,0},{3,1},{4,6},{5,7},{6,4},{7,5},{8,10},{9,11},{10,... | collective-permute-start | bytes 417800 | tf_op jit(solution)/shard_map/ppermute | solution.py:657
  70.7 8.6 %copy-start.17 = (bf16[2,272,128]{2,1,0:T(8,128)(2,1)}, bf16[2,272,128]{2,1,0:T(8,128)(2,1)S(1)}, u32[]{:S(2)}) copy-start(bf16[2,272,128]{2,1,0:T(8,128)(2,1)S(1)} %collective-permute-done.11.refs_3_) | copy-start | bytes 417796
  77.7 1.6 copy-start.18
  77.7 1.6 copy-start.19
  77.7 7.0 %collective-permute-start.13 = (bf16[4,16,128]{2,1,0:T(8,128)(2,1)S(1)}, bf16[4,16,128]{2,1,0:T(8,128)(2,1)S(1)}, u32[]{:S(2)}, u32[]{:S(2)}) collective-permute-start(bf16[4,16,128]{2,1,0:T(8,128)(2,1)S(1)} %pad_maximum_fusion.3.refs_0_), channel_id=1, source_target_pairs={{0,1},{1,0},{2,3},{3,2},{4,5},{5,4},{6,7},{7,6},{8,9},{9,8},{10,11... | collective-permute-start | bytes 49160 | tf_op jit(solution)/shard_map/ppermute | solution.py:263
  84.7 2.2 collective-permute-start.14
  84.7 3.9 %collective-permute-start.12 = (bf16[128,2048]{1,0:T(8,128)(2,1)}, bf16[128,2048]{1,0:T(8,128)(2,1)S(1)}, u32[]{:S(2)}, u32[]{:S(2)}) collective-permute-start(bf16[128,2048]{1,0:T(8,128)(2,1)} %get-tuple-element.77), channel_id=1, source_target_pairs={{0,8},{8,0},{16,24},{24,16},{1,9},{9,1},{17,25},{25,17},{2,10},{10... | collective-permute-start | bytes 1572872 | tf_op jit(solution)/shard_map/ppermute | solution.py:255
  88.0 14.0 %collective-permute-start.15 = (bf16[128,2048]{1,0:T(8,128)(2,1)S(1)}, bf16[128,2048]{1,0:T(8,128)(2,1)S(1)}, u32[]{:S(2)}, u32[]{:S(2)}) collective-permute-start(bf16[128,2048]{1,0:T(8,128)(2,1)S(1)} %add_convert_fusion.4), channel_id=1, source_target_pairs={{0,1},{1,0},{2,3},{3,2},{4,5},{5,4},{6,7},{7,6},{8,9},{9,8},{10,11... | collective-permute-start | bytes 1572872 | tf_op jit(solution)/shard_map/ppermute | solution.py:263
  102.1 1.2 copy-start.7
  103.8 13.2 %collective-permute-start.18 = (bf16[128,2048]{1,0:T(8,128)(2,1)S(1)}, bf16[128,2048]{1,0:T(8,128)(2,1)S(1)}, u32[]{:S(2)}, u32[]{:S(2)}) collective-permute-start(bf16[128,2048]{1,0:T(8,128)(2,1)S(1)} %get-tuple-element.87), channel_id=1, source_target_pairs={{0,1},{1,0},{2,3},{3,2},{4,5},{5,4},{6,7},{7,6},{8,9},{9,8},{10,11... | collective-permute-start | bytes 1572872 | tf_op jit(solution)/shard_map/ppermute | solution.py:263
  104.4 12.5 %collective-permute-start.17 = (bf16[128,2048]{1,0:T(8,128)(2,1)S(1)}, bf16[128,2048]{1,0:T(8,128)(2,1)S(1)}, u32[]{:S(2)}, u32[]{:S(2)}) collective-permute-start(bf16[128,2048]{1,0:T(8,128)(2,1)S(1)} %get-tuple-element.87), channel_id=1, source_target_pairs={{2,4},{3,5},{4,2},{5,3},{10,12},{11,13},{12,10},{13,11},{18,20},{1... | collective-permute-start | bytes 1572872 | tf_op jit(solution)/shard_map/ppermute | solution.py:277
  105.1 13.0 %collective-permute-start.16 = (bf16[128,2048]{1,0:T(8,128)(2,1)S(1)}, bf16[128,2048]{1,0:T(8,128)(2,1)}, u32[]{:S(2)}, u32[]{:S(2)}) collective-permute-start(bf16[128,2048]{1,0:T(8,128)(2,1)S(1)} %get-tuple-element.87), channel_id=1, source_target_pairs={{0,2},{1,3},{2,0},{3,1},{4,6},{5,7},{6,4},{7,5},{8,10},{9,11},{10,... | collective-permute-start | bytes 1572872 | tf_op jit(solution)/shard_map/ppermute | solution.py:267
  107.9 4.3 %copy-start.2 = (bf16[4,2048,704]{1,2,0:T(8,128)(2,1)S(1)}, bf16[4,2048,704]{1,2,0:T(8,128)(2,1)}, u32[]{:S(2)}) copy-start(bf16[4,2048,704]{1,2,0:T(8,128)(2,1)} %param.27) | copy-start | bytes 34603012
  118.2 16.1 %collective-permute-start.21 = (bf16[128,2048]{1,0:T(8,128)(2,1)}, bf16[128,2048]{1,0:T(8,128)(2,1)S(1)}, u32[]{:S(2)}, u32[]{:S(2)}) collective-permute-start(bf16[128,2048]{1,0:T(8,128)(2,1)} %collective-permute-done.16), channel_id=1, source_target_pairs={{0,1},{1,0},{2,3},{3,2},{4,5},{5,4},{6,7},{7,6},{8,9},{9,8},{10,11... | collective-permute-start | bytes 1572872 | tf_op jit(solution)/shard_map/ppermute | solution.py:263
  119.6 14.7 %collective-permute-start.20 = (bf16[128,2048]{1,0:T(8,128)(2,1)}, bf16[128,2048]{1,0:T(8,128)(2,1)S(1)}, u32[]{:S(2)}, u32[]{:S(2)}) collective-permute-start(bf16[128,2048]{1,0:T(8,128)(2,1)} %collective-permute-done.16), channel_id=1, source_target_pairs={{2,4},{3,5},{4,2},{5,3},{10,12},{11,13},{12,10},{13,11},{18,20},{1... | collective-permute-start | bytes 1572872 | tf_op jit(solution)/shard_map/ppermute | solution.py:277
  120.3 14.0 %collective-permute-start.19 = (bf16[128,2048]{1,0:T(8,128)(2,1)S(1)}, bf16[128,2048]{1,0:T(8,128)(2,1)S(1)}, u32[]{:S(2)}, u32[]{:S(2)}) collective-permute-start(bf16[128,2048]{1,0:T(8,128)(2,1)S(1)} %collective-permute-done.17), channel_id=1, source_target_pairs={{0,2},{1,3},{2,0},{3,1},{4,6},{5,7},{6,4},{7,5},{8,10},{9,11},{10,... | collective-permute-start | bytes 1572872 | tf_op jit(solution)/shard_map/ppermute | solution.py:267
  124.2 4.3 %copy-start.3 = (bf16[4,704,2048]{2,1,0:T(8,128)(2,1)S(1)}, bf16[4,704,2048]{2,1,0:T(8,128)(2,1)}, u32[]{:S(2)}) copy-start(bf16[4,704,2048]{2,1,0:T(8,128)(2,1)} %source) | copy-start | bytes 34603012
  128.5 26.9 %slice-start = ((s8[11534336]{0:T(1024)(128)(4,1)}), s8[4194304]{0:T(1024)(128)(4,1)S(1)}, s32[]{:S(2)}) async-start(s8[11534336]{0:T(1024)(128)(4,1)} %bitcast.40), calls=%async_computation.1 | async-start | bytes 8388608
  128.5 26.9 %slice-start.1 = ((s8[11534336]{0:T(1024)(128)(4,1)}), s8[4194304]{0:T(1024)(128)(4,1)S(1)}, s32[]{:S(2)}) async-start(s8[11534336]{0:T(1024)(128)(4,1)} %bitcast.40), calls=%async_computation.2 | async-start | bytes 8388608
  131.5 24.0 %slice-start.2 = ((s8[11534336]{0:T(1024)(128)(4,1)}), s8[3145728]{0:T(1024)(128)(4,1)S(1)}, s32[]{:S(2)}) async-start(s8[11534336]{0:T(1024)(128)(4,1)} %bitcast.40), calls=%async_computation.3 | async-start | bytes 6291456
  134.3 12.3 %collective-permute-start.22 = (bf16[128,2048]{1,0:T(8,128)(2,1)S(1)}, bf16[128,2048]{1,0:T(8,128)(2,1)S(1)}, u32[]{:S(2)}, u32[]{:S(2)}) collective-permute-start(bf16[128,2048]{1,0:T(8,128)(2,1)S(1)} %collective-permute-done.20), channel_id=1, source_target_pairs={{0,2},{1,3},{2,0},{3,1},{4,6},{5,7},{6,4},{7,5},{8,10},{9,11},{10,... | collective-permute-start | bytes 1572872 | tf_op jit(solution)/shard_map/ppermute | solution.py:267
  136.3 10.3 %collective-permute-start.23 = (bf16[128,2048]{1,0:T(8,128)(2,1)S(1)}, bf16[128,2048]{1,0:T(8,128)(2,1)S(1)}, u32[]{:S(2)}, u32[]{:S(2)}) collective-permute-start(bf16[128,2048]{1,0:T(8,128)(2,1)S(1)} %broadcast_select_fusion.1), channel_id=1, source_target_pairs={{0,1},{1,0},{2,3},{3,2},{4,5},{5,4},{6,7},{7,6},{8,9},{9,8},{10,11... | collective-permute-start | bytes 1572872 | tf_op jit(solution)/shard_map/ppermute | solution.py:263
  137.3 12.2 %collective-permute-start.26 = (bf16[64,2048]{1,0:T(8,128)(2,1)S(1)}, bf16[64,2048]{1,0:T(8,128)(2,1)S(1)}, u32[]{:S(2)}, u32[]{:S(2)}) collective-permute-start(bf16[64,2048]{1,0:T(8,128)(2,1)S(1)} %slice.92), channel_id=1, source_target_pairs={{2,4},{3,5},{4,2},{5,3},{10,12},{11,13},{12,10},{13,11},{18,20},{1... | collective-permute-start | bytes 786440 | tf_op jit(solution)/shard_map/ppermute | solution.py:277
  146.7 6.4 %collective-permute-start.25 = (bf16[64,2048]{1,0:T(8,128)(2,1)S(1)}, bf16[64,2048]{1,0:T(8,128)(2,1)S(1)}, u32[]{:S(2)}, u32[]{:S(2)}) collective-permute-start(bf16[64,2048]{1,0:T(8,128)(2,1)S(1)} %slice.91), channel_id=1, source_target_pairs={{0,2},{1,3},{2,0},{3,1},{4,6},{5,7},{6,4},{7,5},{8,10},{9,11},{10,... | collective-permute-start | bytes 786440 | tf_op jit(solution)/shard_map/ppermute | solution.py:267
  148.4 6.4 %collective-permute-start.24 = (bf16[64,2048]{1,0:T(8,128)(2,1)S(1)}, bf16[64,2048]{1,0:T(8,128)(2,1)S(1)}, u32[]{:S(2)}, u32[]{:S(2)}) collective-permute-start(bf16[64,2048]{1,0:T(8,128)(2,1)S(1)} %slice.109), channel_id=1, source_target_pairs={{0,1},{1,0},{2,3},{3,2},{4,5},{5,4},{6,7},{7,6},{8,9},{9,8},{10,11... | collective-permute-start | bytes 786440 | tf_op jit(solution)/shard_map/ppermute | solution.py:263
  155.4 65.2 %copy-start.1 = (bf16[256,2048]{1,0:T(8,128)(2,1)S(1)}, bf16[256,2048]{1,0:T(8,128)(2,1)}, u32[]{:S(2)}) copy-start(bf16[256,2048]{1,0:T(8,128)(2,1)} %param.23) | copy-start | bytes 3145732
  167.1 7.5 %collective-permute-start.27 = (bf16[64,2048]{1,0:T(8,128)(2,1)S(1)}, bf16[64,2048]{1,0:T(8,128)(2,1)S(1)}, u32[]{:S(2)}, u32[]{:S(2)}) collective-permute-start(bf16[64,2048]{1,0:T(8,128)(2,1)S(1)} %get-tuple-element.107), channel_id=1, source_target_pairs={{0,1},{1,0},{2,3},{3,2},{4,5},{5,4},{6,7},{7,6},{8,9},{9,8},{10,11... | collective-permute-start | bytes 786440 | tf_op jit(solution)/shard_map/ppermute | solution.py:263
  167.8 6.8 %collective-permute-start.29 = (bf16[64,2048]{1,0:T(8,128)(2,1)S(1)}, bf16[64,2048]{1,0:T(8,128)(2,1)S(1)}, u32[]{:S(2)}, u32[]{:S(2)}) collective-permute-start(bf16[64,2048]{1,0:T(8,128)(2,1)S(1)} %get-tuple-element.108), channel_id=1, source_target_pairs={{2,4},{3,5},{4,2},{5,3},{10,12},{11,13},{12,10},{13,11},{18,20},{1... | collective-permute-start | bytes 786440 | tf_op jit(solution)/shard_map/ppermute | solution.py:277
  168.5 9.9 %collective-permute-start.28 = (bf16[64,2048]{1,0:T(8,128)(2,1)S(1)}, bf16[64,2048]{1,0:T(8,128)(2,1)S(1)}, u32[]{:S(2)}, u32[]{:S(2)}) collective-permute-start(bf16[64,2048]{1,0:T(8,128)(2,1)S(1)} %get-tuple-element.108), channel_id=1, source_target_pairs={{0,2},{1,3},{2,0},{3,1},{4,6},{5,7},{6,4},{7,5},{8,10},{9,11},{10,... | collective-permute-start | bytes 786440 | tf_op jit(solution)/shard_map/ppermute | solution.py:267
  178.6 12.2 %collective-permute-start.33 = (bf16[128,2048]{1,0:T(8,128)(2,1)S(1)}, bf16[128,2048]{1,0:T(8,128)(2,1)S(1)}, u32[]{:S(2)}, u32[]{:S(2)}) collective-permute-start(bf16[128,2048]{1,0:T(8,128)(2,1)S(1)} %pad_maximum_fusion.2), channel_id=1, source_target_pairs={{0,2},{1,3},{2,0},{3,1},{4,6},{5,7},{6,4},{7,5},{8,10},{9,11},{10,... | collective-permute-start | bytes 1572872 | tf_op jit(solution)/shard_map/ppermute | solution.py:267
  180.7 13.6 %collective-permute-start.32 = (bf16[128,2048]{1,0:T(8,128)(2,1)S(1)}, bf16[128,2048]{1,0:T(8,128)(2,1)S(1)}, u32[]{:S(2)}, u32[]{:S(2)}) collective-permute-start(bf16[128,2048]{1,0:T(8,128)(2,1)S(1)} %pad_maximum_fusion.1), channel_id=1, source_target_pairs={{0,1},{1,0},{2,3},{3,2},{4,5},{5,4},{6,7},{7,6},{8,9},{9,8},{10,11... | collective-permute-start | bytes 1572872 | tf_op jit(solution)/shard_map/ppermute | solution.py:263
  182.2 19.5 %collective-permute-start.31 = (bf16[128,2048]{1,0:T(8,128)(2,1)S(1)}, bf16[128,2048]{1,0:T(8,128)(2,1)S(1)}, u32[]{:S(2)}, u32[]{:S(2)}) collective-permute-start(bf16[128,2048]{1,0:T(8,128)(2,1)S(1)} %get-tuple-element.111), channel_id=1, source_target_pairs={{0,1},{1,0},{2,3},{3,2},{4,5},{5,4},{6,7},{7,6},{8,9},{9,8},{10,11... | collective-permute-start | bytes 1572872 | tf_op jit(solution)/shard_map/ppermute | solution.py:263
  194.6 7.1 %collective-permute-start.35 = (bf16[128,2048]{1,0:T(8,128)(2,1)S(1)}, bf16[128,2048]{1,0:T(8,128)(2,1)S(1)}, u32[]{:S(2)}, u32[]{:S(2)}) collective-permute-start(bf16[128,2048]{1,0:T(8,128)(2,1)S(1)} %add_convert_fusion.3), channel_id=1, source_target_pairs={{2,4},{3,5},{4,2},{5,3},{10,12},{11,13},{12,10},{13,11},{18,20},{1... | collective-permute-start | bytes 1572872 | tf_op jit(solution)/shard_map/ppermute | solution.py:277
  195.3 12.9 %collective-permute-start.34 = (bf16[128,2048]{1,0:T(8,128)(2,1)S(1)}, bf16[128,2048]{1,0:T(8,128)(2,1)S(1)}, u32[]{:S(2)}, u32[]{:S(2)}) collective-permute-start(bf16[128,2048]{1,0:T(8,128)(2,1)S(1)} %add_convert_fusion.3), channel_id=1, source_target_pairs={{0,2},{1,3},{2,0},{3,1},{4,6},{5,7},{6,4},{7,5},{8,10},{9,11},{10,... | collective-permute-start | bytes 1572872 | tf_op jit(solution)/shard_map/ppermute | solution.py:267
  198.2 14.8 %collective-permute-start.30 = (bf16[128,2048]{1,0:T(8,128)(2,1)S(1)}, bf16[128,2048]{1,0:T(8,128)(2,1)S(1)}, u32[]{:S(2)}, u32[]{:S(2)}) collective-permute-start(bf16[128,2048]{1,0:T(8,128)(2,1)S(1)} %pad_maximum_fusion), channel_id=1, source_target_pairs={{0,1},{1,0},{2,3},{3,2},{4,5},{5,4},{6,7},{7,6},{8,9},{9,8},{10,11... | collective-permute-start | bytes 1572872 | tf_op jit(solution)/shard_map/ppermute | solution.py:263
  208.6 10.9 %collective-permute-start.36 = (bf16[128,2048]{1,0:T(8,128)(2,1)S(1)}, bf16[128,2048]{1,0:T(8,128)(2,1)S(1)}, u32[]{:S(2)}, u32[]{:S(2)}) collective-permute-start(bf16[128,2048]{1,0:T(8,128)(2,1)S(1)} %add_convert_fusion.2), channel_id=1, source_target_pairs={{0,2},{1,3},{2,0},{3,1},{4,6},{5,7},{6,4},{7,5},{8,10},{9,11},{10,... | collective-permute-start | bytes 1572872 | tf_op jit(solution)/shard_map/ppermute | solution.py:267
  212.3 7.2 %collective-permute-start.37 = (bf16[128,2048]{1,0:T(8,128)(2,1)S(1)}, bf16[128,2048]{1,0:T(8,128)(2,1)S(1)}, u32[]{:S(2)}, u32[]{:S(2)}) collective-permute-start(bf16[128,2048]{1,0:T(8,128)(2,1)S(1)} %add_convert_fusion.1), channel_id=1, source_target_pairs={{2,4},{3,5},{4,2},{5,3},{10,12},{11,13},{12,10},{13,11},{18,20},{1... | collective-permute-start | bytes 1572872 | tf_op jit(solution)/shard_map/ppermute | solution.py:277
  (1 other events, 0.5 us)
Sparse Core Ops, SparseCore 0:
  15.9 46.2 all-gather.1
